TPU v7x, 32 devices: a whole 2x2x4 slice. The times are simulated.
32 devices in a mesh: section: 2 (over x), seq: 4 (over y, core), dp: 4 (over z).
Axes of the slice: x: 2, y: 2, z: 4, core: 2. Of those that a mesh axis runs over, the one named last changes fastest.
Arguments:
- frozen_queries: bfloat16 [2, 4, 512, 4096], P('section', 'dp', 'seq'), may hold values from -128 to 128
- key_value_pairs: bfloat16 [2, 4, 512, 1024], P('section', 'dp', 'seq'), may hold values from -8 to 8
- adapter_input: bfloat16 [2, 4, 512, 64], P('section', 'dp', 'seq'), may hold values from -6 to 6
- adapter_up_matrix: bfloat16 [2, 64, 4096], P('section', None, 'seq'), may hold values from -0.75 to 0.75
- upstream: bfloat16 [2, 4, 512, 4096], P('section', 'dp', 'seq'), may hold values from -6 to 6
- document_index: int32 [2, 4, 512], P('section', 'dp'), may hold values from 0 to 15, as said below
Outputs:
- query_gradient: bfloat16 [2, 4, 512, 4096], P('section', 'dp', 'seq')
- key_value_gradient: bfloat16 [2, 4, 512, 1024], P('section', 'dp', 'seq')
- adapter_input_gradient: bfloat16 [2, 4, 512, 64], P('section', 'dp', 'seq')
- adapter_up_gradient: float32 [2, 64, 4096], P('section', 'dp', 'seq')
Inputs may be any that keep to these rules, and one draw needn't show every extreme that they name: `document_index`: along each pack the numbers never fall; every number appears; every document spans at most 64 positions, and one document of each pack spans exactly that many.
All inputs are finite; a program needn't handle non-finite values.
Results may differ from a plain program's by a relative error of at most 0.014.
Values may be sent and summed in bfloat16 or wider, within the bound.
No kernel may reach another device: no remote copies, remote signals or barrier semaphores. Data moves between devices by JAX's collectives and lax.ppermute only.
A program may use at most 64 MiB of HBM per device.

v0:
```python
import functools
import math
from types import SimpleNamespace

import jax
import jax.numpy as jnp
from jax import lax
from jax.experimental import pallas as pl
from jax.experimental.pallas import tpu as pltpu
from jax.sharding import PartitionSpec as P

QUERY_HEADS = 32
HK = 4
HEAD_SIZE = 128
PAIR = 2 * HEAD_SIZE
SCALE = 1.0 / math.sqrt(HEAD_SIZE)
SPAN_PARTS = 8
BLOCKS = 2
COPIES = 4
LIMIT = 16 * 1024 * 1024
IN = "_in"
IN_HBM = ("upstream", "pairs", "matrix", "dq", "dq" + IN)
VMEM = pl.BlockSpec(memory_space=pltpu.VMEM)
HBM = pl.BlockSpec(memory_space=pltpu.HBM)


def passed_along(value, axis, steps):
    count = lax.axis_size(axis)
    pairs = [(source, (source + steps) % count) for source in range(count)]
    return lax.ppermute(value, axis, pairs)


def dot(left, right, left_dim, right_dim):
    return lax.dot_general(
        left, right, (((left_dim,), (right_dim,)), ((), ())), preferred_element_type=jnp.float32
    )


def numbered(name, arrays):
    return {name + str(index): array for index, array in enumerate(arrays)}


def listed(refs, name):
    found = []
    while hasattr(refs, name + str(len(found))):
        found.append(getattr(refs, name + str(len(found))))
    return found


def run(body, sizes, inputs, outputs, scratch, flops=0):
    names = list(inputs) + list(outputs) + list(scratch)

    def kernel(*refs):
        body(sizes, SimpleNamespace(**dict(zip(names, refs))))

    operands = [
        pltpu.with_memory_space_constraint(array, pltpu.HBM) if name in IN_HBM[:3] else array
        for name, array in inputs.items()
    ]
    places = list(inputs)
    aliases = {
        places.index(name + IN): index
        for index, name in enumerate(outputs)
        if name + IN in inputs
    }
    results = pl.pallas_call(
        kernel,
        in_specs=[HBM if name in IN_HBM else VMEM for name in inputs],
        out_specs=[HBM if name in IN_HBM else VMEM for name in outputs],
        out_shape=[jax.ShapeDtypeStruct(shape, kind) for shape, kind in outputs.values()],
        scratch_shapes=list(scratch.values()),
        input_output_aliases=aliases,
        compiler_params=pltpu.CompilerParams(vmem_limit_bytes=LIMIT),
        cost_estimate=pl.CostEstimate(
            flops=flops, bytes_accessed=1024 * 1024, transcendentals=flops // 1024
        ),
        name=body.__name__,
    )(*operands)
    return SimpleNamespace(**dict(zip(outputs, results)))


def copy_rows(source, target, sems, copies):
    rows = source.shape[0] // COPIES
    for part in range(COPIES):
        piece = pl.ds(part * rows, rows)
        copies.append(
            pltpu.make_async_copy(source.at[piece], target.at[piece], sems.at[len(copies)])
        )
        copies[-1].start()


def chunk_at(step, chunks):
    return lax.rem(lax.axis_index("seq") + (2 * chunks - 1 - step), chunks)


def chunk_columns(z, step):
    return pl.ds(pl.multiple_of(chunk_at(step, z.chunks) * z.width, HEAD_SIZE), z.width)


def pair_columns(z, step):
    return pl.ds(pl.multiple_of(chunk_at(step, z.chunks) * PAIR, HEAD_SIZE), PAIR)


def split_first(z, refs):
    copies = []
    for step in (0, 1):
        target = refs.piece.at[:, pl.ds(step * z.width, z.width)]
        copy_rows(refs.upstream.at[:, chunk_columns(z, step)], target, refs.sems, copies)
    for copy in copies:
        copy.wait()


def split_rest(z, refs):
    copies = []
    pieces = listed(refs, "piece")
    for step, piece in zip(range(2, z.chunks - 1), pieces):
        copy_rows(refs.upstream.at[:, chunk_columns(z, step)], piece, refs.sems, copies)
    for index, piece in enumerate(pieces[-BLOCKS:]):
        rows = pl.ds(index * z.block, z.block)
        source = refs.upstream.at[rows, chunk_columns(z, z.chunks - 1)]
        copy_rows(source, piece, refs.sems, copies)
    copy_rows(refs.matrix, refs.matrix_copy, refs.sems, copies)
    if hasattr(refs, "bundle"):
        near = refs.pairs.at[pl.ds(z.rows - z.span, z.span)]
        copy_rows(near, refs.bundle.at[pl.ds(0, z.span)], refs.sems, copies)
        copy_rows(refs.matrix, refs.bundle.at[pl.ds(z.span, z.rank)], refs.sems, copies)
    for copy in copies:
        copy.wait()


def stacked(array, rows):
    heads = array.shape[1] // HEAD_SIZE
    parts = [array[rows, head * HEAD_SIZE : (head + 1) * HEAD_SIZE] for head in range(heads)]
    return jnp.concatenate(parts, axis=0)


def seen_rows(z, refs, step, second):
    per_head = z.chunks // HK
    chunk = chunk_at(step, z.chunks)
    place = lax.div(chunk, per_head) if per_head > 1 else chunk
    start = pl.multiple_of(place * PAIR + second * HEAD_SIZE, HEAD_SIZE)
    columns = pl.ds(start, HEAD_SIZE)
    return jnp.concatenate([refs.halo[: z.span, columns], refs.own[:, columns]], axis=0)


def windowed(z, array, index):
    return array[index * z.block : index * z.block + z.window]


def softmax_blocks(z, refs, step, matrix, keys):
    queries = refs.fq[:, chunk_columns(z, step)].astype(jnp.float32)
    queries = (queries + dot(refs.at[...], matrix, 0, 0)).astype(jnp.bfloat16)
    stacks, probs = [], []
    for index in range(BLOCKS):
        stack = stacked(queries, slice(index * z.block, (index + 1) * z.block))
        hidden = refs.bias[index * z.window : (index + 1) * z.window]
        scores = dot(windowed(z, keys, index), stack, 1, 1) * SCALE
        scores += jnp.concatenate([hidden] * (stack.shape[0] // hidden.shape[1]), axis=1)
        shifted = jnp.exp(scores - jnp.max(scores, axis=0, keepdims=True))
        stacks.append(stack)
        probs.append(shifted * (1.0 / jnp.sum(shifted, axis=0, keepdims=True)))
    return stacks, probs


def score_grads(z, index, probs, keys, values, cot_stack):
    dprobs = dot(windowed(z, values, index), cot_stack, 1, 1)
    deltas = jnp.sum(probs * dprobs, axis=0, keepdims=True)
    dscores = (probs * (dprobs - deltas)).astype(jnp.bfloat16)
    return dscores, (dot(dscores, windowed(z, keys, index), 0, 0) * SCALE).astype(jnp.bfloat16)


def unstack(z, grad_stack, target, start):
    for head in range(grad_stack.shape[0] // z.block):
        columns = slice(head * HEAD_SIZE, (head + 1) * HEAD_SIZE)
        target[start : start + z.block, columns] = grad_stack[head * z.block : (head + 1) * z.block]


def pair_terms(z, index, dscores, probs, query_stack, cot_stack):
    key_term = dot(dscores, query_stack, 1, 0) * SCALE
    value_term = dot(probs.astype(jnp.bfloat16), cot_stack, 1, 0)
    term = jnp.concatenate([key_term, value_term], axis=1)
    start = index * z.block
    rest = z.span + z.rows - z.window - start
    if start > 0:
        term = jnp.concatenate([jnp.zeros((start, PAIR), jnp.float32), term], axis=0)
    if rest > 0:
        term = jnp.concatenate([term, jnp.zeros((rest, PAIR), jnp.float32)], axis=0)
    return term


def padded(z, grad, index):
    blank = jnp.zeros((z.block, grad.shape[1]), grad.dtype)
    return jnp.concatenate([grad if place == index else blank for place in range(BLOCKS)], axis=0)


def forward(z, refs):
    step = z.chunks - 1
    keys = seen_rows(z, refs, step, 0)
    stacks, probs = softmax_blocks(z, refs, step, refs.up[...], keys)
    for index in range(BLOCKS):
        listed(refs, "stack")[index][...] = stacks[index]
        listed(refs, "probs")[index][...] = probs[index]


def whole(steps, z, refs):
    copies = []
    if hasattr(refs, "pending"):
        target = refs.dq.at[:, chunk_columns(z, steps[0] - 1)]
        copy_rows(refs.pending, target, refs.sems, copies)
    input_sum = refs.input_sum[...] if hasattr(refs, "input_sum") else 0.0
    for place, step in enumerate(steps):
        up = listed(refs, "up")[place]
        matrix = up[up.shape[0] - z.rank :]
        keys, values = seen_rows(z, refs, step, 0), seen_rows(z, refs, step, 1)
        stacks, probs = softmax_blocks(z, refs, step, matrix, keys)
        grad_ref = refs.grad if step == steps[-1] else refs.early
        cots = refs.cot[:, place * z.width : (place + 1) * z.width]
        pair_total = 0.0
        for index in range(BLOCKS):
            start = index * z.block
            cot_stack = stacked(cots, slice(start, start + z.block))
            dscores, grad_stack = score_grads(z, index, probs[index], keys, values, cot_stack)
            unstack(z, grad_stack, grad_ref, start)
            pair_total += pair_terms(z, index, dscores, probs[index], stacks[index], cot_stack)
        if step != steps[-1]:
            copy_rows(grad_ref, refs.dq.at[:, chunk_columns(z, step)], refs.sems, copies)
        grad = grad_ref[...]
        listed(refs, "term")[place][...] = dot(refs.at[...], grad, 1, 0).astype(jnp.bfloat16)
        refs.halo_grads[:, pair_columns(z, step)] = pair_total[: z.span].astype(
            refs.halo_grads.dtype
        )
        refs.own_grads[:, pair_columns(z, step)] = pair_total[z.span :]
        input_sum += dot(matrix, grad, 1, 1)
    refs.input_grad[...] = input_sum
    for copy in copies:
        copy.wait()


def front(z, refs):
    copies = []
    step = z.chunks - 1
    copy_rows(refs.pending, refs.dq.at[:, chunk_columns(z, step - 1)], refs.sems, copies)
    keys, values = seen_rows(z, refs, step, 0), seen_rows(z, refs, step, 1)
    probs = refs.probs[...]
    cot_stack = stacked(refs.cot, slice(0, z.block))
    dscores, grad_stack = score_grads(z, 0, probs, keys, values, cot_stack)
    unstack(z, grad_stack, refs.grad, 0)
    pair_total = pair_terms(z, 0, dscores, probs, refs.stack[...], cot_stack)
    refs.halo_grads[:, pair_columns(z, step)] = pair_total[: z.span].astype(refs.halo_grads.dtype)
    refs.own_part[...] = pair_total[z.span :]
    grad = padded(z, refs.grad[...], 0)
    weight = dot(refs.at[...], grad, 1, 0)
    for term in listed(refs, "term"):
        weight += term[...].astype(jnp.float32)
    refs.weight_part[...] = weight
    refs.input_grad[...] = refs.input_sum[...] + dot(refs.up[...], grad, 1, 1)
    for copy in copies:
        copy.wait()


def back(z, refs):
    step = z.chunks - 1
    keys, values = seen_rows(z, refs, step, 0), seen_rows(z, refs, step, 1)
    cot_stack = stacked(refs.cot, slice(0, z.block))
    dscores, grad_stack = score_grads(z, 1, refs.probs[...], keys, values, cot_stack)
    refs.dscores[...] = dscores
    unstack(z, grad_stack, refs.grad, 0)
    weight = refs.weight_part[...] + dot(refs.at[...], padded(z, refs.grad[...], 1), 1, 0)
    for term in listed(refs, "term"):
        weight += term[...].astype(jnp.float32)
    refs.total[...] = weight.astype(jnp.bfloat16)
    shares = listed(refs, "share")
    rows = z.rank // len(shares)
    for away, share in enumerate(shares):
        target = lax.rem(lax.axis_index("dp") + away, len(shares))
        share[...] = refs.total[pl.ds(pl.multiple_of(target * rows, rows), rows)]


def finish(z, refs):
    copies = []
    step = z.chunks - 1
    for index, grad in enumerate(listed(refs, "pending")):
        target = refs.dq.at[pl.ds(index * z.block, z.block), chunk_columns(z, step)]
        copy_rows(grad, target, refs.sems, copies)
    cot_stack = stacked(refs.cot, slice(0, z.block))
    pair_total = pair_terms(z, 1, refs.dscores[...], refs.probs[...], refs.stack[...], cot_stack)
    refs.own_grads[:, pair_columns(z, step)] = refs.own_part[...] + pair_total[z.span :]
    grad = padded(z, refs.pending1[...], 1)
    input_grad = refs.input_sum[...] + dot(refs.up[...], grad, 1, 1)
    refs.input_grad[...] = input_grad.astype(jnp.bfloat16)
    if hasattr(refs, "halo_back"):
        low = z.rows - z.span
        refs.pair_grads[:low] = refs.own_grads[:low].astype(jnp.bfloat16)
        total = refs.own_grads[low:] + refs.halo_back[...].astype(jnp.float32)
        refs.pair_grads[low:] = total.astype(jnp.bfloat16)
    for copy in copies:
        copy.wait()


def per_device(
    frozen_queries, key_value_pairs, adapter_input, adapter_up_matrix, upstream, document_index
):
    bf16, f32 = jnp.bfloat16, jnp.float32
    chunks = lax.axis_size("seq")
    packs = lax.axis_size("dp")
    place = lax.axis_index("seq")
    rows = frozen_queries.shape[2]
    columns = QUERY_HEADS * HEAD_SIZE
    block = rows // BLOCKS
    span = document_index.shape[2] // SPAN_PARTS
    window = span + block
    width = columns // chunks
    rank = adapter_input.shape[3]
    stack_rows = width // HEAD_SIZE * block
    per_head = chunks // HK
    last = chunks - 1
    z = SimpleNamespace(
        chunks=chunks, rows=rows, block=block, span=span, window=window, width=width, rank=rank
    )
    flops = 10 * stack_rows * window * HEAD_SIZE

    pieces = []
    left = span
    while left > 0:
        pieces.append((len(pieces) + 1, min(rows, left)))
        left -= rows

    own = key_value_pairs[0, 0]
    matrix = adapter_up_matrix[0]
    cotangents = upstream[0, 0]
    bundled = len(pieces) == 1 and matrix.shape[1] == own.shape[1]

    def sems(count):
        return dict(sems=pltpu.SemaphoreType.DMA((count * COPIES,)))

    first = run(
        split_first,
        z,
        dict(upstream=cotangents),
        dict(piece=((rows, 2 * width), bf16)),
        sems(2),
    ).piece
    cots = {0: passed_along(first, "section", -1)}
    held = [((rows, width), bf16)] * (last - 2) + [((block, width), bf16)] * BLOCKS
    outputs = numbered("piece", held) | dict(matrix_copy=((rank, width), bf16))
    if bundled:
        outputs.update(bundle=((span + rank, width), bf16))
    parts = run(
        split_rest,
        z,
        dict(upstream=cotangents, pairs=own, matrix=matrix, after=first),
        outputs,
        sems(len(outputs) + 1),
    )
    held = listed(parts, "piece")
    matrix_copy = parts.matrix_copy
    if bundled:
        halo = passed_along(parts.bundle, "seq", 1)
        ups = [halo]
    else:
        halo = [passed_along(own[rows - count :], "seq", distance) for distance, count in pieces]
        halo = jnp.concatenate(halo[::-1], axis=0)
        ups = [passed_along(matrix_copy, "seq", 1)]
    ups += [passed_along(matrix_copy, "seq", step + 1) for step in range(1, last)]

    numbers = jnp.concatenate([jnp.full((span,), -1, jnp.int32), document_index[0, 0]])
    numbers = lax.dynamic_slice_in_dim(numbers, place * rows, span + rows, 0)
    reach = jnp.arange(window, dtype=jnp.int32)[:, None] <= (
        jnp.arange(block, dtype=jnp.int32)[None, :] + span
    )
    bias = []
    for start in range(0, rows, block):
        seen = numbers[start : start + window, None]
        same = seen == numbers[None, start + span : start + span + block]
        bias.append(jnp.where(same & reach, 0.0, -jnp.inf))
    bias = jnp.concatenate(bias, axis=0).astype(f32)
    bias = jnp.concatenate([bias, bias], axis=1)
    fq = frozen_queries[0, 0]
    at = adapter_input[0, 0].T

    outputs = numbered("stack", [((stack_rows, HEAD_SIZE), bf16)] * BLOCKS)
    outputs |= numbered("probs", [((window, stack_rows), f32)] * BLOCKS)
    outputs.update(held=(held[0].shape, bf16))
    ahead = run(
        forward,
        z,
        dict(fq=fq, at=at, up=matrix_copy, halo=halo, own=own, bias=bias, held_in=held[0]),
        outputs,
        {},
        flops,
    )
    cots[2] = passed_along(ahead.held, "section", -1)

    halo_type = bf16 if per_head == 1 else f32
    halo_shape = ((span, chunks * PAIR), halo_type)
    own_shape = ((rows, chunks * PAIR), f32)
    dq_shape = ((rows, columns), bf16)
    input_shape = ((rank, rows), f32)
    terms = []
    state = None
    for steps in [(0, 1)] + [(step,) for step in range(2, last)]:
        inputs = dict(fq=fq, at=at, halo=halo, own=own, bias=bias, cot=cots[steps[0]])
        inputs |= numbered("up", [ups[step] for step in steps])
        outputs = dict(
            dq=dq_shape,
            halo_grads=halo_shape,
            own_grads=own_shape,
            input_grad=input_shape,
            grad=((rows, width), bf16),
        )
        outputs |= numbered("term", [((rank, width), bf16)] * len(steps))
        scratch = sems(len(steps))
        later = []
        if state is None:
            later = held[1:-1]
            scratch.update(early=pltpu.VMEM((rows, width), bf16))
        else:
            inputs.update(
                dq_in=state.dq,
                halo_grads_in=state.halo_grads,
                own_grads_in=state.own_grads,
                input_sum=state.input_grad,
                pending=state.grad,
            )
        if steps[0] == 2:
            later = held[-1:]
        named = numbered("later", later)
        inputs |= {name + IN: array for name, array in named.items()}
        outputs |= {name: (array.shape, bf16) for name, array in named.items()}
        body = functools.partial(whole, steps)
        body.__name__ = whole.__name__
        state = run(body, z, inputs, outputs, scratch, 2 * len(steps) * flops)
        for array in listed(state, "later"):
            cots[len(cots) + 1] = passed_along(array, "section", -1)
        for step, term in zip(steps, listed(state, "term")):
            terms.append(passed_along(term, "seq", -(step + 1)))

    common = dict(at=at, up=matrix, halo=halo, own=own)
    outputs = dict(
        dq=dq_shape,
        halo_grads=halo_shape,
        own_part=((rows, PAIR), f32),
        weight_part=((rank, width), f32),
        input_grad=input_shape,
        grad=((block, width), bf16),
    )
    early = run(
        front,
        z,
        common
        | dict(
            cot=cots[last],
            stack=ahead.stack0,
            probs=ahead.probs0,
            dq_in=state.dq,
            halo_grads_in=state.halo_grads,
            input_sum=state.input_grad,
            pending=state.grad,
        )
        | numbered("term", terms[:-1]),
        outputs,
        sems(1),
        flops,
    )
    halo_grads = early.halo_grads
    if per_head > 1:
        halo_grads = jnp.sum(halo_grads.reshape(span, HK, per_head, PAIR), axis=2)
        halo_grads = halo_grads.astype(bf16).reshape(span, HK * PAIR)
    backs = []
    stop = span
    for distance, count in pieces:
        backs.append(passed_along(halo_grads[stop - count : stop], "seq", -distance))
        stop -= count

    outputs = dict(grad=((block, width), bf16), dscores=((window, stack_rows), bf16))
    outputs |= numbered("share", [((rank // packs, width), bf16)] * packs)
    late = run(
        back,
        z,
        common
        | dict(cot=cots[last + 1], probs=ahead.probs1, weight_part=early.weight_part)
        | numbered("term", terms[-1:]),
        outputs,
        dict(total=pltpu.VMEM((rank, width), bf16)),
        flops,
    )
    shares = listed(late, "share")
    shares[1:] = [passed_along(shares[away], "dp", away) for away in range(1, packs)]

    merged = per_head == 1 and len(pieces) == 1
    outputs = dict(dq=dq_shape, own_grads=own_shape, input_grad=((rank, rows), bf16))
    inputs = dict(
        at=at,
        up=matrix,
        cot=cots[last + 1],
        stack=ahead.stack1,
        probs=ahead.probs1,
        dscores=late.dscores,
        own_part=early.own_part,
        input_sum=early.input_grad,
        dq_in=early.dq,
        own_grads_in=state.own_grads,
        share_in=shares[0],
    )
    outputs.update(share=(shares[0].shape, bf16))
    if merged:
        inputs.update(halo_back=backs[0])
        outputs.update(pair_grads=((rows, HK * PAIR), bf16))
    final = run(
        finish,
        z,
        inputs | numbered("pending", [early.grad, late.grad]),
        outputs,
        sems(BLOCKS),
        flops,
    )
    weight_share = final.share.astype(f32)
    for share in shares[1:]:
        weight_share += share.astype(f32)
    if merged:
        pair_grads = final.pair_grads
    else:
        own_grads = jnp.sum(final.own_grads.reshape(rows, HK, per_head, PAIR), axis=2)
        own_grads = own_grads.reshape(rows, HK * PAIR)
        for rows_back in backs:
            low = rows - rows_back.shape[0]
            own_grads = own_grads.at[low:].add(rows_back.astype(f32))
        pair_grads = own_grads.astype(bf16)

    return (
        final.dq[None, None],
        pair_grads[None, None],
        final.input_grad.T[None, None],
        weight_share[None],
    )


def solution(mesh):
    placed = (
        P("section", "dp", "seq", None),
        P("section", "dp", "seq", None),
        P("section", "dp", "seq", None),
        P("section", None, "seq"),
        P("section", "dp", "seq", None),
        P("section", "dp", None),
    )
    return jax.shard_map(
        per_device,
        mesh=mesh,
        in_specs=placed,
        out_specs=(
            P("section", "dp", "seq", None),
            P("section", "dp", "seq", None),
            P("section", "dp", "seq", None),
            P("section", "dp", "seq"),
        ),
        check_vma=False,
    )
```

profile of v0, /device:TPU:0, one launch (start us, length us, event | category | flops | bytes accessed | tf_op | source)
XLA Modules:
  0.0 41.3 jit_solution(15453645330507601613)
XLA Ops:
  0.6 1.1 %split_first.1.refs_3_ = bf16[128,2048]{1,0:T(8,128)(2,1)S(1)} custom-call(bf16[128,4096]{1,0:T(8,128)(2,1)} %bitcast.35), custom_call_target="tpu_custom_call" | custom-call | bytes 1048576 | tf_op jit(solution)/shard_map/split_first/pallas_call | solution.py:66
  1.8 3.0 %collective-permute-start.3 = (bf16[128,2048]{1,0:T(8,128)(2,1)S(1)}, bf16[128,2048]{1,0:T(8,128)(2,1)S(1)}, u32[]{:S(2)}, u32[]{:S(2)}) collective-permute-start(bf16[128,2048]{1,0:T(8,128)(2,1)S(1)} %split_first.1.refs_3_), channel_id=1, source_target_pairs={{0,16},{16,0},{1,17},{17,1},{2,18},{18,2},{3,19},{19,3},{4,20},{20... | collective-permute-start | bytes 1572872 | tf_op jit(solution)/shard_map/ppermute | solution.py:30
  4.8 1.4 %split_rest.1 = (bf16[128,1024]{1,0:T(8,128)(2,1)S(1)}, bf16[64,1024]{1,0:T(8,128)(2,1)S(1)}, bf16[64,1024]{1,0:T(8,128)(2,1)S(1)}, bf16[64,1024]{1,0:T(8,128)(2,1)S(1)}, bf16[128,1024]{1,0:T(8,128)(2,1)S(1)}) custom-call(bf16[128,4096]{1,0:T(8,128)(2,1)} %bitcast.36, bf16[128,1024]{1,0:T(8,128)(2,1)} %bitcast.18, bf16[64,1024]{1,0:T(8,128)(2,1)} %bitcast.24, ...), custom_call_target="tpu_custom_call" | custom-call | bytes 1048576 | tf_op jit(solution)/shard_map/split_rest/pallas_call | solution.py:66
  6.2 0.0 copy-start.1
  6.2 0.1 collective-permute-start
  6.3 0.1 pad_dynamic-slice_fusion
  6.4 0.1 fusion.5
  6.5 0.1 fusion.4
  6.5 0.1 fusion.2
  6.7 0.0 copy-start.3
  6.7 0.1 maximum_maximum_fusion.refs_5_.refs_4_
  6.8 5.3 %collective-permute-done.refs_3_.refs_2_.refs_6_ = bf16[128,1024]{1,0:T(8,128)(2,1)S(1)} collective-permute-done((bf16[128,1024]{1,0:T(8,128)(2,1)S(1)}, bf16[128,1024]{1,0:T(8,128)(2,1)S(1)}, u32[]{:S(2)}, u32[]{:S(2)}) %collective-permute-start) | collective-permute-done | bytes 262176 | tf_op jit(solution)/shard_map/ppermute | solution.py:30
  12.1 0.6 %forward.1 = (bf16[512,128]{1,0:T(8,128)(2,1)S(1)}, bf16[512,128]{1,0:T(8,128)(2,1)S(1)}, f32[128,512]{1,0:T(8,128)S(1)}, f32[128,512]{1,0:T(8,128)S(1)}, bf16[128,1024]{1,0:T(8,128)(2,1)S(1)}) custom-call(bf16[128,4096]{1,0:T(8,128)(2,1)S(1)} %bitcast.15, bf16[64,128]{1,0:T(8,128)(2,1)S(1)} %bitcast.28, ...), custom_call_target="tpu_custom_call", output_to_operand_aliasing={{4}: (6, {})} | custom-call | flops 83886080 | bytes 1048576 | tf_op jit(solution)/shard_map/forward/pallas_call | solution.py:66
  12.7 0.1 collective-permute-start.1
  12.8 2.0 %collective-permute-start.4 = (bf16[64,1024]{1,0:T(8,128)(2,1)S(1)}, bf16[64,1024]{1,0:T(8,128)(2,1)S(1)}, u32[]{:S(2)}, u32[]{:S(2)}) collective-permute-start(bf16[64,1024]{1,0:T(8,128)(2,1)S(1)} %get-tuple-element.46.refs_2_), channel_id=1, source_target_pairs={{0,8},{4,12},{8,0},{12,4},{1,9},{5,13},{9,1},{13,5},{2,10},{6,14},... | collective-permute-start | bytes 393224 | tf_op jit(solution)/shard_map/ppermute | solution.py:30
  14.8 3.0 %collective-permute-done.4.refs_7_ = bf16[64,1024]{1,0:T(8,128)(2,1)S(1)} collective-permute-done((bf16[64,1024]{1,0:T(8,128)(2,1)S(1)}, bf16[64,1024]{1,0:T(8,128)(2,1)S(1)}, u32[]{:S(2)}, u32[]{:S(2)}) %collective-permute-start.4) | collective-permute-done | bytes 131104 | tf_op jit(solution)/shard_map/ppermute | solution.py:30
  17.8 2.9 %whole.2 = (bf16[128,4096]{1,0:T(8,128)(2,1)}, bf16[64,1024]{1,0:T(8,128)(2,1)S(1)}, f32[128,1024]{1,0:T(8,128)S(1)}, f32[64,128]{1,0:T(8,128)S(1)}, bf16[128,10...) custom-call(bf16[128,4096]{1,0:T(8,128)(2,1)S(1)} %bitcast.16, ...), custom_call_target="tpu_custom_call", output_to_operand_aliasing={{7}: (8, {})} | custom-call | flops 335544320 | bytes 1048576 | tf_op jit(solution)/shard_map/whole/pallas_call | solution.py:66
  20.7 2.0 %collective-permute-start.6 = (bf16[64,1024]{1,0:T(8,128)(2,1)S(1)}, bf16[64,1024]{1,0:T(8,128)(2,1)S(1)}, u32[]{:S(2)}, u32[]{:S(2)}) collective-permute-start(bf16[64,1024]{1,0:T(8,128)(2,1)S(1)} %get-tuple-element.59), channel_id=1, source_target_pairs={{0,16},{16,0},{1,17},{17,1},{2,18},{18,2},{3,19},{19,3},{4,20},{20... | collective-permute-start | bytes 393224 | tf_op jit(solution)/shard_map/ppermute | solution.py:30
  22.7 1.5 %collective-permute-start.8 = (bf16[64,1024]{1,0:T(8,128)(2,1)S(1)}, bf16[64,1024]{1,0:T(8,128)(2,1)S(1)}, u32[]{:S(2)}, u32[]{:S(2)}) collective-permute-start(bf16[64,1024]{1,0:T(8,128)(2,1)S(1)} %get-tuple-element.67), channel_id=1, source_target_pairs={{0,8},{4,12},{8,0},{12,4},{1,9},{5,13},{9,1},{13,5},{2,10},{6,14},... | collective-permute-start | bytes 393224 | tf_op jit(solution)/shard_map/ppermute | solution.py:30
  24.2 1.9 %whole.3 = (bf16[128,4096]{1,0:T(8,128)(2,1)}, bf16[64,1024]{1,0:T(8,128)(2,1)S(1)}, f32[128,1024]{1,0:T(8,128)S(1)}, f32[64,128]{1,0:T(8,128)S(1)}, bf16[128,10...) custom-call(bf16[128,4096]{1,0:T(8,128)(2,1)S(1)} %bitcast.17, ...), custom_call_target="tpu_custom_call", output_to_operand_aliasing={{0}: (7, {}), {1}: (8, {}), {2}: (9, {}), {6}: (12, {})} | custom-call | flops 167772160 | bytes 1048576 | tf_op jit(solution)/shard_map/whole/pallas_call | solution.py:66
  26.1 0.6 %collective-permute-start.5 = (bf16[64,1024]{1,0:T(8,128)(2,1)S(1)}, bf16[64,1024]{1,0:T(8,128)(2,1)S(1)}, u32[]{:S(2)}, u32[]{:S(2)}) collective-permute-start(bf16[64,1024]{1,0:T(8,128)(2,1)S(1)} %get-tuple-element.56), channel_id=1, source_target_pairs={{0,16},{16,0},{1,17},{17,1},{2,18},{18,2},{3,19},{19,3},{4,20},{20... | collective-permute-start | bytes 393224 | tf_op jit(solution)/shard_map/ppermute | solution.py:30
  26.8 3.3 %collective-permute-done.8.refs_12_ = bf16[64,1024]{1,0:T(8,128)(2,1)S(1)} collective-permute-done((bf16[64,1024]{1,0:T(8,128)(2,1)S(1)}, bf16[64,1024]{1,0:T(8,128)(2,1)S(1)}, u32[]{:S(2)}, u32[]{:S(2)}) %collective-permute-start.8) | collective-permute-done | bytes 131104 | tf_op jit(solution)/shard_map/ppermute | solution.py:30
  30.1 1.2 %front.1 = (bf16[128,4096]{1,0:T(8,128)(2,1)}, bf16[64,1024]{1,0:T(8,128)(2,1)S(1)}, f32[128,256]{1,0:T(8,128)S(1)}, f32[64,1024]{1,0:T(8,128)S(1)}, f32[64,128]...) custom-call(bf16[64,128]{1,0:T(8,128)(2,1)S(1)} %bitcast.31, ...), custom_call_target="tpu_custom_call", output_to_operand_aliasing={{0}: (7, {}), {1}: (8, {})} | custom-call | flops 83886080 | bytes 1048576 | tf_op jit(solution)/shard_map/front/pallas_call | solution.py:66
  31.3 0.1 collective-permute-start.10
  31.4 0.5 %collective-permute-done.5.refs_4_.refs_2_ = bf16[64,1024]{1,0:T(8,128)(2,1)S(1)} collective-permute-done((bf16[64,1024]{1,0:T(8,128)(2,1)S(1)}, bf16[64,1024]{1,0:T(8,128)(2,1)S(1)}, u32[]{:S(2)}, u32[]{:S(2)}) %collective-permute-start.5) | collective-permute-done | bytes 131104 | tf_op jit(solution)/shard_map/ppermute | solution.py:30
  31.9 0.6 %back.1 = (bf16[64,1024]{1,0:T(8,128)(2,1)S(1)}, bf16[128,512]{1,0:T(8,128)(2,1)S(1)}, bf16[16,1024]{1,0:T(8,128)(2,1)S(1)}, bf16[16,1024]{1,0:T(8,128)(2,1)S(1)...) custom-call(bf16[64,128]{1,0:T(8,128)(2,1)S(1)} %bitcast.32, bf16[64,1024]{1,0:T(8,128)(2,1)S(1)} %bitcast.26, ...), custom_call_target="tpu_custom_call" | custom-call | flops 83886080 | bytes 1048576 | tf_op jit(solution)/shard_map/back/pallas_call | solution.py:66
  32.5 1.6 %collective-permute-start.11 = (bf16[16,1024]{1,0:T(8,128)(2,1)S(1)}, bf16[16,1024]{1,0:T(8,128)(2,1)S(1)}, u32[]{:S(2)}, u32[]{:S(2)}) collective-permute-start(bf16[16,1024]{1,0:T(8,128)(2,1)S(1)} %get-tuple-element.83), channel_id=1, source_target_pairs={{0,1},{1,2},{2,3},{3,0},{4,5},{5,6},{6,7},{7,4},{8,9},{9,10},{10,1... | collective-permute-start | bytes 98312 | tf_op jit(solution)/shard_map/ppermute | solution.py:30
  34.1 2.6 %collective-permute-start.12 = (bf16[16,1024]{1,0:T(8,128)(2,1)S(1)}, bf16[16,1024]{1,0:T(8,128)(2,1)S(1)}, u32[]{:S(2)}, u32[]{:S(2)}) collective-permute-start(bf16[16,1024]{1,0:T(8,128)(2,1)S(1)} %get-tuple-element.84), channel_id=1, source_target_pairs={{0,2},{1,3},{2,0},{3,1},{4,6},{5,7},{6,4},{7,5},{8,10},{9,11},{10,... | collective-permute-start | bytes 98312 | tf_op jit(solution)/shard_map/ppermute | solution.py:30
  36.7 1.3 %collective-permute-start.13 = (bf16[16,1024]{1,0:T(8,128)(2,1)S(1)}, bf16[16,1024]{1,0:T(8,128)(2,1)S(1)}, u32[]{:S(2)}, u32[]{:S(2)}) collective-permute-start(bf16[16,1024]{1,0:T(8,128)(2,1)S(1)} %get-tuple-element.85), channel_id=1, source_target_pairs={{0,3},{1,0},{2,1},{3,2},{4,7},{5,4},{6,5},{7,6},{8,11},{9,8},{10,9... | collective-permute-start | bytes 98312 | tf_op jit(solution)/shard_map/ppermute | solution.py:30
  38.0 1.7 %finish.1 = (bf16[128,4096]{1,0:T(8,128)(2,1)}, f32[128,1024]{1,0:T(8,128)S(1)}, bf16[64,128]{1,0:T(8,128)(2,1)}, bf16[16,1024]{1,0:T(8,128)(2,1)S(1)}, bf16[128,1024]{1,0:T(8,128)(2,1)}) custom-call(bf16[64,128]{1,0:T(8,128)(2,1)S(1)} %bitcast.33, bf16[64,1024]{1,0:T(8,128)(2,1)S(1)} %bitcast.27, ...), custom_call_target="tpu_custom_call", output_to_operand_aliasing={{0}: (8, {}), {1}: (9, {}), {3}: (10, {})} | custom-call | flops 83886080 | bytes 1048576 | tf_op jit(solution)/shard_map/finish/pallas_call | solution.py:66
  39.8 0.8 %collective-permute-done.13 = bf16[16,1024]{1,0:T(8,128)(2,1)S(1)} collective-permute-done((bf16[16,1024]{1,0:T(8,128)(2,1)S(1)}, bf16[16,1024]{1,0:T(8,128)(2,1)S(1)}, u32[]{:S(2)}, u32[]{:S(2)}) %collective-permute-start.13) | collective-permute-done | bytes 32800 | tf_op jit(solution)/shard_map/ppermute | solution.py:30
  40.6 0.6 %add_bitcast_fusion = f32[1,16,1024]{2,1,0:T(8,128)} fusion(bf16[16,1024]{1,0:T(8,128)(2,1)S(1)} %collective-permute-done.13, bf16[16,1024]{1,0:T(8,128)(2,1)S(1)} %collective-permute-done.12, bf16[16,1024]{1,0:T(8,128)(2,1)S(1)} %collective-permute-done.11, bf16[16,1024]{1,0:T(8,128)(2,1)S(1)} %get-tuple-element.82), kind=kLoop, calls=%fused_computation.1 | loop fusion | flops 114688 | bytes 196608 | tf_op jit(solution)/shard_map/broadcast_in_dim | solution.py:534
  (20 shorter events, 0.0 us)
Async XLA Ops:
  1.8 16.0 %collective-permute-start.3 = (bf16[128,2048]{1,0:T(8,128)(2,1)S(1)}, bf16[128,2048]{1,0:T(8,128)(2,1)S(1)}, u32[]{:S(2)}, u32[]{:S(2)}) collective-permute-start(bf16[128,2048]{1,0:T(8,128)(2,1)S(1)} %split_first.1.refs_3_), channel_id=1, source_target_pairs={{0,16},{16,0},{1,17},{17,1},{2,18},{18,2},{3,19},{19,3},{4,20},{20... | collective-permute-start | bytes 1572872 | tf_op jit(solution)/shard_map/ppermute | solution.py:30
  4.8 1.5 %copy-start.4 = (s32[1,1,512]{2,1,0:T(1,128)S(1)}, s32[1,1,512]{2,1,0:T(1,128)}, u32[]{:S(2)}) copy-start(s32[1,1,512]{2,1,0:T(1,128)} %param.11) | copy-start | bytes 6148
  4.8 7.3 %copy-start = (bf16[1,1,128,4096]{3,2,1,0:T(8,128)(2,1)S(1)}, bf16[1,1,128,4096]{3,2,1,0:T(8,128)(2,1)}, u32[]{:S(2)}) copy-start(bf16[1,1,128,4096]{3,2,1,0:T(8,128)(2,1)} %param.6) | copy-start | bytes 3145732
  6.2 5.9 %copy-start.1 = (bf16[1,1,128,1024]{3,2,1,0:T(8,128)(2,1)S(1)}, bf16[1,1,128,1024]{3,2,1,0:T(8,128)(2,1)}, u32[]{:S(2)}) copy-start(bf16[1,1,128,1024]{3,2,1,0:T(8,128)(2,1)} %param.7) | copy-start | bytes 786436
  6.2 5.8 %collective-permute-start = (bf16[128,1024]{1,0:T(8,128)(2,1)S(1)}, bf16[128,1024]{1,0:T(8,128)(2,1)S(1)}, u32[]{:S(2)}, u32[]{:S(2)}) collective-permute-start(bf16[128,1024]{1,0:T(8,128)(2,1)S(1)} %get-tuple-element.45), channel_id=1, source_target_pairs={{0,4},{4,8},{8,12},{12,0},{1,5},{5,9},{9,13},{13,1},{2,6},{6,10},{... | collective-permute-start | bytes 786440 | tf_op jit(solution)/shard_map/ppermute | solution.py:30
  6.7 5.4 %copy-start.3 = (bf16[1,1,128,64]{2,3,1,0:T(8,128)(2,1)S(1)}, bf16[1,1,128,64]{2,3,1,0:T(8,128)(2,1)}, u32[]{:S(2)}) copy-start(bf16[1,1,128,64]{2,3,1,0:T(8,128)(2,1)} %param.8) | copy-start | bytes 49156
  12.7 11.6 %collective-permute-start.1 = (bf16[128,1024]{1,0:T(8,128)(2,1)S(1)}, bf16[128,1024]{1,0:T(8,128)(2,1)S(1)}, u32[]{:S(2)}, u32[]{:S(2)}) collective-permute-start(bf16[128,1024]{1,0:T(8,128)(2,1)S(1)} %get-tuple-element.48), channel_id=1, source_target_pairs={{0,16},{16,0},{1,17},{17,1},{2,18},{18,2},{3,19},{19,3},{4,20},{20... | collective-permute-start | bytes 786440 | tf_op jit(solution)/shard_map/ppermute | solution.py:30
  12.8 5.0 %collective-permute-start.4 = (bf16[64,1024]{1,0:T(8,128)(2,1)S(1)}, bf16[64,1024]{1,0:T(8,128)(2,1)S(1)}, u32[]{:S(2)}, u32[]{:S(2)}) collective-permute-start(bf16[64,1024]{1,0:T(8,128)(2,1)S(1)} %get-tuple-element.46.refs_2_), channel_id=1, source_target_pairs={{0,8},{4,12},{8,0},{12,4},{1,9},{5,13},{9,1},{13,5},{2,10},{6,14},... | collective-permute-start | bytes 393224 | tf_op jit(solution)/shard_map/ppermute | solution.py:30
  14.8 9.4 %collective-permute-start.2 = (bf16[64,1024]{1,0:T(8,128)(2,1)S(1)}, bf16[64,1024]{1,0:T(8,128)(2,1)S(1)}, u32[]{:S(2)}, u32[]{:S(2)}) collective-permute-start(bf16[64,1024]{1,0:T(8,128)(2,1)S(1)} %get-tuple-element.46.refs_2_), channel_id=1, source_target_pairs={{0,12},{4,0},{8,4},{12,8},{1,13},{5,1},{9,5},{13,9},{2,14},{6,2},{... | collective-permute-start | bytes 393224 | tf_op jit(solution)/shard_map/ppermute | solution.py:30
  20.7 6.1 %collective-permute-start.6 = (bf16[64,1024]{1,0:T(8,128)(2,1)S(1)}, bf16[64,1024]{1,0:T(8,128)(2,1)S(1)}, u32[]{:S(2)}, u32[]{:S(2)}) collective-permute-start(bf16[64,1024]{1,0:T(8,128)(2,1)S(1)} %get-tuple-element.59), channel_id=1, source_target_pairs={{0,16},{16,0},{1,17},{17,1},{2,18},{18,2},{3,19},{19,3},{4,20},{20... | collective-permute-start | bytes 393224 | tf_op jit(solution)/shard_map/ppermute | solution.py:30
  22.7 4.1 %collective-permute-start.7 = (bf16[64,1024]{1,0:T(8,128)(2,1)S(1)}, bf16[64,1024]{1,0:T(8,128)(2,1)S(1)}, u32[]{:S(2)}, u32[]{:S(2)}) collective-permute-start(bf16[64,1024]{1,0:T(8,128)(2,1)S(1)} %get-tuple-element.66), channel_id=1, source_target_pairs={{0,12},{4,0},{8,4},{12,8},{1,13},{5,1},{9,5},{13,9},{2,14},{6,2},{... | collective-permute-start | bytes 393224 | tf_op jit(solution)/shard_map/ppermute | solution.py:30
  22.7 7.4 %collective-permute-start.8 = (bf16[64,1024]{1,0:T(8,128)(2,1)S(1)}, bf16[64,1024]{1,0:T(8,128)(2,1)S(1)}, u32[]{:S(2)}, u32[]{:S(2)}) collective-permute-start(bf16[64,1024]{1,0:T(8,128)(2,1)S(1)} %get-tuple-element.67), channel_id=1, source_target_pairs={{0,8},{4,12},{8,0},{12,4},{1,9},{5,13},{9,1},{13,5},{2,10},{6,14},... | collective-permute-start | bytes 393224 | tf_op jit(solution)/shard_map/ppermute | solution.py:30
  24.2 5.9 %copy-start.2 = (bf16[1,64,1024]{2,1,0:T(8,128)(2,1)S(1)}, bf16[1,64,1024]{2,1,0:T(8,128)(2,1)}, u32[]{:S(2)}) copy-start(bf16[1,64,1024]{2,1,0:T(8,128)(2,1)} %param.9) | copy-start | bytes 393220
  26.1 5.7 %collective-permute-start.5 = (bf16[64,1024]{1,0:T(8,128)(2,1)S(1)}, bf16[64,1024]{1,0:T(8,128)(2,1)S(1)}, u32[]{:S(2)}, u32[]{:S(2)}) collective-permute-start(bf16[64,1024]{1,0:T(8,128)(2,1)S(1)} %get-tuple-element.56), channel_id=1, source_target_pairs={{0,16},{16,0},{1,17},{17,1},{2,18},{18,2},{3,19},{19,3},{4,20},{20... | collective-permute-start | bytes 393224 | tf_op jit(solution)/shard_map/ppermute | solution.py:30
  26.8 5.1 %collective-permute-start.9 = (bf16[64,1024]{1,0:T(8,128)(2,1)S(1)}, bf16[64,1024]{1,0:T(8,128)(2,1)S(1)}, u32[]{:S(2)}, u32[]{:S(2)}) collective-permute-start(bf16[64,1024]{1,0:T(8,128)(2,1)S(1)} %get-tuple-element.69), channel_id=1, source_target_pairs={{0,4},{4,8},{8,12},{12,0},{1,5},{5,9},{9,13},{13,1},{2,6},{6,10},{... | collective-permute-start | bytes 393224 | tf_op jit(solution)/shard_map/ppermute | solution.py:30
  31.3 6.7 %collective-permute-start.10 = (bf16[64,1024]{1,0:T(8,128)(2,1)S(1)}, bf16[64,1024]{1,0:T(8,128)(2,1)S(1)}, u32[]{:S(2)}, u32[]{:S(2)}) collective-permute-start(bf16[64,1024]{1,0:T(8,128)(2,1)S(1)} %get-tuple-element.76), channel_id=1, source_target_pairs={{0,12},{4,0},{8,4},{12,8},{1,13},{5,1},{9,5},{13,9},{2,14},{6,2},{... | collective-permute-start | bytes 393224 | tf_op jit(solution)/shard_map/ppermute | solution.py:30
  32.5 7.3 %collective-permute-start.11 = (bf16[16,1024]{1,0:T(8,128)(2,1)S(1)}, bf16[16,1024]{1,0:T(8,128)(2,1)S(1)}, u32[]{:S(2)}, u32[]{:S(2)}) collective-permute-start(bf16[16,1024]{1,0:T(8,128)(2,1)S(1)} %get-tuple-element.83), channel_id=1, source_target_pairs={{0,1},{1,2},{2,3},{3,0},{4,5},{5,6},{6,7},{7,4},{8,9},{9,10},{10,1... | collective-permute-start | bytes 98312 | tf_op jit(solution)/shard_map/ppermute | solution.py:30
  34.1 5.7 %collective-permute-start.12 = (bf16[16,1024]{1,0:T(8,128)(2,1)S(1)}, bf16[16,1024]{1,0:T(8,128)(2,1)S(1)}, u32[]{:S(2)}, u32[]{:S(2)}) collective-permute-start(bf16[16,1024]{1,0:T(8,128)(2,1)S(1)} %get-tuple-element.84), channel_id=1, source_target_pairs={{0,2},{1,3},{2,0},{3,1},{4,6},{5,7},{6,4},{7,5},{8,10},{9,11},{10,... | collective-permute-start | bytes 98312 | tf_op jit(solution)/shard_map/ppermute | solution.py:30
  36.7 3.9 %collective-permute-start.13 = (bf16[16,1024]{1,0:T(8,128)(2,1)S(1)}, bf16[16,1024]{1,0:T(8,128)(2,1)S(1)}, u32[]{:S(2)}, u32[]{:S(2)}) collective-permute-start(bf16[16,1024]{1,0:T(8,128)(2,1)S(1)} %get-tuple-element.85), channel_id=1, source_target_pairs={{0,3},{1,0},{2,1},{3,2},{4,7},{5,4},{6,5},{7,6},{8,11},{9,8},{10,9... | collective-permute-start | bytes 98312 | tf_op jit(solution)/shard_map/ppermute | solution.py:30
where the time goes:
time: 41.4 us; the launch traced here: 41.3 us
  starting transfers between devices  15 us (36%)
  waiting for transfers between devices  12.9 us (31%)
  Pallas kernels  11.4 us (28%)
  other arithmetic  0.92 us (2%)
  between operations  0.79 us (2%)
    ppermute x14, starting transfers between devices, passed_along(): return lax.ppermute(value, axis, pairs)  15 us
    ppermute x14, waiting for transfers between devices, passed_along(): return lax.ppermute(value, axis, pairs)  12.9 us
    pallas_call x8, Pallas kernels, run(): pl.pallas_call(kernel, in_specs=[HBM if name in IN_HBM else VMEM for name...  11.4 us
  transfers between devices with their start and end apart: 14, of which 5 were waited for; matrix products, arithmetic and copies ran while one was open for 1% of the time, Pallas kernels for 25%

commit v1 on v0

--- a/solution.py
+++ b/solution.py
@@ -30,10 +30,19 @@
     return lax.ppermute(value, axis, pairs)
 
 
+def swapped(value, axis, bit):
+    pairs = [(source, source ^ bit) for source in range(lax.axis_size(axis))]
+    return lax.ppermute(value, axis, pairs)
+
+
 def dot(left, right, left_dim, right_dim):
     return lax.dot_general(
         left, right, (((left_dim,), (right_dim,)), ((), ())), preferred_element_type=jnp.float32
     )
+
+
+def low_bit(number):
+    return number & -number
 
 
 def numbered(name, arrays):
@@ -79,9 +88,9 @@
     return SimpleNamespace(**dict(zip(outputs, results)))
 
 
-def copy_rows(source, target, sems, copies):
-    rows = source.shape[0] // COPIES
-    for part in range(COPIES):
+def copy_rows(source, target, sems, copies, parts=1):
+    rows = source.shape[0] // parts
+    for part in range(parts):
         piece = pl.ds(part * rows, rows)
         copies.append(
             pltpu.make_async_copy(source.at[piece], target.at[piece], sems.at[len(copies)])
@@ -90,7 +99,7 @@
 
 
 def chunk_at(step, chunks):
-    return lax.rem(lax.axis_index("seq") + (2 * chunks - 1 - step), chunks)
+    return lax.axis_index("seq") ^ (chunks - 1 - step)
 
 
 def chunk_columns(z, step):
@@ -103,9 +112,8 @@
 
 def split_first(z, refs):
     copies = []
-    for step in (0, 1):
-        target = refs.piece.at[:, pl.ds(step * z.width, z.width)]
-        copy_rows(refs.upstream.at[:, chunk_columns(z, step)], target, refs.sems, copies)
+    source = refs.upstream.at[:, chunk_columns(z, 0)]
+    copy_rows(source, refs.piece, refs.sems, copies, COPIES)
     for copy in copies:
         copy.wait()
 
@@ -113,17 +121,14 @@
 def split_rest(z, refs):
     copies = []
     pieces = listed(refs, "piece")
-    for step, piece in zip(range(2, z.chunks - 1), pieces):
-        copy_rows(refs.upstream.at[:, chunk_columns(z, step)], piece, refs.sems, copies)
+    for step, piece in zip(range(1, z.chunks - 1), pieces):
+        copy_rows(refs.upstream.at[:, chunk_columns(z, step)], piece, refs.sems, copies, COPIES)
     for index, piece in enumerate(pieces[-BLOCKS:]):
         rows = pl.ds(index * z.block, z.block)
         source = refs.upstream.at[rows, chunk_columns(z, z.chunks - 1)]
-        copy_rows(source, piece, refs.sems, copies)
-    copy_rows(refs.matrix, refs.matrix_copy, refs.sems, copies)
-    if hasattr(refs, "bundle"):
-        near = refs.pairs.at[pl.ds(z.rows - z.span, z.span)]
-        copy_rows(near, refs.bundle.at[pl.ds(0, z.span)], refs.sems, copies)
-        copy_rows(refs.matrix, refs.bundle.at[pl.ds(z.span, z.rank)], refs.sems, copies)
+        copy_rows(source, piece, refs.sems, copies, COPIES)
+    copy_rows(refs.matrix, refs.matrix_copy, refs.sems, copies, COPIES)
+    copy_rows(refs.pairs, refs.pairs_copy, refs.sems, copies, COPIES)
     for copy in copies:
         copy.wait()
 
@@ -202,36 +207,32 @@
         listed(refs, "probs")[index][...] = probs[index]
 
 
-def whole(steps, z, refs):
+def whole(step, z, refs):
     copies = []
     if hasattr(refs, "pending"):
-        target = refs.dq.at[:, chunk_columns(z, steps[0] - 1)]
-        copy_rows(refs.pending, target, refs.sems, copies)
-    input_sum = refs.input_sum[...] if hasattr(refs, "input_sum") else 0.0
-    for place, step in enumerate(steps):
-        up = listed(refs, "up")[place]
-        matrix = up[up.shape[0] - z.rank :]
-        keys, values = seen_rows(z, refs, step, 0), seen_rows(z, refs, step, 1)
-        stacks, probs = softmax_blocks(z, refs, step, matrix, keys)
-        grad_ref = refs.grad if step == steps[-1] else refs.early
-        cots = refs.cot[:, place * z.width : (place + 1) * z.width]
-        pair_total = 0.0
-        for index in range(BLOCKS):
-            start = index * z.block
-            cot_stack = stacked(cots, slice(start, start + z.block))
-            dscores, grad_stack = score_grads(z, index, probs[index], keys, values, cot_stack)
-            unstack(z, grad_stack, grad_ref, start)
-            pair_total += pair_terms(z, index, dscores, probs[index], stacks[index], cot_stack)
-        if step != steps[-1]:
-            copy_rows(grad_ref, refs.dq.at[:, chunk_columns(z, step)], refs.sems, copies)
-        grad = grad_ref[...]
-        listed(refs, "term")[place][...] = dot(refs.at[...], grad, 1, 0).astype(jnp.bfloat16)
-        refs.halo_grads[:, pair_columns(z, step)] = pair_total[: z.span].astype(
-            refs.halo_grads.dtype
-        )
-        refs.own_grads[:, pair_columns(z, step)] = pair_total[z.span :]
-        input_sum += dot(matrix, grad, 1, 1)
-    refs.input_grad[...] = input_sum
+        copy_rows(refs.pending, refs.dq.at[:, chunk_columns(z, step - 1)], refs.sems, copies)
+    matrix = refs.up[...]
+    keys, values = seen_rows(z, refs, step, 0), seen_rows(z, refs, step, 1)
+    stacks, probs = softmax_blocks(z, refs, step, matrix, keys)
+    pair_total = 0.0
+    for index in range(BLOCKS):
+        start = index * z.block
+        cot_stack = stacked(refs.cot, slice(start, start + z.block))
+        dscores, grad_stack = score_grads(z, index, probs[index], keys, values, cot_stack)
+        unstack(z, grad_stack, refs.grad, start)
+        pair_total += pair_terms(z, index, dscores, probs[index], stacks[index], cot_stack)
+    grad = refs.grad[...]
+    weight = dot(refs.at[...], grad, 1, 0)
+    for term in listed(refs, "term"):
+        weight += term[...].astype(jnp.float32)
+    refs.weight[...] = weight.astype(jnp.bfloat16)
+    kind = refs.halo_grads.dtype
+    refs.halo_grads[:, pair_columns(z, step)] = pair_total[: z.span].astype(kind)
+    refs.own_grads[:, pair_columns(z, step)] = pair_total[z.span :]
+    input_grad = dot(matrix, grad, 1, 1)
+    if step > 0:
+        input_grad += refs.input_sum[...]
+    refs.input_grad[...] = input_grad
     for copy in copies:
         copy.wait()
 
@@ -239,7 +240,9 @@
 def front(z, refs):
     copies = []
     step = z.chunks - 1
-    copy_rows(refs.pending, refs.dq.at[:, chunk_columns(z, step - 1)], refs.sems, copies)
+    for place, grad in enumerate(listed(refs, "pending")):
+        target = refs.dq.at[:, chunk_columns(z, step - BLOCKS + place)]
+        copy_rows(grad, target, refs.sems, copies)
     keys, values = seen_rows(z, refs, step, 0), seen_rows(z, refs, step, 1)
     probs = refs.probs[...]
     cot_stack = stacked(refs.cot, slice(0, z.block))
@@ -328,40 +331,31 @@
     own = key_value_pairs[0, 0]
     matrix = adapter_up_matrix[0]
     cotangents = upstream[0, 0]
-    bundled = len(pieces) == 1 and matrix.shape[1] == own.shape[1]
 
     def sems(count):
-        return dict(sems=pltpu.SemaphoreType.DMA((count * COPIES,)))
-
-    first = run(
-        split_first,
-        z,
-        dict(upstream=cotangents),
-        dict(piece=((rows, 2 * width), bf16)),
-        sems(2),
-    ).piece
-    cots = {0: passed_along(first, "section", -1)}
-    held = [((rows, width), bf16)] * (last - 2) + [((block, width), bf16)] * BLOCKS
-    outputs = numbered("piece", held) | dict(matrix_copy=((rank, width), bf16))
-    if bundled:
-        outputs.update(bundle=((span + rank, width), bf16))
+        return dict(sems=pltpu.SemaphoreType.DMA((count,)))
+
+    piece = ((rows, width), bf16)
+    first = run(split_first, z, dict(upstream=cotangents), dict(piece=piece), sems(COPIES)).piece
+    cots = [passed_along(first, "section", -1)]
+    outputs = numbered("piece", [piece] * (last - 1) + [((block, width), bf16)] * BLOCKS)
+    outputs.update(matrix_copy=((rank, width), bf16), pairs_copy=(own.shape, bf16))
     parts = run(
         split_rest,
         z,
         dict(upstream=cotangents, pairs=own, matrix=matrix, after=first),
         outputs,
-        sems(len(outputs) + 1),
+        sems(COPIES * len(outputs)),
     )
     held = listed(parts, "piece")
-    matrix_copy = parts.matrix_copy
-    if bundled:
-        halo = passed_along(parts.bundle, "seq", 1)
-        ups = [halo]
-    else:
-        halo = [passed_along(own[rows - count :], "seq", distance) for distance, count in pieces]
-        halo = jnp.concatenate(halo[::-1], axis=0)
-        ups = [passed_along(matrix_copy, "seq", 1)]
-    ups += [passed_along(matrix_copy, "seq", step + 1) for step in range(1, last)]
+    cots.append(passed_along(held[0], "section", -1))
+    own, matrix = parts.pairs_copy, parts.matrix_copy
+    halo = [passed_along(own[rows - count :], "seq", distance) for distance, count in pieces]
+    halo = jnp.concatenate(halo[::-1], axis=0)
+    ups = {0: matrix}
+    for away in sorted(range(1, chunks), key=low_bit, reverse=True):
+        bit = low_bit(away)
+        ups[away] = swapped(ups[away - bit], "seq", bit)
 
     numbers = jnp.concatenate([jnp.full((span,), -1, jnp.int32), document_index[0, 0]])
     numbers = lax.dynamic_slice_in_dim(numbers, place * rows, span + rows, 0)
@@ -380,60 +374,58 @@
 
     outputs = numbered("stack", [((stack_rows, HEAD_SIZE), bf16)] * BLOCKS)
     outputs |= numbered("probs", [((window, stack_rows), f32)] * BLOCKS)
-    outputs.update(held=(held[0].shape, bf16))
+    outputs.update(held=(held[1].shape, bf16))
     ahead = run(
         forward,
         z,
-        dict(fq=fq, at=at, up=matrix_copy, halo=halo, own=own, bias=bias, held_in=held[0]),
+        dict(fq=fq, at=at, up=matrix, halo=halo, own=own, bias=bias, held_in=held[1]),
         outputs,
         {},
         flops,
     )
-    cots[2] = passed_along(ahead.held, "section", -1)
-
-    halo_type = bf16 if per_head == 1 else f32
-    halo_shape = ((span, chunks * PAIR), halo_type)
+    cots.append(passed_along(ahead.held, "section", -1))
+
+    halo_shape = ((span, chunks * PAIR), bf16 if per_head == 1 else f32)
     own_shape = ((rows, chunks * PAIR), f32)
     dq_shape = ((rows, columns), bf16)
     input_shape = ((rank, rows), f32)
-    terms = []
+    terms = {away: [] for away in range(chunks)}
+    grads = []
     state = None
-    for steps in [(0, 1)] + [(step,) for step in range(2, last)]:
-        inputs = dict(fq=fq, at=at, halo=halo, own=own, bias=bias, cot=cots[steps[0]])
-        inputs |= numbered("up", [ups[step] for step in steps])
+    for step in range(last):
+        away = last - step
+        inputs = dict(fq=fq, at=at, halo=halo, own=own, bias=bias, cot=cots[step], up=ups[away])
+        inputs |= numbered("term", terms[away])
         outputs = dict(
-            dq=dq_shape,
             halo_grads=halo_shape,
             own_grads=own_shape,
             input_grad=input_shape,
-            grad=((rows, width), bf16),
+            grad=piece,
+            weight=((rank, width), bf16),
         )
-        outputs |= numbered("term", [((rank, width), bf16)] * len(steps))
-        scratch = sems(len(steps))
-        later = []
-        if state is None:
-            later = held[1:-1]
-            scratch.update(early=pltpu.VMEM((rows, width), bf16))
-        else:
+        if step > 0:
             inputs.update(
-                dq_in=state.dq,
                 halo_grads_in=state.halo_grads,
                 own_grads_in=state.own_grads,
                 input_sum=state.input_grad,
-                pending=state.grad,
             )
-        if steps[0] == 2:
-            later = held[-1:]
-        named = numbered("later", later)
-        inputs |= {name + IN: array for name, array in named.items()}
-        outputs |= {name: (array.shape, bf16) for name, array in named.items()}
-        body = functools.partial(whole, steps)
+        if 0 < step < last - 1:
+            inputs.update(pending=grads[-1])
+            outputs.update(dq=dq_shape)
+            if step > 1:
+                inputs.update(dq_in=dq)
+        if step + 2 < len(held):
+            inputs.update(held_in=held[step + 2])
+            outputs.update(held=(held[step + 2].shape, bf16))
+        body = functools.partial(whole, step)
         body.__name__ = whole.__name__
-        state = run(body, z, inputs, outputs, scratch, 2 * len(steps) * flops)
-        for array in listed(state, "later"):
-            cots[len(cots) + 1] = passed_along(array, "section", -1)
-        for step, term in zip(steps, listed(state, "term")):
-            terms.append(passed_along(term, "seq", -(step + 1)))
+        state = run(body, z, inputs, outputs, sems(1), 2 * flops)
+        grads.append(state.grad)
+        dq = getattr(state, "dq", None) if step < last - 1 else dq
+        if step + 2 < len(held):
+            cots.append(passed_along(state.held, "section", -1))
+        bit = low_bit(away)
+        terms[away - bit].append(swapped(state.weight, "seq", bit))
 
     common = dict(at=at, up=matrix, halo=halo, own=own)
     outputs = dict(
@@ -452,14 +444,14 @@
             cot=cots[last],
             stack=ahead.stack0,
             probs=ahead.probs0,
-            dq_in=state.dq,
+            dq_in=dq,
             halo_grads_in=state.halo_grads,
             input_sum=state.input_grad,
-            pending=state.grad,
         )
-        | numbered("term", terms[:-1]),
+        | numbered("pending", grads[-BLOCKS:])
+        | numbered("term", terms[0][:-1]),
         outputs,
-        sems(1),
+        sems(BLOCKS),
         flops,
     )
     halo_grads = early.halo_grads
@@ -479,7 +471,7 @@
         z,
         common
         | dict(cot=cots[last + 1], probs=ahead.probs1, weight_part=early.weight_part)
-        | numbered("term", terms[-1:]),
+        | numbered("term", terms[0][-1:]),
         outputs,
         dict(total=pltpu.VMEM((rank, width), bf16)),
         flops,

time: 41.4 us -> 38.4 us (0.928)
  waiting for transfers between devices: 12.9 us -> 6.82 us
  starting transfers between devices: 15 us -> 17.2 us
  local copies, waits for them, and re-layouts: 0.18 us -> 1.44 us
    ppermute x14 -> x10, waiting for transfers between devices: 12.9 us -> 3.56 us  [passed_along(): return lax.ppermute(value, axis, pairs)]
    ppermute x0 -> x6, starting transfers between devices: none -> 4.71 us  [swapped(): return lax.ppermute(value, axis, pairs)]
    ppermute x0 -> x6, waiting for transfers between devices: none -> 3.26 us  [swapped(): return lax.ppermute(value, axis, pairs)]
    ppermute x14 -> x10, starting transfers between devices: 15 us -> 12.5 us  [passed_along(): return lax.ppermute(value, axis, pairs)]
    unnamed x10 -> x6, local copies, waits for them, and re-layouts: 0.02 us -> 1.28 us
    pallas_call x8 -> x9, Pallas kernels: 11.4 us -> 11 us  [run(): pl.pallas_call(kernel, in_specs=[HBM if name in IN_HBM else VMEM for name...]
  transfers between devices with their start and end apart: 14 -> 16, of which waited for: 5 -> 5; matrix products, arithmetic and copies ran while one was open for 1% -> 1% of each run, Pallas kernels for 25% -> 26%
where the time goes in v1:
time: 38.4 us; the launch traced here: 38.2 us
  starting transfers between devices  17.2 us (45%)
  Pallas kernels  11 us (29%)
  waiting for transfers between devices  6.82 us (18%)
  local copies, waits for them, and re-layouts  1.44 us (4%)
  other arithmetic  0.92 us (2%)
  between operations  0.79 us (2%)
    ppermute x10, starting transfers between devices, passed_along(): return lax.ppermute(value, axis, pairs)  12.5 us
    pallas_call x9, Pallas kernels, run(): pl.pallas_call(kernel, in_specs=[HBM if name in IN_HBM else VMEM for name...  11 us
    ppermute x6, starting transfers between devices, swapped(): return lax.ppermute(value, axis, pairs)  4.71 us
    ppermute x10, waiting for transfers between devices, passed_along(): return lax.ppermute(value, axis, pairs)  3.56 us
    ppermute x6, waiting for transfers between devices, swapped(): return lax.ppermute(value, axis, pairs)  3.26 us
    unnamed x6, local copies, waits for them, and re-layouts  1.28 us
  transfers between devices with their start and end apart: 16, of which 5 were waited for; matrix products, arithmetic and copies ran while one was open for 1% of the time, Pallas kernels for 26%

profile of v1, /device:TPU:0, one launch (start us, length us, event | category | flops | bytes accessed | tf_op | source)
XLA Modules:
  0.0 38.2 jit_solution(11697560403717074784)
XLA Ops:
  0.6 1.0 %split_first.1.refs_3_ = bf16[128,1024]{1,0:T(8,128)(2,1)S(1)} custom-call(bf16[128,4096]{1,0:T(8,128)(2,1)} %bitcast.26), custom_call_target="tpu_custom_call" | custom-call | bytes 1048576 | tf_op jit(solution)/shard_map/split_first/pallas_call | solution.py:75
  1.6 3.0 %collective-permute-start.3 = (bf16[128,1024]{1,0:T(8,128)(2,1)S(1)}, bf16[128,1024]{1,0:T(8,128)(2,1)S(1)}, u32[]{:S(2)}, u32[]{:S(2)}) collective-permute-start(bf16[128,1024]{1,0:T(8,128)(2,1)S(1)} %split_first.1.refs_3_), channel_id=1, source_target_pairs={{0,16},{16,0},{1,17},{17,1},{2,18},{18,2},{3,19},{19,3},{4,20},{20... | collective-permute-start | bytes 786440 | tf_op jit(solution)/shard_map/ppermute | solution.py:30
  4.6 1.6 %split_rest.1 = (bf16[128,1024]{1,0:T(8,128)(2,1)S(1)}, bf16[128,1024]{1,0:T(8,128)(2,1)S(1)}, bf16[64,1024]{1,0:T(8,128)(2,1)S(1)}, bf16[64,1024]{1,0:T(8,128)(...) custom-call(bf16[128,4096]{1,0:T(8,128)(2,1)} %bitcast.27, bf16[128,1024]{1,0:T(8,128)(2,1)} %bitcast.29, ...), custom_call_target="tpu_custom_call" | custom-call | bytes 1048576 | tf_op jit(solution)/shard_map/split_rest/pallas_call | solution.py:75
  6.3 1.6 %collective-permute-start.2 = (bf16[64,1024]{1,0:T(8,128)(2,1)S(1)}, bf16[64,1024]{1,0:T(8,128)(2,1)S(1)}, u32[]{:S(2)}, u32[]{:S(2)}) collective-permute-start(bf16[64,1024]{1,0:T(8,128)(2,1)S(1)} %get-tuple-element.49.refs_2_.refs_1_), channel_id=1, source_target_pairs={{0,8},{4,12},{8,0},{12,4},{1,9},{5,13},{9,1},{13,5},{2,10},{6,14},... | collective-permute-start | bytes 393224 | tf_op jit(solution)/shard_map/ppermute | solution.py:35
  7.9 0.5 %collective-permute-start.1 = (bf16[128,1024]{1,0:T(8,128)(2,1)S(1)}, bf16[128,1024]{1,0:T(8,128)(2,1)S(1)}, u32[]{:S(2)}, u32[]{:S(2)}) collective-permute-start(bf16[128,1024]{1,0:T(8,128)(2,1)S(1)} %get-tuple-element.51), channel_id=1, source_target_pairs={{0,16},{16,0},{1,17},{17,1},{2,18},{18,2},{3,19},{19,3},{4,20},{20... | collective-permute-start | bytes 786440 | tf_op jit(solution)/shard_map/ppermute | solution.py:30
  8.4 0.7 %copy-done.2 = s32[1,1,512]{2,1,0:T(1,128)S(1)} copy-done((s32[1,1,512]{2,1,0:T(1,128)S(1)}, s32[1,1,512]{2,1,0:T(1,128)}, u32[]{:S(2)}) %copy-start.2) | copy-done | bytes 2072
  9.3 0.1 fusion.2
  9.4 3.2 %collective-permute-done.2.refs_6_ = bf16[64,1024]{1,0:T(8,128)(2,1)S(1)} collective-permute-done((bf16[64,1024]{1,0:T(8,128)(2,1)S(1)}, bf16[64,1024]{1,0:T(8,128)(2,1)S(1)}, u32[]{:S(2)}, u32[]{:S(2)}) %collective-permute-start.2) | collective-permute-done | bytes 131104 | tf_op jit(solution)/shard_map/ppermute | solution.py:35
  12.7 0.9 %collective-permute-start.4 = (bf16[64,1024]{1,0:T(8,128)(2,1)S(1)}, bf16[64,1024]{1,0:T(8,128)(2,1)S(1)}, u32[]{:S(2)}, u32[]{:S(2)}) collective-permute-start(bf16[64,1024]{1,0:T(8,128)(2,1)S(1)} %collective-permute-done.2.refs_6_), channel_id=1, source_target_pairs={{0,4},{4,0},{8,12},{12,8},{1,5},{5,1},{9,13},{13,9},{2,6},{6,2},{1... | collective-permute-start | bytes 393224 | tf_op jit(solution)/shard_map/ppermute | solution.py:35
  13.6 0.1 maximum_maximum_fusion.refs_4_.refs_5_
  13.7 0.6 %copy-done.1 = bf16[1,1,128,64]{2,3,1,0:T(8,128)(2,1)S(1)} copy-done((bf16[1,1,128,64]{2,3,1,0:T(8,128)(2,1)S(1)}, bf16[1,1,128,64]{2,3,1,0:T(8,128)(2,1)}, u32[]{:S(2)}) %copy-start.1) | copy-done | bytes 16408
  14.3 0.6 %forward.1 = (bf16[512,128]{1,0:T(8,128)(2,1)S(1)}, bf16[512,128]{1,0:T(8,128)(2,1)S(1)}, f32[128,512]{1,0:T(8,128)S(1)}, f32[128,512]{1,0:T(8,128)S(1)}, bf16[128,1024]{1,0:T(8,128)(2,1)S(1)}) custom-call(bf16[128,4096]{1,0:T(8,128)(2,1)S(1)} %bitcast.15, bf16[64,128]{1,0:T(8,128)(2,1)S(1)} %bitcast.19, ...), custom_call_target="tpu_custom_call", output_to_operand_aliasing={{4}: (6, {})} | custom-call | flops 83886080 | bytes 1048576 | tf_op jit(solution)/shard_map/forward/pallas_call | solution.py:75
  14.9 0.1 collective-permute-start.8
  15.0 1.4 %whole.3 = (bf16[64,1024]{1,0:T(8,128)(2,1)S(1)}, f32[128,1024]{1,0:T(8,128)S(1)}, f32[64,128]{1,0:T(8,128)S(1)}, bf16[128,1024]{1,0:T(8,128)(2,1)S(1)}, bf16[64...) custom-call(bf16[128,4096]{1,0:T(8,128)(2,1)S(1)} %bitcast.16, ...), custom_call_target="tpu_custom_call", output_to_operand_aliasing={{5}: (7, {})} | custom-call | flops 167772160 | bytes 1048576 | tf_op jit(solution)/shard_map/whole/pallas_call | solution.py:75
  16.5 0.5 %collective-permute-start.9 = (bf16[64,1024]{1,0:T(8,128)(2,1)S(1)}, bf16[64,1024]{1,0:T(8,128)(2,1)S(1)}, u32[]{:S(2)}, u32[]{:S(2)}) collective-permute-start(bf16[64,1024]{1,0:T(8,128)(2,1)S(1)} %get-tuple-element.49.refs_2_.refs_1_), channel_id=1, source_target_pairs={{0,4},{4,0},{8,12},{12,8},{1,5},{5,1},{9,13},{13,9},{2,6},{6,2},{1... | collective-permute-start | bytes 393224 | tf_op jit(solution)/shard_map/ppermute | solution.py:35
  17.0 2.0 %collective-permute-start.7 = (bf16[64,1024]{1,0:T(8,128)(2,1)S(1)}, bf16[64,1024]{1,0:T(8,128)(2,1)S(1)}, u32[]{:S(2)}, u32[]{:S(2)}) collective-permute-start(bf16[64,1024]{1,0:T(8,128)(2,1)S(1)} %get-tuple-element.63), channel_id=1, source_target_pairs={{0,16},{16,0},{1,17},{17,1},{2,18},{18,2},{3,19},{19,3},{4,20},{20... | collective-permute-start | bytes 393224 | tf_op jit(solution)/shard_map/ppermute | solution.py:30
  19.0 1.6 %whole.4 = (bf16[64,1024]{1,0:T(8,128)(2,1)S(1)}, f32[128,1024]{1,0:T(8,128)S(1)}, f32[64,128]{1,0:T(8,128)S(1)}, bf16[128,1024]{1,0:T(8,128)(2,1)S(1)}, bf16[64...) custom-call(bf16[128,4096]{1,0:T(8,128)(2,1)S(1)} %bitcast.17, ...), custom_call_target="tpu_custom_call", output_to_operand_aliasing={{0}: (8, {}), {1}: (9, {}), {6}: (12, {})} | custom-call | flops 167772160 | bytes 1048576 | tf_op jit(solution)/shard_map/whole/pallas_call | solution.py:75
  20.6 1.6 %collective-permute-start.10 = (bf16[64,1024]{1,0:T(8,128)(2,1)S(1)}, bf16[64,1024]{1,0:T(8,128)(2,1)S(1)}, u32[]{:S(2)}, u32[]{:S(2)}) collective-permute-start(bf16[64,1024]{1,0:T(8,128)(2,1)S(1)} %get-tuple-element.75), channel_id=1, source_target_pairs={{0,8},{4,12},{8,0},{12,4},{1,9},{5,13},{9,1},{13,5},{2,10},{6,14},... | collective-permute-start | bytes 393224 | tf_op jit(solution)/shard_map/ppermute | solution.py:35
  22.1 0.8 %collective-permute-start.6 = (bf16[64,1024]{1,0:T(8,128)(2,1)S(1)}, bf16[64,1024]{1,0:T(8,128)(2,1)S(1)}, u32[]{:S(2)}, u32[]{:S(2)}) collective-permute-start(bf16[64,1024]{1,0:T(8,128)(2,1)S(1)} %get-tuple-element.59), channel_id=1, source_target_pairs={{0,16},{16,0},{1,17},{17,1},{2,18},{18,2},{3,19},{19,3},{4,20},{20... | collective-permute-start | bytes 393224 | tf_op jit(solution)/shard_map/ppermute | solution.py:30
  23.0 1.2 %collective-permute-done.8.refs_5_ = bf16[128,1024]{1,0:T(8,128)(2,1)S(1)} collective-permute-done((bf16[128,1024]{1,0:T(8,128)(2,1)S(1)}, bf16[128,1024]{1,0:T(8,128)(2,1)S(1)}, u32[]{:S(2)}, u32[]{:S(2)}) %collective-permute-start.8) | collective-permute-done | bytes 262176 | tf_op jit(solution)/shard_map/ppermute | solution.py:30
  24.1 1.4 %whole.5 = (bf16[64,1024]{1,0:T(8,128)(2,1)S(1)}, f32[128,1024]{1,0:T(8,128)S(1)}, f32[64,128]{1,0:T(8,128)S(1)}, bf16[128,1024]{1,0:T(8,128)(2,1)S(1)}, bf16[64,1024]{1,0:T(8,128)(2,1)S(1)}) custom-call(bf16[128,4096]{1,0:T(8,128)(2,1)S(1)} %bitcast.18, bf16[64,128]{1,0:T(8,128)(2,1)S(1)} %bitcast.22, ...), custom_call_target="tpu_custom_call", output_to_operand_aliasing={{0}: (7, {}), {1}: (8, {})} | custom-call | flops 167772160 | bytes 1048576 | tf_op jit(solution)/shard_map/whole/pallas_call | solution.py:75
  25.6 1.3 %collective-permute-done.7.refs_4_ = bf16[64,1024]{1,0:T(8,128)(2,1)S(1)} collective-permute-done((bf16[64,1024]{1,0:T(8,128)(2,1)S(1)}, bf16[64,1024]{1,0:T(8,128)(2,1)S(1)}, u32[]{:S(2)}, u32[]{:S(2)}) %collective-permute-start.7) | collective-permute-done | bytes 131104 | tf_op jit(solution)/shard_map/ppermute | solution.py:30
  26.9 1.3 %front.1 = (bf16[128,4096]{1,0:T(8,128)(2,1)}, bf16[64,1024]{1,0:T(8,128)(2,1)S(1)}, f32[128,256]{1,0:T(8,128)S(1)}, f32[64,1024]{1,0:T(8,128)S(1)}, f32[64,128]...) custom-call(bf16[64,128]{1,0:T(8,128)(2,1)S(1)} %bitcast.23, ...), custom_call_target="tpu_custom_call", output_to_operand_aliasing={{0}: (7, {}), {1}: (8, {})} | custom-call | flops 83886080 | bytes 1048576 | tf_op jit(solution)/shard_map/front/pallas_call | solution.py:75
  28.2 0.4 collective-permute-start.12
  28.6 0.2 collective-permute-done.6.refs_4_.refs_2_
  28.8 0.6 %back.1 = (bf16[64,1024]{1,0:T(8,128)(2,1)S(1)}, bf16[128,512]{1,0:T(8,128)(2,1)S(1)}, bf16[16,1024]{1,0:T(8,128)(2,1)S(1)}, bf16[16,1024]{1,0:T(8,128)(2,1)S(1)...) custom-call(bf16[64,128]{1,0:T(8,128)(2,1)S(1)} %bitcast.24, ...), custom_call_target="tpu_custom_call" | custom-call | flops 83886080 | bytes 1048576 | tf_op jit(solution)/shard_map/back/pallas_call | solution.py:75
  29.4 1.6 %collective-permute-start.13 = (bf16[16,1024]{1,0:T(8,128)(2,1)S(1)}, bf16[16,1024]{1,0:T(8,128)(2,1)S(1)}, u32[]{:S(2)}, u32[]{:S(2)}) collective-permute-start(bf16[16,1024]{1,0:T(8,128)(2,1)S(1)} %get-tuple-element.91), channel_id=1, source_target_pairs={{0,1},{1,2},{2,3},{3,0},{4,5},{5,6},{6,7},{7,4},{8,9},{9,10},{10,1... | collective-permute-start | bytes 98312 | tf_op jit(solution)/shard_map/ppermute | solution.py:30
  31.0 2.6 %collective-permute-start.14 = (bf16[16,1024]{1,0:T(8,128)(2,1)S(1)}, bf16[16,1024]{1,0:T(8,128)(2,1)S(1)}, u32[]{:S(2)}, u32[]{:S(2)}) collective-permute-start(bf16[16,1024]{1,0:T(8,128)(2,1)S(1)} %get-tuple-element.92), channel_id=1, source_target_pairs={{0,2},{1,3},{2,0},{3,1},{4,6},{5,7},{6,4},{7,5},{8,10},{9,11},{10,... | collective-permute-start | bytes 98312 | tf_op jit(solution)/shard_map/ppermute | solution.py:30
  33.6 1.3 %collective-permute-start.15 = (bf16[16,1024]{1,0:T(8,128)(2,1)S(1)}, bf16[16,1024]{1,0:T(8,128)(2,1)S(1)}, u32[]{:S(2)}, u32[]{:S(2)}) collective-permute-start(bf16[16,1024]{1,0:T(8,128)(2,1)S(1)} %get-tuple-element.93), channel_id=1, source_target_pairs={{0,3},{1,0},{2,1},{3,2},{4,7},{5,4},{6,5},{7,6},{8,11},{9,8},{10,9... | collective-permute-start | bytes 98312 | tf_op jit(solution)/shard_map/ppermute | solution.py:30
  35.0 1.6 %finish.1 = (bf16[128,4096]{1,0:T(8,128)(2,1)}, f32[128,1024]{1,0:T(8,128)S(1)}, bf16[64,128]{1,0:T(8,128)(2,1)}, bf16[16,1024]{1,0:T(8,128)(2,1)S(1)}, bf16[128,1024]{1,0:T(8,128)(2,1)}) custom-call(bf16[64,128]{1,0:T(8,128)(2,1)S(1)} %bitcast.25, ...), custom_call_target="tpu_custom_call", output_to_operand_aliasing={{0}: (8, {}), {1}: (9, {}), {3}: (10, {})} | custom-call | flops 83886080 | bytes 1048576 | tf_op jit(solution)/shard_map/finish/pallas_call | solution.py:75
  36.6 0.9 %collective-permute-done.15 = bf16[16,1024]{1,0:T(8,128)(2,1)S(1)} collective-permute-done((bf16[16,1024]{1,0:T(8,128)(2,1)S(1)}, bf16[16,1024]{1,0:T(8,128)(2,1)S(1)}, u32[]{:S(2)}, u32[]{:S(2)}) %collective-permute-start.15) | collective-permute-done | bytes 32800 | tf_op jit(solution)/shard_map/ppermute | solution.py:30
  37.5 0.6 %add_bitcast_fusion = f32[1,16,1024]{2,1,0:T(8,128)} fusion(bf16[16,1024]{1,0:T(8,128)(2,1)S(1)} %collective-permute-done.15, bf16[16,1024]{1,0:T(8,128)(2,1)S(1)} %collective-permute-done.14, bf16[16,1024]{1,0:T(8,128)(2,1)S(1)} %collective-permute-done.13, bf16[16,1024]{1,0:T(8,128)(2,1)S(1)} %get-tuple-element.90), kind=kLoop, calls=%fused_computation.1 | loop fusion | flops 114688 | bytes 196608 | tf_op jit(solution)/shard_map/broadcast_in_dim | solution.py:526
  (22 shorter events, 0.5 us)
Async XLA Ops:
  1.6 13.4 %collective-permute-start.3 = (bf16[128,1024]{1,0:T(8,128)(2,1)S(1)}, bf16[128,1024]{1,0:T(8,128)(2,1)S(1)}, u32[]{:S(2)}, u32[]{:S(2)}) collective-permute-start(bf16[128,1024]{1,0:T(8,128)(2,1)S(1)} %split_first.1.refs_3_), channel_id=1, source_target_pairs={{0,16},{16,0},{1,17},{17,1},{2,18},{18,2},{3,19},{19,3},{4,20},{20... | collective-permute-start | bytes 786440 | tf_op jit(solution)/shard_map/ppermute | solution.py:30
  4.6 9.1 %copy-start = (bf16[1,1,128,4096]{3,2,1,0:T(8,128)(2,1)S(1)}, bf16[1,1,128,4096]{3,2,1,0:T(8,128)(2,1)}, u32[]{:S(2)}) copy-start(bf16[1,1,128,4096]{3,2,1,0:T(8,128)(2,1)} %param.6) | copy-start | bytes 3145732
  6.2 7.5 %collective-permute-start = (bf16[64,1024]{1,0:T(8,128)(2,1)S(1)}, bf16[64,1024]{1,0:T(8,128)(2,1)S(1)}, u32[]{:S(2)}, u32[]{:S(2)}) collective-permute-start(bf16[64,1024]{1,0:T(8,128)(2,1)S(1)} %slice.15), channel_id=1, source_target_pairs={{0,4},{4,8},{8,12},{12,0},{1,5},{5,9},{9,13},{13,1},{2,6},{6,10},{... | collective-permute-start | bytes 393224 | tf_op jit(solution)/shard_map/ppermute | solution.py:30
  6.3 6.4 %collective-permute-start.2 = (bf16[64,1024]{1,0:T(8,128)(2,1)S(1)}, bf16[64,1024]{1,0:T(8,128)(2,1)S(1)}, u32[]{:S(2)}, u32[]{:S(2)}) collective-permute-start(bf16[64,1024]{1,0:T(8,128)(2,1)S(1)} %get-tuple-element.49.refs_2_.refs_1_), channel_id=1, source_target_pairs={{0,8},{4,12},{8,0},{12,4},{1,9},{5,13},{9,1},{13,5},{2,10},{6,14},... | collective-permute-start | bytes 393224 | tf_op jit(solution)/shard_map/ppermute | solution.py:35
  7.9 11.1 %collective-permute-start.1 = (bf16[128,1024]{1,0:T(8,128)(2,1)S(1)}, bf16[128,1024]{1,0:T(8,128)(2,1)S(1)}, u32[]{:S(2)}, u32[]{:S(2)}) collective-permute-start(bf16[128,1024]{1,0:T(8,128)(2,1)S(1)} %get-tuple-element.51), channel_id=1, source_target_pairs={{0,16},{16,0},{1,17},{17,1},{2,18},{18,2},{3,19},{19,3},{4,20},{20... | collective-permute-start | bytes 786440 | tf_op jit(solution)/shard_map/ppermute | solution.py:30
  8.4 0.7 %copy-start.2 = (s32[1,1,512]{2,1,0:T(1,128)S(1)}, s32[1,1,512]{2,1,0:T(1,128)}, u32[]{:S(2)}) copy-start(s32[1,1,512]{2,1,0:T(1,128)} %param.11) | copy-start | bytes 6148
  12.7 2.3 %collective-permute-start.4 = (bf16[64,1024]{1,0:T(8,128)(2,1)S(1)}, bf16[64,1024]{1,0:T(8,128)(2,1)S(1)}, u32[]{:S(2)}, u32[]{:S(2)}) collective-permute-start(bf16[64,1024]{1,0:T(8,128)(2,1)S(1)} %collective-permute-done.2.refs_6_), channel_id=1, source_target_pairs={{0,4},{4,0},{8,12},{12,8},{1,5},{5,1},{9,13},{13,9},{2,6},{6,2},{1... | collective-permute-start | bytes 393224 | tf_op jit(solution)/shard_map/ppermute | solution.py:35
  13.6 0.7 %copy-start.1 = (bf16[1,1,128,64]{2,3,1,0:T(8,128)(2,1)S(1)}, bf16[1,1,128,64]{2,3,1,0:T(8,128)(2,1)}, u32[]{:S(2)}) copy-start(bf16[1,1,128,64]{2,3,1,0:T(8,128)(2,1)} %param.8) | copy-start | bytes 49156
  14.9 9.2 %collective-permute-start.8 = (bf16[128,1024]{1,0:T(8,128)(2,1)S(1)}, bf16[128,1024]{1,0:T(8,128)(2,1)S(1)}, u32[]{:S(2)}, u32[]{:S(2)}) collective-permute-start(bf16[128,1024]{1,0:T(8,128)(2,1)S(1)} %get-tuple-element.67), channel_id=1, source_target_pairs={{0,16},{16,0},{1,17},{17,1},{2,18},{18,2},{3,19},{19,3},{4,20},{20... | collective-permute-start | bytes 786440 | tf_op jit(solution)/shard_map/ppermute | solution.py:30
  16.4 2.6 %collective-permute-start.5 = (bf16[64,1024]{1,0:T(8,128)(2,1)S(1)}, bf16[64,1024]{1,0:T(8,128)(2,1)S(1)}, u32[]{:S(2)}, u32[]{:S(2)}) collective-permute-start(bf16[64,1024]{1,0:T(8,128)(2,1)S(1)} %get-tuple-element.53), channel_id=1, source_target_pairs={{0,4},{4,0},{8,12},{12,8},{1,5},{5,1},{9,13},{13,9},{2,6},{6,2},{1... | collective-permute-start | bytes 393224 | tf_op jit(solution)/shard_map/ppermute | solution.py:35
  16.5 6.5 %collective-permute-start.9 = (bf16[64,1024]{1,0:T(8,128)(2,1)S(1)}, bf16[64,1024]{1,0:T(8,128)(2,1)S(1)}, u32[]{:S(2)}, u32[]{:S(2)}) collective-permute-start(bf16[64,1024]{1,0:T(8,128)(2,1)S(1)} %get-tuple-element.49.refs_2_.refs_1_), channel_id=1, source_target_pairs={{0,4},{4,0},{8,12},{12,8},{1,5},{5,1},{9,13},{13,9},{2,6},{6,2},{1... | collective-permute-start | bytes 393224 | tf_op jit(solution)/shard_map/ppermute | solution.py:35
  17.0 9.9 %collective-permute-start.7 = (bf16[64,1024]{1,0:T(8,128)(2,1)S(1)}, bf16[64,1024]{1,0:T(8,128)(2,1)S(1)}, u32[]{:S(2)}, u32[]{:S(2)}) collective-permute-start(bf16[64,1024]{1,0:T(8,128)(2,1)S(1)} %get-tuple-element.63), channel_id=1, source_target_pairs={{0,16},{16,0},{1,17},{17,1},{2,18},{18,2},{3,19},{19,3},{4,20},{20... | collective-permute-start | bytes 393224 | tf_op jit(solution)/shard_map/ppermute | solution.py:30
  20.6 6.4 %collective-permute-start.10 = (bf16[64,1024]{1,0:T(8,128)(2,1)S(1)}, bf16[64,1024]{1,0:T(8,128)(2,1)S(1)}, u32[]{:S(2)}, u32[]{:S(2)}) collective-permute-start(bf16[64,1024]{1,0:T(8,128)(2,1)S(1)} %get-tuple-element.75), channel_id=1, source_target_pairs={{0,8},{4,12},{8,0},{12,4},{1,9},{5,13},{9,1},{13,5},{2,10},{6,14},... | collective-permute-start | bytes 393224 | tf_op jit(solution)/shard_map/ppermute | solution.py:35
  22.1 6.6 %collective-permute-start.6 = (bf16[64,1024]{1,0:T(8,128)(2,1)S(1)}, bf16[64,1024]{1,0:T(8,128)(2,1)S(1)}, u32[]{:S(2)}, u32[]{:S(2)}) collective-permute-start(bf16[64,1024]{1,0:T(8,128)(2,1)S(1)} %get-tuple-element.59), channel_id=1, source_target_pairs={{0,16},{16,0},{1,17},{17,1},{2,18},{18,2},{3,19},{19,3},{4,20},{20... | collective-permute-start | bytes 393224 | tf_op jit(solution)/shard_map/ppermute | solution.py:30
  25.5 3.3 %collective-permute-start.11 = (bf16[64,1024]{1,0:T(8,128)(2,1)S(1)}, bf16[64,1024]{1,0:T(8,128)(2,1)S(1)}, u32[]{:S(2)}, u32[]{:S(2)}) collective-permute-start(bf16[64,1024]{1,0:T(8,128)(2,1)S(1)} %get-tuple-element.77), channel_id=1, source_target_pairs={{0,4},{4,0},{8,12},{12,8},{1,5},{5,1},{9,13},{13,9},{2,6},{6,2},{1... | collective-permute-start | bytes 393224 | tf_op jit(solution)/shard_map/ppermute | solution.py:35
  28.2 6.7 %collective-permute-start.12 = (bf16[64,1024]{1,0:T(8,128)(2,1)S(1)}, bf16[64,1024]{1,0:T(8,128)(2,1)S(1)}, u32[]{:S(2)}, u32[]{:S(2)}) collective-permute-start(bf16[64,1024]{1,0:T(8,128)(2,1)S(1)} %get-tuple-element.84), channel_id=1, source_target_pairs={{0,12},{4,0},{8,4},{12,8},{1,13},{5,1},{9,5},{13,9},{2,14},{6,2},{... | collective-permute-start | bytes 393224 | tf_op jit(solution)/shard_map/ppermute | solution.py:30
  29.4 7.2 %collective-permute-start.13 = (bf16[16,1024]{1,0:T(8,128)(2,1)S(1)}, bf16[16,1024]{1,0:T(8,128)(2,1)S(1)}, u32[]{:S(2)}, u32[]{:S(2)}) collective-permute-start(bf16[16,1024]{1,0:T(8,128)(2,1)S(1)} %get-tuple-element.91), channel_id=1, source_target_pairs={{0,1},{1,2},{2,3},{3,0},{4,5},{5,6},{6,7},{7,4},{8,9},{9,10},{10,1... | collective-permute-start | bytes 98312 | tf_op jit(solution)/shard_map/ppermute | solution.py:30
  31.0 5.6 %collective-permute-start.14 = (bf16[16,1024]{1,0:T(8,128)(2,1)S(1)}, bf16[16,1024]{1,0:T(8,128)(2,1)S(1)}, u32[]{:S(2)}, u32[]{:S(2)}) collective-permute-start(bf16[16,1024]{1,0:T(8,128)(2,1)S(1)} %get-tuple-element.92), channel_id=1, source_target_pairs={{0,2},{1,3},{2,0},{3,1},{4,6},{5,7},{6,4},{7,5},{8,10},{9,11},{10,... | collective-permute-start | bytes 98312 | tf_op jit(solution)/shard_map/ppermute | solution.py:30
  33.6 3.9 %collective-permute-start.15 = (bf16[16,1024]{1,0:T(8,128)(2,1)S(1)}, bf16[16,1024]{1,0:T(8,128)(2,1)S(1)}, u32[]{:S(2)}, u32[]{:S(2)}) collective-permute-start(bf16[16,1024]{1,0:T(8,128)(2,1)S(1)} %get-tuple-element.93), channel_id=1, source_target_pairs={{0,3},{1,0},{2,1},{3,2},{4,7},{5,4},{6,5},{7,6},{8,11},{9,8},{10,9... | collective-permute-start | bytes 98312 | tf_op jit(solution)/shard_map/ppermute | solution.py:30

commit v2 on v1

--- a/solution.py
+++ b/solution.py
@@ -20,8 +20,10 @@
 LIMIT = 16 * 1024 * 1024
 IN = "_in"
 IN_HBM = ("upstream", "pairs", "matrix", "dq", "dq" + IN)
+ANYWHERE = ("held", "held" + IN, "after")
 VMEM = pl.BlockSpec(memory_space=pltpu.VMEM)
 HBM = pl.BlockSpec(memory_space=pltpu.HBM)
+ANY = pl.BlockSpec(memory_space=pl.ANY)
 
 
 def passed_along(value, axis, steps):
@@ -54,6 +56,10 @@
     while hasattr(refs, name + str(len(found))):
         found.append(getattr(refs, name + str(len(found))))
     return found
+
+
+def spec_of(name):
+    return HBM if name in IN_HBM else ANY if name in ANYWHERE else VMEM
 
 
 def run(body, sizes, inputs, outputs, scratch, flops=0):
@@ -74,14 +80,14 @@
     }
     results = pl.pallas_call(
         kernel,
-        in_specs=[HBM if name in IN_HBM else VMEM for name in inputs],
-        out_specs=[HBM if name in IN_HBM else VMEM for name in outputs],
+        in_specs=[spec_of(name) for name in inputs],
+        out_specs=[spec_of(name) for name in outputs],
         out_shape=[jax.ShapeDtypeStruct(shape, kind) for shape, kind in outputs.values()],
         scratch_shapes=list(scratch.values()),
         input_output_aliases=aliases,
         compiler_params=pltpu.CompilerParams(vmem_limit_bytes=LIMIT),
         cost_estimate=pl.CostEstimate(
-            flops=flops, bytes_accessed=1024 * 1024, transcendentals=flops // 1024
+            flops=flops // 1024, bytes_accessed=1024, transcendentals=flops // 1024
         ),
         name=body.__name__,
     )(*operands)
@@ -118,17 +124,25 @@
         copy.wait()
 
 
+def split_second(z, refs):
+    copies = []
+    source = refs.upstream.at[:, chunk_columns(z, 1)]
+    copy_rows(source, refs.piece, refs.sems, copies, COPIES)
+    copy_rows(refs.matrix, refs.matrix_copy, refs.sems, copies, COPIES)
+    copy_rows(refs.pairs, refs.pairs_copy, refs.sems, copies, COPIES)
+    for copy in copies:
+        copy.wait()
+
+
 def split_rest(z, refs):
     copies = []
     pieces = listed(refs, "piece")
-    for step, piece in zip(range(1, z.chunks - 1), pieces):
+    for step, piece in zip(range(2, z.chunks - 1), pieces):
         copy_rows(refs.upstream.at[:, chunk_columns(z, step)], piece, refs.sems, copies, COPIES)
     for index, piece in enumerate(pieces[-BLOCKS:]):
         rows = pl.ds(index * z.block, z.block)
         source = refs.upstream.at[rows, chunk_columns(z, z.chunks - 1)]
         copy_rows(source, piece, refs.sems, copies, COPIES)
-    copy_rows(refs.matrix, refs.matrix_copy, refs.sems, copies, COPIES)
-    copy_rows(refs.pairs, refs.pairs_copy, refs.sems, copies, COPIES)
     for copy in copies:
         copy.wait()
 
@@ -226,9 +240,8 @@
     for term in listed(refs, "term"):
         weight += term[...].astype(jnp.float32)
     refs.weight[...] = weight.astype(jnp.bfloat16)
-    kind = refs.halo_grads.dtype
-    refs.halo_grads[:, pair_columns(z, step)] = pair_total[: z.span].astype(kind)
-    refs.own_grads[:, pair_columns(z, step)] = pair_total[z.span :]
+    refs.halo_part[...] = pair_total[: z.span].astype(refs.halo_part.dtype)
+    refs.own_part[...] = pair_total[z.span :]
     input_grad = dot(matrix, grad, 1, 1)
     if step > 0:
         input_grad += refs.input_sum[...]
@@ -249,7 +262,10 @@
     dscores, grad_stack = score_grads(z, 0, probs, keys, values, cot_stack)
     unstack(z, grad_stack, refs.grad, 0)
     pair_total = pair_terms(z, 0, dscores, probs, refs.stack[...], cot_stack)
-    refs.halo_grads[:, pair_columns(z, step)] = pair_total[: z.span].astype(refs.halo_grads.dtype)
+    kind = refs.halo_grads.dtype
+    for place, part in enumerate(listed(refs, "halo_part")):
+        refs.halo_grads[:, pair_columns(z, place)] = part[...]
+    refs.halo_grads[:, pair_columns(z, step)] = pair_total[: z.span].astype(kind)
     refs.own_part[...] = pair_total[z.span :]
     grad = padded(z, refs.grad[...], 0)
     weight = dot(refs.at[...], grad, 1, 0)
@@ -287,15 +303,21 @@
         copy_rows(grad, target, refs.sems, copies)
     cot_stack = stacked(refs.cot, slice(0, z.block))
     pair_total = pair_terms(z, 1, refs.dscores[...], refs.probs[...], refs.stack[...], cot_stack)
-    refs.own_grads[:, pair_columns(z, step)] = refs.own_part[...] + pair_total[z.span :]
+    parts = [part[...] for part in listed(refs, "own_part")]
+    parts[step] += pair_total[z.span :]
+    low = z.rows - z.span
+    for place, part in enumerate(parts):
+        columns = pair_columns(z, place)
+        if hasattr(refs, "halo_back"):
+            refs.pair_grads[:low, columns] = part[:low].astype(jnp.bfloat16)
+            part = part[low:] + refs.halo_back[:, columns].astype(jnp.float32)
+            refs.pair_grads[low:, columns] = part.astype(jnp.bfloat16)
+        else:
+            refs.own_grads[:, columns] = part
+    refs.share_out[...] = refs.share[...]
     grad = padded(z, refs.pending1[...], 1)
     input_grad = refs.input_sum[...] + dot(refs.up[...], grad, 1, 1)
     refs.input_grad[...] = input_grad.astype(jnp.bfloat16)
-    if hasattr(refs, "halo_back"):
-        low = z.rows - z.span
-        refs.pair_grads[:low] = refs.own_grads[:low].astype(jnp.bfloat16)
-        total = refs.own_grads[low:] + refs.halo_back[...].astype(jnp.float32)
-        refs.pair_grads[low:] = total.astype(jnp.bfloat16)
     for copy in copies:
         copy.wait()
 
@@ -338,18 +360,28 @@
     piece = ((rows, width), bf16)
     first = run(split_first, z, dict(upstream=cotangents), dict(piece=piece), sems(COPIES)).piece
     cots = [passed_along(first, "section", -1)]
-    outputs = numbered("piece", [piece] * (last - 1) + [((block, width), bf16)] * BLOCKS)
-    outputs.update(matrix_copy=((rank, width), bf16), pairs_copy=(own.shape, bf16))
-    parts = run(
-        split_rest,
+    outputs = dict(
+        piece=piece, matrix_copy=((rank, width), bf16), pairs_copy=(own.shape, bf16)
+    )
+    second = run(
+        split_second,
         z,
         dict(upstream=cotangents, pairs=own, matrix=matrix, after=first),
         outputs,
         sems(COPIES * len(outputs)),
     )
-    held = listed(parts, "piece")
+    cots.append(passed_along(second.piece, "section", -1))
+    own, matrix = second.pairs_copy, second.matrix_copy
+    outputs = numbered("piece", [piece] * (last - 2) + [((block, width), bf16)] * BLOCKS)
+    rest = run(
+        split_rest,
+        z,
+        dict(upstream=cotangents, after=second.piece),
+        outputs,
+        sems(COPIES * len(outputs)),
+    )
+    held = listed(rest, "piece")
     cots.append(passed_along(held[0], "section", -1))
-    own, matrix = parts.pairs_copy, parts.matrix_copy
     halo = [passed_along(own[rows - count :], "seq", distance) for distance, count in pieces]
     halo = jnp.concatenate(halo[::-1], axis=0)
     ups = {0: matrix}
@@ -375,40 +407,32 @@
     outputs = numbered("stack", [((stack_rows, HEAD_SIZE), bf16)] * BLOCKS)
     outputs |= numbered("probs", [((window, stack_rows), f32)] * BLOCKS)
     outputs.update(held=(held[1].shape, bf16))
-    ahead = run(
-        forward,
-        z,
-        dict(fq=fq, at=at, up=matrix, halo=halo, own=own, bias=bias, held_in=held[1]),
-        outputs,
-        {},
-        flops,
-    )
+    inputs = dict(fq=fq, at=at, up=matrix, halo=halo, own=own, bias=bias, held_in=held[1])
+    ahead = run(forward, z, inputs, outputs, {}, flops)
     cots.append(passed_along(ahead.held, "section", -1))
 
-    halo_shape = ((span, chunks * PAIR), bf16 if per_head == 1 else f32)
-    own_shape = ((rows, chunks * PAIR), f32)
+    halo_type = bf16 if per_head == 1 else f32
+    halo_part, own_part = ((span, PAIR), halo_type), ((rows, PAIR), f32)
     dq_shape = ((rows, columns), bf16)
     input_shape = ((rank, rows), f32)
     terms = {away: [] for away in range(chunks)}
-    grads = []
+    grads, halo_parts, own_parts = [], [], []
     state = None
     for step in range(last):
         away = last - step
         inputs = dict(fq=fq, at=at, halo=halo, own=own, bias=bias, cot=cots[step], up=ups[away])
         inputs |= numbered("term", terms[away])
         outputs = dict(
-            halo_grads=halo_shape,
-            own_grads=own_shape,
+            halo_part=halo_part,
+            own_part=own_part,
             input_grad=input_shape,
             grad=piece,
             weight=((rank, width), bf16),
         )
         if step > 0:
-            inputs.update(
-                halo_grads_in=state.halo_grads,
-                own_grads_in=state.own_grads,
-                input_sum=state.input_grad,
-            )
+            inputs.update(input_sum=state.input_grad)
+        else:
+            inputs.update(after=ahead.stack0)
         if 0 < step < last - 1:
             inputs.update(pending=grads[-1])
             outputs.update(dq=dq_shape)
@@ -421,6 +445,8 @@
         body.__name__ = whole.__name__
         state = run(body, z, inputs, outputs, sems(1), 2 * flops)
         grads.append(state.grad)
+        halo_parts.append(state.halo_part)
+        own_parts.append(state.own_part)
         dq = getattr(state, "dq", None) if step < last - 1 else dq
         if step + 2 < len(held):
             cots.append(passed_along(state.held, "section", -1))
@@ -430,8 +456,8 @@
     common = dict(at=at, up=matrix, halo=halo, own=own)
     outputs = dict(
         dq=dq_shape,
-        halo_grads=halo_shape,
-        own_part=((rows, PAIR), f32),
+        halo_grads=((span, chunks * PAIR), halo_type),
+        own_part=own_part,
         weight_part=((rank, width), f32),
         input_grad=input_shape,
         grad=((block, width), bf16),
@@ -445,9 +471,9 @@
             stack=ahead.stack0,
             probs=ahead.probs0,
             dq_in=dq,
-            halo_grads_in=state.halo_grads,
             input_sum=state.input_grad,
         )
+        | numbered("halo_part", halo_parts)
         | numbered("pending", grads[-BLOCKS:])
         | numbered("term", terms[0][:-1]),
         outputs,
@@ -480,7 +506,8 @@
     shares[1:] = [passed_along(shares[away], "dp", away) for away in range(1, packs)]
 
     merged = per_head == 1 and len(pieces) == 1
-    outputs = dict(dq=dq_shape, own_grads=own_shape, input_grad=((rank, rows), bf16))
+    outputs = dict(dq=dq_shape, input_grad=((rank, rows), bf16))
+    outputs.update(share_out=((rank // packs, width), bf16))
     inputs = dict(
         at=at,
         up=matrix,
@@ -488,16 +515,16 @@
         stack=ahead.stack1,
         probs=ahead.probs1,
         dscores=late.dscores,
-        own_part=early.own_part,
         input_sum=early.input_grad,
         dq_in=early.dq,
-        own_grads_in=state.own_grads,
-        share_in=shares[0],
-    )
-    outputs.update(share=(shares[0].shape, bf16))
+        share=shares[0],
+    )
+    inputs |= numbered("own_part", own_parts + [early.own_part])
     if merged:
         inputs.update(halo_back=backs[0])
         outputs.update(pair_grads=((rows, HK * PAIR), bf16))
+    else:
+        outputs.update(own_grads=((rows, chunks * PAIR), f32))
     final = run(
         finish,
         z,
@@ -506,7 +533,7 @@
         sems(BLOCKS),
         flops,
     )
-    weight_share = final.share.astype(f32)
+    weight_share = final.share_out.astype(f32)
     for share in shares[1:]:
         weight_share += share.astype(f32)
     if merged:

time: 38.4 us -> 37.8 us (0.984)
  waiting for transfers between devices: 6.82 us -> 3.93 us
  Pallas kernels: 11 us -> 12 us
  local copies, waits for them, and re-layouts: 1.44 us -> 2.09 us
  starting transfers between devices: 17.2 us -> 17.7 us
    ppermute x6, waiting for transfers between devices: 3.26 us -> 1.62 us  [swapped(): return lax.ppermute(value, axis, pairs)]
    ppermute x10, waiting for transfers between devices: 3.56 us -> 2.31 us  [passed_along(): return lax.ppermute(value, axis, pairs)]
    pallas_call x9 -> x10, Pallas kernels: 11 us -> 12 us  [run(): pl.pallas_call(kernel, in_specs=[spec_of(name) for name in inputs], out_s...]
    slice x1, local copies, waits for them, and re-layouts: 0.01 us -> 0.66 us  [per_device(): own[rows - count:]]
  transfers between devices with their start and end apart: 16 -> 16, of which waited for: 5 -> 6; matrix products, arithmetic and copies ran while one was open for 1% -> 3% of each run, Pallas kernels for 26% -> 29%
where the time goes in v2:
time: 37.8 us; the launch traced here: 37.4 us
  starting transfers between devices  17.7 us (47%)
  Pallas kernels  12 us (32%)
  waiting for transfers between devices  3.93 us (10%)
  local copies, waits for them, and re-layouts  2.09 us (6%)
  other arithmetic  0.92 us (2%)
  between operations  0.82 us (2%)
    ppermute x10, starting transfers between devices, passed_along(): return lax.ppermute(value, axis, pairs)  12.7 us
    pallas_call x10, Pallas kernels, run(): pl.pallas_call(kernel, in_specs=[spec_of(name) for name in inputs], out_s...  12 us
    ppermute x6, starting transfers between devices, swapped(): return lax.ppermute(value, axis, pairs)  4.98 us
    ppermute x10, waiting for transfers between devices, passed_along(): return lax.ppermute(value, axis, pairs)  2.31 us
    ppermute x6, waiting for transfers between devices, swapped(): return lax.ppermute(value, axis, pairs)  1.62 us
    unnamed x6, local copies, waits for them, and re-layouts  1.27 us
  transfers between devices with their start and end apart: 16, of which 6 were waited for; matrix products, arithmetic and copies ran while one was open for 3% of the time, Pallas kernels for 29%

profile of v2, /device:TPU:0, one launch (start us, length us, event | category | flops | bytes accessed | tf_op | source)
XLA Modules:
  0.0 37.4 jit_solution(3037332842262051215)
XLA Ops:
  0.6 1.0 %split_first.1.refs_3_ = bf16[128,1024]{1,0:T(8,128)(2,1)S(1)} custom-call(bf16[128,4096]{1,0:T(8,128)(2,1)} %bitcast.26), custom_call_target="tpu_custom_call" | custom-call | bytes 1024 | tf_op jit(solution)/shard_map/split_first/pallas_call | solution.py:81
  1.6 3.0 %collective-permute-start.1 = (bf16[128,1024]{1,0:T(8,128)(2,1)S(1)}, bf16[128,1024]{1,0:T(8,128)(2,1)S(1)}, u32[]{:S(2)}, u32[]{:S(2)}) collective-permute-start(bf16[128,1024]{1,0:T(8,128)(2,1)S(1)} %split_first.1.refs_3_), channel_id=1, source_target_pairs={{0,16},{16,0},{1,17},{17,1},{2,18},{18,2},{3,19},{19,3},{4,20},{20... | collective-permute-start | bytes 786440 | tf_op jit(solution)/shard_map/ppermute | solution.py:32
  4.6 1.2 %split_second.1 = (bf16[128,1024]{1,0:T(8,128)(2,1)S(1)}, bf16[64,1024]{1,0:T(8,128)(2,1)S(1)}, bf16[128,1024]{1,0:T(8,128)(2,1)S(1)}) custom-call(bf16[128,4096]{1,0:T(8,128)(2,1)} %bitcast.27, bf16[128,1024]{1,0:T(8,128)(2,1)} %bitcast.30, bf16[64,1024]{1,0:T(8,128)(2,1)} %bitcast.31, bf16[128,1024]{1,0:T(8,128)(2,1)S(1)} %split_first.1.refs_3_), custom_call_target="tpu_custom_call" | custom-call | bytes 1024 | tf_op jit(solution)/shard_map/split_second/pallas_call | solution.py:81
  5.9 0.7 %slice.15 = bf16[64,1024]{1,0:T(8,128)(2,1)} slice(bf16[128,1024]{1,0:T(8,128)(2,1)S(1)} %get-tuple-element.49.refs_4_.refs_3_), slice={[64:128], [0:1024]} | slice | bytes 262144 | tf_op jit(solution)/shard_map/slice | solution.py:385
  6.5 1.6 %collective-permute-start.2 = (bf16[64,1024]{1,0:T(8,128)(2,1)S(1)}, bf16[64,1024]{1,0:T(8,128)(2,1)S(1)}, u32[]{:S(2)}, u32[]{:S(2)}) collective-permute-start(bf16[64,1024]{1,0:T(8,128)(2,1)S(1)} %get-tuple-element.48.refs_2_.refs_1_), channel_id=1, source_target_pairs={{0,8},{4,12},{8,0},{12,4},{1,9},{5,13},{9,1},{13,5},{2,10},{6,14},... | collective-permute-start | bytes 393224 | tf_op jit(solution)/shard_map/ppermute | solution.py:37
  8.1 0.5 %collective-permute-start.6 = (bf16[128,1024]{1,0:T(8,128)(2,1)S(1)}, bf16[128,1024]{1,0:T(8,128)(2,1)S(1)}, u32[]{:S(2)}, u32[]{:S(2)}) collective-permute-start(bf16[128,1024]{1,0:T(8,128)(2,1)S(1)} %get-tuple-element.50.refs_1_), channel_id=1, source_target_pairs={{0,16},{16,0},{1,17},{17,1},{2,18},{18,2},{3,19},{19,3},{4,20},{20... | collective-permute-start | bytes 786440 | tf_op jit(solution)/shard_map/ppermute | solution.py:32
  8.6 1.1 %split_rest.1 = (bf16[128,1024]{1,0:T(8,128)(2,1)S(1)}, bf16[64,1024]{1,0:T(8,128)(2,1)S(1)}, bf16[64,1024]{1,0:T(8,128)(2,1)S(1)}) custom-call(bf16[128,4096]{1,0:T(8,128)(2,1)} %bitcast.28, bf16[128,1024]{1,0:T(8,128)(2,1)S(1)} %get-tuple-element.50.refs_1_), custom_call_target="tpu_custom_call" | custom-call | bytes 1024 | tf_op jit(solution)/shard_map/split_rest/pallas_call | solution.py:81
  9.7 1.6 %collective-permute-start.8 = (bf16[128,1024]{1,0:T(8,128)(2,1)S(1)}, bf16[128,1024]{1,0:T(8,128)(2,1)S(1)}, u32[]{:S(2)}, u32[]{:S(2)}) collective-permute-start(bf16[128,1024]{1,0:T(8,128)(2,1)S(1)} %get-tuple-element.63), channel_id=1, source_target_pairs={{0,16},{16,0},{1,17},{17,1},{2,18},{18,2},{3,19},{19,3},{4,20},{20... | collective-permute-start | bytes 786440 | tf_op jit(solution)/shard_map/ppermute | solution.py:32
  11.3 0.7 %copy-done.2 = s32[1,1,512]{2,1,0:T(1,128)S(1)} copy-done((s32[1,1,512]{2,1,0:T(1,128)S(1)}, s32[1,1,512]{2,1,0:T(1,128)}, u32[]{:S(2)}) %copy-start.2) | copy-done | bytes 2072
  12.2 0.7 %collective-permute-done.2.refs_6_ = bf16[64,1024]{1,0:T(8,128)(2,1)S(1)} collective-permute-done((bf16[64,1024]{1,0:T(8,128)(2,1)S(1)}, bf16[64,1024]{1,0:T(8,128)(2,1)S(1)}, u32[]{:S(2)}, u32[]{:S(2)}) %collective-permute-start.2) | collective-permute-done | bytes 131104 | tf_op jit(solution)/shard_map/ppermute | solution.py:37
  12.8 1.2 %collective-permute-start.3 = (bf16[64,1024]{1,0:T(8,128)(2,1)S(1)}, bf16[64,1024]{1,0:T(8,128)(2,1)S(1)}, u32[]{:S(2)}, u32[]{:S(2)}) collective-permute-start(bf16[64,1024]{1,0:T(8,128)(2,1)S(1)} %collective-permute-done.2.refs_6_), channel_id=1, source_target_pairs={{0,4},{4,0},{8,12},{12,8},{1,5},{5,1},{9,13},{13,9},{2,6},{6,2},{1... | collective-permute-start | bytes 393224 | tf_op jit(solution)/shard_map/ppermute | solution.py:37
  14.3 0.6 %copy-done.1 = bf16[1,1,128,64]{2,3,1,0:T(8,128)(2,1)S(1)} copy-done((bf16[1,1,128,64]{2,3,1,0:T(8,128)(2,1)S(1)}, bf16[1,1,128,64]{2,3,1,0:T(8,128)(2,1)}, u32[]{:S(2)}) %copy-start.1) | copy-done | bytes 16408
  14.9 0.6 %forward.1 = (bf16[512,128]{1,0:T(8,128)(2,1)S(1)}, bf16[512,128]{1,0:T(8,128)(2,1)S(1)}, f32[128,512]{1,0:T(8,128)S(1)}, f32[128,512]{1,0:T(8,128)S(1)}, bf16[64,1024]{1,0:T(8,128)(2,1)S(1)}) custom-call(bf16[128,4096]{1,0:T(8,128)(2,1)S(1)} %bitcast.15, bf16[64,128]{1,0:T(8,128)(2,1)S(1)} %bitcast.19, ...), custom_call_target="tpu_custom_call", output_to_operand_aliasing={{4}: (6, {})} | custom-call | flops 81920 | bytes 1024 | tf_op jit(solution)/shard_map/forward/pallas_call | solution.py:81
  15.5 1.4 %whole.3 = (bf16[64,256]{1,0:T(8,128)(2,1)S(1)}, f32[128,256]{1,0:T(8,128)S(1)}, f32[64,128]{1,0:T(8,128)S(1)}, bf16[128,1024]{1,0:T(8,128)(2,1)S(1)}, bf16[64,1...) custom-call(bf16[128,4096]{1,0:T(8,128)(2,1)S(1)} %bitcast.16, ...), custom_call_target="tpu_custom_call", output_to_operand_aliasing={{5}: (8, {})} | custom-call | flops 163840 | bytes 1024 | tf_op jit(solution)/shard_map/whole/pallas_call | solution.py:81
  17.0 0.5 %collective-permute-start.9 = (bf16[64,1024]{1,0:T(8,128)(2,1)S(1)}, bf16[64,1024]{1,0:T(8,128)(2,1)S(1)}, u32[]{:S(2)}, u32[]{:S(2)}) collective-permute-start(bf16[64,1024]{1,0:T(8,128)(2,1)S(1)} %get-tuple-element.48.refs_2_.refs_1_), channel_id=1, source_target_pairs={{0,4},{4,0},{8,12},{12,8},{1,5},{5,1},{9,13},{13,9},{2,6},{6,2},{1... | collective-permute-start | bytes 393224 | tf_op jit(solution)/shard_map/ppermute | solution.py:37
  17.5 0.8 %collective-permute-done.7.refs_7_ = bf16[64,1024]{1,0:T(8,128)(2,1)S(1)} collective-permute-done((bf16[64,1024]{1,0:T(8,128)(2,1)S(1)}, bf16[64,1024]{1,0:T(8,128)(2,1)S(1)}, u32[]{:S(2)}, u32[]{:S(2)}) %collective-permute-start.7) | collective-permute-done | bytes 131104 | tf_op jit(solution)/shard_map/ppermute | solution.py:37
  18.3 1.8 %whole.4 = (bf16[64,256]{1,0:T(8,128)(2,1)S(1)}, f32[128,256]{1,0:T(8,128)S(1)}, f32[64,128]{1,0:T(8,128)S(1)}, bf16[128,1024]{1,0:T(8,128)(2,1)S(1)}, bf16[64,1...) custom-call(bf16[128,4096]{1,0:T(8,128)(2,1)S(1)} %bitcast.17, bf16[64,128]{1,0:T(8,128)(2,1)S(1)} %bitcast.21, ...), custom_call_target="tpu_custom_call" | custom-call | flops 163840 | bytes 1024 | tf_op jit(solution)/shard_map/whole/pallas_call | solution.py:81
  20.2 1.6 %collective-permute-start.10 = (bf16[64,1024]{1,0:T(8,128)(2,1)S(1)}, bf16[64,1024]{1,0:T(8,128)(2,1)S(1)}, u32[]{:S(2)}, u32[]{:S(2)}) collective-permute-start(bf16[64,1024]{1,0:T(8,128)(2,1)S(1)} %get-tuple-element.71), channel_id=1, source_target_pairs={{0,8},{4,12},{8,0},{12,4},{1,9},{5,13},{9,1},{13,5},{2,10},{6,14},... | collective-permute-start | bytes 393224 | tf_op jit(solution)/shard_map/ppermute | solution.py:37
  21.7 1.2 %collective-permute-start.4 = (bf16[64,1024]{1,0:T(8,128)(2,1)S(1)}, bf16[64,1024]{1,0:T(8,128)(2,1)S(1)}, u32[]{:S(2)}, u32[]{:S(2)}) collective-permute-start(bf16[64,1024]{1,0:T(8,128)(2,1)S(1)} %get-tuple-element.54), channel_id=1, source_target_pairs={{0,16},{16,0},{1,17},{17,1},{2,18},{18,2},{3,19},{19,3},{4,20},{20... | collective-permute-start | bytes 393224 | tf_op jit(solution)/shard_map/ppermute | solution.py:32
  22.9 1.4 %whole.5 = (bf16[64,256]{1,0:T(8,128)(2,1)S(1)}, f32[128,256]{1,0:T(8,128)S(1)}, f32[64,128]{1,0:T(8,128)S(1)}, bf16[128,1024]{1,0:T(8,128)(2,1)S(1)}, bf16[64,1024]{1,0:T(8,128)(2,1)S(1)}) custom-call(bf16[128,4096]{1,0:T(8,128)(2,1)S(1)} %bitcast.18, bf16[64,128]{1,0:T(8,128)(2,1)S(1)} %bitcast.22, ...), custom_call_target="tpu_custom_call" | custom-call | flops 163840 | bytes 1024 | tf_op jit(solution)/shard_map/whole/pallas_call | solution.py:81
  24.4 1.2 %collective-permute-done.5.refs_4_ = bf16[64,1024]{1,0:T(8,128)(2,1)S(1)} collective-permute-done((bf16[64,1024]{1,0:T(8,128)(2,1)S(1)}, bf16[64,1024]{1,0:T(8,128)(2,1)S(1)}, u32[]{:S(2)}, u32[]{:S(2)}) %collective-permute-start.5) | collective-permute-done | bytes 131104 | tf_op jit(solution)/shard_map/ppermute | solution.py:32
  25.6 0.1 collective-permute-done.10.refs_14_
  25.8 1.3 %front.1 = (bf16[128,4096]{1,0:T(8,128)(2,1)}, bf16[64,1024]{1,0:T(8,128)(2,1)S(1)}, f32[128,256]{1,0:T(8,128)S(1)}, f32[64,1024]{1,0:T(8,128)S(1)}, f32[64,128]...) custom-call(bf16[64,128]{1,0:T(8,128)(2,1)S(1)} %bitcast.23, ...), custom_call_target="tpu_custom_call", output_to_operand_aliasing={{0}: (7, {})} | custom-call | flops 81920 | bytes 1024 | tf_op jit(solution)/shard_map/front/pallas_call | solution.py:81
  27.1 0.6 %collective-permute-start.12 = (bf16[64,1024]{1,0:T(8,128)(2,1)S(1)}, bf16[64,1024]{1,0:T(8,128)(2,1)S(1)}, u32[]{:S(2)}, u32[]{:S(2)}) collective-permute-start(bf16[64,1024]{1,0:T(8,128)(2,1)S(1)} %get-tuple-element.82), channel_id=1, source_target_pairs={{0,12},{4,0},{8,4},{12,8},{1,13},{5,1},{9,5},{13,9},{2,14},{6,2},{... | collective-permute-start | bytes 393224 | tf_op jit(solution)/shard_map/ppermute | solution.py:32
  27.7 0.1 collective-permute-done.4.refs_4_.refs_2_
  27.8 0.6 %back.1 = (bf16[64,1024]{1,0:T(8,128)(2,1)S(1)}, bf16[128,512]{1,0:T(8,128)(2,1)S(1)}, bf16[16,1024]{1,0:T(8,128)(2,1)S(1)}, bf16[16,1024]{1,0:T(8,128)(2,1)S(1)...) custom-call(bf16[64,128]{1,0:T(8,128)(2,1)S(1)} %bitcast.24, ...), custom_call_target="tpu_custom_call" | custom-call | flops 81920 | bytes 1024 | tf_op jit(solution)/shard_map/back/pallas_call | solution.py:81
  28.4 1.8 %collective-permute-start.13 = (bf16[16,1024]{1,0:T(8,128)(2,1)S(1)}, bf16[16,1024]{1,0:T(8,128)(2,1)S(1)}, u32[]{:S(2)}, u32[]{:S(2)}) collective-permute-start(bf16[16,1024]{1,0:T(8,128)(2,1)S(1)} %get-tuple-element.89), channel_id=1, source_target_pairs={{0,1},{1,2},{2,3},{3,0},{4,5},{5,6},{6,7},{7,4},{8,9},{9,10},{10,1... | collective-permute-start | bytes 98312 | tf_op jit(solution)/shard_map/ppermute | solution.py:32
  30.3 2.6 %collective-permute-start.14 = (bf16[16,1024]{1,0:T(8,128)(2,1)S(1)}, bf16[16,1024]{1,0:T(8,128)(2,1)S(1)}, u32[]{:S(2)}, u32[]{:S(2)}) collective-permute-start(bf16[16,1024]{1,0:T(8,128)(2,1)S(1)} %get-tuple-element.90), channel_id=1, source_target_pairs={{0,2},{1,3},{2,0},{3,1},{4,6},{5,7},{6,4},{7,5},{8,10},{9,11},{10,... | collective-permute-start | bytes 98312 | tf_op jit(solution)/shard_map/ppermute | solution.py:32
  32.9 1.3 %collective-permute-start.15 = (bf16[16,1024]{1,0:T(8,128)(2,1)S(1)}, bf16[16,1024]{1,0:T(8,128)(2,1)S(1)}, u32[]{:S(2)}, u32[]{:S(2)}) collective-permute-start(bf16[16,1024]{1,0:T(8,128)(2,1)S(1)} %get-tuple-element.91), channel_id=1, source_target_pairs={{0,3},{1,0},{2,1},{3,2},{4,7},{5,4},{6,5},{7,6},{8,11},{9,8},{10,9... | collective-permute-start | bytes 98312 | tf_op jit(solution)/shard_map/ppermute | solution.py:32
  34.2 1.6 %finish.1 = (bf16[128,4096]{1,0:T(8,128)(2,1)}, bf16[64,128]{1,0:T(8,128)(2,1)}, bf16[16,1024]{1,0:T(8,128)(2,1)S(1)}, bf16[128,1024]{1,0:T(8,128)(2,1)}) custom-call(bf16[64,128]{1,0:T(8,128)(2,1)S(1)} %bitcast.25, bf16[64,1024]{1,0:T(8,128)(2,1)S(1)} %get-tuple-element.48.refs_2_.refs_1_, ...), custom_call_target="tpu_custom_call", output_to_operand_aliasing={{0}: (7, {})} | custom-call | flops 81920 | bytes 1024 | tf_op jit(solution)/shard_map/finish/pallas_call | solution.py:81
  35.8 1.0 %collective-permute-done.15 = bf16[16,1024]{1,0:T(8,128)(2,1)S(1)} collective-permute-done((bf16[16,1024]{1,0:T(8,128)(2,1)S(1)}, bf16[16,1024]{1,0:T(8,128)(2,1)S(1)}, u32[]{:S(2)}, u32[]{:S(2)}) %collective-permute-start.15) | collective-permute-done | bytes 32800 | tf_op jit(solution)/shard_map/ppermute | solution.py:32
  36.8 0.6 %add_bitcast_fusion = f32[1,16,1024]{2,1,0:T(8,128)} fusion(bf16[16,1024]{1,0:T(8,128)(2,1)S(1)} %collective-permute-done.15, bf16[16,1024]{1,0:T(8,128)(2,1)S(1)} %collective-permute-done.14, bf16[16,1024]{1,0:T(8,128)(2,1)S(1)} %collective-permute-done.13, bf16[16,1024]{1,0:T(8,128)(2,1)S(1)} %get-tuple-element.88), kind=kLoop, calls=%fused_computation.1 | loop fusion | flops 114688 | bytes 196608 | tf_op jit(solution)/shard_map/broadcast_in_dim | solution.py:553
  (23 shorter events, 0.6 us)
Async XLA Ops:
  1.6 13.8 %collective-permute-start.1 = (bf16[128,1024]{1,0:T(8,128)(2,1)S(1)}, bf16[128,1024]{1,0:T(8,128)(2,1)S(1)}, u32[]{:S(2)}, u32[]{:S(2)}) collective-permute-start(bf16[128,1024]{1,0:T(8,128)(2,1)S(1)} %split_first.1.refs_3_), channel_id=1, source_target_pairs={{0,16},{16,0},{1,17},{17,1},{2,18},{18,2},{3,19},{19,3},{4,20},{20... | collective-permute-start | bytes 786440 | tf_op jit(solution)/shard_map/ppermute | solution.py:32
  5.9 8.4 %copy-start = (bf16[1,1,128,4096]{3,2,1,0:T(8,128)(2,1)S(1)}, bf16[1,1,128,4096]{3,2,1,0:T(8,128)(2,1)}, u32[]{:S(2)}) copy-start(bf16[1,1,128,4096]{3,2,1,0:T(8,128)(2,1)} %param.6) | copy-start | bytes 3145732
  6.5 7.8 %collective-permute-start = (bf16[64,1024]{1,0:T(8,128)(2,1)}, bf16[64,1024]{1,0:T(8,128)(2,1)S(1)}, u32[]{:S(2)}, u32[]{:S(2)}) collective-permute-start(bf16[64,1024]{1,0:T(8,128)(2,1)} %slice.15), channel_id=1, source_target_pairs={{0,4},{4,8},{8,12},{12,0},{1,5},{5,9},{9,13},{13,1},{2,6},{6,10},{... | collective-permute-start | bytes 393224 | tf_op jit(solution)/shard_map/ppermute | solution.py:32
  6.5 6.3 %collective-permute-start.2 = (bf16[64,1024]{1,0:T(8,128)(2,1)S(1)}, bf16[64,1024]{1,0:T(8,128)(2,1)S(1)}, u32[]{:S(2)}, u32[]{:S(2)}) collective-permute-start(bf16[64,1024]{1,0:T(8,128)(2,1)S(1)} %get-tuple-element.48.refs_2_.refs_1_), channel_id=1, source_target_pairs={{0,8},{4,12},{8,0},{12,4},{1,9},{5,13},{9,1},{13,5},{2,10},{6,14},... | collective-permute-start | bytes 393224 | tf_op jit(solution)/shard_map/ppermute | solution.py:37
  8.1 9.4 %collective-permute-start.6 = (bf16[128,1024]{1,0:T(8,128)(2,1)S(1)}, bf16[128,1024]{1,0:T(8,128)(2,1)S(1)}, u32[]{:S(2)}, u32[]{:S(2)}) collective-permute-start(bf16[128,1024]{1,0:T(8,128)(2,1)S(1)} %get-tuple-element.50.refs_1_), channel_id=1, source_target_pairs={{0,16},{16,0},{1,17},{17,1},{2,18},{18,2},{3,19},{19,3},{4,20},{20... | collective-permute-start | bytes 786440 | tf_op jit(solution)/shard_map/ppermute | solution.py:32
  9.7 13.2 %collective-permute-start.8 = (bf16[128,1024]{1,0:T(8,128)(2,1)S(1)}, bf16[128,1024]{1,0:T(8,128)(2,1)S(1)}, u32[]{:S(2)}, u32[]{:S(2)}) collective-permute-start(bf16[128,1024]{1,0:T(8,128)(2,1)S(1)} %get-tuple-element.63), channel_id=1, source_target_pairs={{0,16},{16,0},{1,17},{17,1},{2,18},{18,2},{3,19},{19,3},{4,20},{20... | collective-permute-start | bytes 786440 | tf_op jit(solution)/shard_map/ppermute | solution.py:32
  11.3 0.7 %copy-start.2 = (s32[1,1,512]{2,1,0:T(1,128)S(1)}, s32[1,1,512]{2,1,0:T(1,128)}, u32[]{:S(2)}) copy-start(s32[1,1,512]{2,1,0:T(1,128)} %param.11) | copy-start | bytes 6148
  12.8 2.6 %collective-permute-start.3 = (bf16[64,1024]{1,0:T(8,128)(2,1)S(1)}, bf16[64,1024]{1,0:T(8,128)(2,1)S(1)}, u32[]{:S(2)}, u32[]{:S(2)}) collective-permute-start(bf16[64,1024]{1,0:T(8,128)(2,1)S(1)} %collective-permute-done.2.refs_6_), channel_id=1, source_target_pairs={{0,4},{4,0},{8,12},{12,8},{1,5},{5,1},{9,13},{13,9},{2,6},{6,2},{1... | collective-permute-start | bytes 393224 | tf_op jit(solution)/shard_map/ppermute | solution.py:37
  14.2 0.7 %copy-start.1 = (bf16[1,1,128,64]{2,3,1,0:T(8,128)(2,1)S(1)}, bf16[1,1,128,64]{2,3,1,0:T(8,128)(2,1)}, u32[]{:S(2)}) copy-start(bf16[1,1,128,64]{2,3,1,0:T(8,128)(2,1)} %param.8) | copy-start | bytes 49156
  16.9 1.4 %collective-permute-start.7 = (bf16[64,1024]{1,0:T(8,128)(2,1)S(1)}, bf16[64,1024]{1,0:T(8,128)(2,1)S(1)}, u32[]{:S(2)}, u32[]{:S(2)}) collective-permute-start(bf16[64,1024]{1,0:T(8,128)(2,1)S(1)} %get-tuple-element.59), channel_id=1, source_target_pairs={{0,4},{4,0},{8,12},{12,8},{1,5},{5,1},{9,13},{13,9},{2,6},{6,2},{1... | collective-permute-start | bytes 393224 | tf_op jit(solution)/shard_map/ppermute | solution.py:37
  17.0 6.0 %collective-permute-start.9 = (bf16[64,1024]{1,0:T(8,128)(2,1)S(1)}, bf16[64,1024]{1,0:T(8,128)(2,1)S(1)}, u32[]{:S(2)}, u32[]{:S(2)}) collective-permute-start(bf16[64,1024]{1,0:T(8,128)(2,1)S(1)} %get-tuple-element.48.refs_2_.refs_1_), channel_id=1, source_target_pairs={{0,4},{4,0},{8,12},{12,8},{1,5},{5,1},{9,13},{13,9},{2,6},{6,2},{1... | collective-permute-start | bytes 393224 | tf_op jit(solution)/shard_map/ppermute | solution.py:37
  17.5 8.2 %collective-permute-start.5 = (bf16[64,1024]{1,0:T(8,128)(2,1)S(1)}, bf16[64,1024]{1,0:T(8,128)(2,1)S(1)}, u32[]{:S(2)}, u32[]{:S(2)}) collective-permute-start(bf16[64,1024]{1,0:T(8,128)(2,1)S(1)} %get-tuple-element.57), channel_id=1, source_target_pairs={{0,16},{16,0},{1,17},{17,1},{2,18},{18,2},{3,19},{19,3},{4,20},{20... | collective-permute-start | bytes 393224 | tf_op jit(solution)/shard_map/ppermute | solution.py:32
  20.2 5.6 %collective-permute-start.10 = (bf16[64,1024]{1,0:T(8,128)(2,1)S(1)}, bf16[64,1024]{1,0:T(8,128)(2,1)S(1)}, u32[]{:S(2)}, u32[]{:S(2)}) collective-permute-start(bf16[64,1024]{1,0:T(8,128)(2,1)S(1)} %get-tuple-element.71), channel_id=1, source_target_pairs={{0,8},{4,12},{8,0},{12,4},{1,9},{5,13},{9,1},{13,5},{2,10},{6,14},... | collective-permute-start | bytes 393224 | tf_op jit(solution)/shard_map/ppermute | solution.py:37
  21.7 6.1 %collective-permute-start.4 = (bf16[64,1024]{1,0:T(8,128)(2,1)S(1)}, bf16[64,1024]{1,0:T(8,128)(2,1)S(1)}, u32[]{:S(2)}, u32[]{:S(2)}) collective-permute-start(bf16[64,1024]{1,0:T(8,128)(2,1)S(1)} %get-tuple-element.54), channel_id=1, source_target_pairs={{0,16},{16,0},{1,17},{17,1},{2,18},{18,2},{3,19},{19,3},{4,20},{20... | collective-permute-start | bytes 393224 | tf_op jit(solution)/shard_map/ppermute | solution.py:32
  24.4 3.5 %collective-permute-start.11 = (bf16[64,1024]{1,0:T(8,128)(2,1)S(1)}, bf16[64,1024]{1,0:T(8,128)(2,1)S(1)}, u32[]{:S(2)}, u32[]{:S(2)}) collective-permute-start(bf16[64,1024]{1,0:T(8,128)(2,1)S(1)} %get-tuple-element.73), channel_id=1, source_target_pairs={{0,4},{4,0},{8,12},{12,8},{1,5},{5,1},{9,13},{13,9},{2,6},{6,2},{1... | collective-permute-start | bytes 393224 | tf_op jit(solution)/shard_map/ppermute | solution.py:37
  27.1 7.1 %collective-permute-start.12 = (bf16[64,1024]{1,0:T(8,128)(2,1)S(1)}, bf16[64,1024]{1,0:T(8,128)(2,1)S(1)}, u32[]{:S(2)}, u32[]{:S(2)}) collective-permute-start(bf16[64,1024]{1,0:T(8,128)(2,1)S(1)} %get-tuple-element.82), channel_id=1, source_target_pairs={{0,12},{4,0},{8,4},{12,8},{1,13},{5,1},{9,5},{13,9},{2,14},{6,2},{... | collective-permute-start | bytes 393224 | tf_op jit(solution)/shard_map/ppermute | solution.py:32
  28.4 7.3 %collective-permute-start.13 = (bf16[16,1024]{1,0:T(8,128)(2,1)S(1)}, bf16[16,1024]{1,0:T(8,128)(2,1)S(1)}, u32[]{:S(2)}, u32[]{:S(2)}) collective-permute-start(bf16[16,1024]{1,0:T(8,128)(2,1)S(1)} %get-tuple-element.89), channel_id=1, source_target_pairs={{0,1},{1,2},{2,3},{3,0},{4,5},{5,6},{6,7},{7,4},{8,9},{9,10},{10,1... | collective-permute-start | bytes 98312 | tf_op jit(solution)/shard_map/ppermute | solution.py:32
  30.3 5.5 %collective-permute-start.14 = (bf16[16,1024]{1,0:T(8,128)(2,1)S(1)}, bf16[16,1024]{1,0:T(8,128)(2,1)S(1)}, u32[]{:S(2)}, u32[]{:S(2)}) collective-permute-start(bf16[16,1024]{1,0:T(8,128)(2,1)S(1)} %get-tuple-element.90), channel_id=1, source_target_pairs={{0,2},{1,3},{2,0},{3,1},{4,6},{5,7},{6,4},{7,5},{8,10},{9,11},{10,... | collective-permute-start | bytes 98312 | tf_op jit(solution)/shard_map/ppermute | solution.py:32
  32.9 3.9 %collective-permute-start.15 = (bf16[16,1024]{1,0:T(8,128)(2,1)S(1)}, bf16[16,1024]{1,0:T(8,128)(2,1)S(1)}, u32[]{:S(2)}, u32[]{:S(2)}) collective-permute-start(bf16[16,1024]{1,0:T(8,128)(2,1)S(1)} %get-tuple-element.91), channel_id=1, source_target_pairs={{0,3},{1,0},{2,1},{3,2},{4,7},{5,4},{6,5},{7,6},{8,11},{9,8},{10,9... | collective-permute-start | bytes 98312 | tf_op jit(solution)/shard_map/ppermute | solution.py:32

commit v3 on v2

--- a/solution.py
+++ b/solution.py
@@ -291,7 +291,7 @@
     shares = listed(refs, "share")
     rows = z.rank // len(shares)
     for away, share in enumerate(shares):
-        target = lax.rem(lax.axis_index("dp") + away, len(shares))
+        target = lax.axis_index("dp") ^ away
         share[...] = refs.total[pl.ds(pl.multiple_of(target * rows, rows), rows)]
 
 
@@ -491,6 +491,7 @@
         stop -= count
 
     outputs = dict(grad=((block, width), bf16), dscores=((window, stack_rows), bf16))
+    assert packs == 4
     outputs |= numbered("share", [((rank // packs, width), bf16)] * packs)
     late = run(
         back,
@@ -503,7 +504,8 @@
         flops,
     )
     shares = listed(late, "share")
-    shares[1:] = [passed_along(shares[away], "dp", away) for away in range(1, packs)]
+    for away in (2, 3, 1):
+        shares[away] = swapped(shares[away], "dp", away)
 
     merged = per_head == 1 and len(pieces) == 1
     outputs = dict(dq=dq_shape, input_grad=((rank, rows), bf16))

time: 37.8 us -> 39.6 us (1.048)
  waiting for transfers between devices: 3.93 us -> 7.06 us
  starting transfers between devices: 17.7 us -> 16.3 us
    ppermute x10 -> x7, starting transfers between devices: 12.7 us -> 6.92 us  [passed_along(): return lax.ppermute(value, axis, pairs)]
    ppermute x6 -> x9, starting transfers between devices: 4.98 us -> 9.43 us  [swapped(): return lax.ppermute(value, axis, pairs)]
    ppermute x6 -> x9, waiting for transfers between devices: 1.62 us -> 5.72 us  [swapped(): return lax.ppermute(value, axis, pairs)]
    ppermute x10 -> x7, waiting for transfers between devices: 2.31 us -> 1.34 us  [passed_along(): return lax.ppermute(value, axis, pairs)]
  transfers between devices with their start and end apart: 16 -> 16, of which waited for: 6 -> 7; matrix products, arithmetic and copies ran while one was open for 3% -> 3% of each run, Pallas kernels for 29% -> 28%
where the time goes in v3:
time: 39.6 us; the launch traced here: 39.2 us
  starting transfers between devices  16.3 us (41%)
  Pallas kernels  12 us (30%)
  waiting for transfers between devices  7.06 us (18%)
  local copies, waits for them, and re-layouts  2.09 us (5%)
  other arithmetic  0.92 us (2%)
  between operations  0.81 us (2%)
    pallas_call x10, Pallas kernels, run(): pl.pallas_call(kernel, in_specs=[spec_of(name) for name in inputs], out_s...  12 us
    ppermute x9, starting transfers between devices, swapped(): return lax.ppermute(value, axis, pairs)  9.43 us
    ppermute x7, starting transfers between devices, passed_along(): return lax.ppermute(value, axis, pairs)  6.92 us
    ppermute x9, waiting for transfers between devices, swapped(): return lax.ppermute(value, axis, pairs)  5.72 us
    ppermute x7, waiting for transfers between devices, passed_along(): return lax.ppermute(value, axis, pairs)  1.34 us
    unnamed x6, local copies, waits for them, and re-layouts  1.27 us
  transfers between devices with their start and end apart: 16, of which 7 were waited for; matrix products, arithmetic and copies ran while one was open for 3% of the time, Pallas kernels for 28%

profile of v3, /device:TPU:0, one launch (start us, length us, event | category | flops | bytes accessed | tf_op | source)
XLA Modules:
  0.0 39.2 jit_solution(601157751515226289)
XLA Ops:
  0.6 1.0 %split_first.1.refs_3_ = bf16[128,1024]{1,0:T(8,128)(2,1)S(1)} custom-call(bf16[128,4096]{1,0:T(8,128)(2,1)} %bitcast.26), custom_call_target="tpu_custom_call" | custom-call | bytes 1024 | tf_op jit(solution)/shard_map/split_first/pallas_call | solution.py:81
  1.6 3.0 %collective-permute-start.1 = (bf16[128,1024]{1,0:T(8,128)(2,1)S(1)}, bf16[128,1024]{1,0:T(8,128)(2,1)S(1)}, u32[]{:S(2)}, u32[]{:S(2)}) collective-permute-start(bf16[128,1024]{1,0:T(8,128)(2,1)S(1)} %split_first.1.refs_3_), channel_id=1, source_target_pairs={{0,16},{16,0},{1,17},{17,1},{2,18},{18,2},{3,19},{19,3},{4,20},{20... | collective-permute-start | bytes 786440 | tf_op jit(solution)/shard_map/ppermute | solution.py:32
  4.6 1.2 %split_second.1 = (bf16[128,1024]{1,0:T(8,128)(2,1)S(1)}, bf16[64,1024]{1,0:T(8,128)(2,1)S(1)}, bf16[128,1024]{1,0:T(8,128)(2,1)S(1)}) custom-call(bf16[128,4096]{1,0:T(8,128)(2,1)} %bitcast.27, bf16[128,1024]{1,0:T(8,128)(2,1)} %bitcast.30, bf16[64,1024]{1,0:T(8,128)(2,1)} %bitcast.31, bf16[128,1024]{1,0:T(8,128)(2,1)S(1)} %split_first.1.refs_3_), custom_call_target="tpu_custom_call" | custom-call | bytes 1024 | tf_op jit(solution)/shard_map/split_second/pallas_call | solution.py:81
  5.9 0.7 %slice.15 = bf16[64,1024]{1,0:T(8,128)(2,1)} slice(bf16[128,1024]{1,0:T(8,128)(2,1)S(1)} %get-tuple-element.49.refs_4_.refs_3_), slice={[64:128], [0:1024]} | slice | bytes 262144 | tf_op jit(solution)/shard_map/slice | solution.py:385
  6.5 1.6 %collective-permute-start.2 = (bf16[64,1024]{1,0:T(8,128)(2,1)S(1)}, bf16[64,1024]{1,0:T(8,128)(2,1)S(1)}, u32[]{:S(2)}, u32[]{:S(2)}) collective-permute-start(bf16[64,1024]{1,0:T(8,128)(2,1)S(1)} %get-tuple-element.48.refs_2_.refs_1_), channel_id=1, source_target_pairs={{0,8},{4,12},{8,0},{12,4},{1,9},{5,13},{9,1},{13,5},{2,10},{6,14},... | collective-permute-start | bytes 393224 | tf_op jit(solution)/shard_map/ppermute | solution.py:37
  8.1 0.5 %collective-permute-start.6 = (bf16[128,1024]{1,0:T(8,128)(2,1)S(1)}, bf16[128,1024]{1,0:T(8,128)(2,1)S(1)}, u32[]{:S(2)}, u32[]{:S(2)}) collective-permute-start(bf16[128,1024]{1,0:T(8,128)(2,1)S(1)} %get-tuple-element.50.refs_1_), channel_id=1, source_target_pairs={{0,16},{16,0},{1,17},{17,1},{2,18},{18,2},{3,19},{19,3},{4,20},{20... | collective-permute-start | bytes 786440 | tf_op jit(solution)/shard_map/ppermute | solution.py:32
  8.6 1.1 %split_rest.1 = (bf16[128,1024]{1,0:T(8,128)(2,1)S(1)}, bf16[64,1024]{1,0:T(8,128)(2,1)S(1)}, bf16[64,1024]{1,0:T(8,128)(2,1)S(1)}) custom-call(bf16[128,4096]{1,0:T(8,128)(2,1)} %bitcast.28, bf16[128,1024]{1,0:T(8,128)(2,1)S(1)} %get-tuple-element.50.refs_1_), custom_call_target="tpu_custom_call" | custom-call | bytes 1024 | tf_op jit(solution)/shard_map/split_rest/pallas_call | solution.py:81
  9.7 1.6 %collective-permute-start.8 = (bf16[128,1024]{1,0:T(8,128)(2,1)S(1)}, bf16[128,1024]{1,0:T(8,128)(2,1)S(1)}, u32[]{:S(2)}, u32[]{:S(2)}) collective-permute-start(bf16[128,1024]{1,0:T(8,128)(2,1)S(1)} %get-tuple-element.63), channel_id=1, source_target_pairs={{0,16},{16,0},{1,17},{17,1},{2,18},{18,2},{3,19},{19,3},{4,20},{20... | collective-permute-start | bytes 786440 | tf_op jit(solution)/shard_map/ppermute | solution.py:32
  11.3 0.7 %copy-done.2 = s32[1,1,512]{2,1,0:T(1,128)S(1)} copy-done((s32[1,1,512]{2,1,0:T(1,128)S(1)}, s32[1,1,512]{2,1,0:T(1,128)}, u32[]{:S(2)}) %copy-start.2) | copy-done | bytes 2072
  12.2 0.7 %collective-permute-done.2.refs_6_ = bf16[64,1024]{1,0:T(8,128)(2,1)S(1)} collective-permute-done((bf16[64,1024]{1,0:T(8,128)(2,1)S(1)}, bf16[64,1024]{1,0:T(8,128)(2,1)S(1)}, u32[]{:S(2)}, u32[]{:S(2)}) %collective-permute-start.2) | collective-permute-done | bytes 131104 | tf_op jit(solution)/shard_map/ppermute | solution.py:37
  12.8 1.2 %collective-permute-start.3 = (bf16[64,1024]{1,0:T(8,128)(2,1)S(1)}, bf16[64,1024]{1,0:T(8,128)(2,1)S(1)}, u32[]{:S(2)}, u32[]{:S(2)}) collective-permute-start(bf16[64,1024]{1,0:T(8,128)(2,1)S(1)} %collective-permute-done.2.refs_6_), channel_id=1, source_target_pairs={{0,4},{4,0},{8,12},{12,8},{1,5},{5,1},{9,13},{13,9},{2,6},{6,2},{1... | collective-permute-start | bytes 393224 | tf_op jit(solution)/shard_map/ppermute | solution.py:37
  14.3 0.6 %copy-done.1 = bf16[1,1,128,64]{2,3,1,0:T(8,128)(2,1)S(1)} copy-done((bf16[1,1,128,64]{2,3,1,0:T(8,128)(2,1)S(1)}, bf16[1,1,128,64]{2,3,1,0:T(8,128)(2,1)}, u32[]{:S(2)}) %copy-start.1) | copy-done | bytes 16408
  14.9 0.6 %forward.1 = (bf16[512,128]{1,0:T(8,128)(2,1)S(1)}, bf16[512,128]{1,0:T(8,128)(2,1)S(1)}, f32[128,512]{1,0:T(8,128)S(1)}, f32[128,512]{1,0:T(8,128)S(1)}, bf16[64,1024]{1,0:T(8,128)(2,1)S(1)}) custom-call(bf16[128,4096]{1,0:T(8,128)(2,1)S(1)} %bitcast.15, bf16[64,128]{1,0:T(8,128)(2,1)S(1)} %bitcast.19, ...), custom_call_target="tpu_custom_call", output_to_operand_aliasing={{4}: (6, {})} | custom-call | flops 81920 | bytes 1024 | tf_op jit(solution)/shard_map/forward/pallas_call | solution.py:81
  15.5 1.4 %whole.3 = (bf16[64,256]{1,0:T(8,128)(2,1)S(1)}, f32[128,256]{1,0:T(8,128)S(1)}, f32[64,128]{1,0:T(8,128)S(1)}, bf16[128,1024]{1,0:T(8,128)(2,1)S(1)}, bf16[64,1...) custom-call(bf16[128,4096]{1,0:T(8,128)(2,1)S(1)} %bitcast.16, ...), custom_call_target="tpu_custom_call", output_to_operand_aliasing={{5}: (8, {})} | custom-call | flops 163840 | bytes 1024 | tf_op jit(solution)/shard_map/whole/pallas_call | solution.py:81
  17.0 0.5 %collective-permute-start.9 = (bf16[64,1024]{1,0:T(8,128)(2,1)S(1)}, bf16[64,1024]{1,0:T(8,128)(2,1)S(1)}, u32[]{:S(2)}, u32[]{:S(2)}) collective-permute-start(bf16[64,1024]{1,0:T(8,128)(2,1)S(1)} %get-tuple-element.48.refs_2_.refs_1_), channel_id=1, source_target_pairs={{0,4},{4,0},{8,12},{12,8},{1,5},{5,1},{9,13},{13,9},{2,6},{6,2},{1... | collective-permute-start | bytes 393224 | tf_op jit(solution)/shard_map/ppermute | solution.py:37
  17.5 0.8 %collective-permute-done.7.refs_7_ = bf16[64,1024]{1,0:T(8,128)(2,1)S(1)} collective-permute-done((bf16[64,1024]{1,0:T(8,128)(2,1)S(1)}, bf16[64,1024]{1,0:T(8,128)(2,1)S(1)}, u32[]{:S(2)}, u32[]{:S(2)}) %collective-permute-start.7) | collective-permute-done | bytes 131104 | tf_op jit(solution)/shard_map/ppermute | solution.py:37
  18.3 1.8 %whole.4 = (bf16[64,256]{1,0:T(8,128)(2,1)S(1)}, f32[128,256]{1,0:T(8,128)S(1)}, f32[64,128]{1,0:T(8,128)S(1)}, bf16[128,1024]{1,0:T(8,128)(2,1)S(1)}, bf16[64,1...) custom-call(bf16[128,4096]{1,0:T(8,128)(2,1)S(1)} %bitcast.17, bf16[64,128]{1,0:T(8,128)(2,1)S(1)} %bitcast.21, ...), custom_call_target="tpu_custom_call" | custom-call | flops 163840 | bytes 1024 | tf_op jit(solution)/shard_map/whole/pallas_call | solution.py:81
  20.2 1.6 %collective-permute-start.10 = (bf16[64,1024]{1,0:T(8,128)(2,1)S(1)}, bf16[64,1024]{1,0:T(8,128)(2,1)S(1)}, u32[]{:S(2)}, u32[]{:S(2)}) collective-permute-start(bf16[64,1024]{1,0:T(8,128)(2,1)S(1)} %get-tuple-element.71), channel_id=1, source_target_pairs={{0,8},{4,12},{8,0},{12,4},{1,9},{5,13},{9,1},{13,5},{2,10},{6,14},... | collective-permute-start | bytes 393224 | tf_op jit(solution)/shard_map/ppermute | solution.py:37
  21.7 1.2 %collective-permute-start.4 = (bf16[64,1024]{1,0:T(8,128)(2,1)S(1)}, bf16[64,1024]{1,0:T(8,128)(2,1)S(1)}, u32[]{:S(2)}, u32[]{:S(2)}) collective-permute-start(bf16[64,1024]{1,0:T(8,128)(2,1)S(1)} %get-tuple-element.54), channel_id=1, source_target_pairs={{0,16},{16,0},{1,17},{17,1},{2,18},{18,2},{3,19},{19,3},{4,20},{20... | collective-permute-start | bytes 393224 | tf_op jit(solution)/shard_map/ppermute | solution.py:32
  22.9 1.4 %whole.5 = (bf16[64,256]{1,0:T(8,128)(2,1)S(1)}, f32[128,256]{1,0:T(8,128)S(1)}, f32[64,128]{1,0:T(8,128)S(1)}, bf16[128,1024]{1,0:T(8,128)(2,1)S(1)}, bf16[64,1024]{1,0:T(8,128)(2,1)S(1)}) custom-call(bf16[128,4096]{1,0:T(8,128)(2,1)S(1)} %bitcast.18, bf16[64,128]{1,0:T(8,128)(2,1)S(1)} %bitcast.22, ...), custom_call_target="tpu_custom_call" | custom-call | flops 163840 | bytes 1024 | tf_op jit(solution)/shard_map/whole/pallas_call | solution.py:81
  24.4 1.2 %collective-permute-done.5.refs_4_ = bf16[64,1024]{1,0:T(8,128)(2,1)S(1)} collective-permute-done((bf16[64,1024]{1,0:T(8,128)(2,1)S(1)}, bf16[64,1024]{1,0:T(8,128)(2,1)S(1)}, u32[]{:S(2)}, u32[]{:S(2)}) %collective-permute-start.5) | collective-permute-done | bytes 131104 | tf_op jit(solution)/shard_map/ppermute | solution.py:32
  25.6 0.1 collective-permute-done.10.refs_14_
  25.8 1.3 %front.1 = (bf16[128,4096]{1,0:T(8,128)(2,1)}, bf16[64,1024]{1,0:T(8,128)(2,1)S(1)}, f32[128,256]{1,0:T(8,128)S(1)}, f32[64,1024]{1,0:T(8,128)S(1)}, f32[64,128]...) custom-call(bf16[64,128]{1,0:T(8,128)(2,1)S(1)} %bitcast.23, ...), custom_call_target="tpu_custom_call", output_to_operand_aliasing={{0}: (7, {})} | custom-call | flops 81920 | bytes 1024 | tf_op jit(solution)/shard_map/front/pallas_call | solution.py:81
  27.1 0.6 %collective-permute-start.12 = (bf16[64,1024]{1,0:T(8,128)(2,1)S(1)}, bf16[64,1024]{1,0:T(8,128)(2,1)S(1)}, u32[]{:S(2)}, u32[]{:S(2)}) collective-permute-start(bf16[64,1024]{1,0:T(8,128)(2,1)S(1)} %get-tuple-element.82), channel_id=1, source_target_pairs={{0,12},{4,0},{8,4},{12,8},{1,13},{5,1},{9,5},{13,9},{2,14},{6,2},{... | collective-permute-start | bytes 393224 | tf_op jit(solution)/shard_map/ppermute | solution.py:32
  27.7 0.1 collective-permute-done.4.refs_4_.refs_2_
  27.8 0.6 %back.1 = (bf16[64,1024]{1,0:T(8,128)(2,1)S(1)}, bf16[128,512]{1,0:T(8,128)(2,1)S(1)}, bf16[16,1024]{1,0:T(8,128)(2,1)S(1)}, bf16[16,1024]{1,0:T(8,128)(2,1)S(1)...) custom-call(bf16[64,128]{1,0:T(8,128)(2,1)S(1)} %bitcast.24, ...), custom_call_target="tpu_custom_call" | custom-call | flops 81920 | bytes 1024 | tf_op jit(solution)/shard_map/back/pallas_call | solution.py:81
  28.4 1.8 %collective-permute-start.13 = (bf16[16,1024]{1,0:T(8,128)(2,1)S(1)}, bf16[16,1024]{1,0:T(8,128)(2,1)S(1)}, u32[]{:S(2)}, u32[]{:S(2)}) collective-permute-start(bf16[16,1024]{1,0:T(8,128)(2,1)S(1)} %get-tuple-element.89), channel_id=1, source_target_pairs={{0,1},{1,0},{2,3},{3,2},{4,5},{5,4},{6,7},{7,6},{8,9},{9,8},{10,11... | collective-permute-start | bytes 98312 | tf_op jit(solution)/shard_map/ppermute | solution.py:37
  30.3 2.6 %collective-permute-start.14 = (bf16[16,1024]{1,0:T(8,128)(2,1)S(1)}, bf16[16,1024]{1,0:T(8,128)(2,1)S(1)}, u32[]{:S(2)}, u32[]{:S(2)}) collective-permute-start(bf16[16,1024]{1,0:T(8,128)(2,1)S(1)} %get-tuple-element.90), channel_id=1, source_target_pairs={{0,2},{1,3},{2,0},{3,1},{4,6},{5,7},{6,4},{7,5},{8,10},{9,11},{10,... | collective-permute-start | bytes 98312 | tf_op jit(solution)/shard_map/ppermute | solution.py:37
  32.9 1.6 %finish.1 = (bf16[128,4096]{1,0:T(8,128)(2,1)}, bf16[64,128]{1,0:T(8,128)(2,1)}, bf16[16,1024]{1,0:T(8,128)(2,1)S(1)}, bf16[128,1024]{1,0:T(8,128)(2,1)}) custom-call(bf16[64,128]{1,0:T(8,128)(2,1)S(1)} %bitcast.25, bf16[64,1024]{1,0:T(8,128)(2,1)S(1)} %get-tuple-element.48.refs_2_.refs_1_, ...), custom_call_target="tpu_custom_call", output_to_operand_aliasing={{0}: (7, {})} | custom-call | flops 81920 | bytes 1024 | tf_op jit(solution)/shard_map/finish/pallas_call | solution.py:81
  34.5 1.0 %collective-permute-done.14 = bf16[16,1024]{1,0:T(8,128)(2,1)S(1)} collective-permute-done((bf16[16,1024]{1,0:T(8,128)(2,1)S(1)}, bf16[16,1024]{1,0:T(8,128)(2,1)S(1)}, u32[]{:S(2)}, u32[]{:S(2)}) %collective-permute-start.14) | collective-permute-done | bytes 32800 | tf_op jit(solution)/shard_map/ppermute | solution.py:37
  35.5 3.0 %collective-permute-done.15 = bf16[16,1024]{1,0:T(8,128)(2,1)S(1)} collective-permute-done((bf16[16,1024]{1,0:T(8,128)(2,1)S(1)}, bf16[16,1024]{1,0:T(8,128)(2,1)S(1)}, u32[]{:S(2)}, u32[]{:S(2)}) %collective-permute-start.15) | collective-permute-done | bytes 32800 | tf_op jit(solution)/shard_map/ppermute | solution.py:37
  38.6 0.6 %add_bitcast_fusion = f32[1,16,1024]{2,1,0:T(8,128)} fusion(bf16[16,1024]{1,0:T(8,128)(2,1)S(1)} %collective-permute-done.15, bf16[16,1024]{1,0:T(8,128)(2,1)S(1)} %collective-permute-done.14, bf16[16,1024]{1,0:T(8,128)(2,1)S(1)} %collective-permute-done.13, bf16[16,1024]{1,0:T(8,128)(2,1)S(1)} %get-tuple-element.88), kind=kLoop, calls=%fused_computation.1 | loop fusion | flops 114688 | bytes 196608 | tf_op jit(solution)/shard_map/broadcast_in_dim | solution.py:555
  (23 shorter events, 0.7 us)
Async XLA Ops:
  1.6 13.8 %collective-permute-start.1 = (bf16[128,1024]{1,0:T(8,128)(2,1)S(1)}, bf16[128,1024]{1,0:T(8,128)(2,1)S(1)}, u32[]{:S(2)}, u32[]{:S(2)}) collective-permute-start(bf16[128,1024]{1,0:T(8,128)(2,1)S(1)} %split_first.1.refs_3_), channel_id=1, source_target_pairs={{0,16},{16,0},{1,17},{17,1},{2,18},{18,2},{3,19},{19,3},{4,20},{20... | collective-permute-start | bytes 786440 | tf_op jit(solution)/shard_map/ppermute | solution.py:32
  5.9 8.4 %copy-start = (bf16[1,1,128,4096]{3,2,1,0:T(8,128)(2,1)S(1)}, bf16[1,1,128,4096]{3,2,1,0:T(8,128)(2,1)}, u32[]{:S(2)}) copy-start(bf16[1,1,128,4096]{3,2,1,0:T(8,128)(2,1)} %param.6) | copy-start | bytes 3145732
  6.5 7.8 %collective-permute-start = (bf16[64,1024]{1,0:T(8,128)(2,1)}, bf16[64,1024]{1,0:T(8,128)(2,1)S(1)}, u32[]{:S(2)}, u32[]{:S(2)}) collective-permute-start(bf16[64,1024]{1,0:T(8,128)(2,1)} %slice.15), channel_id=1, source_target_pairs={{0,4},{4,8},{8,12},{12,0},{1,5},{5,9},{9,13},{13,1},{2,6},{6,10},{... | collective-permute-start | bytes 393224 | tf_op jit(solution)/shard_map/ppermute | solution.py:32
  6.5 6.3 %collective-permute-start.2 = (bf16[64,1024]{1,0:T(8,128)(2,1)S(1)}, bf16[64,1024]{1,0:T(8,128)(2,1)S(1)}, u32[]{:S(2)}, u32[]{:S(2)}) collective-permute-start(bf16[64,1024]{1,0:T(8,128)(2,1)S(1)} %get-tuple-element.48.refs_2_.refs_1_), channel_id=1, source_target_pairs={{0,8},{4,12},{8,0},{12,4},{1,9},{5,13},{9,1},{13,5},{2,10},{6,14},... | collective-permute-start | bytes 393224 | tf_op jit(solution)/shard_map/ppermute | solution.py:37
  8.1 9.4 %collective-permute-start.6 = (bf16[128,1024]{1,0:T(8,128)(2,1)S(1)}, bf16[128,1024]{1,0:T(8,128)(2,1)S(1)}, u32[]{:S(2)}, u32[]{:S(2)}) collective-permute-start(bf16[128,1024]{1,0:T(8,128)(2,1)S(1)} %get-tuple-element.50.refs_1_), channel_id=1, source_target_pairs={{0,16},{16,0},{1,17},{17,1},{2,18},{18,2},{3,19},{19,3},{4,20},{20... | collective-permute-start | bytes 786440 | tf_op jit(solution)/shard_map/ppermute | solution.py:32
  9.7 13.2 %collective-permute-start.8 = (bf16[128,1024]{1,0:T(8,128)(2,1)S(1)}, bf16[128,1024]{1,0:T(8,128)(2,1)S(1)}, u32[]{:S(2)}, u32[]{:S(2)}) collective-permute-start(bf16[128,1024]{1,0:T(8,128)(2,1)S(1)} %get-tuple-element.63), channel_id=1, source_target_pairs={{0,16},{16,0},{1,17},{17,1},{2,18},{18,2},{3,19},{19,3},{4,20},{20... | collective-permute-start | bytes 786440 | tf_op jit(solution)/shard_map/ppermute | solution.py:32
  11.3 0.7 %copy-start.2 = (s32[1,1,512]{2,1,0:T(1,128)S(1)}, s32[1,1,512]{2,1,0:T(1,128)}, u32[]{:S(2)}) copy-start(s32[1,1,512]{2,1,0:T(1,128)} %param.11) | copy-start | bytes 6148
  12.8 2.6 %collective-permute-start.3 = (bf16[64,1024]{1,0:T(8,128)(2,1)S(1)}, bf16[64,1024]{1,0:T(8,128)(2,1)S(1)}, u32[]{:S(2)}, u32[]{:S(2)}) collective-permute-start(bf16[64,1024]{1,0:T(8,128)(2,1)S(1)} %collective-permute-done.2.refs_6_), channel_id=1, source_target_pairs={{0,4},{4,0},{8,12},{12,8},{1,5},{5,1},{9,13},{13,9},{2,6},{6,2},{1... | collective-permute-start | bytes 393224 | tf_op jit(solution)/shard_map/ppermute | solution.py:37
  14.2 0.7 %copy-start.1 = (bf16[1,1,128,64]{2,3,1,0:T(8,128)(2,1)S(1)}, bf16[1,1,128,64]{2,3,1,0:T(8,128)(2,1)}, u32[]{:S(2)}) copy-start(bf16[1,1,128,64]{2,3,1,0:T(8,128)(2,1)} %param.8) | copy-start | bytes 49156
  16.9 1.4 %collective-permute-start.7 = (bf16[64,1024]{1,0:T(8,128)(2,1)S(1)}, bf16[64,1024]{1,0:T(8,128)(2,1)S(1)}, u32[]{:S(2)}, u32[]{:S(2)}) collective-permute-start(bf16[64,1024]{1,0:T(8,128)(2,1)S(1)} %get-tuple-element.59), channel_id=1, source_target_pairs={{0,4},{4,0},{8,12},{12,8},{1,5},{5,1},{9,13},{13,9},{2,6},{6,2},{1... | collective-permute-start | bytes 393224 | tf_op jit(solution)/shard_map/ppermute | solution.py:37
  17.0 6.0 %collective-permute-start.9 = (bf16[64,1024]{1,0:T(8,128)(2,1)S(1)}, bf16[64,1024]{1,0:T(8,128)(2,1)S(1)}, u32[]{:S(2)}, u32[]{:S(2)}) collective-permute-start(bf16[64,1024]{1,0:T(8,128)(2,1)S(1)} %get-tuple-element.48.refs_2_.refs_1_), channel_id=1, source_target_pairs={{0,4},{4,0},{8,12},{12,8},{1,5},{5,1},{9,13},{13,9},{2,6},{6,2},{1... | collective-permute-start | bytes 393224 | tf_op jit(solution)/shard_map/ppermute | solution.py:37
  17.5 8.2 %collective-permute-start.5 = (bf16[64,1024]{1,0:T(8,128)(2,1)S(1)}, bf16[64,1024]{1,0:T(8,128)(2,1)S(1)}, u32[]{:S(2)}, u32[]{:S(2)}) collective-permute-start(bf16[64,1024]{1,0:T(8,128)(2,1)S(1)} %get-tuple-element.57), channel_id=1, source_target_pairs={{0,16},{16,0},{1,17},{17,1},{2,18},{18,2},{3,19},{19,3},{4,20},{20... | collective-permute-start | bytes 393224 | tf_op jit(solution)/shard_map/ppermute | solution.py:32
  20.2 5.6 %collective-permute-start.10 = (bf16[64,1024]{1,0:T(8,128)(2,1)S(1)}, bf16[64,1024]{1,0:T(8,128)(2,1)S(1)}, u32[]{:S(2)}, u32[]{:S(2)}) collective-permute-start(bf16[64,1024]{1,0:T(8,128)(2,1)S(1)} %get-tuple-element.71), channel_id=1, source_target_pairs={{0,8},{4,12},{8,0},{12,4},{1,9},{5,13},{9,1},{13,5},{2,10},{6,14},... | collective-permute-start | bytes 393224 | tf_op jit(solution)/shard_map/ppermute | solution.py:37
  21.7 6.1 %collective-permute-start.4 = (bf16[64,1024]{1,0:T(8,128)(2,1)S(1)}, bf16[64,1024]{1,0:T(8,128)(2,1)S(1)}, u32[]{:S(2)}, u32[]{:S(2)}) collective-permute-start(bf16[64,1024]{1,0:T(8,128)(2,1)S(1)} %get-tuple-element.54), channel_id=1, source_target_pairs={{0,16},{16,0},{1,17},{17,1},{2,18},{18,2},{3,19},{19,3},{4,20},{20... | collective-permute-start | bytes 393224 | tf_op jit(solution)/shard_map/ppermute | solution.py:32
  24.4 3.5 %collective-permute-start.11 = (bf16[64,1024]{1,0:T(8,128)(2,1)S(1)}, bf16[64,1024]{1,0:T(8,128)(2,1)S(1)}, u32[]{:S(2)}, u32[]{:S(2)}) collective-permute-start(bf16[64,1024]{1,0:T(8,128)(2,1)S(1)} %get-tuple-element.73), channel_id=1, source_target_pairs={{0,4},{4,0},{8,12},{12,8},{1,5},{5,1},{9,13},{13,9},{2,6},{6,2},{1... | collective-permute-start | bytes 393224 | tf_op jit(solution)/shard_map/ppermute | solution.py:37
  27.1 5.8 %collective-permute-start.12 = (bf16[64,1024]{1,0:T(8,128)(2,1)S(1)}, bf16[64,1024]{1,0:T(8,128)(2,1)S(1)}, u32[]{:S(2)}, u32[]{:S(2)}) collective-permute-start(bf16[64,1024]{1,0:T(8,128)(2,1)S(1)} %get-tuple-element.82), channel_id=1, source_target_pairs={{0,12},{4,0},{8,4},{12,8},{1,13},{5,1},{9,5},{13,9},{2,14},{6,2},{... | collective-permute-start | bytes 393224 | tf_op jit(solution)/shard_map/ppermute | solution.py:32
  28.4 6.0 %collective-permute-start.13 = (bf16[16,1024]{1,0:T(8,128)(2,1)S(1)}, bf16[16,1024]{1,0:T(8,128)(2,1)S(1)}, u32[]{:S(2)}, u32[]{:S(2)}) collective-permute-start(bf16[16,1024]{1,0:T(8,128)(2,1)S(1)} %get-tuple-element.89), channel_id=1, source_target_pairs={{0,1},{1,0},{2,3},{3,2},{4,5},{5,4},{6,7},{7,6},{8,9},{9,8},{10,11... | collective-permute-start | bytes 98312 | tf_op jit(solution)/shard_map/ppermute | solution.py:37
  30.3 5.3 %collective-permute-start.14 = (bf16[16,1024]{1,0:T(8,128)(2,1)S(1)}, bf16[16,1024]{1,0:T(8,128)(2,1)S(1)}, u32[]{:S(2)}, u32[]{:S(2)}) collective-permute-start(bf16[16,1024]{1,0:T(8,128)(2,1)S(1)} %get-tuple-element.90), channel_id=1, source_target_pairs={{0,2},{1,3},{2,0},{3,1},{4,6},{5,7},{6,4},{7,5},{8,10},{9,11},{10,... | collective-permute-start | bytes 98312 | tf_op jit(solution)/shard_map/ppermute | solution.py:37
  32.9 5.7 %collective-permute-start.15 = (bf16[16,1024]{1,0:T(8,128)(2,1)S(1)}, bf16[16,1024]{1,0:T(8,128)(2,1)S(1)}, u32[]{:S(2)}, u32[]{:S(2)}) collective-permute-start(bf16[16,1024]{1,0:T(8,128)(2,1)S(1)} %get-tuple-element.91), channel_id=1, source_target_pairs={{0,3},{1,2},{2,1},{3,0},{4,7},{5,6},{6,5},{7,4},{8,11},{9,10},{10,... | collective-permute-start | bytes 98312 | tf_op jit(solution)/shard_map/ppermute | solution.py:37

commit v4 on v2

--- a/solution.py
+++ b/solution.py
@@ -29,6 +29,12 @@
 def passed_along(value, axis, steps):
     count = lax.axis_size(axis)
     pairs = [(source, (source + steps) % count) for source in range(count)]
+    return lax.ppermute(value, axis, pairs)
+
+
+def shifted(value, axis, steps):
+    count = lax.axis_size(axis)
+    pairs = [(source, source + steps) for source in range(count) if 0 <= source + steps < count]
     return lax.ppermute(value, axis, pairs)
 
 
@@ -382,7 +388,7 @@
     )
     held = listed(rest, "piece")
     cots.append(passed_along(held[0], "section", -1))
-    halo = [passed_along(own[rows - count :], "seq", distance) for distance, count in pieces]
+    halo = [shifted(own[rows - count :], "seq", distance) for distance, count in pieces]
     halo = jnp.concatenate(halo[::-1], axis=0)
     ups = {0: matrix}
     for away in sorted(range(1, chunks), key=low_bit, reverse=True):
@@ -487,7 +493,7 @@
     backs = []
     stop = span
     for distance, count in pieces:
-        backs.append(passed_along(halo_grads[stop - count : stop], "seq", -distance))
+        backs.append(shifted(halo_grads[stop - count : stop], "seq", -distance))
         stop -= count
 
     outputs = dict(grad=((block, width), bf16), dscores=((window, stack_rows), bf16))

time: 37.8 us -> 40 us (1.058)
  starting transfers between devices: 17.7 us -> 21.2 us
  waiting for transfers between devices: 3.93 us -> 2.59 us
    ppermute x0 -> x2, starting transfers between devices: none -> 2.75 us  [shifted(): return lax.ppermute(value, axis, pairs)]
    ppermute x6, waiting for transfers between devices: 1.62 us -> 0.07 us  [swapped(): return lax.ppermute(value, axis, pairs)]
    ppermute x6, starting transfers between devices: 4.98 us -> 6.05 us  [swapped(): return lax.ppermute(value, axis, pairs)]
    ppermute x10 -> x8, starting transfers between devices: 12.7 us -> 12.4 us  [passed_along(): return lax.ppermute(value, axis, pairs)]
    ppermute x10 -> x8, waiting for transfers between devices: 2.31 us -> 2.51 us  [passed_along(): return lax.ppermute(value, axis, pairs)]
  transfers between devices with their start and end apart: 16 -> 16, of which waited for: 6 -> 4; matrix products, arithmetic and copies ran while one was open for 3% -> 3% of each run, Pallas kernels for 29% -> 28%
where the time goes in v4:
time: 40 us; the launch traced here: 39.6 us
  starting transfers between devices  21.2 us (53%)
  Pallas kernels  12 us (30%)
  waiting for transfers between devices  2.59 us (6%)
  local copies, waits for them, and re-layouts  2.09 us (5%)
  other arithmetic  0.92 us (2%)
  between operations  0.85 us (2%)
    ppermute x8, starting transfers between devices, passed_along(): return lax.ppermute(value, axis, pairs)  12.4 us
    pallas_call x10, Pallas kernels, run(): pl.pallas_call(kernel, in_specs=[spec_of(name) for name in inputs], out_s...  12 us
    ppermute x6, starting transfers between devices, swapped(): return lax.ppermute(value, axis, pairs)  6.05 us
    ppermute x2, starting transfers between devices, shifted(): return lax.ppermute(value, axis, pairs)  2.75 us
    ppermute x8, waiting for transfers between devices, passed_along(): return lax.ppermute(value, axis, pairs)  2.51 us
    unnamed x6, local copies, waits for them, and re-layouts  1.27 us
  transfers between devices with their start and end apart: 16, of which 4 were waited for; matrix products, arithmetic and copies ran while one was open for 3% of the time, Pallas kernels for 28%

profile of v4, /device:TPU:0, one launch (start us, length us, event | category | flops | bytes accessed | tf_op | source)
XLA Modules:
  0.0 39.6 jit_solution(17406696311293583803)
XLA Ops:
  0.6 1.0 %split_first.1.refs_3_ = bf16[128,1024]{1,0:T(8,128)(2,1)S(1)} custom-call(bf16[128,4096]{1,0:T(8,128)(2,1)} %bitcast.26), custom_call_target="tpu_custom_call" | custom-call | bytes 1024 | tf_op jit(solution)/shard_map/split_first/pallas_call | solution.py:87
  1.6 3.0 %collective-permute-start.1 = (bf16[128,1024]{1,0:T(8,128)(2,1)S(1)}, bf16[128,1024]{1,0:T(8,128)(2,1)S(1)}, u32[]{:S(2)}, u32[]{:S(2)}) collective-permute-start(bf16[128,1024]{1,0:T(8,128)(2,1)S(1)} %split_first.1.refs_3_), channel_id=1, source_target_pairs={{0,16},{16,0},{1,17},{17,1},{2,18},{18,2},{3,19},{19,3},{4,20},{20... | collective-permute-start | bytes 786440 | tf_op jit(solution)/shard_map/ppermute | solution.py:32
  4.6 1.2 %split_second.1 = (bf16[128,1024]{1,0:T(8,128)(2,1)S(1)}, bf16[64,1024]{1,0:T(8,128)(2,1)S(1)}, bf16[128,1024]{1,0:T(8,128)(2,1)S(1)}) custom-call(bf16[128,4096]{1,0:T(8,128)(2,1)} %bitcast.27, bf16[128,1024]{1,0:T(8,128)(2,1)} %bitcast.30, bf16[64,1024]{1,0:T(8,128)(2,1)} %bitcast.31, bf16[128,1024]{1,0:T(8,128)(2,1)S(1)} %split_first.1.refs_3_), custom_call_target="tpu_custom_call" | custom-call | bytes 1024 | tf_op jit(solution)/shard_map/split_second/pallas_call | solution.py:87
  5.9 0.7 %slice.15 = bf16[64,1024]{1,0:T(8,128)(2,1)} slice(bf16[128,1024]{1,0:T(8,128)(2,1)S(1)} %get-tuple-element.49.refs_4_.refs_3_), slice={[64:128], [0:1024]} | slice | bytes 262144 | tf_op jit(solution)/shard_map/slice | solution.py:391
  6.5 1.5 %collective-permute-start = (bf16[64,1024]{1,0:T(8,128)(2,1)}, bf16[64,1024]{1,0:T(8,128)(2,1)S(1)}, u32[]{:S(2)}, u32[]{:S(2)}) collective-permute-start(bf16[64,1024]{1,0:T(8,128)(2,1)} %slice.15), channel_id=1, source_target_pairs={{0,4},{4,8},{8,12},{1,5},{5,9},{9,13},{2,6},{6,10},{10,14},{3,7},{... | collective-permute-start | bytes 393224 | tf_op jit(solution)/shard_map/ppermute | solution.py:38
  8.0 2.0 %collective-permute-start.2 = (bf16[64,1024]{1,0:T(8,128)(2,1)S(1)}, bf16[64,1024]{1,0:T(8,128)(2,1)S(1)}, u32[]{:S(2)}, u32[]{:S(2)}) collective-permute-start(bf16[64,1024]{1,0:T(8,128)(2,1)S(1)} %get-tuple-element.48.refs_2_.refs_1_), channel_id=1, source_target_pairs={{0,8},{4,12},{8,0},{12,4},{1,9},{5,13},{9,1},{13,5},{2,10},{6,14},... | collective-permute-start | bytes 393224 | tf_op jit(solution)/shard_map/ppermute | solution.py:43
  10.0 0.5 %collective-permute-start.6 = (bf16[128,1024]{1,0:T(8,128)(2,1)S(1)}, bf16[128,1024]{1,0:T(8,128)(2,1)S(1)}, u32[]{:S(2)}, u32[]{:S(2)}) collective-permute-start(bf16[128,1024]{1,0:T(8,128)(2,1)S(1)} %get-tuple-element.50.refs_1_), channel_id=1, source_target_pairs={{0,16},{16,0},{1,17},{17,1},{2,18},{18,2},{3,19},{19,3},{4,20},{20... | collective-permute-start | bytes 786440 | tf_op jit(solution)/shard_map/ppermute | solution.py:32
  10.6 1.1 %split_rest.1 = (bf16[128,1024]{1,0:T(8,128)(2,1)S(1)}, bf16[64,1024]{1,0:T(8,128)(2,1)S(1)}, bf16[64,1024]{1,0:T(8,128)(2,1)S(1)}) custom-call(bf16[128,4096]{1,0:T(8,128)(2,1)} %bitcast.28, bf16[128,1024]{1,0:T(8,128)(2,1)S(1)} %get-tuple-element.50.refs_1_), custom_call_target="tpu_custom_call" | custom-call | bytes 1024 | tf_op jit(solution)/shard_map/split_rest/pallas_call | solution.py:87
  11.7 1.6 %collective-permute-start.8 = (bf16[128,1024]{1,0:T(8,128)(2,1)S(1)}, bf16[128,1024]{1,0:T(8,128)(2,1)S(1)}, u32[]{:S(2)}, u32[]{:S(2)}) collective-permute-start(bf16[128,1024]{1,0:T(8,128)(2,1)S(1)} %get-tuple-element.63), channel_id=1, source_target_pairs={{0,16},{16,0},{1,17},{17,1},{2,18},{18,2},{3,19},{19,3},{4,20},{20... | collective-permute-start | bytes 786440 | tf_op jit(solution)/shard_map/ppermute | solution.py:32
  13.2 0.7 %copy-done.2 = s32[1,1,512]{2,1,0:T(1,128)S(1)} copy-done((s32[1,1,512]{2,1,0:T(1,128)S(1)}, s32[1,1,512]{2,1,0:T(1,128)}, u32[]{:S(2)}) %copy-start.2) | copy-done | bytes 2072
  14.1 0.8 %collective-permute-start.3 = (bf16[64,1024]{1,0:T(8,128)(2,1)S(1)}, bf16[64,1024]{1,0:T(8,128)(2,1)S(1)}, u32[]{:S(2)}, u32[]{:S(2)}) collective-permute-start(bf16[64,1024]{1,0:T(8,128)(2,1)S(1)} %collective-permute-done.2.refs_6_), channel_id=1, source_target_pairs={{0,4},{4,0},{8,12},{12,8},{1,5},{5,1},{9,13},{13,9},{2,6},{6,2},{1... | collective-permute-start | bytes 393224 | tf_op jit(solution)/shard_map/ppermute | solution.py:43
  15.1 0.1 maximum_maximum_fusion.refs_5_.refs_4_
  15.2 0.6 %copy-done.1 = bf16[1,1,128,64]{2,3,1,0:T(8,128)(2,1)S(1)} copy-done((bf16[1,1,128,64]{2,3,1,0:T(8,128)(2,1)S(1)}, bf16[1,1,128,64]{2,3,1,0:T(8,128)(2,1)}, u32[]{:S(2)}) %copy-start.1) | copy-done | bytes 16408
  15.8 0.6 %forward.1 = (bf16[512,128]{1,0:T(8,128)(2,1)S(1)}, bf16[512,128]{1,0:T(8,128)(2,1)S(1)}, f32[128,512]{1,0:T(8,128)S(1)}, f32[128,512]{1,0:T(8,128)S(1)}, bf16[64,1024]{1,0:T(8,128)(2,1)S(1)}) custom-call(bf16[128,4096]{1,0:T(8,128)(2,1)S(1)} %bitcast.15, bf16[64,128]{1,0:T(8,128)(2,1)S(1)} %bitcast.19, ...), custom_call_target="tpu_custom_call", output_to_operand_aliasing={{4}: (6, {})} | custom-call | flops 81920 | bytes 1024 | tf_op jit(solution)/shard_map/forward/pallas_call | solution.py:87
  16.4 1.4 %whole.3 = (bf16[64,256]{1,0:T(8,128)(2,1)S(1)}, f32[128,256]{1,0:T(8,128)S(1)}, f32[64,128]{1,0:T(8,128)S(1)}, bf16[128,1024]{1,0:T(8,128)(2,1)S(1)}, bf16[64,1...) custom-call(bf16[128,4096]{1,0:T(8,128)(2,1)S(1)} %bitcast.16, ...), custom_call_target="tpu_custom_call", output_to_operand_aliasing={{5}: (8, {})} | custom-call | flops 163840 | bytes 1024 | tf_op jit(solution)/shard_map/whole/pallas_call | solution.py:87
  17.9 0.5 %collective-permute-start.9 = (bf16[64,1024]{1,0:T(8,128)(2,1)S(1)}, bf16[64,1024]{1,0:T(8,128)(2,1)S(1)}, u32[]{:S(2)}, u32[]{:S(2)}) collective-permute-start(bf16[64,1024]{1,0:T(8,128)(2,1)S(1)} %get-tuple-element.48.refs_2_.refs_1_), channel_id=1, source_target_pairs={{0,4},{4,0},{8,12},{12,8},{1,5},{5,1},{9,13},{13,9},{2,6},{6,2},{1... | collective-permute-start | bytes 393224 | tf_op jit(solution)/shard_map/ppermute | solution.py:43
  18.4 0.5 %collective-permute-start.5 = (bf16[64,1024]{1,0:T(8,128)(2,1)S(1)}, bf16[64,1024]{1,0:T(8,128)(2,1)S(1)}, u32[]{:S(2)}, u32[]{:S(2)}) collective-permute-start(bf16[64,1024]{1,0:T(8,128)(2,1)S(1)} %get-tuple-element.57), channel_id=1, source_target_pairs={{0,16},{16,0},{1,17},{17,1},{2,18},{18,2},{3,19},{19,3},{4,20},{20... | collective-permute-start | bytes 393224 | tf_op jit(solution)/shard_map/ppermute | solution.py:32
  18.9 0.2 collective-permute-done.6.refs_5_
  19.2 1.8 %whole.4 = (bf16[64,256]{1,0:T(8,128)(2,1)S(1)}, f32[128,256]{1,0:T(8,128)S(1)}, f32[64,128]{1,0:T(8,128)S(1)}, bf16[128,1024]{1,0:T(8,128)(2,1)S(1)}, bf16[64,1...) custom-call(bf16[128,4096]{1,0:T(8,128)(2,1)S(1)} %bitcast.17, bf16[64,128]{1,0:T(8,128)(2,1)S(1)} %bitcast.21, ...), custom_call_target="tpu_custom_call" | custom-call | flops 163840 | bytes 1024 | tf_op jit(solution)/shard_map/whole/pallas_call | solution.py:87
  21.1 2.5 %collective-permute-start.10 = (bf16[64,1024]{1,0:T(8,128)(2,1)S(1)}, bf16[64,1024]{1,0:T(8,128)(2,1)S(1)}, u32[]{:S(2)}, u32[]{:S(2)}) collective-permute-start(bf16[64,1024]{1,0:T(8,128)(2,1)S(1)} %get-tuple-element.71), channel_id=1, source_target_pairs={{0,8},{4,12},{8,0},{12,4},{1,9},{5,13},{9,1},{13,5},{2,10},{6,14},... | collective-permute-start | bytes 393224 | tf_op jit(solution)/shard_map/ppermute | solution.py:43
  23.6 1.2 %collective-permute-start.4 = (bf16[64,1024]{1,0:T(8,128)(2,1)S(1)}, bf16[64,1024]{1,0:T(8,128)(2,1)S(1)}, u32[]{:S(2)}, u32[]{:S(2)}) collective-permute-start(bf16[64,1024]{1,0:T(8,128)(2,1)S(1)} %get-tuple-element.54), channel_id=1, source_target_pairs={{0,16},{16,0},{1,17},{17,1},{2,18},{18,2},{3,19},{19,3},{4,20},{20... | collective-permute-start | bytes 393224 | tf_op jit(solution)/shard_map/ppermute | solution.py:32
  24.8 1.4 %whole.5 = (bf16[64,256]{1,0:T(8,128)(2,1)S(1)}, f32[128,256]{1,0:T(8,128)S(1)}, f32[64,128]{1,0:T(8,128)S(1)}, bf16[128,1024]{1,0:T(8,128)(2,1)S(1)}, bf16[64,1024]{1,0:T(8,128)(2,1)S(1)}) custom-call(bf16[128,4096]{1,0:T(8,128)(2,1)S(1)} %bitcast.18, bf16[64,128]{1,0:T(8,128)(2,1)S(1)} %bitcast.22, ...), custom_call_target="tpu_custom_call" | custom-call | flops 163840 | bytes 1024 | tf_op jit(solution)/shard_map/whole/pallas_call | solution.py:87
  26.3 1.3 %collective-permute-done.5.refs_4_ = bf16[64,1024]{1,0:T(8,128)(2,1)S(1)} collective-permute-done((bf16[64,1024]{1,0:T(8,128)(2,1)S(1)}, bf16[64,1024]{1,0:T(8,128)(2,1)S(1)}, u32[]{:S(2)}, u32[]{:S(2)}) %collective-permute-start.5) | collective-permute-done | bytes 131104 | tf_op jit(solution)/shard_map/ppermute | solution.py:32
  27.6 1.3 %front.1 = (bf16[128,4096]{1,0:T(8,128)(2,1)}, bf16[64,1024]{1,0:T(8,128)(2,1)S(1)}, f32[128,256]{1,0:T(8,128)S(1)}, f32[64,1024]{1,0:T(8,128)S(1)}, f32[64,128]...) custom-call(bf16[64,128]{1,0:T(8,128)(2,1)S(1)} %bitcast.23, ...), custom_call_target="tpu_custom_call", output_to_operand_aliasing={{0}: (7, {})} | custom-call | flops 81920 | bytes 1024 | tf_op jit(solution)/shard_map/front/pallas_call | solution.py:87
  28.9 1.3 %collective-permute-start.12 = (bf16[64,1024]{1,0:T(8,128)(2,1)S(1)}, bf16[64,1024]{1,0:T(8,128)(2,1)S(1)}, u32[]{:S(2)}, u32[]{:S(2)}) collective-permute-start(bf16[64,1024]{1,0:T(8,128)(2,1)S(1)} %get-tuple-element.82), channel_id=1, source_target_pairs={{4,0},{8,4},{12,8},{5,1},{9,5},{13,9},{6,2},{10,6},{14,10},{7,3},{... | collective-permute-start | bytes 393224 | tf_op jit(solution)/shard_map/ppermute | solution.py:38
  30.2 0.6 %back.1 = (bf16[64,1024]{1,0:T(8,128)(2,1)S(1)}, bf16[128,512]{1,0:T(8,128)(2,1)S(1)}, bf16[16,1024]{1,0:T(8,128)(2,1)S(1)}, bf16[16,1024]{1,0:T(8,128)(2,1)S(1)...) custom-call(bf16[64,128]{1,0:T(8,128)(2,1)S(1)} %bitcast.24, ...), custom_call_target="tpu_custom_call" | custom-call | flops 81920 | bytes 1024 | tf_op jit(solution)/shard_map/back/pallas_call | solution.py:87
  30.9 1.6 %collective-permute-start.13 = (bf16[16,1024]{1,0:T(8,128)(2,1)S(1)}, bf16[16,1024]{1,0:T(8,128)(2,1)S(1)}, u32[]{:S(2)}, u32[]{:S(2)}) collective-permute-start(bf16[16,1024]{1,0:T(8,128)(2,1)S(1)} %get-tuple-element.89), channel_id=1, source_target_pairs={{0,1},{1,2},{2,3},{3,0},{4,5},{5,6},{6,7},{7,4},{8,9},{9,10},{10,1... | collective-permute-start | bytes 98312 | tf_op jit(solution)/shard_map/ppermute | solution.py:32
  32.5 2.6 %collective-permute-start.14 = (bf16[16,1024]{1,0:T(8,128)(2,1)S(1)}, bf16[16,1024]{1,0:T(8,128)(2,1)S(1)}, u32[]{:S(2)}, u32[]{:S(2)}) collective-permute-start(bf16[16,1024]{1,0:T(8,128)(2,1)S(1)} %get-tuple-element.90), channel_id=1, source_target_pairs={{0,2},{1,3},{2,0},{3,1},{4,6},{5,7},{6,4},{7,5},{8,10},{9,11},{10,... | collective-permute-start | bytes 98312 | tf_op jit(solution)/shard_map/ppermute | solution.py:32
  35.1 1.3 %collective-permute-start.15 = (bf16[16,1024]{1,0:T(8,128)(2,1)S(1)}, bf16[16,1024]{1,0:T(8,128)(2,1)S(1)}, u32[]{:S(2)}, u32[]{:S(2)}) collective-permute-start(bf16[16,1024]{1,0:T(8,128)(2,1)S(1)} %get-tuple-element.91), channel_id=1, source_target_pairs={{0,3},{1,0},{2,1},{3,2},{4,7},{5,4},{6,5},{7,6},{8,11},{9,8},{10,9... | collective-permute-start | bytes 98312 | tf_op jit(solution)/shard_map/ppermute | solution.py:32
  36.4 1.6 %finish.1 = (bf16[128,4096]{1,0:T(8,128)(2,1)}, bf16[64,128]{1,0:T(8,128)(2,1)}, bf16[16,1024]{1,0:T(8,128)(2,1)S(1)}, bf16[128,1024]{1,0:T(8,128)(2,1)}) custom-call(bf16[64,128]{1,0:T(8,128)(2,1)S(1)} %bitcast.25, bf16[64,1024]{1,0:T(8,128)(2,1)S(1)} %get-tuple-element.48.refs_2_.refs_1_, ...), custom_call_target="tpu_custom_call", output_to_operand_aliasing={{0}: (7, {})} | custom-call | flops 81920 | bytes 1024 | tf_op jit(solution)/shard_map/finish/pallas_call | solution.py:87
  38.0 1.0 %collective-permute-done.15 = bf16[16,1024]{1,0:T(8,128)(2,1)S(1)} collective-permute-done((bf16[16,1024]{1,0:T(8,128)(2,1)S(1)}, bf16[16,1024]{1,0:T(8,128)(2,1)S(1)}, u32[]{:S(2)}, u32[]{:S(2)}) %collective-permute-start.15) | collective-permute-done | bytes 32800 | tf_op jit(solution)/shard_map/ppermute | solution.py:32
  39.0 0.6 %add_bitcast_fusion = f32[1,16,1024]{2,1,0:T(8,128)} fusion(bf16[16,1024]{1,0:T(8,128)(2,1)S(1)} %collective-permute-done.15, bf16[16,1024]{1,0:T(8,128)(2,1)S(1)} %collective-permute-done.14, bf16[16,1024]{1,0:T(8,128)(2,1)S(1)} %collective-permute-done.13, bf16[16,1024]{1,0:T(8,128)(2,1)S(1)} %get-tuple-element.88), kind=kLoop, calls=%fused_computation.1 | loop fusion | flops 114688 | bytes 196608 | tf_op jit(solution)/shard_map/broadcast_in_dim | solution.py:559
  (23 shorter events, 0.6 us)
Async XLA Ops:
  1.6 14.8 %collective-permute-start.1 = (bf16[128,1024]{1,0:T(8,128)(2,1)S(1)}, bf16[128,1024]{1,0:T(8,128)(2,1)S(1)}, u32[]{:S(2)}, u32[]{:S(2)}) collective-permute-start(bf16[128,1024]{1,0:T(8,128)(2,1)S(1)} %split_first.1.refs_3_), channel_id=1, source_target_pairs={{0,16},{16,0},{1,17},{17,1},{2,18},{18,2},{3,19},{19,3},{4,20},{20... | collective-permute-start | bytes 786440 | tf_op jit(solution)/shard_map/ppermute | solution.py:32
  5.9 9.4 %copy-start = (bf16[1,1,128,4096]{3,2,1,0:T(8,128)(2,1)S(1)}, bf16[1,1,128,4096]{3,2,1,0:T(8,128)(2,1)}, u32[]{:S(2)}) copy-start(bf16[1,1,128,4096]{3,2,1,0:T(8,128)(2,1)} %param.6) | copy-start | bytes 3145732
  6.5 8.7 %collective-permute-start = (bf16[64,1024]{1,0:T(8,128)(2,1)}, bf16[64,1024]{1,0:T(8,128)(2,1)S(1)}, u32[]{:S(2)}, u32[]{:S(2)}) collective-permute-start(bf16[64,1024]{1,0:T(8,128)(2,1)} %slice.15), channel_id=1, source_target_pairs={{0,4},{4,8},{8,12},{1,5},{5,9},{9,13},{2,6},{6,10},{10,14},{3,7},{... | collective-permute-start | bytes 393224 | tf_op jit(solution)/shard_map/ppermute | solution.py:38
  8.0 6.2 %collective-permute-start.2 = (bf16[64,1024]{1,0:T(8,128)(2,1)S(1)}, bf16[64,1024]{1,0:T(8,128)(2,1)S(1)}, u32[]{:S(2)}, u32[]{:S(2)}) collective-permute-start(bf16[64,1024]{1,0:T(8,128)(2,1)S(1)} %get-tuple-element.48.refs_2_.refs_1_), channel_id=1, source_target_pairs={{0,8},{4,12},{8,0},{12,4},{1,9},{5,13},{9,1},{13,5},{2,10},{6,14},... | collective-permute-start | bytes 393224 | tf_op jit(solution)/shard_map/ppermute | solution.py:43
  10.0 9.1 %collective-permute-start.6 = (bf16[128,1024]{1,0:T(8,128)(2,1)S(1)}, bf16[128,1024]{1,0:T(8,128)(2,1)S(1)}, u32[]{:S(2)}, u32[]{:S(2)}) collective-permute-start(bf16[128,1024]{1,0:T(8,128)(2,1)S(1)} %get-tuple-element.50.refs_1_), channel_id=1, source_target_pairs={{0,16},{16,0},{1,17},{17,1},{2,18},{18,2},{3,19},{19,3},{4,20},{20... | collective-permute-start | bytes 786440 | tf_op jit(solution)/shard_map/ppermute | solution.py:32
  11.7 13.1 %collective-permute-start.8 = (bf16[128,1024]{1,0:T(8,128)(2,1)S(1)}, bf16[128,1024]{1,0:T(8,128)(2,1)S(1)}, u32[]{:S(2)}, u32[]{:S(2)}) collective-permute-start(bf16[128,1024]{1,0:T(8,128)(2,1)S(1)} %get-tuple-element.63), channel_id=1, source_target_pairs={{0,16},{16,0},{1,17},{17,1},{2,18},{18,2},{3,19},{19,3},{4,20},{20... | collective-permute-start | bytes 786440 | tf_op jit(solution)/shard_map/ppermute | solution.py:32
  13.2 0.7 %copy-start.2 = (s32[1,1,512]{2,1,0:T(1,128)S(1)}, s32[1,1,512]{2,1,0:T(1,128)}, u32[]{:S(2)}) copy-start(s32[1,1,512]{2,1,0:T(1,128)} %param.11) | copy-start | bytes 6148
  14.1 2.2 %collective-permute-start.3 = (bf16[64,1024]{1,0:T(8,128)(2,1)S(1)}, bf16[64,1024]{1,0:T(8,128)(2,1)S(1)}, u32[]{:S(2)}, u32[]{:S(2)}) collective-permute-start(bf16[64,1024]{1,0:T(8,128)(2,1)S(1)} %collective-permute-done.2.refs_6_), channel_id=1, source_target_pairs={{0,4},{4,0},{8,12},{12,8},{1,5},{5,1},{9,13},{13,9},{2,6},{6,2},{1... | collective-permute-start | bytes 393224 | tf_op jit(solution)/shard_map/ppermute | solution.py:43
  15.1 0.7 %copy-start.1 = (bf16[1,1,128,64]{2,3,1,0:T(8,128)(2,1)S(1)}, bf16[1,1,128,64]{2,3,1,0:T(8,128)(2,1)}, u32[]{:S(2)}) copy-start(bf16[1,1,128,64]{2,3,1,0:T(8,128)(2,1)} %param.8) | copy-start | bytes 49156
  17.8 1.4 %collective-permute-start.7 = (bf16[64,1024]{1,0:T(8,128)(2,1)S(1)}, bf16[64,1024]{1,0:T(8,128)(2,1)S(1)}, u32[]{:S(2)}, u32[]{:S(2)}) collective-permute-start(bf16[64,1024]{1,0:T(8,128)(2,1)S(1)} %get-tuple-element.59), channel_id=1, source_target_pairs={{0,4},{4,0},{8,12},{12,8},{1,5},{5,1},{9,13},{13,9},{2,6},{6,2},{1... | collective-permute-start | bytes 393224 | tf_op jit(solution)/shard_map/ppermute | solution.py:43
  17.9 6.9 %collective-permute-start.9 = (bf16[64,1024]{1,0:T(8,128)(2,1)S(1)}, bf16[64,1024]{1,0:T(8,128)(2,1)S(1)}, u32[]{:S(2)}, u32[]{:S(2)}) collective-permute-start(bf16[64,1024]{1,0:T(8,128)(2,1)S(1)} %get-tuple-element.48.refs_2_.refs_1_), channel_id=1, source_target_pairs={{0,4},{4,0},{8,12},{12,8},{1,5},{5,1},{9,13},{13,9},{2,6},{6,2},{1... | collective-permute-start | bytes 393224 | tf_op jit(solution)/shard_map/ppermute | solution.py:43
  18.4 9.2 %collective-permute-start.5 = (bf16[64,1024]{1,0:T(8,128)(2,1)S(1)}, bf16[64,1024]{1,0:T(8,128)(2,1)S(1)}, u32[]{:S(2)}, u32[]{:S(2)}) collective-permute-start(bf16[64,1024]{1,0:T(8,128)(2,1)S(1)} %get-tuple-element.57), channel_id=1, source_target_pairs={{0,16},{16,0},{1,17},{17,1},{2,18},{18,2},{3,19},{19,3},{4,20},{20... | collective-permute-start | bytes 393224 | tf_op jit(solution)/shard_map/ppermute | solution.py:32
  21.1 6.5 %collective-permute-start.10 = (bf16[64,1024]{1,0:T(8,128)(2,1)S(1)}, bf16[64,1024]{1,0:T(8,128)(2,1)S(1)}, u32[]{:S(2)}, u32[]{:S(2)}) collective-permute-start(bf16[64,1024]{1,0:T(8,128)(2,1)S(1)} %get-tuple-element.71), channel_id=1, source_target_pairs={{0,8},{4,12},{8,0},{12,4},{1,9},{5,13},{9,1},{13,5},{2,10},{6,14},... | collective-permute-start | bytes 393224 | tf_op jit(solution)/shard_map/ppermute | solution.py:43
  23.6 6.6 %collective-permute-start.4 = (bf16[64,1024]{1,0:T(8,128)(2,1)S(1)}, bf16[64,1024]{1,0:T(8,128)(2,1)S(1)}, u32[]{:S(2)}, u32[]{:S(2)}) collective-permute-start(bf16[64,1024]{1,0:T(8,128)(2,1)S(1)} %get-tuple-element.54), channel_id=1, source_target_pairs={{0,16},{16,0},{1,17},{17,1},{2,18},{18,2},{3,19},{19,3},{4,20},{20... | collective-permute-start | bytes 393224 | tf_op jit(solution)/shard_map/ppermute | solution.py:32
  26.2 4.0 %collective-permute-start.11 = (bf16[64,1024]{1,0:T(8,128)(2,1)S(1)}, bf16[64,1024]{1,0:T(8,128)(2,1)S(1)}, u32[]{:S(2)}, u32[]{:S(2)}) collective-permute-start(bf16[64,1024]{1,0:T(8,128)(2,1)S(1)} %get-tuple-element.73), channel_id=1, source_target_pairs={{0,4},{4,0},{8,12},{12,8},{1,5},{5,1},{9,13},{13,9},{2,6},{6,2},{1... | collective-permute-start | bytes 393224 | tf_op jit(solution)/shard_map/ppermute | solution.py:43
  28.9 7.5 %collective-permute-start.12 = (bf16[64,1024]{1,0:T(8,128)(2,1)S(1)}, bf16[64,1024]{1,0:T(8,128)(2,1)S(1)}, u32[]{:S(2)}, u32[]{:S(2)}) collective-permute-start(bf16[64,1024]{1,0:T(8,128)(2,1)S(1)} %get-tuple-element.82), channel_id=1, source_target_pairs={{4,0},{8,4},{12,8},{5,1},{9,5},{13,9},{6,2},{10,6},{14,10},{7,3},{... | collective-permute-start | bytes 393224 | tf_op jit(solution)/shard_map/ppermute | solution.py:38
  30.9 7.2 %collective-permute-start.13 = (bf16[16,1024]{1,0:T(8,128)(2,1)S(1)}, bf16[16,1024]{1,0:T(8,128)(2,1)S(1)}, u32[]{:S(2)}, u32[]{:S(2)}) collective-permute-start(bf16[16,1024]{1,0:T(8,128)(2,1)S(1)} %get-tuple-element.89), channel_id=1, source_target_pairs={{0,1},{1,2},{2,3},{3,0},{4,5},{5,6},{6,7},{7,4},{8,9},{9,10},{10,1... | collective-permute-start | bytes 98312 | tf_op jit(solution)/shard_map/ppermute | solution.py:32
  32.5 5.5 %collective-permute-start.14 = (bf16[16,1024]{1,0:T(8,128)(2,1)S(1)}, bf16[16,1024]{1,0:T(8,128)(2,1)S(1)}, u32[]{:S(2)}, u32[]{:S(2)}) collective-permute-start(bf16[16,1024]{1,0:T(8,128)(2,1)S(1)} %get-tuple-element.90), channel_id=1, source_target_pairs={{0,2},{1,3},{2,0},{3,1},{4,6},{5,7},{6,4},{7,5},{8,10},{9,11},{10,... | collective-permute-start | bytes 98312 | tf_op jit(solution)/shard_map/ppermute | solution.py:32
  35.1 3.9 %collective-permute-start.15 = (bf16[16,1024]{1,0:T(8,128)(2,1)S(1)}, bf16[16,1024]{1,0:T(8,128)(2,1)S(1)}, u32[]{:S(2)}, u32[]{:S(2)}) collective-permute-start(bf16[16,1024]{1,0:T(8,128)(2,1)S(1)} %get-tuple-element.91), channel_id=1, source_target_pairs={{0,3},{1,0},{2,1},{3,2},{4,7},{5,4},{6,5},{7,6},{8,11},{9,8},{10,9... | collective-permute-start | bytes 98312 | tf_op jit(solution)/shard_map/ppermute | solution.py:32

commit v5 on v2

--- a/solution.py
+++ b/solution.py
@@ -534,6 +534,7 @@
         flops,
     )
     weight_share = final.share_out.astype(f32)
+    shares[1:] = shares[1:2] + shares[:1:-1]
     for share in shares[1:]:
         weight_share += share.astype(f32)
     if merged:

time: 37.8 us -> 38.2 us (1.011)
  waiting for transfers between devices: 3.93 us -> 5.22 us
  starting transfers between devices: 17.7 us -> 16.8 us
    ppermute x10, waiting for transfers between devices: 2.31 us -> 3.6 us  [passed_along(): return lax.ppermute(value, axis, pairs)]
    ppermute x10, starting transfers between devices: 12.7 us -> 11.8 us  [passed_along(): return lax.ppermute(value, axis, pairs)]
where the time goes in v5:
time: 38.2 us; the launch traced here: 37.8 us
  starting transfers between devices  16.8 us (44%)
  Pallas kernels  12 us (31%)
  waiting for transfers between devices  5.22 us (14%)
  local copies, waits for them, and re-layouts  2.09 us (5%)
  other arithmetic  0.92 us (2%)
  between operations  0.82 us (2%)
    pallas_call x10, Pallas kernels, run(): pl.pallas_call(kernel, in_specs=[spec_of(name) for name in inputs], out_s...  12 us
    ppermute x10, starting transfers between devices, passed_along(): return lax.ppermute(value, axis, pairs)  11.8 us
    ppermute x6, starting transfers between devices, swapped(): return lax.ppermute(value, axis, pairs)  4.98 us
    ppermute x10, waiting for transfers between devices, passed_along(): return lax.ppermute(value, axis, pairs)  3.6 us
    ppermute x6, waiting for transfers between devices, swapped(): return lax.ppermute(value, axis, pairs)  1.62 us
    unnamed x6, local copies, waits for them, and re-layouts  1.27 us
  transfers between devices with their start and end apart: 16, of which 6 were waited for; matrix products, arithmetic and copies ran while one was open for 3% of the time, Pallas kernels for 29%

profile of v5, /device:TPU:0, one launch (start us, length us, event | category | flops | bytes accessed | tf_op | source)
XLA Modules:
  0.0 37.8 jit_solution(6277134547290510817)
XLA Ops:
  0.6 1.0 %split_first.1.refs_3_ = bf16[128,1024]{1,0:T(8,128)(2,1)S(1)} custom-call(bf16[128,4096]{1,0:T(8,128)(2,1)} %bitcast.26), custom_call_target="tpu_custom_call" | custom-call | bytes 1024 | tf_op jit(solution)/shard_map/split_first/pallas_call | solution.py:81
  1.6 3.0 %collective-permute-start.1 = (bf16[128,1024]{1,0:T(8,128)(2,1)S(1)}, bf16[128,1024]{1,0:T(8,128)(2,1)S(1)}, u32[]{:S(2)}, u32[]{:S(2)}) collective-permute-start(bf16[128,1024]{1,0:T(8,128)(2,1)S(1)} %split_first.1.refs_3_), channel_id=1, source_target_pairs={{0,16},{16,0},{1,17},{17,1},{2,18},{18,2},{3,19},{19,3},{4,20},{20... | collective-permute-start | bytes 786440 | tf_op jit(solution)/shard_map/ppermute | solution.py:32
  4.6 1.2 %split_second.1 = (bf16[128,1024]{1,0:T(8,128)(2,1)S(1)}, bf16[64,1024]{1,0:T(8,128)(2,1)S(1)}, bf16[128,1024]{1,0:T(8,128)(2,1)S(1)}) custom-call(bf16[128,4096]{1,0:T(8,128)(2,1)} %bitcast.27, bf16[128,1024]{1,0:T(8,128)(2,1)} %bitcast.30, bf16[64,1024]{1,0:T(8,128)(2,1)} %bitcast.31, bf16[128,1024]{1,0:T(8,128)(2,1)S(1)} %split_first.1.refs_3_), custom_call_target="tpu_custom_call" | custom-call | bytes 1024 | tf_op jit(solution)/shard_map/split_second/pallas_call | solution.py:81
  5.9 0.7 %slice.15 = bf16[64,1024]{1,0:T(8,128)(2,1)} slice(bf16[128,1024]{1,0:T(8,128)(2,1)S(1)} %get-tuple-element.49.refs_4_.refs_3_), slice={[64:128], [0:1024]} | slice | bytes 262144 | tf_op jit(solution)/shard_map/slice | solution.py:385
  6.5 1.6 %collective-permute-start.2 = (bf16[64,1024]{1,0:T(8,128)(2,1)S(1)}, bf16[64,1024]{1,0:T(8,128)(2,1)S(1)}, u32[]{:S(2)}, u32[]{:S(2)}) collective-permute-start(bf16[64,1024]{1,0:T(8,128)(2,1)S(1)} %get-tuple-element.48.refs_2_.refs_1_), channel_id=1, source_target_pairs={{0,8},{4,12},{8,0},{12,4},{1,9},{5,13},{9,1},{13,5},{2,10},{6,14},... | collective-permute-start | bytes 393224 | tf_op jit(solution)/shard_map/ppermute | solution.py:37
  8.1 0.5 %collective-permute-start.6 = (bf16[128,1024]{1,0:T(8,128)(2,1)S(1)}, bf16[128,1024]{1,0:T(8,128)(2,1)S(1)}, u32[]{:S(2)}, u32[]{:S(2)}) collective-permute-start(bf16[128,1024]{1,0:T(8,128)(2,1)S(1)} %get-tuple-element.50.refs_1_), channel_id=1, source_target_pairs={{0,16},{16,0},{1,17},{17,1},{2,18},{18,2},{3,19},{19,3},{4,20},{20... | collective-permute-start | bytes 786440 | tf_op jit(solution)/shard_map/ppermute | solution.py:32
  8.6 1.1 %split_rest.1 = (bf16[128,1024]{1,0:T(8,128)(2,1)S(1)}, bf16[64,1024]{1,0:T(8,128)(2,1)S(1)}, bf16[64,1024]{1,0:T(8,128)(2,1)S(1)}) custom-call(bf16[128,4096]{1,0:T(8,128)(2,1)} %bitcast.28, bf16[128,1024]{1,0:T(8,128)(2,1)S(1)} %get-tuple-element.50.refs_1_), custom_call_target="tpu_custom_call" | custom-call | bytes 1024 | tf_op jit(solution)/shard_map/split_rest/pallas_call | solution.py:81
  9.7 1.6 %collective-permute-start.8 = (bf16[128,1024]{1,0:T(8,128)(2,1)S(1)}, bf16[128,1024]{1,0:T(8,128)(2,1)S(1)}, u32[]{:S(2)}, u32[]{:S(2)}) collective-permute-start(bf16[128,1024]{1,0:T(8,128)(2,1)S(1)} %get-tuple-element.63), channel_id=1, source_target_pairs={{0,16},{16,0},{1,17},{17,1},{2,18},{18,2},{3,19},{19,3},{4,20},{20... | collective-permute-start | bytes 786440 | tf_op jit(solution)/shard_map/ppermute | solution.py:32
  11.3 0.7 %copy-done.2 = s32[1,1,512]{2,1,0:T(1,128)S(1)} copy-done((s32[1,1,512]{2,1,0:T(1,128)S(1)}, s32[1,1,512]{2,1,0:T(1,128)}, u32[]{:S(2)}) %copy-start.2) | copy-done | bytes 2072
  12.2 0.7 %collective-permute-done.2.refs_6_ = bf16[64,1024]{1,0:T(8,128)(2,1)S(1)} collective-permute-done((bf16[64,1024]{1,0:T(8,128)(2,1)S(1)}, bf16[64,1024]{1,0:T(8,128)(2,1)S(1)}, u32[]{:S(2)}, u32[]{:S(2)}) %collective-permute-start.2) | collective-permute-done | bytes 131104 | tf_op jit(solution)/shard_map/ppermute | solution.py:37
  12.8 1.2 %collective-permute-start.3 = (bf16[64,1024]{1,0:T(8,128)(2,1)S(1)}, bf16[64,1024]{1,0:T(8,128)(2,1)S(1)}, u32[]{:S(2)}, u32[]{:S(2)}) collective-permute-start(bf16[64,1024]{1,0:T(8,128)(2,1)S(1)} %collective-permute-done.2.refs_6_), channel_id=1, source_target_pairs={{0,4},{4,0},{8,12},{12,8},{1,5},{5,1},{9,13},{13,9},{2,6},{6,2},{1... | collective-permute-start | bytes 393224 | tf_op jit(solution)/shard_map/ppermute | solution.py:37
  14.3 0.6 %copy-done.1 = bf16[1,1,128,64]{2,3,1,0:T(8,128)(2,1)S(1)} copy-done((bf16[1,1,128,64]{2,3,1,0:T(8,128)(2,1)S(1)}, bf16[1,1,128,64]{2,3,1,0:T(8,128)(2,1)}, u32[]{:S(2)}) %copy-start.1) | copy-done | bytes 16408
  14.9 0.6 %forward.1 = (bf16[512,128]{1,0:T(8,128)(2,1)S(1)}, bf16[512,128]{1,0:T(8,128)(2,1)S(1)}, f32[128,512]{1,0:T(8,128)S(1)}, f32[128,512]{1,0:T(8,128)S(1)}, bf16[64,1024]{1,0:T(8,128)(2,1)S(1)}) custom-call(bf16[128,4096]{1,0:T(8,128)(2,1)S(1)} %bitcast.15, bf16[64,128]{1,0:T(8,128)(2,1)S(1)} %bitcast.19, ...), custom_call_target="tpu_custom_call", output_to_operand_aliasing={{4}: (6, {})} | custom-call | flops 81920 | bytes 1024 | tf_op jit(solution)/shard_map/forward/pallas_call | solution.py:81
  15.5 1.4 %whole.3 = (bf16[64,256]{1,0:T(8,128)(2,1)S(1)}, f32[128,256]{1,0:T(8,128)S(1)}, f32[64,128]{1,0:T(8,128)S(1)}, bf16[128,1024]{1,0:T(8,128)(2,1)S(1)}, bf16[64,1...) custom-call(bf16[128,4096]{1,0:T(8,128)(2,1)S(1)} %bitcast.16, ...), custom_call_target="tpu_custom_call", output_to_operand_aliasing={{5}: (8, {})} | custom-call | flops 163840 | bytes 1024 | tf_op jit(solution)/shard_map/whole/pallas_call | solution.py:81
  17.0 0.5 %collective-permute-start.9 = (bf16[64,1024]{1,0:T(8,128)(2,1)S(1)}, bf16[64,1024]{1,0:T(8,128)(2,1)S(1)}, u32[]{:S(2)}, u32[]{:S(2)}) collective-permute-start(bf16[64,1024]{1,0:T(8,128)(2,1)S(1)} %get-tuple-element.48.refs_2_.refs_1_), channel_id=1, source_target_pairs={{0,4},{4,0},{8,12},{12,8},{1,5},{5,1},{9,13},{13,9},{2,6},{6,2},{1... | collective-permute-start | bytes 393224 | tf_op jit(solution)/shard_map/ppermute | solution.py:37
  17.5 0.8 %collective-permute-done.7.refs_7_ = bf16[64,1024]{1,0:T(8,128)(2,1)S(1)} collective-permute-done((bf16[64,1024]{1,0:T(8,128)(2,1)S(1)}, bf16[64,1024]{1,0:T(8,128)(2,1)S(1)}, u32[]{:S(2)}, u32[]{:S(2)}) %collective-permute-start.7) | collective-permute-done | bytes 131104 | tf_op jit(solution)/shard_map/ppermute | solution.py:37
  18.3 1.8 %whole.4 = (bf16[64,256]{1,0:T(8,128)(2,1)S(1)}, f32[128,256]{1,0:T(8,128)S(1)}, f32[64,128]{1,0:T(8,128)S(1)}, bf16[128,1024]{1,0:T(8,128)(2,1)S(1)}, bf16[64,1...) custom-call(bf16[128,4096]{1,0:T(8,128)(2,1)S(1)} %bitcast.17, bf16[64,128]{1,0:T(8,128)(2,1)S(1)} %bitcast.21, ...), custom_call_target="tpu_custom_call" | custom-call | flops 163840 | bytes 1024 | tf_op jit(solution)/shard_map/whole/pallas_call | solution.py:81
  20.2 1.6 %collective-permute-start.10 = (bf16[64,1024]{1,0:T(8,128)(2,1)S(1)}, bf16[64,1024]{1,0:T(8,128)(2,1)S(1)}, u32[]{:S(2)}, u32[]{:S(2)}) collective-permute-start(bf16[64,1024]{1,0:T(8,128)(2,1)S(1)} %get-tuple-element.71), channel_id=1, source_target_pairs={{0,8},{4,12},{8,0},{12,4},{1,9},{5,13},{9,1},{13,5},{2,10},{6,14},... | collective-permute-start | bytes 393224 | tf_op jit(solution)/shard_map/ppermute | solution.py:37
  21.7 1.2 %collective-permute-start.4 = (bf16[64,1024]{1,0:T(8,128)(2,1)S(1)}, bf16[64,1024]{1,0:T(8,128)(2,1)S(1)}, u32[]{:S(2)}, u32[]{:S(2)}) collective-permute-start(bf16[64,1024]{1,0:T(8,128)(2,1)S(1)} %get-tuple-element.54), channel_id=1, source_target_pairs={{0,16},{16,0},{1,17},{17,1},{2,18},{18,2},{3,19},{19,3},{4,20},{20... | collective-permute-start | bytes 393224 | tf_op jit(solution)/shard_map/ppermute | solution.py:32
  22.9 1.4 %whole.5 = (bf16[64,256]{1,0:T(8,128)(2,1)S(1)}, f32[128,256]{1,0:T(8,128)S(1)}, f32[64,128]{1,0:T(8,128)S(1)}, bf16[128,1024]{1,0:T(8,128)(2,1)S(1)}, bf16[64,1024]{1,0:T(8,128)(2,1)S(1)}) custom-call(bf16[128,4096]{1,0:T(8,128)(2,1)S(1)} %bitcast.18, bf16[64,128]{1,0:T(8,128)(2,1)S(1)} %bitcast.22, ...), custom_call_target="tpu_custom_call" | custom-call | flops 163840 | bytes 1024 | tf_op jit(solution)/shard_map/whole/pallas_call | solution.py:81
  24.4 1.2 %collective-permute-done.5.refs_4_ = bf16[64,1024]{1,0:T(8,128)(2,1)S(1)} collective-permute-done((bf16[64,1024]{1,0:T(8,128)(2,1)S(1)}, bf16[64,1024]{1,0:T(8,128)(2,1)S(1)}, u32[]{:S(2)}, u32[]{:S(2)}) %collective-permute-start.5) | collective-permute-done | bytes 131104 | tf_op jit(solution)/shard_map/ppermute | solution.py:32
  25.6 0.1 collective-permute-done.10.refs_14_
  25.8 1.3 %front.1 = (bf16[128,4096]{1,0:T(8,128)(2,1)}, bf16[64,1024]{1,0:T(8,128)(2,1)S(1)}, f32[128,256]{1,0:T(8,128)S(1)}, f32[64,1024]{1,0:T(8,128)S(1)}, f32[64,128]...) custom-call(bf16[64,128]{1,0:T(8,128)(2,1)S(1)} %bitcast.23, ...), custom_call_target="tpu_custom_call", output_to_operand_aliasing={{0}: (7, {})} | custom-call | flops 81920 | bytes 1024 | tf_op jit(solution)/shard_map/front/pallas_call | solution.py:81
  27.1 0.6 %collective-permute-start.12 = (bf16[64,1024]{1,0:T(8,128)(2,1)S(1)}, bf16[64,1024]{1,0:T(8,128)(2,1)S(1)}, u32[]{:S(2)}, u32[]{:S(2)}) collective-permute-start(bf16[64,1024]{1,0:T(8,128)(2,1)S(1)} %get-tuple-element.82), channel_id=1, source_target_pairs={{0,12},{4,0},{8,4},{12,8},{1,13},{5,1},{9,5},{13,9},{2,14},{6,2},{... | collective-permute-start | bytes 393224 | tf_op jit(solution)/shard_map/ppermute | solution.py:32
  27.7 0.1 collective-permute-done.4.refs_4_.refs_2_
  27.8 0.6 %back.1 = (bf16[64,1024]{1,0:T(8,128)(2,1)S(1)}, bf16[128,512]{1,0:T(8,128)(2,1)S(1)}, bf16[16,1024]{1,0:T(8,128)(2,1)S(1)}, bf16[16,1024]{1,0:T(8,128)(2,1)S(1)...) custom-call(bf16[64,128]{1,0:T(8,128)(2,1)S(1)} %bitcast.24, ...), custom_call_target="tpu_custom_call" | custom-call | flops 81920 | bytes 1024 | tf_op jit(solution)/shard_map/back/pallas_call | solution.py:81
  28.4 1.8 %collective-permute-start.13 = (bf16[16,1024]{1,0:T(8,128)(2,1)S(1)}, bf16[16,1024]{1,0:T(8,128)(2,1)S(1)}, u32[]{:S(2)}, u32[]{:S(2)}) collective-permute-start(bf16[16,1024]{1,0:T(8,128)(2,1)S(1)} %get-tuple-element.89), channel_id=1, source_target_pairs={{0,1},{1,2},{2,3},{3,0},{4,5},{5,6},{6,7},{7,4},{8,9},{9,10},{10,1... | collective-permute-start | bytes 98312 | tf_op jit(solution)/shard_map/ppermute | solution.py:32
  30.3 2.1 %collective-permute-start.14 = (bf16[16,1024]{1,0:T(8,128)(2,1)S(1)}, bf16[16,1024]{1,0:T(8,128)(2,1)S(1)}, u32[]{:S(2)}, u32[]{:S(2)}) collective-permute-start(bf16[16,1024]{1,0:T(8,128)(2,1)S(1)} %get-tuple-element.90), channel_id=1, source_target_pairs={{0,3},{1,0},{2,1},{3,2},{4,7},{5,4},{6,5},{7,6},{8,11},{9,8},{10,9... | collective-permute-start | bytes 98312 | tf_op jit(solution)/shard_map/ppermute | solution.py:32
  32.4 0.9 %collective-permute-start.15 = (bf16[16,1024]{1,0:T(8,128)(2,1)S(1)}, bf16[16,1024]{1,0:T(8,128)(2,1)S(1)}, u32[]{:S(2)}, u32[]{:S(2)}) collective-permute-start(bf16[16,1024]{1,0:T(8,128)(2,1)S(1)} %get-tuple-element.91), channel_id=1, source_target_pairs={{0,2},{1,3},{2,0},{3,1},{4,6},{5,7},{6,4},{7,5},{8,10},{9,11},{10,... | collective-permute-start | bytes 98312 | tf_op jit(solution)/shard_map/ppermute | solution.py:32
  33.3 1.6 %finish.1 = (bf16[128,4096]{1,0:T(8,128)(2,1)}, bf16[64,128]{1,0:T(8,128)(2,1)}, bf16[16,1024]{1,0:T(8,128)(2,1)S(1)}, bf16[128,1024]{1,0:T(8,128)(2,1)}) custom-call(bf16[64,128]{1,0:T(8,128)(2,1)S(1)} %bitcast.25, bf16[64,1024]{1,0:T(8,128)(2,1)S(1)} %get-tuple-element.48.refs_2_.refs_1_, ...), custom_call_target="tpu_custom_call", output_to_operand_aliasing={{0}: (7, {})} | custom-call | flops 81920 | bytes 1024 | tf_op jit(solution)/shard_map/finish/pallas_call | solution.py:81
  34.9 2.3 %collective-permute-done.15 = bf16[16,1024]{1,0:T(8,128)(2,1)S(1)} collective-permute-done((bf16[16,1024]{1,0:T(8,128)(2,1)S(1)}, bf16[16,1024]{1,0:T(8,128)(2,1)S(1)}, u32[]{:S(2)}, u32[]{:S(2)}) %collective-permute-start.15) | collective-permute-done | bytes 32800 | tf_op jit(solution)/shard_map/ppermute | solution.py:32
  37.2 0.6 %add_bitcast_fusion = f32[1,16,1024]{2,1,0:T(8,128)} fusion(bf16[16,1024]{1,0:T(8,128)(2,1)S(1)} %collective-permute-done.15, bf16[16,1024]{1,0:T(8,128)(2,1)S(1)} %collective-permute-done.14, bf16[16,1024]{1,0:T(8,128)(2,1)S(1)} %collective-permute-done.13, bf16[16,1024]{1,0:T(8,128)(2,1)S(1)} %get-tuple-element.88), kind=kLoop, calls=%fused_computation.1 | loop fusion | flops 114688 | bytes 196608 | tf_op jit(solution)/shard_map/broadcast_in_dim | solution.py:554
  (23 shorter events, 0.6 us)
Async XLA Ops:
  1.6 13.8 %collective-permute-start.1 = (bf16[128,1024]{1,0:T(8,128)(2,1)S(1)}, bf16[128,1024]{1,0:T(8,128)(2,1)S(1)}, u32[]{:S(2)}, u32[]{:S(2)}) collective-permute-start(bf16[128,1024]{1,0:T(8,128)(2,1)S(1)} %split_first.1.refs_3_), channel_id=1, source_target_pairs={{0,16},{16,0},{1,17},{17,1},{2,18},{18,2},{3,19},{19,3},{4,20},{20... | collective-permute-start | bytes 786440 | tf_op jit(solution)/shard_map/ppermute | solution.py:32
  5.9 8.4 %copy-start = (bf16[1,1,128,4096]{3,2,1,0:T(8,128)(2,1)S(1)}, bf16[1,1,128,4096]{3,2,1,0:T(8,128)(2,1)}, u32[]{:S(2)}) copy-start(bf16[1,1,128,4096]{3,2,1,0:T(8,128)(2,1)} %param.6) | copy-start | bytes 3145732
  6.5 7.8 %collective-permute-start = (bf16[64,1024]{1,0:T(8,128)(2,1)}, bf16[64,1024]{1,0:T(8,128)(2,1)S(1)}, u32[]{:S(2)}, u32[]{:S(2)}) collective-permute-start(bf16[64,1024]{1,0:T(8,128)(2,1)} %slice.15), channel_id=1, source_target_pairs={{0,4},{4,8},{8,12},{12,0},{1,5},{5,9},{9,13},{13,1},{2,6},{6,10},{... | collective-permute-start | bytes 393224 | tf_op jit(solution)/shard_map/ppermute | solution.py:32
  6.5 6.3 %collective-permute-start.2 = (bf16[64,1024]{1,0:T(8,128)(2,1)S(1)}, bf16[64,1024]{1,0:T(8,128)(2,1)S(1)}, u32[]{:S(2)}, u32[]{:S(2)}) collective-permute-start(bf16[64,1024]{1,0:T(8,128)(2,1)S(1)} %get-tuple-element.48.refs_2_.refs_1_), channel_id=1, source_target_pairs={{0,8},{4,12},{8,0},{12,4},{1,9},{5,13},{9,1},{13,5},{2,10},{6,14},... | collective-permute-start | bytes 393224 | tf_op jit(solution)/shard_map/ppermute | solution.py:37
  8.1 9.4 %collective-permute-start.6 = (bf16[128,1024]{1,0:T(8,128)(2,1)S(1)}, bf16[128,1024]{1,0:T(8,128)(2,1)S(1)}, u32[]{:S(2)}, u32[]{:S(2)}) collective-permute-start(bf16[128,1024]{1,0:T(8,128)(2,1)S(1)} %get-tuple-element.50.refs_1_), channel_id=1, source_target_pairs={{0,16},{16,0},{1,17},{17,1},{2,18},{18,2},{3,19},{19,3},{4,20},{20... | collective-permute-start | bytes 786440 | tf_op jit(solution)/shard_map/ppermute | solution.py:32
  9.7 13.2 %collective-permute-start.8 = (bf16[128,1024]{1,0:T(8,128)(2,1)S(1)}, bf16[128,1024]{1,0:T(8,128)(2,1)S(1)}, u32[]{:S(2)}, u32[]{:S(2)}) collective-permute-start(bf16[128,1024]{1,0:T(8,128)(2,1)S(1)} %get-tuple-element.63), channel_id=1, source_target_pairs={{0,16},{16,0},{1,17},{17,1},{2,18},{18,2},{3,19},{19,3},{4,20},{20... | collective-permute-start | bytes 786440 | tf_op jit(solution)/shard_map/ppermute | solution.py:32
  11.3 0.7 %copy-start.2 = (s32[1,1,512]{2,1,0:T(1,128)S(1)}, s32[1,1,512]{2,1,0:T(1,128)}, u32[]{:S(2)}) copy-start(s32[1,1,512]{2,1,0:T(1,128)} %param.11) | copy-start | bytes 6148
  12.8 2.6 %collective-permute-start.3 = (bf16[64,1024]{1,0:T(8,128)(2,1)S(1)}, bf16[64,1024]{1,0:T(8,128)(2,1)S(1)}, u32[]{:S(2)}, u32[]{:S(2)}) collective-permute-start(bf16[64,1024]{1,0:T(8,128)(2,1)S(1)} %collective-permute-done.2.refs_6_), channel_id=1, source_target_pairs={{0,4},{4,0},{8,12},{12,8},{1,5},{5,1},{9,13},{13,9},{2,6},{6,2},{1... | collective-permute-start | bytes 393224 | tf_op jit(solution)/shard_map/ppermute | solution.py:37
  14.2 0.7 %copy-start.1 = (bf16[1,1,128,64]{2,3,1,0:T(8,128)(2,1)S(1)}, bf16[1,1,128,64]{2,3,1,0:T(8,128)(2,1)}, u32[]{:S(2)}) copy-start(bf16[1,1,128,64]{2,3,1,0:T(8,128)(2,1)} %param.8) | copy-start | bytes 49156
  16.9 1.4 %collective-permute-start.7 = (bf16[64,1024]{1,0:T(8,128)(2,1)S(1)}, bf16[64,1024]{1,0:T(8,128)(2,1)S(1)}, u32[]{:S(2)}, u32[]{:S(2)}) collective-permute-start(bf16[64,1024]{1,0:T(8,128)(2,1)S(1)} %get-tuple-element.59), channel_id=1, source_target_pairs={{0,4},{4,0},{8,12},{12,8},{1,5},{5,1},{9,13},{13,9},{2,6},{6,2},{1... | collective-permute-start | bytes 393224 | tf_op jit(solution)/shard_map/ppermute | solution.py:37
  17.0 6.0 %collective-permute-start.9 = (bf16[64,1024]{1,0:T(8,128)(2,1)S(1)}, bf16[64,1024]{1,0:T(8,128)(2,1)S(1)}, u32[]{:S(2)}, u32[]{:S(2)}) collective-permute-start(bf16[64,1024]{1,0:T(8,128)(2,1)S(1)} %get-tuple-element.48.refs_2_.refs_1_), channel_id=1, source_target_pairs={{0,4},{4,0},{8,12},{12,8},{1,5},{5,1},{9,13},{13,9},{2,6},{6,2},{1... | collective-permute-start | bytes 393224 | tf_op jit(solution)/shard_map/ppermute | solution.py:37
  17.5 8.2 %collective-permute-start.5 = (bf16[64,1024]{1,0:T(8,128)(2,1)S(1)}, bf16[64,1024]{1,0:T(8,128)(2,1)S(1)}, u32[]{:S(2)}, u32[]{:S(2)}) collective-permute-start(bf16[64,1024]{1,0:T(8,128)(2,1)S(1)} %get-tuple-element.57), channel_id=1, source_target_pairs={{0,16},{16,0},{1,17},{17,1},{2,18},{18,2},{3,19},{19,3},{4,20},{20... | collective-permute-start | bytes 393224 | tf_op jit(solution)/shard_map/ppermute | solution.py:32
  20.2 5.6 %collective-permute-start.10 = (bf16[64,1024]{1,0:T(8,128)(2,1)S(1)}, bf16[64,1024]{1,0:T(8,128)(2,1)S(1)}, u32[]{:S(2)}, u32[]{:S(2)}) collective-permute-start(bf16[64,1024]{1,0:T(8,128)(2,1)S(1)} %get-tuple-element.71), channel_id=1, source_target_pairs={{0,8},{4,12},{8,0},{12,4},{1,9},{5,13},{9,1},{13,5},{2,10},{6,14},... | collective-permute-start | bytes 393224 | tf_op jit(solution)/shard_map/ppermute | solution.py:37
  21.7 6.1 %collective-permute-start.4 = (bf16[64,1024]{1,0:T(8,128)(2,1)S(1)}, bf16[64,1024]{1,0:T(8,128)(2,1)S(1)}, u32[]{:S(2)}, u32[]{:S(2)}) collective-permute-start(bf16[64,1024]{1,0:T(8,128)(2,1)S(1)} %get-tuple-element.54), channel_id=1, source_target_pairs={{0,16},{16,0},{1,17},{17,1},{2,18},{18,2},{3,19},{19,3},{4,20},{20... | collective-permute-start | bytes 393224 | tf_op jit(solution)/shard_map/ppermute | solution.py:32
  24.4 3.5 %collective-permute-start.11 = (bf16[64,1024]{1,0:T(8,128)(2,1)S(1)}, bf16[64,1024]{1,0:T(8,128)(2,1)S(1)}, u32[]{:S(2)}, u32[]{:S(2)}) collective-permute-start(bf16[64,1024]{1,0:T(8,128)(2,1)S(1)} %get-tuple-element.73), channel_id=1, source_target_pairs={{0,4},{4,0},{8,12},{12,8},{1,5},{5,1},{9,13},{13,9},{2,6},{6,2},{1... | collective-permute-start | bytes 393224 | tf_op jit(solution)/shard_map/ppermute | solution.py:37
  27.1 6.2 %collective-permute-start.12 = (bf16[64,1024]{1,0:T(8,128)(2,1)S(1)}, bf16[64,1024]{1,0:T(8,128)(2,1)S(1)}, u32[]{:S(2)}, u32[]{:S(2)}) collective-permute-start(bf16[64,1024]{1,0:T(8,128)(2,1)S(1)} %get-tuple-element.82), channel_id=1, source_target_pairs={{0,12},{4,0},{8,4},{12,8},{1,13},{5,1},{9,5},{13,9},{2,14},{6,2},{... | collective-permute-start | bytes 393224 | tf_op jit(solution)/shard_map/ppermute | solution.py:32
  28.4 6.5 %collective-permute-start.13 = (bf16[16,1024]{1,0:T(8,128)(2,1)S(1)}, bf16[16,1024]{1,0:T(8,128)(2,1)S(1)}, u32[]{:S(2)}, u32[]{:S(2)}) collective-permute-start(bf16[16,1024]{1,0:T(8,128)(2,1)S(1)} %get-tuple-element.89), channel_id=1, source_target_pairs={{0,1},{1,2},{2,3},{3,0},{4,5},{5,6},{6,7},{7,4},{8,9},{9,10},{10,1... | collective-permute-start | bytes 98312 | tf_op jit(solution)/shard_map/ppermute | solution.py:32
  30.3 4.6 %collective-permute-start.14 = (bf16[16,1024]{1,0:T(8,128)(2,1)S(1)}, bf16[16,1024]{1,0:T(8,128)(2,1)S(1)}, u32[]{:S(2)}, u32[]{:S(2)}) collective-permute-start(bf16[16,1024]{1,0:T(8,128)(2,1)S(1)} %get-tuple-element.90), channel_id=1, source_target_pairs={{0,3},{1,0},{2,1},{3,2},{4,7},{5,4},{6,5},{7,6},{8,11},{9,8},{10,9... | collective-permute-start | bytes 98312 | tf_op jit(solution)/shard_map/ppermute | solution.py:32
  32.4 4.8 %collective-permute-start.15 = (bf16[16,1024]{1,0:T(8,128)(2,1)S(1)}, bf16[16,1024]{1,0:T(8,128)(2,1)S(1)}, u32[]{:S(2)}, u32[]{:S(2)}) collective-permute-start(bf16[16,1024]{1,0:T(8,128)(2,1)S(1)} %get-tuple-element.91), channel_id=1, source_target_pairs={{0,2},{1,3},{2,0},{3,1},{4,6},{5,7},{6,4},{7,5},{8,10},{9,11},{10,... | collective-permute-start | bytes 98312 | tf_op jit(solution)/shard_map/ppermute | solution.py:32

commit v6 on v2

--- a/solution.py
+++ b/solution.py
@@ -19,7 +19,7 @@
 COPIES = 4
 LIMIT = 16 * 1024 * 1024
 IN = "_in"
-IN_HBM = ("upstream", "pairs", "matrix", "dq", "dq" + IN)
+IN_HBM = ("upstream", "pairs", "matrix", "dq", "dq" + IN, "weight_grad")
 ANYWHERE = ("held", "held" + IN, "after")
 VMEM = pl.BlockSpec(memory_space=pltpu.VMEM)
 HBM = pl.BlockSpec(memory_space=pltpu.HBM)
@@ -283,8 +283,10 @@
     cot_stack = stacked(refs.cot, slice(0, z.block))
     dscores, grad_stack = score_grads(z, 1, refs.probs[...], keys, values, cot_stack)
     refs.dscores[...] = dscores
-    unstack(z, grad_stack, refs.grad, 0)
-    weight = refs.weight_part[...] + dot(refs.at[...], padded(z, refs.grad[...], 1), 1, 0)
+    parts = [grad_stack[start : start + z.block] for start in range(0, len(grad_stack), z.block)]
+    grad = jnp.concatenate(parts, axis=1)
+    refs.grad[...] = grad
+    weight = refs.weight_part[...] + dot(refs.at[...], padded(z, grad, 1), 1, 0)
     for term in listed(refs, "term"):
         weight += term[...].astype(jnp.float32)
     refs.total[...] = weight.astype(jnp.bfloat16)
@@ -293,6 +295,17 @@
     for away, share in enumerate(shares):
         target = lax.rem(lax.axis_index("dp") + away, len(shares))
         share[...] = refs.total[pl.ds(pl.multiple_of(target * rows, rows), rows)]
+
+
+def add_shares(z, refs):
+    total = refs.share0[...].astype(jnp.float32)
+    for share in listed(refs, "share")[1:]:
+        total += share[...].astype(jnp.float32)
+    refs.total[...] = total
+    copies = []
+    copy_rows(refs.total, refs.weight_grad, refs.sems, copies)
+    for copy in copies:
+        copy.wait()
 
 
 def finish(z, refs):
@@ -533,9 +546,15 @@
         sems(BLOCKS),
         flops,
     )
-    weight_share = final.share_out.astype(f32)
-    for share in shares[1:]:
-        weight_share += share.astype(f32)
+    shares[0] = final.share_out
+    share_shape = ((rank // packs, width), f32)
+    weight_share = run(
+        add_shares,
+        z,
+        numbered("share", shares),
+        dict(weight_grad=share_shape),
+        dict(total=pltpu.VMEM(*share_shape)) | sems(1),
+    ).weight_grad
     if merged:
         pair_grads = final.pair_grads
     else:

time: 37.8 us -> 37.8 us (level)
  other arithmetic: 0.92 us -> 0.27 us
  Pallas kernels: 12 us -> 12.6 us
    broadcast_in_dim x1 -> x0, other arithmetic: 0.65 us -> none  [per_device(): weight_share[None]]
    pallas_call x10 -> x11, Pallas kernels: 12 us -> 12.6 us  [run(): pl.pallas_call(kernel, in_specs=[spec_of(name) for name in inputs], out_s...]
where the time goes in v6:
time: 37.8 us; the launch traced here: 37.4 us
  starting transfers between devices  17.7 us (47%)
  Pallas kernels  12.6 us (33%)
  waiting for transfers between devices  3.93 us (10%)
  local copies, waits for them, and re-layouts  2.09 us (6%)
  between operations  0.82 us (2%)
    ppermute x10, starting transfers between devices, passed_along(): return lax.ppermute(value, axis, pairs)  12.7 us
    pallas_call x11, Pallas kernels, run(): pl.pallas_call(kernel, in_specs=[spec_of(name) for name in inputs], out_s...  12.6 us
    ppermute x6, starting transfers between devices, swapped(): return lax.ppermute(value, axis, pairs)  4.98 us
    ppermute x10, waiting for transfers between devices, passed_along(): return lax.ppermute(value, axis, pairs)  2.31 us
    ppermute x6, waiting for transfers between devices, swapped(): return lax.ppermute(value, axis, pairs)  1.62 us
    unnamed x6, local copies, waits for them, and re-layouts  1.27 us
  transfers between devices with their start and end apart: 16, of which 6 were waited for; matrix products, arithmetic and copies ran while one was open for 3% of the time, Pallas kernels for 29%

profile of v6, /device:TPU:0, one launch (start us, length us, event | category | flops | bytes accessed | tf_op | source)
XLA Modules:
  0.0 37.4 jit_solution(2808340907443851821)
XLA Ops:
  0.6 1.0 %split_first.1.refs_3_ = bf16[128,1024]{1,0:T(8,128)(2,1)S(1)} custom-call(bf16[128,4096]{1,0:T(8,128)(2,1)} %bitcast.25), custom_call_target="tpu_custom_call" | custom-call | bytes 1024 | tf_op jit(solution)/shard_map/split_first/pallas_call | solution.py:81
  1.6 3.0 %collective-permute-start.1 = (bf16[128,1024]{1,0:T(8,128)(2,1)S(1)}, bf16[128,1024]{1,0:T(8,128)(2,1)S(1)}, u32[]{:S(2)}, u32[]{:S(2)}) collective-permute-start(bf16[128,1024]{1,0:T(8,128)(2,1)S(1)} %split_first.1.refs_3_), channel_id=1, source_target_pairs={{0,16},{16,0},{1,17},{17,1},{2,18},{18,2},{3,19},{19,3},{4,20},{20... | collective-permute-start | bytes 786440 | tf_op jit(solution)/shard_map/ppermute | solution.py:32
  4.6 1.2 %split_second.1 = (bf16[128,1024]{1,0:T(8,128)(2,1)S(1)}, bf16[64,1024]{1,0:T(8,128)(2,1)S(1)}, bf16[128,1024]{1,0:T(8,128)(2,1)S(1)}) custom-call(bf16[128,4096]{1,0:T(8,128)(2,1)} %bitcast.26, bf16[128,1024]{1,0:T(8,128)(2,1)} %bitcast.29, bf16[64,1024]{1,0:T(8,128)(2,1)} %bitcast.30, bf16[128,1024]{1,0:T(8,128)(2,1)S(1)} %split_first.1.refs_3_), custom_call_target="tpu_custom_call" | custom-call | bytes 1024 | tf_op jit(solution)/shard_map/split_second/pallas_call | solution.py:81
  5.9 0.7 %slice.15 = bf16[64,1024]{1,0:T(8,128)(2,1)} slice(bf16[128,1024]{1,0:T(8,128)(2,1)S(1)} %get-tuple-element.49.refs_4_.refs_3_), slice={[64:128], [0:1024]} | slice | bytes 262144 | tf_op jit(solution)/shard_map/slice | solution.py:398
  6.5 1.6 %collective-permute-start.2 = (bf16[64,1024]{1,0:T(8,128)(2,1)S(1)}, bf16[64,1024]{1,0:T(8,128)(2,1)S(1)}, u32[]{:S(2)}, u32[]{:S(2)}) collective-permute-start(bf16[64,1024]{1,0:T(8,128)(2,1)S(1)} %get-tuple-element.48.refs_2_.refs_1_), channel_id=1, source_target_pairs={{0,8},{4,12},{8,0},{12,4},{1,9},{5,13},{9,1},{13,5},{2,10},{6,14},... | collective-permute-start | bytes 393224 | tf_op jit(solution)/shard_map/ppermute | solution.py:37
  8.1 0.5 %collective-permute-start.6 = (bf16[128,1024]{1,0:T(8,128)(2,1)S(1)}, bf16[128,1024]{1,0:T(8,128)(2,1)S(1)}, u32[]{:S(2)}, u32[]{:S(2)}) collective-permute-start(bf16[128,1024]{1,0:T(8,128)(2,1)S(1)} %get-tuple-element.50.refs_1_), channel_id=1, source_target_pairs={{0,16},{16,0},{1,17},{17,1},{2,18},{18,2},{3,19},{19,3},{4,20},{20... | collective-permute-start | bytes 786440 | tf_op jit(solution)/shard_map/ppermute | solution.py:32
  8.6 1.1 %split_rest.1 = (bf16[128,1024]{1,0:T(8,128)(2,1)S(1)}, bf16[64,1024]{1,0:T(8,128)(2,1)S(1)}, bf16[64,1024]{1,0:T(8,128)(2,1)S(1)}) custom-call(bf16[128,4096]{1,0:T(8,128)(2,1)} %bitcast.27, bf16[128,1024]{1,0:T(8,128)(2,1)S(1)} %get-tuple-element.50.refs_1_), custom_call_target="tpu_custom_call" | custom-call | bytes 1024 | tf_op jit(solution)/shard_map/split_rest/pallas_call | solution.py:81
  9.7 1.6 %collective-permute-start.8 = (bf16[128,1024]{1,0:T(8,128)(2,1)S(1)}, bf16[128,1024]{1,0:T(8,128)(2,1)S(1)}, u32[]{:S(2)}, u32[]{:S(2)}) collective-permute-start(bf16[128,1024]{1,0:T(8,128)(2,1)S(1)} %get-tuple-element.63), channel_id=1, source_target_pairs={{0,16},{16,0},{1,17},{17,1},{2,18},{18,2},{3,19},{19,3},{4,20},{20... | collective-permute-start | bytes 786440 | tf_op jit(solution)/shard_map/ppermute | solution.py:32
  11.3 0.7 %copy-done.2 = s32[1,1,512]{2,1,0:T(1,128)S(1)} copy-done((s32[1,1,512]{2,1,0:T(1,128)S(1)}, s32[1,1,512]{2,1,0:T(1,128)}, u32[]{:S(2)}) %copy-start.2) | copy-done | bytes 2072
  12.2 0.7 %collective-permute-done.2.refs_6_ = bf16[64,1024]{1,0:T(8,128)(2,1)S(1)} collective-permute-done((bf16[64,1024]{1,0:T(8,128)(2,1)S(1)}, bf16[64,1024]{1,0:T(8,128)(2,1)S(1)}, u32[]{:S(2)}, u32[]{:S(2)}) %collective-permute-start.2) | collective-permute-done | bytes 131104 | tf_op jit(solution)/shard_map/ppermute | solution.py:37
  12.8 1.2 %collective-permute-start.3 = (bf16[64,1024]{1,0:T(8,128)(2,1)S(1)}, bf16[64,1024]{1,0:T(8,128)(2,1)S(1)}, u32[]{:S(2)}, u32[]{:S(2)}) collective-permute-start(bf16[64,1024]{1,0:T(8,128)(2,1)S(1)} %collective-permute-done.2.refs_6_), channel_id=1, source_target_pairs={{0,4},{4,0},{8,12},{12,8},{1,5},{5,1},{9,13},{13,9},{2,6},{6,2},{1... | collective-permute-start | bytes 393224 | tf_op jit(solution)/shard_map/ppermute | solution.py:37
  14.3 0.6 %copy-done.1 = bf16[1,1,128,64]{2,3,1,0:T(8,128)(2,1)S(1)} copy-done((bf16[1,1,128,64]{2,3,1,0:T(8,128)(2,1)S(1)}, bf16[1,1,128,64]{2,3,1,0:T(8,128)(2,1)}, u32[]{:S(2)}) %copy-start.1) | copy-done | bytes 16408
  14.9 0.6 %forward.1 = (bf16[512,128]{1,0:T(8,128)(2,1)S(1)}, bf16[512,128]{1,0:T(8,128)(2,1)S(1)}, f32[128,512]{1,0:T(8,128)S(1)}, f32[128,512]{1,0:T(8,128)S(1)}, bf16[64,1024]{1,0:T(8,128)(2,1)S(1)}) custom-call(bf16[128,4096]{1,0:T(8,128)(2,1)S(1)} %bitcast.14, bf16[64,128]{1,0:T(8,128)(2,1)S(1)} %bitcast.18, ...), custom_call_target="tpu_custom_call", output_to_operand_aliasing={{4}: (6, {})} | custom-call | flops 81920 | bytes 1024 | tf_op jit(solution)/shard_map/forward/pallas_call | solution.py:81
  15.5 1.4 %whole.3 = (bf16[64,256]{1,0:T(8,128)(2,1)S(1)}, f32[128,256]{1,0:T(8,128)S(1)}, f32[64,128]{1,0:T(8,128)S(1)}, bf16[128,1024]{1,0:T(8,128)(2,1)S(1)}, bf16[64,1...) custom-call(bf16[128,4096]{1,0:T(8,128)(2,1)S(1)} %bitcast.15, ...), custom_call_target="tpu_custom_call", output_to_operand_aliasing={{5}: (8, {})} | custom-call | flops 163840 | bytes 1024 | tf_op jit(solution)/shard_map/whole/pallas_call | solution.py:81
  17.0 0.5 %collective-permute-start.9 = (bf16[64,1024]{1,0:T(8,128)(2,1)S(1)}, bf16[64,1024]{1,0:T(8,128)(2,1)S(1)}, u32[]{:S(2)}, u32[]{:S(2)}) collective-permute-start(bf16[64,1024]{1,0:T(8,128)(2,1)S(1)} %get-tuple-element.48.refs_2_.refs_1_), channel_id=1, source_target_pairs={{0,4},{4,0},{8,12},{12,8},{1,5},{5,1},{9,13},{13,9},{2,6},{6,2},{1... | collective-permute-start | bytes 393224 | tf_op jit(solution)/shard_map/ppermute | solution.py:37
  17.5 0.8 %collective-permute-done.7.refs_7_ = bf16[64,1024]{1,0:T(8,128)(2,1)S(1)} collective-permute-done((bf16[64,1024]{1,0:T(8,128)(2,1)S(1)}, bf16[64,1024]{1,0:T(8,128)(2,1)S(1)}, u32[]{:S(2)}, u32[]{:S(2)}) %collective-permute-start.7) | collective-permute-done | bytes 131104 | tf_op jit(solution)/shard_map/ppermute | solution.py:37
  18.3 1.8 %whole.4 = (bf16[64,256]{1,0:T(8,128)(2,1)S(1)}, f32[128,256]{1,0:T(8,128)S(1)}, f32[64,128]{1,0:T(8,128)S(1)}, bf16[128,1024]{1,0:T(8,128)(2,1)S(1)}, bf16[64,1...) custom-call(bf16[128,4096]{1,0:T(8,128)(2,1)S(1)} %bitcast.16, bf16[64,128]{1,0:T(8,128)(2,1)S(1)} %bitcast.20, ...), custom_call_target="tpu_custom_call" | custom-call | flops 163840 | bytes 1024 | tf_op jit(solution)/shard_map/whole/pallas_call | solution.py:81
  20.2 1.6 %collective-permute-start.10 = (bf16[64,1024]{1,0:T(8,128)(2,1)S(1)}, bf16[64,1024]{1,0:T(8,128)(2,1)S(1)}, u32[]{:S(2)}, u32[]{:S(2)}) collective-permute-start(bf16[64,1024]{1,0:T(8,128)(2,1)S(1)} %get-tuple-element.71), channel_id=1, source_target_pairs={{0,8},{4,12},{8,0},{12,4},{1,9},{5,13},{9,1},{13,5},{2,10},{6,14},... | collective-permute-start | bytes 393224 | tf_op jit(solution)/shard_map/ppermute | solution.py:37
  21.7 1.2 %collective-permute-start.4 = (bf16[64,1024]{1,0:T(8,128)(2,1)S(1)}, bf16[64,1024]{1,0:T(8,128)(2,1)S(1)}, u32[]{:S(2)}, u32[]{:S(2)}) collective-permute-start(bf16[64,1024]{1,0:T(8,128)(2,1)S(1)} %get-tuple-element.54), channel_id=1, source_target_pairs={{0,16},{16,0},{1,17},{17,1},{2,18},{18,2},{3,19},{19,3},{4,20},{20... | collective-permute-start | bytes 393224 | tf_op jit(solution)/shard_map/ppermute | solution.py:32
  22.9 1.4 %whole.5 = (bf16[64,256]{1,0:T(8,128)(2,1)S(1)}, f32[128,256]{1,0:T(8,128)S(1)}, f32[64,128]{1,0:T(8,128)S(1)}, bf16[128,1024]{1,0:T(8,128)(2,1)S(1)}, bf16[64,1024]{1,0:T(8,128)(2,1)S(1)}) custom-call(bf16[128,4096]{1,0:T(8,128)(2,1)S(1)} %bitcast.17, bf16[64,128]{1,0:T(8,128)(2,1)S(1)} %bitcast.21, ...), custom_call_target="tpu_custom_call" | custom-call | flops 163840 | bytes 1024 | tf_op jit(solution)/shard_map/whole/pallas_call | solution.py:81
  24.4 1.2 %collective-permute-done.5.refs_4_ = bf16[64,1024]{1,0:T(8,128)(2,1)S(1)} collective-permute-done((bf16[64,1024]{1,0:T(8,128)(2,1)S(1)}, bf16[64,1024]{1,0:T(8,128)(2,1)S(1)}, u32[]{:S(2)}, u32[]{:S(2)}) %collective-permute-start.5) | collective-permute-done | bytes 131104 | tf_op jit(solution)/shard_map/ppermute | solution.py:32
  25.6 0.1 collective-permute-done.10.refs_14_
  25.8 1.3 %front.1 = (bf16[128,4096]{1,0:T(8,128)(2,1)}, bf16[64,1024]{1,0:T(8,128)(2,1)S(1)}, f32[128,256]{1,0:T(8,128)S(1)}, f32[64,1024]{1,0:T(8,128)S(1)}, f32[64,128]...) custom-call(bf16[64,128]{1,0:T(8,128)(2,1)S(1)} %bitcast.22, ...), custom_call_target="tpu_custom_call", output_to_operand_aliasing={{0}: (7, {})} | custom-call | flops 81920 | bytes 1024 | tf_op jit(solution)/shard_map/front/pallas_call | solution.py:81
  27.1 0.6 %collective-permute-start.12 = (bf16[64,1024]{1,0:T(8,128)(2,1)S(1)}, bf16[64,1024]{1,0:T(8,128)(2,1)S(1)}, u32[]{:S(2)}, u32[]{:S(2)}) collective-permute-start(bf16[64,1024]{1,0:T(8,128)(2,1)S(1)} %get-tuple-element.82), channel_id=1, source_target_pairs={{0,12},{4,0},{8,4},{12,8},{1,13},{5,1},{9,5},{13,9},{2,14},{6,2},{... | collective-permute-start | bytes 393224 | tf_op jit(solution)/shard_map/ppermute | solution.py:32
  27.7 0.1 collective-permute-done.4.refs_4_.refs_2_
  27.8 0.6 %back.1 = (bf16[64,1024]{1,0:T(8,128)(2,1)S(1)}, bf16[128,512]{1,0:T(8,128)(2,1)S(1)}, bf16[16,1024]{1,0:T(8,128)(2,1)S(1)}, bf16[16,1024]{1,0:T(8,128)(2,1)S(1)...) custom-call(bf16[64,128]{1,0:T(8,128)(2,1)S(1)} %bitcast.23, ...), custom_call_target="tpu_custom_call" | custom-call | flops 81920 | bytes 1024 | tf_op jit(solution)/shard_map/back/pallas_call | solution.py:81
  28.4 1.8 %collective-permute-start.13 = (bf16[16,1024]{1,0:T(8,128)(2,1)S(1)}, bf16[16,1024]{1,0:T(8,128)(2,1)S(1)}, u32[]{:S(2)}, u32[]{:S(2)}) collective-permute-start(bf16[16,1024]{1,0:T(8,128)(2,1)S(1)} %get-tuple-element.89), channel_id=1, source_target_pairs={{0,1},{1,2},{2,3},{3,0},{4,5},{5,6},{6,7},{7,4},{8,9},{9,10},{10,1... | collective-permute-start | bytes 98312 | tf_op jit(solution)/shard_map/ppermute | solution.py:32
  30.3 2.6 %collective-permute-start.14 = (bf16[16,1024]{1,0:T(8,128)(2,1)S(1)}, bf16[16,1024]{1,0:T(8,128)(2,1)S(1)}, u32[]{:S(2)}, u32[]{:S(2)}) collective-permute-start(bf16[16,1024]{1,0:T(8,128)(2,1)S(1)} %get-tuple-element.90), channel_id=1, source_target_pairs={{0,2},{1,3},{2,0},{3,1},{4,6},{5,7},{6,4},{7,5},{8,10},{9,11},{10,... | collective-permute-start | bytes 98312 | tf_op jit(solution)/shard_map/ppermute | solution.py:32
  32.8 1.3 %collective-permute-start.15 = (bf16[16,1024]{1,0:T(8,128)(2,1)S(1)}, bf16[16,1024]{1,0:T(8,128)(2,1)S(1)}, u32[]{:S(2)}, u32[]{:S(2)}) collective-permute-start(bf16[16,1024]{1,0:T(8,128)(2,1)S(1)} %get-tuple-element.91), channel_id=1, source_target_pairs={{0,3},{1,0},{2,1},{3,2},{4,7},{5,4},{6,5},{7,6},{8,11},{9,8},{10,9... | collective-permute-start | bytes 98312 | tf_op jit(solution)/shard_map/ppermute | solution.py:32
  34.2 1.6 %finish.1 = (bf16[128,4096]{1,0:T(8,128)(2,1)}, bf16[64,128]{1,0:T(8,128)(2,1)}, bf16[16,1024]{1,0:T(8,128)(2,1)S(1)}, bf16[128,1024]{1,0:T(8,128)(2,1)}) custom-call(bf16[64,128]{1,0:T(8,128)(2,1)S(1)} %bitcast.24, bf16[64,1024]{1,0:T(8,128)(2,1)S(1)} %get-tuple-element.48.refs_2_.refs_1_, ...), custom_call_target="tpu_custom_call", output_to_operand_aliasing={{0}: (7, {})} | custom-call | flops 81920 | bytes 1024 | tf_op jit(solution)/shard_map/finish/pallas_call | solution.py:81
  35.8 1.0 %collective-permute-done.15.refs_3_ = bf16[16,1024]{1,0:T(8,128)(2,1)S(1)} collective-permute-done((bf16[16,1024]{1,0:T(8,128)(2,1)S(1)}, bf16[16,1024]{1,0:T(8,128)(2,1)S(1)}, u32[]{:S(2)}, u32[]{:S(2)}) %collective-permute-start.15) | collective-permute-done | bytes 32800 | tf_op jit(solution)/shard_map/ppermute | solution.py:32
  36.8 0.7 %add_shares.1 = f32[16,1024]{1,0:T(8,128)} custom-call(bf16[16,1024]{1,0:T(8,128)(2,1)S(1)} %get-tuple-element.88.refs_0_, bf16[16,1024]{1,0:T(8,128)(2,1)S(1)} %collective-permute-done.13.refs_1_, bf16[16,1024]{1,0:T(8,128)(2,1)S(1)} %collective-permute-done.14.refs_2_, bf16[16,1024]{1,0:T(8,128)(2,1)S(1)} %collective-permute-done.15.refs_3_), custom_call_target="tpu_custom_call" | custom-call | bytes 1024 | tf_op jit(solution)/shard_map/add_shares/pallas_call | solution.py:81
  (23 shorter events, 0.6 us)
Async XLA Ops:
  1.6 13.8 %collective-permute-start.1 = (bf16[128,1024]{1,0:T(8,128)(2,1)S(1)}, bf16[128,1024]{1,0:T(8,128)(2,1)S(1)}, u32[]{:S(2)}, u32[]{:S(2)}) collective-permute-start(bf16[128,1024]{1,0:T(8,128)(2,1)S(1)} %split_first.1.refs_3_), channel_id=1, source_target_pairs={{0,16},{16,0},{1,17},{17,1},{2,18},{18,2},{3,19},{19,3},{4,20},{20... | collective-permute-start | bytes 786440 | tf_op jit(solution)/shard_map/ppermute | solution.py:32
  5.9 8.4 %copy-start = (bf16[1,1,128,4096]{3,2,1,0:T(8,128)(2,1)S(1)}, bf16[1,1,128,4096]{3,2,1,0:T(8,128)(2,1)}, u32[]{:S(2)}) copy-start(bf16[1,1,128,4096]{3,2,1,0:T(8,128)(2,1)} %param.6) | copy-start | bytes 3145732
  6.5 7.8 %collective-permute-start = (bf16[64,1024]{1,0:T(8,128)(2,1)}, bf16[64,1024]{1,0:T(8,128)(2,1)S(1)}, u32[]{:S(2)}, u32[]{:S(2)}) collective-permute-start(bf16[64,1024]{1,0:T(8,128)(2,1)} %slice.15), channel_id=1, source_target_pairs={{0,4},{4,8},{8,12},{12,0},{1,5},{5,9},{9,13},{13,1},{2,6},{6,10},{... | collective-permute-start | bytes 393224 | tf_op jit(solution)/shard_map/ppermute | solution.py:32
  6.5 6.3 %collective-permute-start.2 = (bf16[64,1024]{1,0:T(8,128)(2,1)S(1)}, bf16[64,1024]{1,0:T(8,128)(2,1)S(1)}, u32[]{:S(2)}, u32[]{:S(2)}) collective-permute-start(bf16[64,1024]{1,0:T(8,128)(2,1)S(1)} %get-tuple-element.48.refs_2_.refs_1_), channel_id=1, source_target_pairs={{0,8},{4,12},{8,0},{12,4},{1,9},{5,13},{9,1},{13,5},{2,10},{6,14},... | collective-permute-start | bytes 393224 | tf_op jit(solution)/shard_map/ppermute | solution.py:37
  8.1 9.4 %collective-permute-start.6 = (bf16[128,1024]{1,0:T(8,128)(2,1)S(1)}, bf16[128,1024]{1,0:T(8,128)(2,1)S(1)}, u32[]{:S(2)}, u32[]{:S(2)}) collective-permute-start(bf16[128,1024]{1,0:T(8,128)(2,1)S(1)} %get-tuple-element.50.refs_1_), channel_id=1, source_target_pairs={{0,16},{16,0},{1,17},{17,1},{2,18},{18,2},{3,19},{19,3},{4,20},{20... | collective-permute-start | bytes 786440 | tf_op jit(solution)/shard_map/ppermute | solution.py:32
  9.7 13.2 %collective-permute-start.8 = (bf16[128,1024]{1,0:T(8,128)(2,1)S(1)}, bf16[128,1024]{1,0:T(8,128)(2,1)S(1)}, u32[]{:S(2)}, u32[]{:S(2)}) collective-permute-start(bf16[128,1024]{1,0:T(8,128)(2,1)S(1)} %get-tuple-element.63), channel_id=1, source_target_pairs={{0,16},{16,0},{1,17},{17,1},{2,18},{18,2},{3,19},{19,3},{4,20},{20... | collective-permute-start | bytes 786440 | tf_op jit(solution)/shard_map/ppermute | solution.py:32
  11.3 0.7 %copy-start.2 = (s32[1,1,512]{2,1,0:T(1,128)S(1)}, s32[1,1,512]{2,1,0:T(1,128)}, u32[]{:S(2)}) copy-start(s32[1,1,512]{2,1,0:T(1,128)} %param.11) | copy-start | bytes 6148
  12.8 2.6 %collective-permute-start.3 = (bf16[64,1024]{1,0:T(8,128)(2,1)S(1)}, bf16[64,1024]{1,0:T(8,128)(2,1)S(1)}, u32[]{:S(2)}, u32[]{:S(2)}) collective-permute-start(bf16[64,1024]{1,0:T(8,128)(2,1)S(1)} %collective-permute-done.2.refs_6_), channel_id=1, source_target_pairs={{0,4},{4,0},{8,12},{12,8},{1,5},{5,1},{9,13},{13,9},{2,6},{6,2},{1... | collective-permute-start | bytes 393224 | tf_op jit(solution)/shard_map/ppermute | solution.py:37
  14.2 0.7 %copy-start.1 = (bf16[1,1,128,64]{2,3,1,0:T(8,128)(2,1)S(1)}, bf16[1,1,128,64]{2,3,1,0:T(8,128)(2,1)}, u32[]{:S(2)}) copy-start(bf16[1,1,128,64]{2,3,1,0:T(8,128)(2,1)} %param.8) | copy-start | bytes 49156
  16.9 1.4 %collective-permute-start.7 = (bf16[64,1024]{1,0:T(8,128)(2,1)S(1)}, bf16[64,1024]{1,0:T(8,128)(2,1)S(1)}, u32[]{:S(2)}, u32[]{:S(2)}) collective-permute-start(bf16[64,1024]{1,0:T(8,128)(2,1)S(1)} %get-tuple-element.59), channel_id=1, source_target_pairs={{0,4},{4,0},{8,12},{12,8},{1,5},{5,1},{9,13},{13,9},{2,6},{6,2},{1... | collective-permute-start | bytes 393224 | tf_op jit(solution)/shard_map/ppermute | solution.py:37
  17.0 6.0 %collective-permute-start.9 = (bf16[64,1024]{1,0:T(8,128)(2,1)S(1)}, bf16[64,1024]{1,0:T(8,128)(2,1)S(1)}, u32[]{:S(2)}, u32[]{:S(2)}) collective-permute-start(bf16[64,1024]{1,0:T(8,128)(2,1)S(1)} %get-tuple-element.48.refs_2_.refs_1_), channel_id=1, source_target_pairs={{0,4},{4,0},{8,12},{12,8},{1,5},{5,1},{9,13},{13,9},{2,6},{6,2},{1... | collective-permute-start | bytes 393224 | tf_op jit(solution)/shard_map/ppermute | solution.py:37
  17.5 8.2 %collective-permute-start.5 = (bf16[64,1024]{1,0:T(8,128)(2,1)S(1)}, bf16[64,1024]{1,0:T(8,128)(2,1)S(1)}, u32[]{:S(2)}, u32[]{:S(2)}) collective-permute-start(bf16[64,1024]{1,0:T(8,128)(2,1)S(1)} %get-tuple-element.57), channel_id=1, source_target_pairs={{0,16},{16,0},{1,17},{17,1},{2,18},{18,2},{3,19},{19,3},{4,20},{20... | collective-permute-start | bytes 393224 | tf_op jit(solution)/shard_map/ppermute | solution.py:32
  20.2 5.6 %collective-permute-start.10 = (bf16[64,1024]{1,0:T(8,128)(2,1)S(1)}, bf16[64,1024]{1,0:T(8,128)(2,1)S(1)}, u32[]{:S(2)}, u32[]{:S(2)}) collective-permute-start(bf16[64,1024]{1,0:T(8,128)(2,1)S(1)} %get-tuple-element.71), channel_id=1, source_target_pairs={{0,8},{4,12},{8,0},{12,4},{1,9},{5,13},{9,1},{13,5},{2,10},{6,14},... | collective-permute-start | bytes 393224 | tf_op jit(solution)/shard_map/ppermute | solution.py:37
  21.7 6.1 %collective-permute-start.4 = (bf16[64,1024]{1,0:T(8,128)(2,1)S(1)}, bf16[64,1024]{1,0:T(8,128)(2,1)S(1)}, u32[]{:S(2)}, u32[]{:S(2)}) collective-permute-start(bf16[64,1024]{1,0:T(8,128)(2,1)S(1)} %get-tuple-element.54), channel_id=1, source_target_pairs={{0,16},{16,0},{1,17},{17,1},{2,18},{18,2},{3,19},{19,3},{4,20},{20... | collective-permute-start | bytes 393224 | tf_op jit(solution)/shard_map/ppermute | solution.py:32
  24.4 3.5 %collective-permute-start.11 = (bf16[64,1024]{1,0:T(8,128)(2,1)S(1)}, bf16[64,1024]{1,0:T(8,128)(2,1)S(1)}, u32[]{:S(2)}, u32[]{:S(2)}) collective-permute-start(bf16[64,1024]{1,0:T(8,128)(2,1)S(1)} %get-tuple-element.73), channel_id=1, source_target_pairs={{0,4},{4,0},{8,12},{12,8},{1,5},{5,1},{9,13},{13,9},{2,6},{6,2},{1... | collective-permute-start | bytes 393224 | tf_op jit(solution)/shard_map/ppermute | solution.py:37
  27.1 7.1 %collective-permute-start.12 = (bf16[64,1024]{1,0:T(8,128)(2,1)S(1)}, bf16[64,1024]{1,0:T(8,128)(2,1)S(1)}, u32[]{:S(2)}, u32[]{:S(2)}) collective-permute-start(bf16[64,1024]{1,0:T(8,128)(2,1)S(1)} %get-tuple-element.82), channel_id=1, source_target_pairs={{0,12},{4,0},{8,4},{12,8},{1,13},{5,1},{9,5},{13,9},{2,14},{6,2},{... | collective-permute-start | bytes 393224 | tf_op jit(solution)/shard_map/ppermute | solution.py:32
  28.4 7.3 %collective-permute-start.13 = (bf16[16,1024]{1,0:T(8,128)(2,1)S(1)}, bf16[16,1024]{1,0:T(8,128)(2,1)S(1)}, u32[]{:S(2)}, u32[]{:S(2)}) collective-permute-start(bf16[16,1024]{1,0:T(8,128)(2,1)S(1)} %get-tuple-element.89), channel_id=1, source_target_pairs={{0,1},{1,2},{2,3},{3,0},{4,5},{5,6},{6,7},{7,4},{8,9},{9,10},{10,1... | collective-permute-start | bytes 98312 | tf_op jit(solution)/shard_map/ppermute | solution.py:32
  30.3 5.5 %collective-permute-start.14 = (bf16[16,1024]{1,0:T(8,128)(2,1)S(1)}, bf16[16,1024]{1,0:T(8,128)(2,1)S(1)}, u32[]{:S(2)}, u32[]{:S(2)}) collective-permute-start(bf16[16,1024]{1,0:T(8,128)(2,1)S(1)} %get-tuple-element.90), channel_id=1, source_target_pairs={{0,2},{1,3},{2,0},{3,1},{4,6},{5,7},{6,4},{7,5},{8,10},{9,11},{10,... | collective-permute-start | bytes 98312 | tf_op jit(solution)/shard_map/ppermute | solution.py:32
  32.8 3.9 %collective-permute-start.15 = (bf16[16,1024]{1,0:T(8,128)(2,1)S(1)}, bf16[16,1024]{1,0:T(8,128)(2,1)S(1)}, u32[]{:S(2)}, u32[]{:S(2)}) collective-permute-start(bf16[16,1024]{1,0:T(8,128)(2,1)S(1)} %get-tuple-element.91), channel_id=1, source_target_pairs={{0,3},{1,0},{2,1},{3,2},{4,7},{5,4},{6,5},{7,6},{8,11},{9,8},{10,9... | collective-permute-start | bytes 98312 | tf_op jit(solution)/shard_map/ppermute | solution.py:32

commit v7 on v2

--- a/solution.py
+++ b/solution.py
@@ -534,7 +534,7 @@
         flops,
     )
     weight_share = final.share_out.astype(f32)
-    for share in shares[1:]:
+    for share in shares[2:0:-1] + shares[3:]:
         weight_share += share.astype(f32)
     if merged:
         pair_grads = final.pair_grads

time: 37.8 us -> 38.1 us (level)
  starting transfers between devices: 17.7 us -> 18.6 us
  waiting for transfers between devices: 3.93 us -> 3.38 us
    ppermute x10, starting transfers between devices: 12.7 us -> 13.6 us  [passed_along(): return lax.ppermute(value, axis, pairs)]
    ppermute x10, waiting for transfers between devices: 2.31 us -> 1.76 us  [passed_along(): return lax.ppermute(value, axis, pairs)]
where the time goes in v7:
time: 38.1 us; the launch traced here: 37.8 us
  starting transfers between devices  18.6 us (49%)
  Pallas kernels  12 us (31%)
  waiting for transfers between devices  3.38 us (9%)
  local copies, waits for them, and re-layouts  2.09 us (5%)
  other arithmetic  0.92 us (2%)
  between operations  0.81 us (2%)
    ppermute x10, starting transfers between devices, passed_along(): return lax.ppermute(value, axis, pairs)  13.6 us
    pallas_call x10, Pallas kernels, run(): pl.pallas_call(kernel, in_specs=[spec_of(name) for name in inputs], out_s...  12 us
    ppermute x6, starting transfers between devices, swapped(): return lax.ppermute(value, axis, pairs)  4.98 us
    ppermute x10, waiting for transfers between devices, passed_along(): return lax.ppermute(value, axis, pairs)  1.76 us
    ppermute x6, waiting for transfers between devices, swapped(): return lax.ppermute(value, axis, pairs)  1.62 us
    unnamed x6, local copies, waits for them, and re-layouts  1.27 us
  transfers between devices with their start and end apart: 16, of which 6 were waited for; matrix products, arithmetic and copies ran while one was open for 3% of the time, Pallas kernels for 29%

profile of v7, /device:TPU:0, one launch (start us, length us, event | category | flops | bytes accessed | tf_op | source)
XLA Modules:
  0.0 37.8 jit_solution(14027544124237636583)
XLA Ops:
  0.6 1.0 %split_first.1.refs_3_ = bf16[128,1024]{1,0:T(8,128)(2,1)S(1)} custom-call(bf16[128,4096]{1,0:T(8,128)(2,1)} %bitcast.26), custom_call_target="tpu_custom_call" | custom-call | bytes 1024 | tf_op jit(solution)/shard_map/split_first/pallas_call | solution.py:81
  1.6 3.0 %collective-permute-start.1 = (bf16[128,1024]{1,0:T(8,128)(2,1)S(1)}, bf16[128,1024]{1,0:T(8,128)(2,1)S(1)}, u32[]{:S(2)}, u32[]{:S(2)}) collective-permute-start(bf16[128,1024]{1,0:T(8,128)(2,1)S(1)} %split_first.1.refs_3_), channel_id=1, source_target_pairs={{0,16},{16,0},{1,17},{17,1},{2,18},{18,2},{3,19},{19,3},{4,20},{20... | collective-permute-start | bytes 786440 | tf_op jit(solution)/shard_map/ppermute | solution.py:32
  4.6 1.2 %split_second.1 = (bf16[128,1024]{1,0:T(8,128)(2,1)S(1)}, bf16[64,1024]{1,0:T(8,128)(2,1)S(1)}, bf16[128,1024]{1,0:T(8,128)(2,1)S(1)}) custom-call(bf16[128,4096]{1,0:T(8,128)(2,1)} %bitcast.27, bf16[128,1024]{1,0:T(8,128)(2,1)} %bitcast.30, bf16[64,1024]{1,0:T(8,128)(2,1)} %bitcast.31, bf16[128,1024]{1,0:T(8,128)(2,1)S(1)} %split_first.1.refs_3_), custom_call_target="tpu_custom_call" | custom-call | bytes 1024 | tf_op jit(solution)/shard_map/split_second/pallas_call | solution.py:81
  5.9 0.7 %slice.15 = bf16[64,1024]{1,0:T(8,128)(2,1)} slice(bf16[128,1024]{1,0:T(8,128)(2,1)S(1)} %get-tuple-element.49.refs_4_.refs_3_), slice={[64:128], [0:1024]} | slice | bytes 262144 | tf_op jit(solution)/shard_map/slice | solution.py:385
  6.5 1.6 %collective-permute-start.2 = (bf16[64,1024]{1,0:T(8,128)(2,1)S(1)}, bf16[64,1024]{1,0:T(8,128)(2,1)S(1)}, u32[]{:S(2)}, u32[]{:S(2)}) collective-permute-start(bf16[64,1024]{1,0:T(8,128)(2,1)S(1)} %get-tuple-element.48.refs_2_.refs_1_), channel_id=1, source_target_pairs={{0,8},{4,12},{8,0},{12,4},{1,9},{5,13},{9,1},{13,5},{2,10},{6,14},... | collective-permute-start | bytes 393224 | tf_op jit(solution)/shard_map/ppermute | solution.py:37
  8.1 0.5 %collective-permute-start.6 = (bf16[128,1024]{1,0:T(8,128)(2,1)S(1)}, bf16[128,1024]{1,0:T(8,128)(2,1)S(1)}, u32[]{:S(2)}, u32[]{:S(2)}) collective-permute-start(bf16[128,1024]{1,0:T(8,128)(2,1)S(1)} %get-tuple-element.50.refs_1_), channel_id=1, source_target_pairs={{0,16},{16,0},{1,17},{17,1},{2,18},{18,2},{3,19},{19,3},{4,20},{20... | collective-permute-start | bytes 786440 | tf_op jit(solution)/shard_map/ppermute | solution.py:32
  8.6 1.1 %split_rest.1 = (bf16[128,1024]{1,0:T(8,128)(2,1)S(1)}, bf16[64,1024]{1,0:T(8,128)(2,1)S(1)}, bf16[64,1024]{1,0:T(8,128)(2,1)S(1)}) custom-call(bf16[128,4096]{1,0:T(8,128)(2,1)} %bitcast.28, bf16[128,1024]{1,0:T(8,128)(2,1)S(1)} %get-tuple-element.50.refs_1_), custom_call_target="tpu_custom_call" | custom-call | bytes 1024 | tf_op jit(solution)/shard_map/split_rest/pallas_call | solution.py:81
  9.7 1.6 %collective-permute-start.8 = (bf16[128,1024]{1,0:T(8,128)(2,1)S(1)}, bf16[128,1024]{1,0:T(8,128)(2,1)S(1)}, u32[]{:S(2)}, u32[]{:S(2)}) collective-permute-start(bf16[128,1024]{1,0:T(8,128)(2,1)S(1)} %get-tuple-element.63), channel_id=1, source_target_pairs={{0,16},{16,0},{1,17},{17,1},{2,18},{18,2},{3,19},{19,3},{4,20},{20... | collective-permute-start | bytes 786440 | tf_op jit(solution)/shard_map/ppermute | solution.py:32
  11.3 0.7 %copy-done.2 = s32[1,1,512]{2,1,0:T(1,128)S(1)} copy-done((s32[1,1,512]{2,1,0:T(1,128)S(1)}, s32[1,1,512]{2,1,0:T(1,128)}, u32[]{:S(2)}) %copy-start.2) | copy-done | bytes 2072
  12.2 0.7 %collective-permute-done.2.refs_6_ = bf16[64,1024]{1,0:T(8,128)(2,1)S(1)} collective-permute-done((bf16[64,1024]{1,0:T(8,128)(2,1)S(1)}, bf16[64,1024]{1,0:T(8,128)(2,1)S(1)}, u32[]{:S(2)}, u32[]{:S(2)}) %collective-permute-start.2) | collective-permute-done | bytes 131104 | tf_op jit(solution)/shard_map/ppermute | solution.py:37
  12.8 1.2 %collective-permute-start.3 = (bf16[64,1024]{1,0:T(8,128)(2,1)S(1)}, bf16[64,1024]{1,0:T(8,128)(2,1)S(1)}, u32[]{:S(2)}, u32[]{:S(2)}) collective-permute-start(bf16[64,1024]{1,0:T(8,128)(2,1)S(1)} %collective-permute-done.2.refs_6_), channel_id=1, source_target_pairs={{0,4},{4,0},{8,12},{12,8},{1,5},{5,1},{9,13},{13,9},{2,6},{6,2},{1... | collective-permute-start | bytes 393224 | tf_op jit(solution)/shard_map/ppermute | solution.py:37
  14.3 0.6 %copy-done.1 = bf16[1,1,128,64]{2,3,1,0:T(8,128)(2,1)S(1)} copy-done((bf16[1,1,128,64]{2,3,1,0:T(8,128)(2,1)S(1)}, bf16[1,1,128,64]{2,3,1,0:T(8,128)(2,1)}, u32[]{:S(2)}) %copy-start.1) | copy-done | bytes 16408
  14.9 0.6 %forward.1 = (bf16[512,128]{1,0:T(8,128)(2,1)S(1)}, bf16[512,128]{1,0:T(8,128)(2,1)S(1)}, f32[128,512]{1,0:T(8,128)S(1)}, f32[128,512]{1,0:T(8,128)S(1)}, bf16[64,1024]{1,0:T(8,128)(2,1)S(1)}) custom-call(bf16[128,4096]{1,0:T(8,128)(2,1)S(1)} %bitcast.15, bf16[64,128]{1,0:T(8,128)(2,1)S(1)} %bitcast.19, ...), custom_call_target="tpu_custom_call", output_to_operand_aliasing={{4}: (6, {})} | custom-call | flops 81920 | bytes 1024 | tf_op jit(solution)/shard_map/forward/pallas_call | solution.py:81
  15.5 1.4 %whole.3 = (bf16[64,256]{1,0:T(8,128)(2,1)S(1)}, f32[128,256]{1,0:T(8,128)S(1)}, f32[64,128]{1,0:T(8,128)S(1)}, bf16[128,1024]{1,0:T(8,128)(2,1)S(1)}, bf16[64,1...) custom-call(bf16[128,4096]{1,0:T(8,128)(2,1)S(1)} %bitcast.16, ...), custom_call_target="tpu_custom_call", output_to_operand_aliasing={{5}: (8, {})} | custom-call | flops 163840 | bytes 1024 | tf_op jit(solution)/shard_map/whole/pallas_call | solution.py:81
  17.0 0.5 %collective-permute-start.9 = (bf16[64,1024]{1,0:T(8,128)(2,1)S(1)}, bf16[64,1024]{1,0:T(8,128)(2,1)S(1)}, u32[]{:S(2)}, u32[]{:S(2)}) collective-permute-start(bf16[64,1024]{1,0:T(8,128)(2,1)S(1)} %get-tuple-element.48.refs_2_.refs_1_), channel_id=1, source_target_pairs={{0,4},{4,0},{8,12},{12,8},{1,5},{5,1},{9,13},{13,9},{2,6},{6,2},{1... | collective-permute-start | bytes 393224 | tf_op jit(solution)/shard_map/ppermute | solution.py:37
  17.5 0.8 %collective-permute-done.7.refs_7_ = bf16[64,1024]{1,0:T(8,128)(2,1)S(1)} collective-permute-done((bf16[64,1024]{1,0:T(8,128)(2,1)S(1)}, bf16[64,1024]{1,0:T(8,128)(2,1)S(1)}, u32[]{:S(2)}, u32[]{:S(2)}) %collective-permute-start.7) | collective-permute-done | bytes 131104 | tf_op jit(solution)/shard_map/ppermute | solution.py:37
  18.3 1.8 %whole.4 = (bf16[64,256]{1,0:T(8,128)(2,1)S(1)}, f32[128,256]{1,0:T(8,128)S(1)}, f32[64,128]{1,0:T(8,128)S(1)}, bf16[128,1024]{1,0:T(8,128)(2,1)S(1)}, bf16[64,1...) custom-call(bf16[128,4096]{1,0:T(8,128)(2,1)S(1)} %bitcast.17, bf16[64,128]{1,0:T(8,128)(2,1)S(1)} %bitcast.21, ...), custom_call_target="tpu_custom_call" | custom-call | flops 163840 | bytes 1024 | tf_op jit(solution)/shard_map/whole/pallas_call | solution.py:81
  20.2 1.6 %collective-permute-start.10 = (bf16[64,1024]{1,0:T(8,128)(2,1)S(1)}, bf16[64,1024]{1,0:T(8,128)(2,1)S(1)}, u32[]{:S(2)}, u32[]{:S(2)}) collective-permute-start(bf16[64,1024]{1,0:T(8,128)(2,1)S(1)} %get-tuple-element.71), channel_id=1, source_target_pairs={{0,8},{4,12},{8,0},{12,4},{1,9},{5,13},{9,1},{13,5},{2,10},{6,14},... | collective-permute-start | bytes 393224 | tf_op jit(solution)/shard_map/ppermute | solution.py:37
  21.7 1.2 %collective-permute-start.4 = (bf16[64,1024]{1,0:T(8,128)(2,1)S(1)}, bf16[64,1024]{1,0:T(8,128)(2,1)S(1)}, u32[]{:S(2)}, u32[]{:S(2)}) collective-permute-start(bf16[64,1024]{1,0:T(8,128)(2,1)S(1)} %get-tuple-element.54), channel_id=1, source_target_pairs={{0,16},{16,0},{1,17},{17,1},{2,18},{18,2},{3,19},{19,3},{4,20},{20... | collective-permute-start | bytes 393224 | tf_op jit(solution)/shard_map/ppermute | solution.py:32
  22.9 1.4 %whole.5 = (bf16[64,256]{1,0:T(8,128)(2,1)S(1)}, f32[128,256]{1,0:T(8,128)S(1)}, f32[64,128]{1,0:T(8,128)S(1)}, bf16[128,1024]{1,0:T(8,128)(2,1)S(1)}, bf16[64,1024]{1,0:T(8,128)(2,1)S(1)}) custom-call(bf16[128,4096]{1,0:T(8,128)(2,1)S(1)} %bitcast.18, bf16[64,128]{1,0:T(8,128)(2,1)S(1)} %bitcast.22, ...), custom_call_target="tpu_custom_call" | custom-call | flops 163840 | bytes 1024 | tf_op jit(solution)/shard_map/whole/pallas_call | solution.py:81
  24.4 1.2 %collective-permute-done.5.refs_4_ = bf16[64,1024]{1,0:T(8,128)(2,1)S(1)} collective-permute-done((bf16[64,1024]{1,0:T(8,128)(2,1)S(1)}, bf16[64,1024]{1,0:T(8,128)(2,1)S(1)}, u32[]{:S(2)}, u32[]{:S(2)}) %collective-permute-start.5) | collective-permute-done | bytes 131104 | tf_op jit(solution)/shard_map/ppermute | solution.py:32
  25.6 0.1 collective-permute-done.10.refs_14_
  25.8 1.3 %front.1 = (bf16[128,4096]{1,0:T(8,128)(2,1)}, bf16[64,1024]{1,0:T(8,128)(2,1)S(1)}, f32[128,256]{1,0:T(8,128)S(1)}, f32[64,1024]{1,0:T(8,128)S(1)}, f32[64,128]...) custom-call(bf16[64,128]{1,0:T(8,128)(2,1)S(1)} %bitcast.23, ...), custom_call_target="tpu_custom_call", output_to_operand_aliasing={{0}: (7, {})} | custom-call | flops 81920 | bytes 1024 | tf_op jit(solution)/shard_map/front/pallas_call | solution.py:81
  27.1 0.6 %collective-permute-start.12 = (bf16[64,1024]{1,0:T(8,128)(2,1)S(1)}, bf16[64,1024]{1,0:T(8,128)(2,1)S(1)}, u32[]{:S(2)}, u32[]{:S(2)}) collective-permute-start(bf16[64,1024]{1,0:T(8,128)(2,1)S(1)} %get-tuple-element.82), channel_id=1, source_target_pairs={{0,12},{4,0},{8,4},{12,8},{1,13},{5,1},{9,5},{13,9},{2,14},{6,2},{... | collective-permute-start | bytes 393224 | tf_op jit(solution)/shard_map/ppermute | solution.py:32
  27.7 0.1 collective-permute-done.4.refs_4_.refs_2_
  27.8 0.6 %back.1 = (bf16[64,1024]{1,0:T(8,128)(2,1)S(1)}, bf16[128,512]{1,0:T(8,128)(2,1)S(1)}, bf16[16,1024]{1,0:T(8,128)(2,1)S(1)}, bf16[16,1024]{1,0:T(8,128)(2,1)S(1)...) custom-call(bf16[64,128]{1,0:T(8,128)(2,1)S(1)} %bitcast.24, ...), custom_call_target="tpu_custom_call" | custom-call | flops 81920 | bytes 1024 | tf_op jit(solution)/shard_map/back/pallas_call | solution.py:81
  28.4 2.8 %collective-permute-start.13 = (bf16[16,1024]{1,0:T(8,128)(2,1)S(1)}, bf16[16,1024]{1,0:T(8,128)(2,1)S(1)}, u32[]{:S(2)}, u32[]{:S(2)}) collective-permute-start(bf16[16,1024]{1,0:T(8,128)(2,1)S(1)} %get-tuple-element.89), channel_id=1, source_target_pairs={{0,2},{1,3},{2,0},{3,1},{4,6},{5,7},{6,4},{7,5},{8,10},{9,11},{10,... | collective-permute-start | bytes 98312 | tf_op jit(solution)/shard_map/ppermute | solution.py:32
  31.3 1.6 %collective-permute-start.14 = (bf16[16,1024]{1,0:T(8,128)(2,1)S(1)}, bf16[16,1024]{1,0:T(8,128)(2,1)S(1)}, u32[]{:S(2)}, u32[]{:S(2)}) collective-permute-start(bf16[16,1024]{1,0:T(8,128)(2,1)S(1)} %get-tuple-element.90), channel_id=1, source_target_pairs={{0,1},{1,2},{2,3},{3,0},{4,5},{5,6},{6,7},{7,4},{8,9},{9,10},{10,1... | collective-permute-start | bytes 98312 | tf_op jit(solution)/shard_map/ppermute | solution.py:32
  32.9 2.2 %collective-permute-start.15 = (bf16[16,1024]{1,0:T(8,128)(2,1)S(1)}, bf16[16,1024]{1,0:T(8,128)(2,1)S(1)}, u32[]{:S(2)}, u32[]{:S(2)}) collective-permute-start(bf16[16,1024]{1,0:T(8,128)(2,1)S(1)} %get-tuple-element.91), channel_id=1, source_target_pairs={{0,3},{1,0},{2,1},{3,2},{4,7},{5,4},{6,5},{7,6},{8,11},{9,8},{10,9... | collective-permute-start | bytes 98312 | tf_op jit(solution)/shard_map/ppermute | solution.py:32
  35.1 1.6 %finish.1 = (bf16[128,4096]{1,0:T(8,128)(2,1)}, bf16[64,128]{1,0:T(8,128)(2,1)}, bf16[16,1024]{1,0:T(8,128)(2,1)S(1)}, bf16[128,1024]{1,0:T(8,128)(2,1)}) custom-call(bf16[64,128]{1,0:T(8,128)(2,1)S(1)} %bitcast.25, bf16[64,1024]{1,0:T(8,128)(2,1)S(1)} %get-tuple-element.48.refs_2_.refs_1_, ...), custom_call_target="tpu_custom_call", output_to_operand_aliasing={{0}: (7, {})} | custom-call | flops 81920 | bytes 1024 | tf_op jit(solution)/shard_map/finish/pallas_call | solution.py:81
  36.7 0.4 %collective-permute-done.14 = bf16[16,1024]{1,0:T(8,128)(2,1)S(1)} collective-permute-done((bf16[16,1024]{1,0:T(8,128)(2,1)S(1)}, bf16[16,1024]{1,0:T(8,128)(2,1)S(1)}, u32[]{:S(2)}, u32[]{:S(2)}) %collective-permute-start.14) | collective-permute-done | bytes 32800 | tf_op jit(solution)/shard_map/ppermute | solution.py:32
  37.1 0.6 %add_bitcast_fusion = f32[1,16,1024]{2,1,0:T(8,128)} fusion(bf16[16,1024]{1,0:T(8,128)(2,1)S(1)} %collective-permute-done.15, bf16[16,1024]{1,0:T(8,128)(2,1)S(1)} %collective-permute-done.14, bf16[16,1024]{1,0:T(8,128)(2,1)S(1)} %collective-permute-done.13, bf16[16,1024]{1,0:T(8,128)(2,1)S(1)} %get-tuple-element.88), kind=kLoop, calls=%fused_computation.1 | loop fusion | flops 114688 | bytes 196608 | tf_op jit(solution)/shard_map/broadcast_in_dim | solution.py:553
  (23 shorter events, 0.6 us)
Async XLA Ops:
  1.6 13.8 %collective-permute-start.1 = (bf16[128,1024]{1,0:T(8,128)(2,1)S(1)}, bf16[128,1024]{1,0:T(8,128)(2,1)S(1)}, u32[]{:S(2)}, u32[]{:S(2)}) collective-permute-start(bf16[128,1024]{1,0:T(8,128)(2,1)S(1)} %split_first.1.refs_3_), channel_id=1, source_target_pairs={{0,16},{16,0},{1,17},{17,1},{2,18},{18,2},{3,19},{19,3},{4,20},{20... | collective-permute-start | bytes 786440 | tf_op jit(solution)/shard_map/ppermute | solution.py:32
  5.9 8.4 %copy-start = (bf16[1,1,128,4096]{3,2,1,0:T(8,128)(2,1)S(1)}, bf16[1,1,128,4096]{3,2,1,0:T(8,128)(2,1)}, u32[]{:S(2)}) copy-start(bf16[1,1,128,4096]{3,2,1,0:T(8,128)(2,1)} %param.6) | copy-start | bytes 3145732
  6.5 7.8 %collective-permute-start = (bf16[64,1024]{1,0:T(8,128)(2,1)}, bf16[64,1024]{1,0:T(8,128)(2,1)S(1)}, u32[]{:S(2)}, u32[]{:S(2)}) collective-permute-start(bf16[64,1024]{1,0:T(8,128)(2,1)} %slice.15), channel_id=1, source_target_pairs={{0,4},{4,8},{8,12},{12,0},{1,5},{5,9},{9,13},{13,1},{2,6},{6,10},{... | collective-permute-start | bytes 393224 | tf_op jit(solution)/shard_map/ppermute | solution.py:32
  6.5 6.3 %collective-permute-start.2 = (bf16[64,1024]{1,0:T(8,128)(2,1)S(1)}, bf16[64,1024]{1,0:T(8,128)(2,1)S(1)}, u32[]{:S(2)}, u32[]{:S(2)}) collective-permute-start(bf16[64,1024]{1,0:T(8,128)(2,1)S(1)} %get-tuple-element.48.refs_2_.refs_1_), channel_id=1, source_target_pairs={{0,8},{4,12},{8,0},{12,4},{1,9},{5,13},{9,1},{13,5},{2,10},{6,14},... | collective-permute-start | bytes 393224 | tf_op jit(solution)/shard_map/ppermute | solution.py:37
  8.1 9.4 %collective-permute-start.6 = (bf16[128,1024]{1,0:T(8,128)(2,1)S(1)}, bf16[128,1024]{1,0:T(8,128)(2,1)S(1)}, u32[]{:S(2)}, u32[]{:S(2)}) collective-permute-start(bf16[128,1024]{1,0:T(8,128)(2,1)S(1)} %get-tuple-element.50.refs_1_), channel_id=1, source_target_pairs={{0,16},{16,0},{1,17},{17,1},{2,18},{18,2},{3,19},{19,3},{4,20},{20... | collective-permute-start | bytes 786440 | tf_op jit(solution)/shard_map/ppermute | solution.py:32
  9.7 13.2 %collective-permute-start.8 = (bf16[128,1024]{1,0:T(8,128)(2,1)S(1)}, bf16[128,1024]{1,0:T(8,128)(2,1)S(1)}, u32[]{:S(2)}, u32[]{:S(2)}) collective-permute-start(bf16[128,1024]{1,0:T(8,128)(2,1)S(1)} %get-tuple-element.63), channel_id=1, source_target_pairs={{0,16},{16,0},{1,17},{17,1},{2,18},{18,2},{3,19},{19,3},{4,20},{20... | collective-permute-start | bytes 786440 | tf_op jit(solution)/shard_map/ppermute | solution.py:32
  11.3 0.7 %copy-start.2 = (s32[1,1,512]{2,1,0:T(1,128)S(1)}, s32[1,1,512]{2,1,0:T(1,128)}, u32[]{:S(2)}) copy-start(s32[1,1,512]{2,1,0:T(1,128)} %param.11) | copy-start | bytes 6148
  12.8 2.6 %collective-permute-start.3 = (bf16[64,1024]{1,0:T(8,128)(2,1)S(1)}, bf16[64,1024]{1,0:T(8,128)(2,1)S(1)}, u32[]{:S(2)}, u32[]{:S(2)}) collective-permute-start(bf16[64,1024]{1,0:T(8,128)(2,1)S(1)} %collective-permute-done.2.refs_6_), channel_id=1, source_target_pairs={{0,4},{4,0},{8,12},{12,8},{1,5},{5,1},{9,13},{13,9},{2,6},{6,2},{1... | collective-permute-start | bytes 393224 | tf_op jit(solution)/shard_map/ppermute | solution.py:37
  14.2 0.7 %copy-start.1 = (bf16[1,1,128,64]{2,3,1,0:T(8,128)(2,1)S(1)}, bf16[1,1,128,64]{2,3,1,0:T(8,128)(2,1)}, u32[]{:S(2)}) copy-start(bf16[1,1,128,64]{2,3,1,0:T(8,128)(2,1)} %param.8) | copy-start | bytes 49156
  16.9 1.4 %collective-permute-start.7 = (bf16[64,1024]{1,0:T(8,128)(2,1)S(1)}, bf16[64,1024]{1,0:T(8,128)(2,1)S(1)}, u32[]{:S(2)}, u32[]{:S(2)}) collective-permute-start(bf16[64,1024]{1,0:T(8,128)(2,1)S(1)} %get-tuple-element.59), channel_id=1, source_target_pairs={{0,4},{4,0},{8,12},{12,8},{1,5},{5,1},{9,13},{13,9},{2,6},{6,2},{1... | collective-permute-start | bytes 393224 | tf_op jit(solution)/shard_map/ppermute | solution.py:37
  17.0 6.0 %collective-permute-start.9 = (bf16[64,1024]{1,0:T(8,128)(2,1)S(1)}, bf16[64,1024]{1,0:T(8,128)(2,1)S(1)}, u32[]{:S(2)}, u32[]{:S(2)}) collective-permute-start(bf16[64,1024]{1,0:T(8,128)(2,1)S(1)} %get-tuple-element.48.refs_2_.refs_1_), channel_id=1, source_target_pairs={{0,4},{4,0},{8,12},{12,8},{1,5},{5,1},{9,13},{13,9},{2,6},{6,2},{1... | collective-permute-start | bytes 393224 | tf_op jit(solution)/shard_map/ppermute | solution.py:37
  17.5 8.2 %collective-permute-start.5 = (bf16[64,1024]{1,0:T(8,128)(2,1)S(1)}, bf16[64,1024]{1,0:T(8,128)(2,1)S(1)}, u32[]{:S(2)}, u32[]{:S(2)}) collective-permute-start(bf16[64,1024]{1,0:T(8,128)(2,1)S(1)} %get-tuple-element.57), channel_id=1, source_target_pairs={{0,16},{16,0},{1,17},{17,1},{2,18},{18,2},{3,19},{19,3},{4,20},{20... | collective-permute-start | bytes 393224 | tf_op jit(solution)/shard_map/ppermute | solution.py:32
  20.2 5.6 %collective-permute-start.10 = (bf16[64,1024]{1,0:T(8,128)(2,1)S(1)}, bf16[64,1024]{1,0:T(8,128)(2,1)S(1)}, u32[]{:S(2)}, u32[]{:S(2)}) collective-permute-start(bf16[64,1024]{1,0:T(8,128)(2,1)S(1)} %get-tuple-element.71), channel_id=1, source_target_pairs={{0,8},{4,12},{8,0},{12,4},{1,9},{5,13},{9,1},{13,5},{2,10},{6,14},... | collective-permute-start | bytes 393224 | tf_op jit(solution)/shard_map/ppermute | solution.py:37
  21.7 6.1 %collective-permute-start.4 = (bf16[64,1024]{1,0:T(8,128)(2,1)S(1)}, bf16[64,1024]{1,0:T(8,128)(2,1)S(1)}, u32[]{:S(2)}, u32[]{:S(2)}) collective-permute-start(bf16[64,1024]{1,0:T(8,128)(2,1)S(1)} %get-tuple-element.54), channel_id=1, source_target_pairs={{0,16},{16,0},{1,17},{17,1},{2,18},{18,2},{3,19},{19,3},{4,20},{20... | collective-permute-start | bytes 393224 | tf_op jit(solution)/shard_map/ppermute | solution.py:32
  24.4 3.5 %collective-permute-start.11 = (bf16[64,1024]{1,0:T(8,128)(2,1)S(1)}, bf16[64,1024]{1,0:T(8,128)(2,1)S(1)}, u32[]{:S(2)}, u32[]{:S(2)}) collective-permute-start(bf16[64,1024]{1,0:T(8,128)(2,1)S(1)} %get-tuple-element.73), channel_id=1, source_target_pairs={{0,4},{4,0},{8,12},{12,8},{1,5},{5,1},{9,13},{13,9},{2,6},{6,2},{1... | collective-permute-start | bytes 393224 | tf_op jit(solution)/shard_map/ppermute | solution.py:37
  27.1 8.0 %collective-permute-start.12 = (bf16[64,1024]{1,0:T(8,128)(2,1)S(1)}, bf16[64,1024]{1,0:T(8,128)(2,1)S(1)}, u32[]{:S(2)}, u32[]{:S(2)}) collective-permute-start(bf16[64,1024]{1,0:T(8,128)(2,1)S(1)} %get-tuple-element.82), channel_id=1, source_target_pairs={{0,12},{4,0},{8,4},{12,8},{1,13},{5,1},{9,5},{13,9},{2,14},{6,2},{... | collective-permute-start | bytes 393224 | tf_op jit(solution)/shard_map/ppermute | solution.py:32
  28.4 8.3 %collective-permute-start.13 = (bf16[16,1024]{1,0:T(8,128)(2,1)S(1)}, bf16[16,1024]{1,0:T(8,128)(2,1)S(1)}, u32[]{:S(2)}, u32[]{:S(2)}) collective-permute-start(bf16[16,1024]{1,0:T(8,128)(2,1)S(1)} %get-tuple-element.89), channel_id=1, source_target_pairs={{0,2},{1,3},{2,0},{3,1},{4,6},{5,7},{6,4},{7,5},{8,10},{9,11},{10,... | collective-permute-start | bytes 98312 | tf_op jit(solution)/shard_map/ppermute | solution.py:32
  31.3 5.8 %collective-permute-start.14 = (bf16[16,1024]{1,0:T(8,128)(2,1)S(1)}, bf16[16,1024]{1,0:T(8,128)(2,1)S(1)}, u32[]{:S(2)}, u32[]{:S(2)}) collective-permute-start(bf16[16,1024]{1,0:T(8,128)(2,1)S(1)} %get-tuple-element.90), channel_id=1, source_target_pairs={{0,1},{1,2},{2,3},{3,0},{4,5},{5,6},{6,7},{7,4},{8,9},{9,10},{10,1... | collective-permute-start | bytes 98312 | tf_op jit(solution)/shard_map/ppermute | solution.py:32
  32.9 4.3 %collective-permute-start.15 = (bf16[16,1024]{1,0:T(8,128)(2,1)S(1)}, bf16[16,1024]{1,0:T(8,128)(2,1)S(1)}, u32[]{:S(2)}, u32[]{:S(2)}) collective-permute-start(bf16[16,1024]{1,0:T(8,128)(2,1)S(1)} %get-tuple-element.91), channel_id=1, source_target_pairs={{0,3},{1,0},{2,1},{3,2},{4,7},{5,4},{6,5},{7,6},{8,11},{9,8},{10,9... | collective-permute-start | bytes 98312 | tf_op jit(solution)/shard_map/ppermute | solution.py:32

commit v8 on v2

--- a/solution.py
+++ b/solution.py
@@ -118,7 +118,7 @@
 
 def split_first(z, refs):
     copies = []
-    source = refs.upstream.at[:, chunk_columns(z, 0)]
+    source = refs.upstream.at[pl.ds(0, z.block), chunk_columns(z, 0)]
     copy_rows(source, refs.piece, refs.sems, copies, COPIES)
     for copy in copies:
         copy.wait()
@@ -126,6 +126,8 @@
 
 def split_second(z, refs):
     copies = []
+    source = refs.upstream.at[pl.ds(z.block, z.block), chunk_columns(z, 0)]
+    copy_rows(source, refs.second, refs.sems, copies, COPIES)
     source = refs.upstream.at[:, chunk_columns(z, 1)]
     copy_rows(source, refs.piece, refs.sems, copies, COPIES)
     copy_rows(refs.matrix, refs.matrix_copy, refs.sems, copies, COPIES)
@@ -231,7 +233,10 @@
     pair_total = 0.0
     for index in range(BLOCKS):
         start = index * z.block
-        cot_stack = stacked(refs.cot, slice(start, start + z.block))
+        if step > 0:
+            cot_stack = stacked(refs.cot, slice(start, start + z.block))
+        else:
+            cot_stack = stacked((refs.cot, refs.second)[index], slice(0, z.block))
         dscores, grad_stack = score_grads(z, index, probs[index], keys, values, cot_stack)
         unstack(z, grad_stack, refs.grad, start)
         pair_total += pair_terms(z, index, dscores, probs[index], stacks[index], cot_stack)
@@ -358,10 +363,11 @@
         return dict(sems=pltpu.SemaphoreType.DMA((count,)))
 
     piece = ((rows, width), bf16)
-    first = run(split_first, z, dict(upstream=cotangents), dict(piece=piece), sems(COPIES)).piece
+    half = ((block, width), bf16)
+    first = run(split_first, z, dict(upstream=cotangents), dict(piece=half), sems(COPIES)).piece
     cots = [passed_along(first, "section", -1)]
     outputs = dict(
-        piece=piece, matrix_copy=((rank, width), bf16), pairs_copy=(own.shape, bf16)
+        second=half, piece=piece, matrix_copy=((rank, width), bf16), pairs_copy=(own.shape, bf16)
     )
     second = run(
         split_second,
@@ -370,6 +376,7 @@
         outputs,
         sems(COPIES * len(outputs)),
     )
+    second_half = passed_along(second.second, "section", -1)
     cots.append(passed_along(second.piece, "section", -1))
     own, matrix = second.pairs_copy, second.matrix_copy
     outputs = numbered("piece", [piece] * (last - 2) + [((block, width), bf16)] * BLOCKS)
@@ -432,7 +439,7 @@
         if step > 0:
             inputs.update(input_sum=state.input_grad)
         else:
-            inputs.update(after=ahead.stack0)
+            inputs.update(after=ahead.stack0, second=second_half)
         if 0 < step < last - 1:
             inputs.update(pending=grads[-1])
             outputs.update(dq=dq_shape)

time: 37.8 us -> 39 us (1.032)
  waiting for transfers between devices: 3.93 us -> 5.89 us
  local copies, waits for them, and re-layouts: 2.09 us -> 0.77 us
  starting transfers between devices: 17.7 us -> 18.2 us
    ppermute x6, waiting for transfers between devices: 1.62 us -> 3.57 us  [swapped(): return lax.ppermute(value, axis, pairs)]
    unnamed x6, local copies, waits for them, and re-layouts: 1.27 us -> 0.61 us
    slice x1, local copies, waits for them, and re-layouts: 0.66 us -> 0.01 us  [per_device(): own[rows - count:]]
    ppermute x10 -> x11, starting transfers between devices: 12.7 us -> 13.2 us  [passed_along(): return lax.ppermute(value, axis, pairs)]
    ppermute x10 -> x11, waiting for transfers between devices: 2.31 us -> 2.33 us  [passed_along(): return lax.ppermute(value, axis, pairs)]
  transfers between devices with their start and end apart: 16 -> 17, of which waited for: 6 -> 6; matrix products, arithmetic and copies ran while one was open for 3% -> 1% of each run, Pallas kernels for 29% -> 29%
where the time goes in v8:
time: 39 us; the launch traced here: 38.6 us
  starting transfers between devices  18.2 us (47%)
  Pallas kernels  12 us (31%)
  waiting for transfers between devices  5.89 us (15%)
  other arithmetic  0.92 us (2%)
  between operations  0.84 us (2%)
  local copies, waits for them, and re-layouts  0.77 us (2%)
    ppermute x11, starting transfers between devices, passed_along(): return lax.ppermute(value, axis, pairs)  13.2 us
    pallas_call x10, Pallas kernels, run(): pl.pallas_call(kernel, in_specs=[spec_of(name) for name in inputs], out_s...  12 us
    ppermute x6, starting transfers between devices, swapped(): return lax.ppermute(value, axis, pairs)  5 us
    ppermute x6, waiting for transfers between devices, swapped(): return lax.ppermute(value, axis, pairs)  3.57 us
    ppermute x11, waiting for transfers between devices, passed_along(): return lax.ppermute(value, axis, pairs)  2.33 us
  transfers between devices with their start and end apart: 17, of which 6 were waited for; matrix products, arithmetic and copies ran while one was open for 1% of the time, Pallas kernels for 29%

profile of v8, /device:TPU:0, one launch (start us, length us, event | category | flops | bytes accessed | tf_op | source)
XLA Modules:
  0.0 38.6 jit_solution(18057088531496806961)
XLA Ops:
  0.6 0.9 %split_first.1.refs_3_ = bf16[64,1024]{1,0:T(8,128)(2,1)S(1)} custom-call(bf16[128,4096]{1,0:T(8,128)(2,1)} %bitcast.26), custom_call_target="tpu_custom_call" | custom-call | bytes 1024 | tf_op jit(solution)/shard_map/split_first/pallas_call | solution.py:81
  1.5 3.0 %collective-permute-start.1 = (bf16[64,1024]{1,0:T(8,128)(2,1)S(1)}, bf16[64,1024]{1,0:T(8,128)(2,1)S(1)}, u32[]{:S(2)}, u32[]{:S(2)}) collective-permute-start(bf16[64,1024]{1,0:T(8,128)(2,1)S(1)} %split_first.1.refs_3_), channel_id=1, source_target_pairs={{0,16},{16,0},{1,17},{17,1},{2,18},{18,2},{3,19},{19,3},{4,20},{20... | collective-permute-start | bytes 393224 | tf_op jit(solution)/shard_map/ppermute | solution.py:32
  4.5 1.3 %split_second.1 = (bf16[64,1024]{1,0:T(8,128)(2,1)S(1)}, bf16[128,1024]{1,0:T(8,128)(2,1)S(1)}, bf16[64,1024]{1,0:T(8,128)(2,1)S(1)}, bf16[128,1024]{1,0:T(8,128)(2,1)S(1)}) custom-call(bf16[128,4096]{1,0:T(8,128)(2,1)} %bitcast.27, bf16[128,1024]{1,0:T(8,128)(2,1)} %bitcast.30, bf16[64,1024]{1,0:T(8,128)(2,1)} %bitcast.31, ...), custom_call_target="tpu_custom_call" | custom-call | bytes 1024 | tf_op jit(solution)/shard_map/split_second/pallas_call | solution.py:81
  5.9 0.1 collective-permute-start.4
  6.0 2.0 %collective-permute-start.2 = (bf16[64,1024]{1,0:T(8,128)(2,1)S(1)}, bf16[64,1024]{1,0:T(8,128)(2,1)S(1)}, u32[]{:S(2)}, u32[]{:S(2)}) collective-permute-start(bf16[64,1024]{1,0:T(8,128)(2,1)S(1)} %get-tuple-element.49.refs_2_.refs_1_), channel_id=1, source_target_pairs={{0,8},{4,12},{8,0},{12,4},{1,9},{5,13},{9,1},{13,5},{2,10},{6,14},... | collective-permute-start | bytes 393224 | tf_op jit(solution)/shard_map/ppermute | solution.py:37
  8.0 1.5 %collective-permute-start.7 = (bf16[128,1024]{1,0:T(8,128)(2,1)S(1)}, bf16[128,1024]{1,0:T(8,128)(2,1)S(1)}, u32[]{:S(2)}, u32[]{:S(2)}) collective-permute-start(bf16[128,1024]{1,0:T(8,128)(2,1)S(1)} %get-tuple-element.51.refs_1_), channel_id=1, source_target_pairs={{0,16},{16,0},{1,17},{17,1},{2,18},{18,2},{3,19},{19,3},{4,20},{20... | collective-permute-start | bytes 786440 | tf_op jit(solution)/shard_map/ppermute | solution.py:32
  9.8 2.6 %collective-permute-done.2.refs_6_ = bf16[64,1024]{1,0:T(8,128)(2,1)S(1)} collective-permute-done((bf16[64,1024]{1,0:T(8,128)(2,1)S(1)}, bf16[64,1024]{1,0:T(8,128)(2,1)S(1)}, u32[]{:S(2)}, u32[]{:S(2)}) %collective-permute-start.2) | collective-permute-done | bytes 131104 | tf_op jit(solution)/shard_map/ppermute | solution.py:37
  12.4 0.8 %collective-permute-start.3 = (bf16[64,1024]{1,0:T(8,128)(2,1)S(1)}, bf16[64,1024]{1,0:T(8,128)(2,1)S(1)}, u32[]{:S(2)}, u32[]{:S(2)}) collective-permute-start(bf16[64,1024]{1,0:T(8,128)(2,1)S(1)} %collective-permute-done.2.refs_6_), channel_id=1, source_target_pairs={{0,4},{4,0},{8,12},{12,8},{1,5},{5,1},{9,13},{13,9},{2,6},{6,2},{1... | collective-permute-start | bytes 393224 | tf_op jit(solution)/shard_map/ppermute | solution.py:37
  13.2 0.1 fusion.2
  13.3 1.1 %split_rest.1 = (bf16[128,1024]{1,0:T(8,128)(2,1)S(1)}, bf16[64,1024]{1,0:T(8,128)(2,1)S(1)}, bf16[64,1024]{1,0:T(8,128)(2,1)S(1)}) custom-call(bf16[128,4096]{1,0:T(8,128)(2,1)} %bitcast.28, bf16[128,1024]{1,0:T(8,128)(2,1)S(1)} %get-tuple-element.51.refs_1_), custom_call_target="tpu_custom_call" | custom-call | bytes 1024 | tf_op jit(solution)/shard_map/split_rest/pallas_call | solution.py:81
  14.5 1.3 %collective-permute-start.9 = (bf16[128,1024]{1,0:T(8,128)(2,1)S(1)}, bf16[128,1024]{1,0:T(8,128)(2,1)S(1)}, u32[]{:S(2)}, u32[]{:S(2)}) collective-permute-start(bf16[128,1024]{1,0:T(8,128)(2,1)S(1)} %get-tuple-element.65), channel_id=1, source_target_pairs={{0,16},{16,0},{1,17},{17,1},{2,18},{18,2},{3,19},{19,3},{4,20},{20... | collective-permute-start | bytes 786440 | tf_op jit(solution)/shard_map/ppermute | solution.py:32
  15.8 0.1 maximum_maximum_fusion.refs_5_.refs_4_
  15.9 0.6 %copy-done.1 = bf16[1,1,128,64]{2,3,1,0:T(8,128)(2,1)S(1)} copy-done((bf16[1,1,128,64]{2,3,1,0:T(8,128)(2,1)S(1)}, bf16[1,1,128,64]{2,3,1,0:T(8,128)(2,1)}, u32[]{:S(2)}) %copy-start.1) | copy-done | bytes 16408
  16.5 0.6 %forward.1 = (bf16[512,128]{1,0:T(8,128)(2,1)S(1)}, bf16[512,128]{1,0:T(8,128)(2,1)S(1)}, f32[128,512]{1,0:T(8,128)S(1)}, f32[128,512]{1,0:T(8,128)S(1)}, bf16[64,1024]{1,0:T(8,128)(2,1)S(1)}) custom-call(bf16[128,4096]{1,0:T(8,128)(2,1)S(1)} %bitcast.15, bf16[64,128]{1,0:T(8,128)(2,1)S(1)} %bitcast.19, ...), custom_call_target="tpu_custom_call", output_to_operand_aliasing={{4}: (6, {})} | custom-call | flops 81920 | bytes 1024 | tf_op jit(solution)/shard_map/forward/pallas_call | solution.py:81
  17.1 1.4 %whole.3 = (bf16[64,256]{1,0:T(8,128)(2,1)S(1)}, f32[128,256]{1,0:T(8,128)S(1)}, f32[64,128]{1,0:T(8,128)S(1)}, bf16[128,1024]{1,0:T(8,128)(2,1)S(1)}, bf16[64,1...) custom-call(bf16[128,4096]{1,0:T(8,128)(2,1)S(1)} %bitcast.16, ...), custom_call_target="tpu_custom_call", output_to_operand_aliasing={{5}: (9, {})} | custom-call | flops 163840 | bytes 1024 | tf_op jit(solution)/shard_map/whole/pallas_call | solution.py:81
  18.6 0.5 %collective-permute-start.10 = (bf16[64,1024]{1,0:T(8,128)(2,1)S(1)}, bf16[64,1024]{1,0:T(8,128)(2,1)S(1)}, u32[]{:S(2)}, u32[]{:S(2)}) collective-permute-start(bf16[64,1024]{1,0:T(8,128)(2,1)S(1)} %get-tuple-element.49.refs_2_.refs_1_), channel_id=1, source_target_pairs={{0,4},{4,0},{8,12},{12,8},{1,5},{5,1},{9,13},{13,9},{2,6},{6,2},{1... | collective-permute-start | bytes 393224 | tf_op jit(solution)/shard_map/ppermute | solution.py:37
  19.1 0.8 %collective-permute-start.6 = (bf16[64,1024]{1,0:T(8,128)(2,1)S(1)}, bf16[64,1024]{1,0:T(8,128)(2,1)S(1)}, u32[]{:S(2)}, u32[]{:S(2)}) collective-permute-start(bf16[64,1024]{1,0:T(8,128)(2,1)S(1)} %get-tuple-element.59), channel_id=1, source_target_pairs={{0,16},{16,0},{1,17},{17,1},{2,18},{18,2},{3,19},{19,3},{4,20},{20... | collective-permute-start | bytes 393224 | tf_op jit(solution)/shard_map/ppermute | solution.py:32
  20.0 1.8 %whole.4 = (bf16[64,256]{1,0:T(8,128)(2,1)S(1)}, f32[128,256]{1,0:T(8,128)S(1)}, f32[64,128]{1,0:T(8,128)S(1)}, bf16[128,1024]{1,0:T(8,128)(2,1)S(1)}, bf16[64,1...) custom-call(bf16[128,4096]{1,0:T(8,128)(2,1)S(1)} %bitcast.17, bf16[64,128]{1,0:T(8,128)(2,1)S(1)} %bitcast.21, ...), custom_call_target="tpu_custom_call" | custom-call | flops 163840 | bytes 1024 | tf_op jit(solution)/shard_map/whole/pallas_call | solution.py:81
  21.8 1.5 %collective-permute-start.11 = (bf16[64,1024]{1,0:T(8,128)(2,1)S(1)}, bf16[64,1024]{1,0:T(8,128)(2,1)S(1)}, u32[]{:S(2)}, u32[]{:S(2)}) collective-permute-start(bf16[64,1024]{1,0:T(8,128)(2,1)S(1)} %get-tuple-element.73), channel_id=1, source_target_pairs={{0,8},{4,12},{8,0},{12,4},{1,9},{5,13},{9,1},{13,5},{2,10},{6,14},... | collective-permute-start | bytes 393224 | tf_op jit(solution)/shard_map/ppermute | solution.py:37
  23.3 0.8 %collective-permute-start.5 = (bf16[64,1024]{1,0:T(8,128)(2,1)S(1)}, bf16[64,1024]{1,0:T(8,128)(2,1)S(1)}, u32[]{:S(2)}, u32[]{:S(2)}) collective-permute-start(bf16[64,1024]{1,0:T(8,128)(2,1)S(1)} %get-tuple-element.56), channel_id=1, source_target_pairs={{0,16},{16,0},{1,17},{17,1},{2,18},{18,2},{3,19},{19,3},{4,20},{20... | collective-permute-start | bytes 393224 | tf_op jit(solution)/shard_map/ppermute | solution.py:32
  24.1 1.4 %whole.5 = (bf16[64,256]{1,0:T(8,128)(2,1)S(1)}, f32[128,256]{1,0:T(8,128)S(1)}, f32[64,128]{1,0:T(8,128)S(1)}, bf16[128,1024]{1,0:T(8,128)(2,1)S(1)}, bf16[64,1024]{1,0:T(8,128)(2,1)S(1)}) custom-call(bf16[128,4096]{1,0:T(8,128)(2,1)S(1)} %bitcast.18, bf16[64,128]{1,0:T(8,128)(2,1)S(1)} %bitcast.22, ...), custom_call_target="tpu_custom_call" | custom-call | flops 163840 | bytes 1024 | tf_op jit(solution)/shard_map/whole/pallas_call | solution.py:81
  25.6 0.9 %collective-permute-done.6.refs_4_ = bf16[64,1024]{1,0:T(8,128)(2,1)S(1)} collective-permute-done((bf16[64,1024]{1,0:T(8,128)(2,1)S(1)}, bf16[64,1024]{1,0:T(8,128)(2,1)S(1)}, u32[]{:S(2)}, u32[]{:S(2)}) %collective-permute-start.6) | collective-permute-done | bytes 131104 | tf_op jit(solution)/shard_map/ppermute | solution.py:32
  26.6 0.8 %collective-permute-done.11.refs_14_ = bf16[64,1024]{1,0:T(8,128)(2,1)S(1)} collective-permute-done((bf16[64,1024]{1,0:T(8,128)(2,1)S(1)}, bf16[64,1024]{1,0:T(8,128)(2,1)S(1)}, u32[]{:S(2)}, u32[]{:S(2)}) %collective-permute-start.11) | collective-permute-done | bytes 131104 | tf_op jit(solution)/shard_map/ppermute | solution.py:37
  27.4 1.3 %front.1 = (bf16[128,4096]{1,0:T(8,128)(2,1)}, bf16[64,1024]{1,0:T(8,128)(2,1)S(1)}, f32[128,256]{1,0:T(8,128)S(1)}, f32[64,1024]{1,0:T(8,128)S(1)}, f32[64,128]...) custom-call(bf16[64,128]{1,0:T(8,128)(2,1)S(1)} %bitcast.23, ...), custom_call_target="tpu_custom_call", output_to_operand_aliasing={{0}: (7, {})} | custom-call | flops 81920 | bytes 1024 | tf_op jit(solution)/shard_map/front/pallas_call | solution.py:81
  28.8 0.4 %collective-permute-done.5.refs_4_.refs_2_ = bf16[64,1024]{1,0:T(8,128)(2,1)S(1)} collective-permute-done((bf16[64,1024]{1,0:T(8,128)(2,1)S(1)}, bf16[64,1024]{1,0:T(8,128)(2,1)S(1)}, u32[]{:S(2)}, u32[]{:S(2)}) %collective-permute-start.5) | collective-permute-done | bytes 131104 | tf_op jit(solution)/shard_map/ppermute | solution.py:32
  29.2 0.6 %back.1 = (bf16[64,1024]{1,0:T(8,128)(2,1)S(1)}, bf16[128,512]{1,0:T(8,128)(2,1)S(1)}, bf16[16,1024]{1,0:T(8,128)(2,1)S(1)}, bf16[16,1024]{1,0:T(8,128)(2,1)S(1)...) custom-call(bf16[64,128]{1,0:T(8,128)(2,1)S(1)} %bitcast.24, ...), custom_call_target="tpu_custom_call" | custom-call | flops 81920 | bytes 1024 | tf_op jit(solution)/shard_map/back/pallas_call | solution.py:81
  29.8 1.6 %collective-permute-start.14 = (bf16[16,1024]{1,0:T(8,128)(2,1)S(1)}, bf16[16,1024]{1,0:T(8,128)(2,1)S(1)}, u32[]{:S(2)}, u32[]{:S(2)}) collective-permute-start(bf16[16,1024]{1,0:T(8,128)(2,1)S(1)} %get-tuple-element.91), channel_id=1, source_target_pairs={{0,1},{1,2},{2,3},{3,0},{4,5},{5,6},{6,7},{7,4},{8,9},{9,10},{10,1... | collective-permute-start | bytes 98312 | tf_op jit(solution)/shard_map/ppermute | solution.py:32
  31.4 2.6 %collective-permute-start.15 = (bf16[16,1024]{1,0:T(8,128)(2,1)S(1)}, bf16[16,1024]{1,0:T(8,128)(2,1)S(1)}, u32[]{:S(2)}, u32[]{:S(2)}) collective-permute-start(bf16[16,1024]{1,0:T(8,128)(2,1)S(1)} %get-tuple-element.92), channel_id=1, source_target_pairs={{0,2},{1,3},{2,0},{3,1},{4,6},{5,7},{6,4},{7,5},{8,10},{9,11},{10,... | collective-permute-start | bytes 98312 | tf_op jit(solution)/shard_map/ppermute | solution.py:32
  34.0 1.3 %collective-permute-start.16 = (bf16[16,1024]{1,0:T(8,128)(2,1)S(1)}, bf16[16,1024]{1,0:T(8,128)(2,1)S(1)}, u32[]{:S(2)}, u32[]{:S(2)}) collective-permute-start(bf16[16,1024]{1,0:T(8,128)(2,1)S(1)} %get-tuple-element.93), channel_id=1, source_target_pairs={{0,3},{1,0},{2,1},{3,2},{4,7},{5,4},{6,5},{7,6},{8,11},{9,8},{10,9... | collective-permute-start | bytes 98312 | tf_op jit(solution)/shard_map/ppermute | solution.py:32
  35.4 1.6 %finish.1 = (bf16[128,4096]{1,0:T(8,128)(2,1)}, bf16[64,128]{1,0:T(8,128)(2,1)}, bf16[16,1024]{1,0:T(8,128)(2,1)S(1)}, bf16[128,1024]{1,0:T(8,128)(2,1)}) custom-call(bf16[64,128]{1,0:T(8,128)(2,1)S(1)} %bitcast.25, bf16[64,1024]{1,0:T(8,128)(2,1)S(1)} %get-tuple-element.49.refs_2_.refs_1_, ...), custom_call_target="tpu_custom_call", output_to_operand_aliasing={{0}: (7, {})} | custom-call | flops 81920 | bytes 1024 | tf_op jit(solution)/shard_map/finish/pallas_call | solution.py:81
  37.0 1.0 %collective-permute-done.16 = bf16[16,1024]{1,0:T(8,128)(2,1)S(1)} collective-permute-done((bf16[16,1024]{1,0:T(8,128)(2,1)S(1)}, bf16[16,1024]{1,0:T(8,128)(2,1)S(1)}, u32[]{:S(2)}, u32[]{:S(2)}) %collective-permute-start.16) | collective-permute-done | bytes 32800 | tf_op jit(solution)/shard_map/ppermute | solution.py:32
  38.0 0.6 %add_bitcast_fusion = f32[1,16,1024]{2,1,0:T(8,128)} fusion(bf16[16,1024]{1,0:T(8,128)(2,1)S(1)} %collective-permute-done.16, bf16[16,1024]{1,0:T(8,128)(2,1)S(1)} %collective-permute-done.15, bf16[16,1024]{1,0:T(8,128)(2,1)S(1)} %collective-permute-done.14, bf16[16,1024]{1,0:T(8,128)(2,1)S(1)} %get-tuple-element.90), kind=kLoop, calls=%fused_computation.1 | loop fusion | flops 114688 | bytes 196608 | tf_op jit(solution)/shard_map/broadcast_in_dim | solution.py:560
  (25 shorter events, 0.6 us)
Async XLA Ops:
  1.5 15.6 %collective-permute-start.1 = (bf16[64,1024]{1,0:T(8,128)(2,1)S(1)}, bf16[64,1024]{1,0:T(8,128)(2,1)S(1)}, u32[]{:S(2)}, u32[]{:S(2)}) collective-permute-start(bf16[64,1024]{1,0:T(8,128)(2,1)S(1)} %split_first.1.refs_3_), channel_id=1, source_target_pairs={{0,16},{16,0},{1,17},{17,1},{2,18},{18,2},{3,19},{19,3},{4,20},{20... | collective-permute-start | bytes 393224 | tf_op jit(solution)/shard_map/ppermute | solution.py:32
  4.5 5.0 %copy-start.2 = (s32[1,1,512]{2,1,0:T(1,128)S(1)}, s32[1,1,512]{2,1,0:T(1,128)}, u32[]{:S(2)}) copy-start(s32[1,1,512]{2,1,0:T(1,128)} %param.11) | copy-start | bytes 6148
  5.8 10.1 %copy-start = (bf16[1,1,128,4096]{3,2,1,0:T(8,128)(2,1)S(1)}, bf16[1,1,128,4096]{3,2,1,0:T(8,128)(2,1)}, u32[]{:S(2)}) copy-start(bf16[1,1,128,4096]{3,2,1,0:T(8,128)(2,1)} %param.6) | copy-start | bytes 3145732
  5.9 8.6 %collective-permute-start = (bf16[64,1024]{1,0:T(8,128)(2,1)S(1)}, bf16[64,1024]{1,0:T(8,128)(2,1)S(1)}, u32[]{:S(2)}, u32[]{:S(2)}) collective-permute-start(bf16[64,1024]{1,0:T(8,128)(2,1)S(1)} %slice.15), channel_id=1, source_target_pairs={{0,4},{4,8},{8,12},{12,0},{1,5},{5,9},{9,13},{13,1},{2,6},{6,10},{... | collective-permute-start | bytes 393224 | tf_op jit(solution)/shard_map/ppermute | solution.py:32
  5.9 11.2 %collective-permute-start.4 = (bf16[64,1024]{1,0:T(8,128)(2,1)S(1)}, bf16[64,1024]{1,0:T(8,128)(2,1)S(1)}, u32[]{:S(2)}, u32[]{:S(2)}) collective-permute-start(bf16[64,1024]{1,0:T(8,128)(2,1)S(1)} %get-tuple-element.54), channel_id=1, source_target_pairs={{0,16},{16,0},{1,17},{17,1},{2,18},{18,2},{3,19},{19,3},{4,20},{20... | collective-permute-start | bytes 393224 | tf_op jit(solution)/shard_map/ppermute | solution.py:32
  6.0 6.4 %collective-permute-start.2 = (bf16[64,1024]{1,0:T(8,128)(2,1)S(1)}, bf16[64,1024]{1,0:T(8,128)(2,1)S(1)}, u32[]{:S(2)}, u32[]{:S(2)}) collective-permute-start(bf16[64,1024]{1,0:T(8,128)(2,1)S(1)} %get-tuple-element.49.refs_2_.refs_1_), channel_id=1, source_target_pairs={{0,8},{4,12},{8,0},{12,4},{1,9},{5,13},{9,1},{13,5},{2,10},{6,14},... | collective-permute-start | bytes 393224 | tf_op jit(solution)/shard_map/ppermute | solution.py:37
  8.0 11.8 %collective-permute-start.7 = (bf16[128,1024]{1,0:T(8,128)(2,1)S(1)}, bf16[128,1024]{1,0:T(8,128)(2,1)S(1)}, u32[]{:S(2)}, u32[]{:S(2)}) collective-permute-start(bf16[128,1024]{1,0:T(8,128)(2,1)S(1)} %get-tuple-element.51.refs_1_), channel_id=1, source_target_pairs={{0,16},{16,0},{1,17},{17,1},{2,18},{18,2},{3,19},{19,3},{4,20},{20... | collective-permute-start | bytes 786440 | tf_op jit(solution)/shard_map/ppermute | solution.py:32
  12.4 4.7 %collective-permute-start.3 = (bf16[64,1024]{1,0:T(8,128)(2,1)S(1)}, bf16[64,1024]{1,0:T(8,128)(2,1)S(1)}, u32[]{:S(2)}, u32[]{:S(2)}) collective-permute-start(bf16[64,1024]{1,0:T(8,128)(2,1)S(1)} %collective-permute-done.2.refs_6_), channel_id=1, source_target_pairs={{0,4},{4,0},{8,12},{12,8},{1,5},{5,1},{9,13},{13,9},{2,6},{6,2},{1... | collective-permute-start | bytes 393224 | tf_op jit(solution)/shard_map/ppermute | solution.py:37
  14.5 9.7 %collective-permute-start.9 = (bf16[128,1024]{1,0:T(8,128)(2,1)S(1)}, bf16[128,1024]{1,0:T(8,128)(2,1)S(1)}, u32[]{:S(2)}, u32[]{:S(2)}) collective-permute-start(bf16[128,1024]{1,0:T(8,128)(2,1)S(1)} %get-tuple-element.65), channel_id=1, source_target_pairs={{0,16},{16,0},{1,17},{17,1},{2,18},{18,2},{3,19},{19,3},{4,20},{20... | collective-permute-start | bytes 786440 | tf_op jit(solution)/shard_map/ppermute | solution.py:32
  15.8 0.7 %copy-start.1 = (bf16[1,1,128,64]{2,3,1,0:T(8,128)(2,1)S(1)}, bf16[1,1,128,64]{2,3,1,0:T(8,128)(2,1)}, u32[]{:S(2)}) copy-start(bf16[1,1,128,64]{2,3,1,0:T(8,128)(2,1)} %param.8) | copy-start | bytes 49156
  18.5 1.4 %collective-permute-start.8 = (bf16[64,1024]{1,0:T(8,128)(2,1)S(1)}, bf16[64,1024]{1,0:T(8,128)(2,1)S(1)}, u32[]{:S(2)}, u32[]{:S(2)}) collective-permute-start(bf16[64,1024]{1,0:T(8,128)(2,1)S(1)} %get-tuple-element.61), channel_id=1, source_target_pairs={{0,4},{4,0},{8,12},{12,8},{1,5},{5,1},{9,13},{13,9},{2,6},{6,2},{1... | collective-permute-start | bytes 393224 | tf_op jit(solution)/shard_map/ppermute | solution.py:37
  18.6 5.5 %collective-permute-start.10 = (bf16[64,1024]{1,0:T(8,128)(2,1)S(1)}, bf16[64,1024]{1,0:T(8,128)(2,1)S(1)}, u32[]{:S(2)}, u32[]{:S(2)}) collective-permute-start(bf16[64,1024]{1,0:T(8,128)(2,1)S(1)} %get-tuple-element.49.refs_2_.refs_1_), channel_id=1, source_target_pairs={{0,4},{4,0},{8,12},{12,8},{1,5},{5,1},{9,13},{13,9},{2,6},{6,2},{1... | collective-permute-start | bytes 393224 | tf_op jit(solution)/shard_map/ppermute | solution.py:37
  19.1 7.5 %collective-permute-start.6 = (bf16[64,1024]{1,0:T(8,128)(2,1)S(1)}, bf16[64,1024]{1,0:T(8,128)(2,1)S(1)}, u32[]{:S(2)}, u32[]{:S(2)}) collective-permute-start(bf16[64,1024]{1,0:T(8,128)(2,1)S(1)} %get-tuple-element.59), channel_id=1, source_target_pairs={{0,16},{16,0},{1,17},{17,1},{2,18},{18,2},{3,19},{19,3},{4,20},{20... | collective-permute-start | bytes 393224 | tf_op jit(solution)/shard_map/ppermute | solution.py:32
  21.8 5.6 %collective-permute-start.11 = (bf16[64,1024]{1,0:T(8,128)(2,1)S(1)}, bf16[64,1024]{1,0:T(8,128)(2,1)S(1)}, u32[]{:S(2)}, u32[]{:S(2)}) collective-permute-start(bf16[64,1024]{1,0:T(8,128)(2,1)S(1)} %get-tuple-element.73), channel_id=1, source_target_pairs={{0,8},{4,12},{8,0},{12,4},{1,9},{5,13},{9,1},{13,5},{2,10},{6,14},... | collective-permute-start | bytes 393224 | tf_op jit(solution)/shard_map/ppermute | solution.py:37
  23.3 5.9 %collective-permute-start.5 = (bf16[64,1024]{1,0:T(8,128)(2,1)S(1)}, bf16[64,1024]{1,0:T(8,128)(2,1)S(1)}, u32[]{:S(2)}, u32[]{:S(2)}) collective-permute-start(bf16[64,1024]{1,0:T(8,128)(2,1)S(1)} %get-tuple-element.56), channel_id=1, source_target_pairs={{0,16},{16,0},{1,17},{17,1},{2,18},{18,2},{3,19},{19,3},{4,20},{20... | collective-permute-start | bytes 393224 | tf_op jit(solution)/shard_map/ppermute | solution.py:32
  25.6 3.7 %collective-permute-start.12 = (bf16[64,1024]{1,0:T(8,128)(2,1)S(1)}, bf16[64,1024]{1,0:T(8,128)(2,1)S(1)}, u32[]{:S(2)}, u32[]{:S(2)}) collective-permute-start(bf16[64,1024]{1,0:T(8,128)(2,1)S(1)} %get-tuple-element.75), channel_id=1, source_target_pairs={{0,4},{4,0},{8,12},{12,8},{1,5},{5,1},{9,13},{13,9},{2,6},{6,2},{1... | collective-permute-start | bytes 393224 | tf_op jit(solution)/shard_map/ppermute | solution.py:37
  28.8 6.6 %collective-permute-start.13 = (bf16[64,1024]{1,0:T(8,128)(2,1)S(1)}, bf16[64,1024]{1,0:T(8,128)(2,1)S(1)}, u32[]{:S(2)}, u32[]{:S(2)}) collective-permute-start(bf16[64,1024]{1,0:T(8,128)(2,1)S(1)} %get-tuple-element.84), channel_id=1, source_target_pairs={{0,12},{4,0},{8,4},{12,8},{1,13},{5,1},{9,5},{13,9},{2,14},{6,2},{... | collective-permute-start | bytes 393224 | tf_op jit(solution)/shard_map/ppermute | solution.py:32
  29.8 7.2 %collective-permute-start.14 = (bf16[16,1024]{1,0:T(8,128)(2,1)S(1)}, bf16[16,1024]{1,0:T(8,128)(2,1)S(1)}, u32[]{:S(2)}, u32[]{:S(2)}) collective-permute-start(bf16[16,1024]{1,0:T(8,128)(2,1)S(1)} %get-tuple-element.91), channel_id=1, source_target_pairs={{0,1},{1,2},{2,3},{3,0},{4,5},{5,6},{6,7},{7,4},{8,9},{9,10},{10,1... | collective-permute-start | bytes 98312 | tf_op jit(solution)/shard_map/ppermute | solution.py:32
  31.4 5.5 %collective-permute-start.15 = (bf16[16,1024]{1,0:T(8,128)(2,1)S(1)}, bf16[16,1024]{1,0:T(8,128)(2,1)S(1)}, u32[]{:S(2)}, u32[]{:S(2)}) collective-permute-start(bf16[16,1024]{1,0:T(8,128)(2,1)S(1)} %get-tuple-element.92), channel_id=1, source_target_pairs={{0,2},{1,3},{2,0},{3,1},{4,6},{5,7},{6,4},{7,5},{8,10},{9,11},{10,... | collective-permute-start | bytes 98312 | tf_op jit(solution)/shard_map/ppermute | solution.py:32
  34.0 3.9 %collective-permute-start.16 = (bf16[16,1024]{1,0:T(8,128)(2,1)S(1)}, bf16[16,1024]{1,0:T(8,128)(2,1)S(1)}, u32[]{:S(2)}, u32[]{:S(2)}) collective-permute-start(bf16[16,1024]{1,0:T(8,128)(2,1)S(1)} %get-tuple-element.93), channel_id=1, source_target_pairs={{0,3},{1,0},{2,1},{3,2},{4,7},{5,4},{6,5},{7,6},{8,11},{9,8},{10,9... | collective-permute-start | bytes 98312 | tf_op jit(solution)/shard_map/ppermute | solution.py:32

commit v9 on v2

--- a/solution.py
+++ b/solution.py
@@ -130,6 +130,9 @@
     copy_rows(source, refs.piece, refs.sems, copies, COPIES)
     copy_rows(refs.matrix, refs.matrix_copy, refs.sems, copies, COPIES)
     copy_rows(refs.pairs, refs.pairs_copy, refs.sems, copies, COPIES)
+    height = refs.near.shape[0]
+    near = refs.pairs.at[pl.ds(z.rows - height, height)]
+    copy_rows(near, refs.near, refs.sems, copies, COPIES)
     for copy in copies:
         copy.wait()
 
@@ -361,7 +364,10 @@
     first = run(split_first, z, dict(upstream=cotangents), dict(piece=piece), sems(COPIES)).piece
     cots = [passed_along(first, "section", -1)]
     outputs = dict(
-        piece=piece, matrix_copy=((rank, width), bf16), pairs_copy=(own.shape, bf16)
+        piece=piece,
+        matrix_copy=((rank, width), bf16),
+        pairs_copy=(own.shape, bf16),
+        near=((pieces[-1][1], own.shape[1]), bf16),
     )
     second = run(
         split_second,
@@ -382,7 +388,8 @@
     )
     held = listed(rest, "piece")
     cots.append(passed_along(held[0], "section", -1))
-    halo = [passed_along(own[rows - count :], "seq", distance) for distance, count in pieces]
+    halo = [passed_along(own, "seq", distance) for distance, _ in pieces[:-1]]
+    halo.append(passed_along(second.near, "seq", pieces[-1][0]))
     halo = jnp.concatenate(halo[::-1], axis=0)
     ups = {0: matrix}
     for away in sorted(range(1, chunks), key=low_bit, reverse=True):

time: 37.8 us -> 37.8 us (level)
  Pallas kernels: 12 us -> 12.7 us
  local copies, waits for them, and re-layouts: 2.09 us -> 1.42 us
    pallas_call x10, Pallas kernels: 12 us -> 12.7 us  [run(): pl.pallas_call(kernel, in_specs=[spec_of(name) for name in inputs], out_s...]
    slice x1 -> x0, local copies, waits for them, and re-layouts: 0.66 us -> none  [per_device(): own[rows - count:]]
  transfers between devices with their start and end apart: 16 -> 16, of which waited for: 6 -> 6; matrix products, arithmetic and copies ran while one was open for 3% -> 1% of each run, Pallas kernels for 29% -> 31%
where the time goes in v9:
time: 37.8 us; the launch traced here: 37.4 us
  starting transfers between devices  17.6 us (47%)
  Pallas kernels  12.7 us (34%)
  waiting for transfers between devices  3.94 us (10%)
  local copies, waits for them, and re-layouts  1.42 us (4%)
  other arithmetic  0.92 us (2%)
  between operations  0.82 us (2%)
    pallas_call x10, Pallas kernels, run(): pl.pallas_call(kernel, in_specs=[spec_of(name) for name in inputs], out_s...  12.7 us
    ppermute x10, starting transfers between devices, passed_along(): return lax.ppermute(value, axis, pairs)  12.6 us
    ppermute x6, starting transfers between devices, swapped(): return lax.ppermute(value, axis, pairs)  4.96 us
    ppermute x10, waiting for transfers between devices, passed_along(): return lax.ppermute(value, axis, pairs)  2.36 us
    ppermute x6, waiting for transfers between devices, swapped(): return lax.ppermute(value, axis, pairs)  1.58 us
    unnamed x6, local copies, waits for them, and re-layouts  1.27 us
  transfers between devices with their start and end apart: 16, of which 6 were waited for; matrix products, arithmetic and copies ran while one was open for 1% of the time, Pallas kernels for 31%

profile of v9, /device:TPU:0, one launch (start us, length us, event | category | flops | bytes accessed | tf_op | source)
XLA Modules:
  0.0 37.4 jit_solution(11179408419519406597)
XLA Ops:
  0.6 1.0 %split_first.1.refs_3_ = bf16[128,1024]{1,0:T(8,128)(2,1)S(1)} custom-call(bf16[128,4096]{1,0:T(8,128)(2,1)} %bitcast.26), custom_call_target="tpu_custom_call" | custom-call | bytes 1024 | tf_op jit(solution)/shard_map/split_first/pallas_call | solution.py:81
  1.6 3.0 %collective-permute-start.1 = (bf16[128,1024]{1,0:T(8,128)(2,1)S(1)}, bf16[128,1024]{1,0:T(8,128)(2,1)S(1)}, u32[]{:S(2)}, u32[]{:S(2)}) collective-permute-start(bf16[128,1024]{1,0:T(8,128)(2,1)S(1)} %split_first.1.refs_3_), channel_id=1, source_target_pairs={{0,16},{16,0},{1,17},{17,1},{2,18},{18,2},{3,19},{19,3},{4,20},{20... | collective-permute-start | bytes 786440 | tf_op jit(solution)/shard_map/ppermute | solution.py:32
  4.6 1.9 %split_second.1 = (bf16[128,1024]{1,0:T(8,128)(2,1)S(1)}, bf16[64,1024]{1,0:T(8,128)(2,1)S(1)}, bf16[128,1024]{1,0:T(8,128)(2,1)S(1)}, bf16[64,1024]{1,0:T(8,128)(2,1)}) custom-call(bf16[128,4096]{1,0:T(8,128)(2,1)} %bitcast.27, bf16[128,1024]{1,0:T(8,128)(2,1)} %bitcast.30, bf16[64,1024]{1,0:T(8,128)(2,1)} %bitcast.31, bf16[128,1024]{1,0:T(8,128)(2,1)S(1)} %split_first.1.refs_3_), custom_call_target="tpu_custom_call" | custom-call | bytes 1024 | tf_op jit(solution)/shard_map/split_second/pallas_call | solution.py:81
  6.6 1.6 %collective-permute-start.2 = (bf16[64,1024]{1,0:T(8,128)(2,1)S(1)}, bf16[64,1024]{1,0:T(8,128)(2,1)S(1)}, u32[]{:S(2)}, u32[]{:S(2)}) collective-permute-start(bf16[64,1024]{1,0:T(8,128)(2,1)S(1)} %get-tuple-element.49.refs_2_.refs_1_), channel_id=1, source_target_pairs={{0,8},{4,12},{8,0},{12,4},{1,9},{5,13},{9,1},{13,5},{2,10},{6,14},... | collective-permute-start | bytes 393224 | tf_op jit(solution)/shard_map/ppermute | solution.py:37
  8.2 0.5 %collective-permute-start.6 = (bf16[128,1024]{1,0:T(8,128)(2,1)S(1)}, bf16[128,1024]{1,0:T(8,128)(2,1)S(1)}, u32[]{:S(2)}, u32[]{:S(2)}) collective-permute-start(bf16[128,1024]{1,0:T(8,128)(2,1)S(1)} %get-tuple-element.52.refs_1_), channel_id=1, source_target_pairs={{0,16},{16,0},{1,17},{17,1},{2,18},{18,2},{3,19},{19,3},{4,20},{20... | collective-permute-start | bytes 786440 | tf_op jit(solution)/shard_map/ppermute | solution.py:32
  8.7 1.1 %split_rest.1 = (bf16[128,1024]{1,0:T(8,128)(2,1)S(1)}, bf16[64,1024]{1,0:T(8,128)(2,1)S(1)}, bf16[64,1024]{1,0:T(8,128)(2,1)S(1)}) custom-call(bf16[128,4096]{1,0:T(8,128)(2,1)} %bitcast.28, bf16[128,1024]{1,0:T(8,128)(2,1)S(1)} %get-tuple-element.52.refs_1_), custom_call_target="tpu_custom_call" | custom-call | bytes 1024 | tf_op jit(solution)/shard_map/split_rest/pallas_call | solution.py:81
  9.9 1.6 %collective-permute-start.8 = (bf16[128,1024]{1,0:T(8,128)(2,1)S(1)}, bf16[128,1024]{1,0:T(8,128)(2,1)S(1)}, u32[]{:S(2)}, u32[]{:S(2)}) collective-permute-start(bf16[128,1024]{1,0:T(8,128)(2,1)S(1)} %get-tuple-element.65), channel_id=1, source_target_pairs={{0,16},{16,0},{1,17},{17,1},{2,18},{18,2},{3,19},{19,3},{4,20},{20... | collective-permute-start | bytes 786440 | tf_op jit(solution)/shard_map/ppermute | solution.py:32
  11.4 0.7 %copy-done.2 = s32[1,1,512]{2,1,0:T(1,128)S(1)} copy-done((s32[1,1,512]{2,1,0:T(1,128)S(1)}, s32[1,1,512]{2,1,0:T(1,128)}, u32[]{:S(2)}) %copy-start.2) | copy-done | bytes 2072
  12.3 0.7 %collective-permute-done.2.refs_6_ = bf16[64,1024]{1,0:T(8,128)(2,1)S(1)} collective-permute-done((bf16[64,1024]{1,0:T(8,128)(2,1)S(1)}, bf16[64,1024]{1,0:T(8,128)(2,1)S(1)}, u32[]{:S(2)}, u32[]{:S(2)}) %collective-permute-start.2) | collective-permute-done | bytes 131104 | tf_op jit(solution)/shard_map/ppermute | solution.py:37
  13.0 1.2 %collective-permute-start.3 = (bf16[64,1024]{1,0:T(8,128)(2,1)S(1)}, bf16[64,1024]{1,0:T(8,128)(2,1)S(1)}, u32[]{:S(2)}, u32[]{:S(2)}) collective-permute-start(bf16[64,1024]{1,0:T(8,128)(2,1)S(1)} %collective-permute-done.2.refs_6_), channel_id=1, source_target_pairs={{0,4},{4,0},{8,12},{12,8},{1,5},{5,1},{9,13},{13,9},{2,6},{6,2},{1... | collective-permute-start | bytes 393224 | tf_op jit(solution)/shard_map/ppermute | solution.py:37
  14.1 0.1 fusion.2
  14.4 0.6 %copy-done.1 = bf16[1,1,128,64]{2,3,1,0:T(8,128)(2,1)S(1)} copy-done((bf16[1,1,128,64]{2,3,1,0:T(8,128)(2,1)S(1)}, bf16[1,1,128,64]{2,3,1,0:T(8,128)(2,1)}, u32[]{:S(2)}) %copy-start.1) | copy-done | bytes 16408
  15.0 0.6 %forward.1 = (bf16[512,128]{1,0:T(8,128)(2,1)S(1)}, bf16[512,128]{1,0:T(8,128)(2,1)S(1)}, f32[128,512]{1,0:T(8,128)S(1)}, f32[128,512]{1,0:T(8,128)S(1)}, bf16[64,1024]{1,0:T(8,128)(2,1)S(1)}) custom-call(bf16[128,4096]{1,0:T(8,128)(2,1)S(1)} %bitcast.15, bf16[64,128]{1,0:T(8,128)(2,1)S(1)} %bitcast.19, ...), custom_call_target="tpu_custom_call", output_to_operand_aliasing={{4}: (6, {})} | custom-call | flops 81920 | bytes 1024 | tf_op jit(solution)/shard_map/forward/pallas_call | solution.py:81
  15.6 1.4 %whole.3 = (bf16[64,256]{1,0:T(8,128)(2,1)S(1)}, f32[128,256]{1,0:T(8,128)S(1)}, f32[64,128]{1,0:T(8,128)S(1)}, bf16[128,1024]{1,0:T(8,128)(2,1)S(1)}, bf16[64,1...) custom-call(bf16[128,4096]{1,0:T(8,128)(2,1)S(1)} %bitcast.16, ...), custom_call_target="tpu_custom_call", output_to_operand_aliasing={{5}: (8, {})} | custom-call | flops 163840 | bytes 1024 | tf_op jit(solution)/shard_map/whole/pallas_call | solution.py:81
  17.1 0.5 %collective-permute-start.9 = (bf16[64,1024]{1,0:T(8,128)(2,1)S(1)}, bf16[64,1024]{1,0:T(8,128)(2,1)S(1)}, u32[]{:S(2)}, u32[]{:S(2)}) collective-permute-start(bf16[64,1024]{1,0:T(8,128)(2,1)S(1)} %get-tuple-element.49.refs_2_.refs_1_), channel_id=1, source_target_pairs={{0,4},{4,0},{8,12},{12,8},{1,5},{5,1},{9,13},{13,9},{2,6},{6,2},{1... | collective-permute-start | bytes 393224 | tf_op jit(solution)/shard_map/ppermute | solution.py:37
  17.6 0.8 %collective-permute-done.7.refs_7_ = bf16[64,1024]{1,0:T(8,128)(2,1)S(1)} collective-permute-done((bf16[64,1024]{1,0:T(8,128)(2,1)S(1)}, bf16[64,1024]{1,0:T(8,128)(2,1)S(1)}, u32[]{:S(2)}, u32[]{:S(2)}) %collective-permute-start.7) | collective-permute-done | bytes 131104 | tf_op jit(solution)/shard_map/ppermute | solution.py:37
  18.4 1.8 %whole.4 = (bf16[64,256]{1,0:T(8,128)(2,1)S(1)}, f32[128,256]{1,0:T(8,128)S(1)}, f32[64,128]{1,0:T(8,128)S(1)}, bf16[128,1024]{1,0:T(8,128)(2,1)S(1)}, bf16[64,1...) custom-call(bf16[128,4096]{1,0:T(8,128)(2,1)S(1)} %bitcast.17, bf16[64,128]{1,0:T(8,128)(2,1)S(1)} %bitcast.21, ...), custom_call_target="tpu_custom_call" | custom-call | flops 163840 | bytes 1024 | tf_op jit(solution)/shard_map/whole/pallas_call | solution.py:81
  20.2 1.6 %collective-permute-start.10 = (bf16[64,1024]{1,0:T(8,128)(2,1)S(1)}, bf16[64,1024]{1,0:T(8,128)(2,1)S(1)}, u32[]{:S(2)}, u32[]{:S(2)}) collective-permute-start(bf16[64,1024]{1,0:T(8,128)(2,1)S(1)} %get-tuple-element.73), channel_id=1, source_target_pairs={{0,8},{4,12},{8,0},{12,4},{1,9},{5,13},{9,1},{13,5},{2,10},{6,14},... | collective-permute-start | bytes 393224 | tf_op jit(solution)/shard_map/ppermute | solution.py:37
  21.8 1.2 %collective-permute-start.4 = (bf16[64,1024]{1,0:T(8,128)(2,1)S(1)}, bf16[64,1024]{1,0:T(8,128)(2,1)S(1)}, u32[]{:S(2)}, u32[]{:S(2)}) collective-permute-start(bf16[64,1024]{1,0:T(8,128)(2,1)S(1)} %get-tuple-element.56), channel_id=1, source_target_pairs={{0,16},{16,0},{1,17},{17,1},{2,18},{18,2},{3,19},{19,3},{4,20},{20... | collective-permute-start | bytes 393224 | tf_op jit(solution)/shard_map/ppermute | solution.py:32
  23.0 1.4 %whole.5 = (bf16[64,256]{1,0:T(8,128)(2,1)S(1)}, f32[128,256]{1,0:T(8,128)S(1)}, f32[64,128]{1,0:T(8,128)S(1)}, bf16[128,1024]{1,0:T(8,128)(2,1)S(1)}, bf16[64,1024]{1,0:T(8,128)(2,1)S(1)}) custom-call(bf16[128,4096]{1,0:T(8,128)(2,1)S(1)} %bitcast.18, bf16[64,128]{1,0:T(8,128)(2,1)S(1)} %bitcast.22, ...), custom_call_target="tpu_custom_call" | custom-call | flops 163840 | bytes 1024 | tf_op jit(solution)/shard_map/whole/pallas_call | solution.py:81
  24.5 1.3 %collective-permute-done.5.refs_4_ = bf16[64,1024]{1,0:T(8,128)(2,1)S(1)} collective-permute-done((bf16[64,1024]{1,0:T(8,128)(2,1)S(1)}, bf16[64,1024]{1,0:T(8,128)(2,1)S(1)}, u32[]{:S(2)}, u32[]{:S(2)}) %collective-permute-start.5) | collective-permute-done | bytes 131104 | tf_op jit(solution)/shard_map/ppermute | solution.py:32
  25.8 0.1 collective-permute-done.10.refs_14_
  25.9 1.3 %front.1 = (bf16[128,4096]{1,0:T(8,128)(2,1)}, bf16[64,1024]{1,0:T(8,128)(2,1)S(1)}, f32[128,256]{1,0:T(8,128)S(1)}, f32[64,1024]{1,0:T(8,128)S(1)}, f32[64,128]...) custom-call(bf16[64,128]{1,0:T(8,128)(2,1)S(1)} %bitcast.23, ...), custom_call_target="tpu_custom_call", output_to_operand_aliasing={{0}: (7, {})} | custom-call | flops 81920 | bytes 1024 | tf_op jit(solution)/shard_map/front/pallas_call | solution.py:81
  27.2 0.6 %collective-permute-start.12 = (bf16[64,1024]{1,0:T(8,128)(2,1)S(1)}, bf16[64,1024]{1,0:T(8,128)(2,1)S(1)}, u32[]{:S(2)}, u32[]{:S(2)}) collective-permute-start(bf16[64,1024]{1,0:T(8,128)(2,1)S(1)} %get-tuple-element.84), channel_id=1, source_target_pairs={{0,12},{4,0},{8,4},{12,8},{1,13},{5,1},{9,5},{13,9},{2,14},{6,2},{... | collective-permute-start | bytes 393224 | tf_op jit(solution)/shard_map/ppermute | solution.py:32
  27.8 0.1 collective-permute-done.4.refs_4_.refs_2_
  27.9 0.6 %back.1 = (bf16[64,1024]{1,0:T(8,128)(2,1)S(1)}, bf16[128,512]{1,0:T(8,128)(2,1)S(1)}, bf16[16,1024]{1,0:T(8,128)(2,1)S(1)}, bf16[16,1024]{1,0:T(8,128)(2,1)S(1)...) custom-call(bf16[64,128]{1,0:T(8,128)(2,1)S(1)} %bitcast.24, ...), custom_call_target="tpu_custom_call" | custom-call | flops 81920 | bytes 1024 | tf_op jit(solution)/shard_map/back/pallas_call | solution.py:81
  28.5 1.7 %collective-permute-start.13 = (bf16[16,1024]{1,0:T(8,128)(2,1)S(1)}, bf16[16,1024]{1,0:T(8,128)(2,1)S(1)}, u32[]{:S(2)}, u32[]{:S(2)}) collective-permute-start(bf16[16,1024]{1,0:T(8,128)(2,1)S(1)} %get-tuple-element.91), channel_id=1, source_target_pairs={{0,1},{1,2},{2,3},{3,0},{4,5},{5,6},{6,7},{7,4},{8,9},{9,10},{10,1... | collective-permute-start | bytes 98312 | tf_op jit(solution)/shard_map/ppermute | solution.py:32
  30.3 2.6 %collective-permute-start.14 = (bf16[16,1024]{1,0:T(8,128)(2,1)S(1)}, bf16[16,1024]{1,0:T(8,128)(2,1)S(1)}, u32[]{:S(2)}, u32[]{:S(2)}) collective-permute-start(bf16[16,1024]{1,0:T(8,128)(2,1)S(1)} %get-tuple-element.92), channel_id=1, source_target_pairs={{0,2},{1,3},{2,0},{3,1},{4,6},{5,7},{6,4},{7,5},{8,10},{9,11},{10,... | collective-permute-start | bytes 98312 | tf_op jit(solution)/shard_map/ppermute | solution.py:32
  32.9 1.3 %collective-permute-start.15 = (bf16[16,1024]{1,0:T(8,128)(2,1)S(1)}, bf16[16,1024]{1,0:T(8,128)(2,1)S(1)}, u32[]{:S(2)}, u32[]{:S(2)}) collective-permute-start(bf16[16,1024]{1,0:T(8,128)(2,1)S(1)} %get-tuple-element.93), channel_id=1, source_target_pairs={{0,3},{1,0},{2,1},{3,2},{4,7},{5,4},{6,5},{7,6},{8,11},{9,8},{10,9... | collective-permute-start | bytes 98312 | tf_op jit(solution)/shard_map/ppermute | solution.py:32
  34.2 1.6 %finish.1 = (bf16[128,4096]{1,0:T(8,128)(2,1)}, bf16[64,128]{1,0:T(8,128)(2,1)}, bf16[16,1024]{1,0:T(8,128)(2,1)S(1)}, bf16[128,1024]{1,0:T(8,128)(2,1)}) custom-call(bf16[64,128]{1,0:T(8,128)(2,1)S(1)} %bitcast.25, bf16[64,1024]{1,0:T(8,128)(2,1)S(1)} %get-tuple-element.49.refs_2_.refs_1_, ...), custom_call_target="tpu_custom_call", output_to_operand_aliasing={{0}: (7, {})} | custom-call | flops 81920 | bytes 1024 | tf_op jit(solution)/shard_map/finish/pallas_call | solution.py:81
  35.8 1.0 %collective-permute-done.15 = bf16[16,1024]{1,0:T(8,128)(2,1)S(1)} collective-permute-done((bf16[16,1024]{1,0:T(8,128)(2,1)S(1)}, bf16[16,1024]{1,0:T(8,128)(2,1)S(1)}, u32[]{:S(2)}, u32[]{:S(2)}) %collective-permute-start.15) | collective-permute-done | bytes 32800 | tf_op jit(solution)/shard_map/ppermute | solution.py:32
  36.8 0.6 %add_bitcast_fusion = f32[1,16,1024]{2,1,0:T(8,128)} fusion(bf16[16,1024]{1,0:T(8,128)(2,1)S(1)} %collective-permute-done.15, bf16[16,1024]{1,0:T(8,128)(2,1)S(1)} %collective-permute-done.14, bf16[16,1024]{1,0:T(8,128)(2,1)S(1)} %collective-permute-done.13, bf16[16,1024]{1,0:T(8,128)(2,1)S(1)} %get-tuple-element.90), kind=kLoop, calls=%fused_computation.1 | loop fusion | flops 114688 | bytes 196608 | tf_op jit(solution)/shard_map/broadcast_in_dim | solution.py:560
  (22 shorter events, 0.6 us)
Async XLA Ops:
  1.6 13.9 %collective-permute-start.1 = (bf16[128,1024]{1,0:T(8,128)(2,1)S(1)}, bf16[128,1024]{1,0:T(8,128)(2,1)S(1)}, u32[]{:S(2)}, u32[]{:S(2)}) collective-permute-start(bf16[128,1024]{1,0:T(8,128)(2,1)S(1)} %split_first.1.refs_3_), channel_id=1, source_target_pairs={{0,16},{16,0},{1,17},{17,1},{2,18},{18,2},{3,19},{19,3},{4,20},{20... | collective-permute-start | bytes 786440 | tf_op jit(solution)/shard_map/ppermute | solution.py:32
  6.5 7.8 %copy-start = (bf16[1,1,128,4096]{3,2,1,0:T(8,128)(2,1)S(1)}, bf16[1,1,128,4096]{3,2,1,0:T(8,128)(2,1)}, u32[]{:S(2)}) copy-start(bf16[1,1,128,4096]{3,2,1,0:T(8,128)(2,1)} %param.6) | copy-start | bytes 3145732
  6.6 7.8 %collective-permute-start = (bf16[64,1024]{1,0:T(8,128)(2,1)}, bf16[64,1024]{1,0:T(8,128)(2,1)S(1)}, u32[]{:S(2)}, u32[]{:S(2)}) collective-permute-start(bf16[64,1024]{1,0:T(8,128)(2,1)} %get-tuple-element.50), channel_id=1, source_target_pairs={{0,4},{4,8},{8,12},{12,0},{1,5},{5,9},{9,13},{13,1},{2,6},{6,10},{... | collective-permute-start | bytes 393224 | tf_op jit(solution)/shard_map/ppermute | solution.py:32
  6.6 6.4 %collective-permute-start.2 = (bf16[64,1024]{1,0:T(8,128)(2,1)S(1)}, bf16[64,1024]{1,0:T(8,128)(2,1)S(1)}, u32[]{:S(2)}, u32[]{:S(2)}) collective-permute-start(bf16[64,1024]{1,0:T(8,128)(2,1)S(1)} %get-tuple-element.49.refs_2_.refs_1_), channel_id=1, source_target_pairs={{0,8},{4,12},{8,0},{12,4},{1,9},{5,13},{9,1},{13,5},{2,10},{6,14},... | collective-permute-start | bytes 393224 | tf_op jit(solution)/shard_map/ppermute | solution.py:37
  8.2 9.4 %collective-permute-start.6 = (bf16[128,1024]{1,0:T(8,128)(2,1)S(1)}, bf16[128,1024]{1,0:T(8,128)(2,1)S(1)}, u32[]{:S(2)}, u32[]{:S(2)}) collective-permute-start(bf16[128,1024]{1,0:T(8,128)(2,1)S(1)} %get-tuple-element.52.refs_1_), channel_id=1, source_target_pairs={{0,16},{16,0},{1,17},{17,1},{2,18},{18,2},{3,19},{19,3},{4,20},{20... | collective-permute-start | bytes 786440 | tf_op jit(solution)/shard_map/ppermute | solution.py:32
  9.9 13.2 %collective-permute-start.8 = (bf16[128,1024]{1,0:T(8,128)(2,1)S(1)}, bf16[128,1024]{1,0:T(8,128)(2,1)S(1)}, u32[]{:S(2)}, u32[]{:S(2)}) collective-permute-start(bf16[128,1024]{1,0:T(8,128)(2,1)S(1)} %get-tuple-element.65), channel_id=1, source_target_pairs={{0,16},{16,0},{1,17},{17,1},{2,18},{18,2},{3,19},{19,3},{4,20},{20... | collective-permute-start | bytes 786440 | tf_op jit(solution)/shard_map/ppermute | solution.py:32
  11.4 0.7 %copy-start.2 = (s32[1,1,512]{2,1,0:T(1,128)S(1)}, s32[1,1,512]{2,1,0:T(1,128)}, u32[]{:S(2)}) copy-start(s32[1,1,512]{2,1,0:T(1,128)} %param.11) | copy-start | bytes 6148
  13.0 2.6 %collective-permute-start.3 = (bf16[64,1024]{1,0:T(8,128)(2,1)S(1)}, bf16[64,1024]{1,0:T(8,128)(2,1)S(1)}, u32[]{:S(2)}, u32[]{:S(2)}) collective-permute-start(bf16[64,1024]{1,0:T(8,128)(2,1)S(1)} %collective-permute-done.2.refs_6_), channel_id=1, source_target_pairs={{0,4},{4,0},{8,12},{12,8},{1,5},{5,1},{9,13},{13,9},{2,6},{6,2},{1... | collective-permute-start | bytes 393224 | tf_op jit(solution)/shard_map/ppermute | solution.py:37
  14.2 0.7 %copy-start.1 = (bf16[1,1,128,64]{2,3,1,0:T(8,128)(2,1)S(1)}, bf16[1,1,128,64]{2,3,1,0:T(8,128)(2,1)}, u32[]{:S(2)}) copy-start(bf16[1,1,128,64]{2,3,1,0:T(8,128)(2,1)} %param.8) | copy-start | bytes 49156
  17.0 1.4 %collective-permute-start.7 = (bf16[64,1024]{1,0:T(8,128)(2,1)S(1)}, bf16[64,1024]{1,0:T(8,128)(2,1)S(1)}, u32[]{:S(2)}, u32[]{:S(2)}) collective-permute-start(bf16[64,1024]{1,0:T(8,128)(2,1)S(1)} %get-tuple-element.61), channel_id=1, source_target_pairs={{0,4},{4,0},{8,12},{12,8},{1,5},{5,1},{9,13},{13,9},{2,6},{6,2},{1... | collective-permute-start | bytes 393224 | tf_op jit(solution)/shard_map/ppermute | solution.py:37
  17.1 6.0 %collective-permute-start.9 = (bf16[64,1024]{1,0:T(8,128)(2,1)S(1)}, bf16[64,1024]{1,0:T(8,128)(2,1)S(1)}, u32[]{:S(2)}, u32[]{:S(2)}) collective-permute-start(bf16[64,1024]{1,0:T(8,128)(2,1)S(1)} %get-tuple-element.49.refs_2_.refs_1_), channel_id=1, source_target_pairs={{0,4},{4,0},{8,12},{12,8},{1,5},{5,1},{9,13},{13,9},{2,6},{6,2},{1... | collective-permute-start | bytes 393224 | tf_op jit(solution)/shard_map/ppermute | solution.py:37
  17.6 8.2 %collective-permute-start.5 = (bf16[64,1024]{1,0:T(8,128)(2,1)S(1)}, bf16[64,1024]{1,0:T(8,128)(2,1)S(1)}, u32[]{:S(2)}, u32[]{:S(2)}) collective-permute-start(bf16[64,1024]{1,0:T(8,128)(2,1)S(1)} %get-tuple-element.59), channel_id=1, source_target_pairs={{0,16},{16,0},{1,17},{17,1},{2,18},{18,2},{3,19},{19,3},{4,20},{20... | collective-permute-start | bytes 393224 | tf_op jit(solution)/shard_map/ppermute | solution.py:32
  20.2 5.6 %collective-permute-start.10 = (bf16[64,1024]{1,0:T(8,128)(2,1)S(1)}, bf16[64,1024]{1,0:T(8,128)(2,1)S(1)}, u32[]{:S(2)}, u32[]{:S(2)}) collective-permute-start(bf16[64,1024]{1,0:T(8,128)(2,1)S(1)} %get-tuple-element.73), channel_id=1, source_target_pairs={{0,8},{4,12},{8,0},{12,4},{1,9},{5,13},{9,1},{13,5},{2,10},{6,14},... | collective-permute-start | bytes 393224 | tf_op jit(solution)/shard_map/ppermute | solution.py:37
  21.8 6.1 %collective-permute-start.4 = (bf16[64,1024]{1,0:T(8,128)(2,1)S(1)}, bf16[64,1024]{1,0:T(8,128)(2,1)S(1)}, u32[]{:S(2)}, u32[]{:S(2)}) collective-permute-start(bf16[64,1024]{1,0:T(8,128)(2,1)S(1)} %get-tuple-element.56), channel_id=1, source_target_pairs={{0,16},{16,0},{1,17},{17,1},{2,18},{18,2},{3,19},{19,3},{4,20},{20... | collective-permute-start | bytes 393224 | tf_op jit(solution)/shard_map/ppermute | solution.py:32
  24.4 3.5 %collective-permute-start.11 = (bf16[64,1024]{1,0:T(8,128)(2,1)S(1)}, bf16[64,1024]{1,0:T(8,128)(2,1)S(1)}, u32[]{:S(2)}, u32[]{:S(2)}) collective-permute-start(bf16[64,1024]{1,0:T(8,128)(2,1)S(1)} %get-tuple-element.75), channel_id=1, source_target_pairs={{0,4},{4,0},{8,12},{12,8},{1,5},{5,1},{9,13},{13,9},{2,6},{6,2},{1... | collective-permute-start | bytes 393224 | tf_op jit(solution)/shard_map/ppermute | solution.py:37
  27.2 7.0 %collective-permute-start.12 = (bf16[64,1024]{1,0:T(8,128)(2,1)S(1)}, bf16[64,1024]{1,0:T(8,128)(2,1)S(1)}, u32[]{:S(2)}, u32[]{:S(2)}) collective-permute-start(bf16[64,1024]{1,0:T(8,128)(2,1)S(1)} %get-tuple-element.84), channel_id=1, source_target_pairs={{0,12},{4,0},{8,4},{12,8},{1,13},{5,1},{9,5},{13,9},{2,14},{6,2},{... | collective-permute-start | bytes 393224 | tf_op jit(solution)/shard_map/ppermute | solution.py:32
  28.5 7.3 %collective-permute-start.13 = (bf16[16,1024]{1,0:T(8,128)(2,1)S(1)}, bf16[16,1024]{1,0:T(8,128)(2,1)S(1)}, u32[]{:S(2)}, u32[]{:S(2)}) collective-permute-start(bf16[16,1024]{1,0:T(8,128)(2,1)S(1)} %get-tuple-element.91), channel_id=1, source_target_pairs={{0,1},{1,2},{2,3},{3,0},{4,5},{5,6},{6,7},{7,4},{8,9},{9,10},{10,1... | collective-permute-start | bytes 98312 | tf_op jit(solution)/shard_map/ppermute | solution.py:32
  30.3 5.5 %collective-permute-start.14 = (bf16[16,1024]{1,0:T(8,128)(2,1)S(1)}, bf16[16,1024]{1,0:T(8,128)(2,1)S(1)}, u32[]{:S(2)}, u32[]{:S(2)}) collective-permute-start(bf16[16,1024]{1,0:T(8,128)(2,1)S(1)} %get-tuple-element.92), channel_id=1, source_target_pairs={{0,2},{1,3},{2,0},{3,1},{4,6},{5,7},{6,4},{7,5},{8,10},{9,11},{10,... | collective-permute-start | bytes 98312 | tf_op jit(solution)/shard_map/ppermute | solution.py:32
  32.9 3.9 %collective-permute-start.15 = (bf16[16,1024]{1,0:T(8,128)(2,1)S(1)}, bf16[16,1024]{1,0:T(8,128)(2,1)S(1)}, u32[]{:S(2)}, u32[]{:S(2)}) collective-permute-start(bf16[16,1024]{1,0:T(8,128)(2,1)S(1)} %get-tuple-element.93), channel_id=1, source_target_pairs={{0,3},{1,0},{2,1},{3,2},{4,7},{5,4},{6,5},{7,6},{8,11},{9,8},{10,9... | collective-permute-start | bytes 98312 | tf_op jit(solution)/shard_map/ppermute | solution.py:32

commit v10 on v9

--- a/solution.py
+++ b/solution.py
@@ -129,7 +129,6 @@
     source = refs.upstream.at[:, chunk_columns(z, 1)]
     copy_rows(source, refs.piece, refs.sems, copies, COPIES)
     copy_rows(refs.matrix, refs.matrix_copy, refs.sems, copies, COPIES)
-    copy_rows(refs.pairs, refs.pairs_copy, refs.sems, copies, COPIES)
     height = refs.near.shape[0]
     near = refs.pairs.at[pl.ds(z.rows - height, height)]
     copy_rows(near, refs.near, refs.sems, copies, COPIES)
@@ -366,7 +365,6 @@
     outputs = dict(
         piece=piece,
         matrix_copy=((rank, width), bf16),
-        pairs_copy=(own.shape, bf16),
         near=((pieces[-1][1], own.shape[1]), bf16),
     )
     second = run(
@@ -377,7 +375,7 @@
         sems(COPIES * len(outputs)),
     )
     cots.append(passed_along(second.piece, "section", -1))
-    own, matrix = second.pairs_copy, second.matrix_copy
+    matrix = second.matrix_copy
     outputs = numbered("piece", [piece] * (last - 2) + [((block, width), bf16)] * BLOCKS)
     rest = run(
         split_rest,

time: 37.8 us -> 37.8 us (level)
  local copies, waits for them, and re-layouts: 1.42 us -> 0.74 us
  waiting for transfers between devices: 3.94 us -> 4.57 us
    unnamed x6 -> x8, local copies, waits for them, and re-layouts: 1.27 us -> 0.59 us
    ppermute x6, waiting for transfers between devices: 1.58 us -> 2.21 us  [swapped(): return lax.ppermute(value, axis, pairs)]
where the time goes in v10:
time: 37.8 us; the launch traced here: 37.4 us
  starting transfers between devices  17.8 us (47%)
  Pallas kernels  12.5 us (33%)
  waiting for transfers between devices  4.57 us (12%)
  other arithmetic  0.92 us (2%)
  between operations  0.84 us (2%)
  local copies, waits for them, and re-layouts  0.74 us (2%)
    ppermute x10, starting transfers between devices, passed_along(): return lax.ppermute(value, axis, pairs)  12.8 us
    pallas_call x10, Pallas kernels, run(): pl.pallas_call(kernel, in_specs=[spec_of(name) for name in inputs], out_s...  12.5 us
    ppermute x6, starting transfers between devices, swapped(): return lax.ppermute(value, axis, pairs)  4.96 us
    ppermute x10, waiting for transfers between devices, passed_along(): return lax.ppermute(value, axis, pairs)  2.36 us
    ppermute x6, waiting for transfers between devices, swapped(): return lax.ppermute(value, axis, pairs)  2.21 us
  transfers between devices with their start and end apart: 16, of which 6 were waited for; matrix products, arithmetic and copies ran while one was open for 1% of the time, Pallas kernels for 31%

profile of v10, /device:TPU:0, one launch (start us, length us, event | category | flops | bytes accessed | tf_op | source)
XLA Modules:
  0.0 37.4 jit_solution(12047092760302579640)
XLA Ops:
  0.6 1.0 %split_first.1.refs_3_ = bf16[128,1024]{1,0:T(8,128)(2,1)S(1)} custom-call(bf16[128,4096]{1,0:T(8,128)(2,1)} %bitcast.33), custom_call_target="tpu_custom_call" | custom-call | bytes 1024 | tf_op jit(solution)/shard_map/split_first/pallas_call | solution.py:81
  1.6 3.0 %collective-permute-start.1 = (bf16[128,1024]{1,0:T(8,128)(2,1)S(1)}, bf16[128,1024]{1,0:T(8,128)(2,1)S(1)}, u32[]{:S(2)}, u32[]{:S(2)}) collective-permute-start(bf16[128,1024]{1,0:T(8,128)(2,1)S(1)} %split_first.1.refs_3_), channel_id=1, source_target_pairs={{0,16},{16,0},{1,17},{17,1},{2,18},{18,2},{3,19},{19,3},{4,20},{20... | collective-permute-start | bytes 786440 | tf_op jit(solution)/shard_map/ppermute | solution.py:32
  4.6 1.8 %split_second.1 = (bf16[128,1024]{1,0:T(8,128)(2,1)S(1)}, bf16[64,1024]{1,0:T(8,128)(2,1)S(1)}, bf16[64,1024]{1,0:T(8,128)(2,1)}) custom-call(bf16[128,4096]{1,0:T(8,128)(2,1)} %bitcast.34, bf16[128,1024]{1,0:T(8,128)(2,1)} %bitcast.19, bf16[64,1024]{1,0:T(8,128)(2,1)} %bitcast.37, bf16[128,1024]{1,0:T(8,128)(2,1)S(1)} %split_first.1.refs_3_), custom_call_target="tpu_custom_call" | custom-call | bytes 1024 | tf_op jit(solution)/shard_map/split_second/pallas_call | solution.py:81
  6.5 1.6 %collective-permute-start.2 = (bf16[64,1024]{1,0:T(8,128)(2,1)S(1)}, bf16[64,1024]{1,0:T(8,128)(2,1)S(1)}, u32[]{:S(2)}, u32[]{:S(2)}) collective-permute-start(bf16[64,1024]{1,0:T(8,128)(2,1)S(1)} %get-tuple-element.48.refs_2_.refs_1_), channel_id=1, source_target_pairs={{0,8},{4,12},{8,0},{12,4},{1,9},{5,13},{9,1},{13,5},{2,10},{6,14},... | collective-permute-start | bytes 393224 | tf_op jit(solution)/shard_map/ppermute | solution.py:37
  8.0 0.5 %collective-permute-start.6 = (bf16[128,1024]{1,0:T(8,128)(2,1)S(1)}, bf16[128,1024]{1,0:T(8,128)(2,1)S(1)}, u32[]{:S(2)}, u32[]{:S(2)}) collective-permute-start(bf16[128,1024]{1,0:T(8,128)(2,1)S(1)} %get-tuple-element.50.refs_1_), channel_id=1, source_target_pairs={{0,16},{16,0},{1,17},{17,1},{2,18},{18,2},{3,19},{19,3},{4,20},{20... | collective-permute-start | bytes 786440 | tf_op jit(solution)/shard_map/ppermute | solution.py:32
  8.6 1.1 %split_rest.1 = (bf16[128,1024]{1,0:T(8,128)(2,1)S(1)}, bf16[64,1024]{1,0:T(8,128)(2,1)S(1)}, bf16[64,1024]{1,0:T(8,128)(2,1)S(1)}) custom-call(bf16[128,4096]{1,0:T(8,128)(2,1)} %bitcast.35, bf16[128,1024]{1,0:T(8,128)(2,1)S(1)} %get-tuple-element.50.refs_1_), custom_call_target="tpu_custom_call" | custom-call | bytes 1024 | tf_op jit(solution)/shard_map/split_rest/pallas_call | solution.py:81
  9.7 1.6 %collective-permute-start.8 = (bf16[128,1024]{1,0:T(8,128)(2,1)S(1)}, bf16[128,1024]{1,0:T(8,128)(2,1)S(1)}, u32[]{:S(2)}, u32[]{:S(2)}) collective-permute-start(bf16[128,1024]{1,0:T(8,128)(2,1)S(1)} %get-tuple-element.63), channel_id=1, source_target_pairs={{0,16},{16,0},{1,17},{17,1},{2,18},{18,2},{3,19},{19,3},{4,20},{20... | collective-permute-start | bytes 786440 | tf_op jit(solution)/shard_map/ppermute | solution.py:32
  11.5 1.3 %collective-permute-done.2.refs_6_ = bf16[64,1024]{1,0:T(8,128)(2,1)S(1)} collective-permute-done((bf16[64,1024]{1,0:T(8,128)(2,1)S(1)}, bf16[64,1024]{1,0:T(8,128)(2,1)S(1)}, u32[]{:S(2)}, u32[]{:S(2)}) %collective-permute-start.2) | collective-permute-done | bytes 131104 | tf_op jit(solution)/shard_map/ppermute | solution.py:37
  12.8 1.2 %collective-permute-start.3 = (bf16[64,1024]{1,0:T(8,128)(2,1)S(1)}, bf16[64,1024]{1,0:T(8,128)(2,1)S(1)}, u32[]{:S(2)}, u32[]{:S(2)}) collective-permute-start(bf16[64,1024]{1,0:T(8,128)(2,1)S(1)} %collective-permute-done.2.refs_6_), channel_id=1, source_target_pairs={{0,4},{4,0},{8,12},{12,8},{1,5},{5,1},{9,13},{13,9},{2,6},{6,2},{1... | collective-permute-start | bytes 393224 | tf_op jit(solution)/shard_map/ppermute | solution.py:37
  14.0 0.1 fusion.2
  14.1 0.1 maximum_maximum_fusion.refs_5_.refs_4_
  14.2 0.6 %copy-done.2 = bf16[1,1,128,64]{2,3,1,0:T(8,128)(2,1)S(1)} copy-done((bf16[1,1,128,64]{2,3,1,0:T(8,128)(2,1)S(1)}, bf16[1,1,128,64]{2,3,1,0:T(8,128)(2,1)}, u32[]{:S(2)}) %copy-start.2) | copy-done | bytes 16408
  14.8 0.6 %forward.1 = (bf16[512,128]{1,0:T(8,128)(2,1)S(1)}, bf16[512,128]{1,0:T(8,128)(2,1)S(1)}, f32[128,512]{1,0:T(8,128)S(1)}, f32[128,512]{1,0:T(8,128)S(1)}, bf16[64,1024]{1,0:T(8,128)(2,1)S(1)}) custom-call(bf16[128,4096]{1,0:T(8,128)(2,1)S(1)} %bitcast.15, bf16[64,128]{1,0:T(8,128)(2,1)S(1)} %bitcast.26, ...), custom_call_target="tpu_custom_call", output_to_operand_aliasing={{4}: (6, {})} | custom-call | flops 81920 | bytes 1024 | tf_op jit(solution)/shard_map/forward/pallas_call | solution.py:81
  15.4 1.4 %whole.3 = (bf16[64,256]{1,0:T(8,128)(2,1)S(1)}, f32[128,256]{1,0:T(8,128)S(1)}, f32[64,128]{1,0:T(8,128)S(1)}, bf16[128,1024]{1,0:T(8,128)(2,1)S(1)}, bf16[64,1...) custom-call(bf16[128,4096]{1,0:T(8,128)(2,1)S(1)} %bitcast.16, ...), custom_call_target="tpu_custom_call", output_to_operand_aliasing={{5}: (8, {})} | custom-call | flops 163840 | bytes 1024 | tf_op jit(solution)/shard_map/whole/pallas_call | solution.py:81
  16.9 0.5 %collective-permute-start.9 = (bf16[64,1024]{1,0:T(8,128)(2,1)S(1)}, bf16[64,1024]{1,0:T(8,128)(2,1)S(1)}, u32[]{:S(2)}, u32[]{:S(2)}) collective-permute-start(bf16[64,1024]{1,0:T(8,128)(2,1)S(1)} %get-tuple-element.48.refs_2_.refs_1_), channel_id=1, source_target_pairs={{0,4},{4,0},{8,12},{12,8},{1,5},{5,1},{9,13},{13,9},{2,6},{6,2},{1... | collective-permute-start | bytes 393224 | tf_op jit(solution)/shard_map/ppermute | solution.py:37
  17.4 0.8 %collective-permute-done.7.refs_7_ = bf16[64,1024]{1,0:T(8,128)(2,1)S(1)} collective-permute-done((bf16[64,1024]{1,0:T(8,128)(2,1)S(1)}, bf16[64,1024]{1,0:T(8,128)(2,1)S(1)}, u32[]{:S(2)}, u32[]{:S(2)}) %collective-permute-start.7) | collective-permute-done | bytes 131104 | tf_op jit(solution)/shard_map/ppermute | solution.py:37
  18.2 1.8 %whole.4 = (bf16[64,256]{1,0:T(8,128)(2,1)S(1)}, f32[128,256]{1,0:T(8,128)S(1)}, f32[64,128]{1,0:T(8,128)S(1)}, bf16[128,1024]{1,0:T(8,128)(2,1)S(1)}, bf16[64,1...) custom-call(bf16[128,4096]{1,0:T(8,128)(2,1)S(1)} %bitcast.17, bf16[64,128]{1,0:T(8,128)(2,1)S(1)} %bitcast.28, ...), custom_call_target="tpu_custom_call" | custom-call | flops 163840 | bytes 1024 | tf_op jit(solution)/shard_map/whole/pallas_call | solution.py:81
  20.1 1.6 %collective-permute-start.10 = (bf16[64,1024]{1,0:T(8,128)(2,1)S(1)}, bf16[64,1024]{1,0:T(8,128)(2,1)S(1)}, u32[]{:S(2)}, u32[]{:S(2)}) collective-permute-start(bf16[64,1024]{1,0:T(8,128)(2,1)S(1)} %get-tuple-element.71), channel_id=1, source_target_pairs={{0,8},{4,12},{8,0},{12,4},{1,9},{5,13},{9,1},{13,5},{2,10},{6,14},... | collective-permute-start | bytes 393224 | tf_op jit(solution)/shard_map/ppermute | solution.py:37
  21.7 1.2 %collective-permute-start.4 = (bf16[64,1024]{1,0:T(8,128)(2,1)S(1)}, bf16[64,1024]{1,0:T(8,128)(2,1)S(1)}, u32[]{:S(2)}, u32[]{:S(2)}) collective-permute-start(bf16[64,1024]{1,0:T(8,128)(2,1)S(1)} %get-tuple-element.54), channel_id=1, source_target_pairs={{0,16},{16,0},{1,17},{17,1},{2,18},{18,2},{3,19},{19,3},{4,20},{20... | collective-permute-start | bytes 393224 | tf_op jit(solution)/shard_map/ppermute | solution.py:32
  22.9 1.4 %whole.5 = (bf16[64,256]{1,0:T(8,128)(2,1)S(1)}, f32[128,256]{1,0:T(8,128)S(1)}, f32[64,128]{1,0:T(8,128)S(1)}, bf16[128,1024]{1,0:T(8,128)(2,1)S(1)}, bf16[64,1024]{1,0:T(8,128)(2,1)S(1)}) custom-call(bf16[128,4096]{1,0:T(8,128)(2,1)S(1)} %bitcast.18, bf16[64,128]{1,0:T(8,128)(2,1)S(1)} %bitcast.29, ...), custom_call_target="tpu_custom_call" | custom-call | flops 163840 | bytes 1024 | tf_op jit(solution)/shard_map/whole/pallas_call | solution.py:81
  24.4 1.2 %collective-permute-done.5.refs_4_ = bf16[64,1024]{1,0:T(8,128)(2,1)S(1)} collective-permute-done((bf16[64,1024]{1,0:T(8,128)(2,1)S(1)}, bf16[64,1024]{1,0:T(8,128)(2,1)S(1)}, u32[]{:S(2)}, u32[]{:S(2)}) %collective-permute-start.5) | collective-permute-done | bytes 131104 | tf_op jit(solution)/shard_map/ppermute | solution.py:32
  25.6 0.1 collective-permute-done.10.refs_14_
  25.7 1.3 %front.1 = (bf16[128,4096]{1,0:T(8,128)(2,1)}, bf16[64,1024]{1,0:T(8,128)(2,1)S(1)}, f32[128,256]{1,0:T(8,128)S(1)}, f32[64,1024]{1,0:T(8,128)S(1)}, f32[64,128]...) custom-call(bf16[64,128]{1,0:T(8,128)(2,1)S(1)} %bitcast.30, ...), custom_call_target="tpu_custom_call", output_to_operand_aliasing={{0}: (7, {})} | custom-call | flops 81920 | bytes 1024 | tf_op jit(solution)/shard_map/front/pallas_call | solution.py:81
  27.0 0.6 %collective-permute-start.12 = (bf16[64,1024]{1,0:T(8,128)(2,1)S(1)}, bf16[64,1024]{1,0:T(8,128)(2,1)S(1)}, u32[]{:S(2)}, u32[]{:S(2)}) collective-permute-start(bf16[64,1024]{1,0:T(8,128)(2,1)S(1)} %get-tuple-element.82), channel_id=1, source_target_pairs={{0,12},{4,0},{8,4},{12,8},{1,13},{5,1},{9,5},{13,9},{2,14},{6,2},{... | collective-permute-start | bytes 393224 | tf_op jit(solution)/shard_map/ppermute | solution.py:32
  27.6 0.1 collective-permute-done.4.refs_4_.refs_2_
  27.8 0.6 %back.1 = (bf16[64,1024]{1,0:T(8,128)(2,1)S(1)}, bf16[128,512]{1,0:T(8,128)(2,1)S(1)}, bf16[16,1024]{1,0:T(8,128)(2,1)S(1)}, bf16[16,1024]{1,0:T(8,128)(2,1)S(1)...) custom-call(bf16[64,128]{1,0:T(8,128)(2,1)S(1)} %bitcast.31, ...), custom_call_target="tpu_custom_call" | custom-call | flops 81920 | bytes 1024 | tf_op jit(solution)/shard_map/back/pallas_call | solution.py:81
  28.4 1.9 %collective-permute-start.13 = (bf16[16,1024]{1,0:T(8,128)(2,1)S(1)}, bf16[16,1024]{1,0:T(8,128)(2,1)S(1)}, u32[]{:S(2)}, u32[]{:S(2)}) collective-permute-start(bf16[16,1024]{1,0:T(8,128)(2,1)S(1)} %get-tuple-element.89), channel_id=1, source_target_pairs={{0,1},{1,2},{2,3},{3,0},{4,5},{5,6},{6,7},{7,4},{8,9},{9,10},{10,1... | collective-permute-start | bytes 98312 | tf_op jit(solution)/shard_map/ppermute | solution.py:32
  30.3 2.6 %collective-permute-start.14 = (bf16[16,1024]{1,0:T(8,128)(2,1)S(1)}, bf16[16,1024]{1,0:T(8,128)(2,1)S(1)}, u32[]{:S(2)}, u32[]{:S(2)}) collective-permute-start(bf16[16,1024]{1,0:T(8,128)(2,1)S(1)} %get-tuple-element.90), channel_id=1, source_target_pairs={{0,2},{1,3},{2,0},{3,1},{4,6},{5,7},{6,4},{7,5},{8,10},{9,11},{10,... | collective-permute-start | bytes 98312 | tf_op jit(solution)/shard_map/ppermute | solution.py:32
  32.9 1.3 %collective-permute-start.15 = (bf16[16,1024]{1,0:T(8,128)(2,1)S(1)}, bf16[16,1024]{1,0:T(8,128)(2,1)S(1)}, u32[]{:S(2)}, u32[]{:S(2)}) collective-permute-start(bf16[16,1024]{1,0:T(8,128)(2,1)S(1)} %get-tuple-element.91), channel_id=1, source_target_pairs={{0,3},{1,0},{2,1},{3,2},{4,7},{5,4},{6,5},{7,6},{8,11},{9,8},{10,9... | collective-permute-start | bytes 98312 | tf_op jit(solution)/shard_map/ppermute | solution.py:32
  34.2 1.6 %finish.1 = (bf16[128,4096]{1,0:T(8,128)(2,1)}, bf16[64,128]{1,0:T(8,128)(2,1)}, bf16[16,1024]{1,0:T(8,128)(2,1)S(1)}, bf16[128,1024]{1,0:T(8,128)(2,1)}) custom-call(bf16[64,128]{1,0:T(8,128)(2,1)S(1)} %bitcast.32, bf16[64,1024]{1,0:T(8,128)(2,1)S(1)} %get-tuple-element.48.refs_2_.refs_1_, ...), custom_call_target="tpu_custom_call", output_to_operand_aliasing={{0}: (7, {})} | custom-call | flops 81920 | bytes 1024 | tf_op jit(solution)/shard_map/finish/pallas_call | solution.py:81
  35.8 1.0 %collective-permute-done.15 = bf16[16,1024]{1,0:T(8,128)(2,1)S(1)} collective-permute-done((bf16[16,1024]{1,0:T(8,128)(2,1)S(1)}, bf16[16,1024]{1,0:T(8,128)(2,1)S(1)}, u32[]{:S(2)}, u32[]{:S(2)}) %collective-permute-start.15) | collective-permute-done | bytes 32800 | tf_op jit(solution)/shard_map/ppermute | solution.py:32
  36.8 0.6 %add_bitcast_fusion = f32[1,16,1024]{2,1,0:T(8,128)} fusion(bf16[16,1024]{1,0:T(8,128)(2,1)S(1)} %collective-permute-done.15, bf16[16,1024]{1,0:T(8,128)(2,1)S(1)} %collective-permute-done.14, bf16[16,1024]{1,0:T(8,128)(2,1)S(1)} %collective-permute-done.13, bf16[16,1024]{1,0:T(8,128)(2,1)S(1)} %get-tuple-element.88), kind=kLoop, calls=%fused_computation.1 | loop fusion | flops 114688 | bytes 196608 | tf_op jit(solution)/shard_map/broadcast_in_dim | solution.py:558
  (24 shorter events, 0.5 us)
Async XLA Ops:
  1.6 13.8 %collective-permute-start.1 = (bf16[128,1024]{1,0:T(8,128)(2,1)S(1)}, bf16[128,1024]{1,0:T(8,128)(2,1)S(1)}, u32[]{:S(2)}, u32[]{:S(2)}) collective-permute-start(bf16[128,1024]{1,0:T(8,128)(2,1)S(1)} %split_first.1.refs_3_), channel_id=1, source_target_pairs={{0,16},{16,0},{1,17},{17,1},{2,18},{18,2},{3,19},{19,3},{4,20},{20... | collective-permute-start | bytes 786440 | tf_op jit(solution)/shard_map/ppermute | solution.py:32
  6.4 7.8 %copy-start = (bf16[1,1,128,4096]{3,2,1,0:T(8,128)(2,1)S(1)}, bf16[1,1,128,4096]{3,2,1,0:T(8,128)(2,1)}, u32[]{:S(2)}) copy-start(bf16[1,1,128,4096]{3,2,1,0:T(8,128)(2,1)} %param.6) | copy-start | bytes 3145732
  6.4 7.8 %collective-permute-start = (bf16[64,1024]{1,0:T(8,128)(2,1)}, bf16[64,1024]{1,0:T(8,128)(2,1)S(1)}, u32[]{:S(2)}, u32[]{:S(2)}) collective-permute-start(bf16[64,1024]{1,0:T(8,128)(2,1)} %get-tuple-element.49), channel_id=1, source_target_pairs={{0,4},{4,8},{8,12},{12,0},{1,5},{5,9},{9,13},{13,1},{2,6},{6,10},{... | collective-permute-start | bytes 393224 | tf_op jit(solution)/shard_map/ppermute | solution.py:32
  6.5 6.4 %collective-permute-start.2 = (bf16[64,1024]{1,0:T(8,128)(2,1)S(1)}, bf16[64,1024]{1,0:T(8,128)(2,1)S(1)}, u32[]{:S(2)}, u32[]{:S(2)}) collective-permute-start(bf16[64,1024]{1,0:T(8,128)(2,1)S(1)} %get-tuple-element.48.refs_2_.refs_1_), channel_id=1, source_target_pairs={{0,8},{4,12},{8,0},{12,4},{1,9},{5,13},{9,1},{13,5},{2,10},{6,14},... | collective-permute-start | bytes 393224 | tf_op jit(solution)/shard_map/ppermute | solution.py:37
  8.0 9.4 %collective-permute-start.6 = (bf16[128,1024]{1,0:T(8,128)(2,1)S(1)}, bf16[128,1024]{1,0:T(8,128)(2,1)S(1)}, u32[]{:S(2)}, u32[]{:S(2)}) collective-permute-start(bf16[128,1024]{1,0:T(8,128)(2,1)S(1)} %get-tuple-element.50.refs_1_), channel_id=1, source_target_pairs={{0,16},{16,0},{1,17},{17,1},{2,18},{18,2},{3,19},{19,3},{4,20},{20... | collective-permute-start | bytes 786440 | tf_op jit(solution)/shard_map/ppermute | solution.py:32
  8.6 2.7 %copy-start.3 = (s32[1,1,512]{2,1,0:T(1,128)S(1)}, s32[1,1,512]{2,1,0:T(1,128)}, u32[]{:S(2)}) copy-start(s32[1,1,512]{2,1,0:T(1,128)} %param.11) | copy-start | bytes 6148
  9.7 4.5 %copy-start.1 = (bf16[1,1,128,1024]{3,2,1,0:T(8,128)(2,1)S(1)}, bf16[1,1,128,1024]{3,2,1,0:T(8,128)(2,1)}, u32[]{:S(2)}) copy-start(bf16[1,1,128,1024]{3,2,1,0:T(8,128)(2,1)} %param.7) | copy-start | bytes 786436
  9.7 13.2 %collective-permute-start.8 = (bf16[128,1024]{1,0:T(8,128)(2,1)S(1)}, bf16[128,1024]{1,0:T(8,128)(2,1)S(1)}, u32[]{:S(2)}, u32[]{:S(2)}) collective-permute-start(bf16[128,1024]{1,0:T(8,128)(2,1)S(1)} %get-tuple-element.63), channel_id=1, source_target_pairs={{0,16},{16,0},{1,17},{17,1},{2,18},{18,2},{3,19},{19,3},{4,20},{20... | collective-permute-start | bytes 786440 | tf_op jit(solution)/shard_map/ppermute | solution.py:32
  12.8 2.6 %collective-permute-start.3 = (bf16[64,1024]{1,0:T(8,128)(2,1)S(1)}, bf16[64,1024]{1,0:T(8,128)(2,1)S(1)}, u32[]{:S(2)}, u32[]{:S(2)}) collective-permute-start(bf16[64,1024]{1,0:T(8,128)(2,1)S(1)} %collective-permute-done.2.refs_6_), channel_id=1, source_target_pairs={{0,4},{4,0},{8,12},{12,8},{1,5},{5,1},{9,13},{13,9},{2,6},{6,2},{1... | collective-permute-start | bytes 393224 | tf_op jit(solution)/shard_map/ppermute | solution.py:37
  14.1 0.7 %copy-start.2 = (bf16[1,1,128,64]{2,3,1,0:T(8,128)(2,1)S(1)}, bf16[1,1,128,64]{2,3,1,0:T(8,128)(2,1)}, u32[]{:S(2)}) copy-start(bf16[1,1,128,64]{2,3,1,0:T(8,128)(2,1)} %param.8) | copy-start | bytes 49156
  16.8 1.4 %collective-permute-start.7 = (bf16[64,1024]{1,0:T(8,128)(2,1)S(1)}, bf16[64,1024]{1,0:T(8,128)(2,1)S(1)}, u32[]{:S(2)}, u32[]{:S(2)}) collective-permute-start(bf16[64,1024]{1,0:T(8,128)(2,1)S(1)} %get-tuple-element.59), channel_id=1, source_target_pairs={{0,4},{4,0},{8,12},{12,8},{1,5},{5,1},{9,13},{13,9},{2,6},{6,2},{1... | collective-permute-start | bytes 393224 | tf_op jit(solution)/shard_map/ppermute | solution.py:37
  16.9 6.0 %collective-permute-start.9 = (bf16[64,1024]{1,0:T(8,128)(2,1)S(1)}, bf16[64,1024]{1,0:T(8,128)(2,1)S(1)}, u32[]{:S(2)}, u32[]{:S(2)}) collective-permute-start(bf16[64,1024]{1,0:T(8,128)(2,1)S(1)} %get-tuple-element.48.refs_2_.refs_1_), channel_id=1, source_target_pairs={{0,4},{4,0},{8,12},{12,8},{1,5},{5,1},{9,13},{13,9},{2,6},{6,2},{1... | collective-permute-start | bytes 393224 | tf_op jit(solution)/shard_map/ppermute | solution.py:37
  17.4 8.2 %collective-permute-start.5 = (bf16[64,1024]{1,0:T(8,128)(2,1)S(1)}, bf16[64,1024]{1,0:T(8,128)(2,1)S(1)}, u32[]{:S(2)}, u32[]{:S(2)}) collective-permute-start(bf16[64,1024]{1,0:T(8,128)(2,1)S(1)} %get-tuple-element.57), channel_id=1, source_target_pairs={{0,16},{16,0},{1,17},{17,1},{2,18},{18,2},{3,19},{19,3},{4,20},{20... | collective-permute-start | bytes 393224 | tf_op jit(solution)/shard_map/ppermute | solution.py:32
  20.1 5.6 %collective-permute-start.10 = (bf16[64,1024]{1,0:T(8,128)(2,1)S(1)}, bf16[64,1024]{1,0:T(8,128)(2,1)S(1)}, u32[]{:S(2)}, u32[]{:S(2)}) collective-permute-start(bf16[64,1024]{1,0:T(8,128)(2,1)S(1)} %get-tuple-element.71), channel_id=1, source_target_pairs={{0,8},{4,12},{8,0},{12,4},{1,9},{5,13},{9,1},{13,5},{2,10},{6,14},... | collective-permute-start | bytes 393224 | tf_op jit(solution)/shard_map/ppermute | solution.py:37
  21.7 6.1 %collective-permute-start.4 = (bf16[64,1024]{1,0:T(8,128)(2,1)S(1)}, bf16[64,1024]{1,0:T(8,128)(2,1)S(1)}, u32[]{:S(2)}, u32[]{:S(2)}) collective-permute-start(bf16[64,1024]{1,0:T(8,128)(2,1)S(1)} %get-tuple-element.54), channel_id=1, source_target_pairs={{0,16},{16,0},{1,17},{17,1},{2,18},{18,2},{3,19},{19,3},{4,20},{20... | collective-permute-start | bytes 393224 | tf_op jit(solution)/shard_map/ppermute | solution.py:32
  24.3 3.5 %collective-permute-start.11 = (bf16[64,1024]{1,0:T(8,128)(2,1)S(1)}, bf16[64,1024]{1,0:T(8,128)(2,1)S(1)}, u32[]{:S(2)}, u32[]{:S(2)}) collective-permute-start(bf16[64,1024]{1,0:T(8,128)(2,1)S(1)} %get-tuple-element.73), channel_id=1, source_target_pairs={{0,4},{4,0},{8,12},{12,8},{1,5},{5,1},{9,13},{13,9},{2,6},{6,2},{1... | collective-permute-start | bytes 393224 | tf_op jit(solution)/shard_map/ppermute | solution.py:37
  27.0 7.2 %collective-permute-start.12 = (bf16[64,1024]{1,0:T(8,128)(2,1)S(1)}, bf16[64,1024]{1,0:T(8,128)(2,1)S(1)}, u32[]{:S(2)}, u32[]{:S(2)}) collective-permute-start(bf16[64,1024]{1,0:T(8,128)(2,1)S(1)} %get-tuple-element.82), channel_id=1, source_target_pairs={{0,12},{4,0},{8,4},{12,8},{1,13},{5,1},{9,5},{13,9},{2,14},{6,2},{... | collective-permute-start | bytes 393224 | tf_op jit(solution)/shard_map/ppermute | solution.py:32
  28.4 7.4 %collective-permute-start.13 = (bf16[16,1024]{1,0:T(8,128)(2,1)S(1)}, bf16[16,1024]{1,0:T(8,128)(2,1)S(1)}, u32[]{:S(2)}, u32[]{:S(2)}) collective-permute-start(bf16[16,1024]{1,0:T(8,128)(2,1)S(1)} %get-tuple-element.89), channel_id=1, source_target_pairs={{0,1},{1,2},{2,3},{3,0},{4,5},{5,6},{6,7},{7,4},{8,9},{9,10},{10,1... | collective-permute-start | bytes 98312 | tf_op jit(solution)/shard_map/ppermute | solution.py:32
  30.3 5.5 %collective-permute-start.14 = (bf16[16,1024]{1,0:T(8,128)(2,1)S(1)}, bf16[16,1024]{1,0:T(8,128)(2,1)S(1)}, u32[]{:S(2)}, u32[]{:S(2)}) collective-permute-start(bf16[16,1024]{1,0:T(8,128)(2,1)S(1)} %get-tuple-element.90), channel_id=1, source_target_pairs={{0,2},{1,3},{2,0},{3,1},{4,6},{5,7},{6,4},{7,5},{8,10},{9,11},{10,... | collective-permute-start | bytes 98312 | tf_op jit(solution)/shard_map/ppermute | solution.py:32
  32.9 3.9 %collective-permute-start.15 = (bf16[16,1024]{1,0:T(8,128)(2,1)S(1)}, bf16[16,1024]{1,0:T(8,128)(2,1)S(1)}, u32[]{:S(2)}, u32[]{:S(2)}) collective-permute-start(bf16[16,1024]{1,0:T(8,128)(2,1)S(1)} %get-tuple-element.91), channel_id=1, source_target_pairs={{0,3},{1,0},{2,1},{3,2},{4,7},{5,4},{6,5},{7,6},{8,11},{9,8},{10,9... | collective-permute-start | bytes 98312 | tf_op jit(solution)/shard_map/ppermute | solution.py:32
